TPU v7x, 512 devices: a whole 4x8x8 slice. The times are simulated.
512 devices in a mesh: dom: 32 (over z, x), tm: 16 (over y, core).
Axes of the slice: x: 4, y: 8, z: 8, core: 2. Of those that a mesh axis runs over, the one named last changes fastest.
Arguments:
- signal: bfloat16 [8, 512, 65536], P(None, 'tm', 'dom'), may hold values from -6 to 6
- weights: bfloat16 [512, 5, 128, 128], P('dom'), may hold values from 0 to 10.5, as said below
- send_list: int32 [32, 4, 3], P('dom'), may hold values from 0 to 15, as said below
- col_ref: int32 [512, 5], P('dom'), may hold values from 0 to 27, as said below
- kernel: bfloat16 [512, 512], P('tm'), may hold values from -0.2 to 1.6
- cheb_coef: float32 [3], replicated, may hold values from 0.5 to 1.5
Outputs:
- filtered: bfloat16 [8, 512, 65536], P(None, 'tm', 'dom')
Inputs may be any that keep to these rules, and one draw needn't show every extreme that they name: `send_list`: for each q and k the 3 entries are distinct block rows of partition q. col_ref[g, 0] = g % 16. An entry e >= 16 of partition p names partition q = p + d_k (k = (e - 16) // 3), which always exists; for each p and k the slots s used run from 0 up to some count of at most 3, every such slot is used by some block row of p, and some partition uses all 3 from some k. `weights`: Nonnegative; every diagonal entry of slot 0 blocks is 0.5 or more.
All inputs are finite; a program needn't handle non-finite values.
Results may differ from a plain program's by a relative error of at most 0.023.
Values may be sent and summed in bfloat16 or wider, within the bound.
No kernel may reach another device: no remote copies, remote signals or barrier semaphores. Data moves between devices by JAX's collectives and lax.ppermute only.
A program may use at most 64 MiB of HBM per device.

v0:
```python
import jax
import jax.numpy as jnp
from jax import lax
from jax.sharding import PartitionSpec as P

REACH = 2


def from_behind(block, axis, distance):
    devices = range(lax.axis_size(axis))
    route = [(i - distance, i) for i in devices if i - distance in devices]
    return lax.ppermute(block, axis, route)


def body(signal, weights, send_list, col_ref, kernel, cheb_coef):
    probes, t_loc, n_loc = signal.shape
    blocks_here = weights.shape[0]
    block_size = weights.shape[2]
    row_count = probes * t_loc
    degree = jnp.sum(weights, axis=(1, 3), dtype=jnp.float32)
    inv_root = lax.rsqrt(degree)[:, None, :]
    signal_blocks = signal.reshape(row_count, blocks_here, block_size).transpose(1, 0, 2)
    offsets = list(range(-REACH, 0)) + list(range(1, REACH + 1))
    send_rows = send_list[0]

    def neighbour_product(field):
        scaled = (field.astype(jnp.float32) * inv_root).astype(jnp.bfloat16)
        received = []
        for way_index, distance in enumerate(offsets):
            outgoing = jnp.take(scaled, send_rows[way_index], axis=0)
            received.append(from_behind(outgoing, "dom", -distance))
        source = jnp.concatenate([scaled] + received, axis=0)
        picked = jnp.take(source, col_ref, axis=0)
        return jnp.einsum("bjrm,bjnm->brn", picked, weights, preferred_element_type=jnp.float32)

    first_sum = neighbour_product(signal_blocks)
    term_one = (-inv_root * first_sum).astype(jnp.bfloat16)
    second_sum = neighbour_product(term_one)
    term_two = (-2.0 * inv_root * second_sum - signal_blocks.astype(jnp.float32)).astype(
        jnp.bfloat16
    )
    combined_field = (
        cheb_coef[0] * signal_blocks.astype(jnp.float32)
        + cheb_coef[1] * term_one.astype(jnp.float32)
        + cheb_coef[2] * term_two.astype(jnp.float32)
    ).astype(jnp.bfloat16)
    time_whole = lax.all_to_all(
        combined_field.transpose(1, 0, 2).reshape(probes, t_loc, n_loc),
        "tm",
        split_axis=2,
        concat_axis=1,
        tiled=True,
    )
    filtered_whole = jnp.einsum(
        "ut,ptn->pun",
        lax.all_gather(kernel, "tm", axis=0, tiled=True),
        time_whole,
        preferred_element_type=jnp.float32,
    ).astype(jnp.bfloat16)
    return lax.all_to_all(filtered_whole, "tm", split_axis=1, concat_axis=2, tiled=True)


def solution(mesh):
    in_specs = (
        P(None, "tm", "dom"),
        P("dom", None, None, None),
        P("dom", None, None),
        P("dom", None),
        P("tm", None),
        P(),
    )
    out_specs = P(None, "tm", "dom")
    return jax.shard_map(body, mesh=mesh, in_specs=in_specs, out_specs=out_specs, check_vma=False)
```

profile of v0, /device:TPU:133, one launch (start us, length us, event | category | flops | bytes accessed | tf_op | source)
XLA Modules:
  0.0 193.9 jit_solution(8609952959684335362)
XLA Ops:
  0.0 1.2 slice_reduce_fusion
  1.2 2.2 %convert_reduce_fusion = f32[16,128]{1,0:T(8,128)S(1)} fusion(bf16[16,5,128,128]{3,2,1,0:T(8,128)(2,1)} %param.11), kind=kLoop, calls=%fused_computation.14 | loop fusion | flops 2619392 | bytes 2629632 | tf_op jit(solution)/shard_map/reduce_sum | solution.py:20
  3.4 0.0 copy-done.1
  3.4 0.3 copy.58
  3.7 0.0 copy-start
  3.7 0.8 constant_dynamic-update-slice_fusion.4
  4.6 0.5 copy-done
  5.1 0.6 gather_fusion
  5.7 0.1 broadcast_select_fusion.7
  5.7 3.9 %collective-permute-start = (bf16[3,256,128]{2,1,0:T(8,128)(2,1)S(1)}, bf16[3,256,128]{2,1,0:T(8,128)(2,1)S(1)}, u32[]{:S(2)}, u32[]{:S(2)}) collective-permute-start(bf16[3,256,128]{2,1,0:T(8,128)(2,1)S(1)} %broadcast_select_fusion.7), channel_id=1, source_target_pairs={{0,32},{16,48},{32,64},{48,80},{64,96},{80,112},{96,128},{112,144}... | collective-permute-start | bytes 589832 | tf_op jit(solution)/shard_map/ppermute | solution.py:12
  9.7 0.6 gather_fusion.1
  10.3 0.8 broadcast_select_fusion.5
  11.1 3.7 %collective-permute-start.1 = (bf16[3,256,128]{2,1,0:T(8,128)(2,1)}, bf16[3,256,128]{2,1,0:T(8,128)(2,1)}, u32[]{:S(2)}, u32[]{:S(2)}) collective-permute-start(bf16[3,256,128]{2,1,0:T(8,128)(2,1)} %broadcast_select_fusion.5), channel_id=1, source_target_pairs={{0,16},{16,32},{32,48},{48,64},{64,80},{80,96},{96,112},{112,128},... | collective-permute-start | bytes 589832 | tf_op jit(solution)/shard_map/ppermute | solution.py:12
  14.8 0.6 gather_fusion.2
  15.4 0.8 broadcast_select_fusion.3
  16.2 1.9 collective-permute-start.2
  18.1 0.6 gather_fusion.3
  18.7 0.1 broadcast_select_fusion.1
  18.8 4.6 %collective-permute-start.3 = (bf16[3,256,128]{2,1,0:T(8,128)(2,1)S(1)}, bf16[3,256,128]{2,1,0:T(8,128)(2,1)S(1)}, u32[]{:S(2)}, u32[]{:S(2)}) collective-permute-start(bf16[3,256,128]{2,1,0:T(8,128)(2,1)S(1)} %broadcast_select_fusion.1), channel_id=1, source_target_pairs={{32,0},{48,16},{64,32},{80,48},{96,64},{112,80},{128,96},{144,112}... | collective-permute-start | bytes 589832 | tf_op jit(solution)/shard_map/ppermute | solution.py:12
  23.4 0.0 copy-done.3
  23.4 0.1 copy.38
  23.5 0.1 reshape.139
  23.6 0.1 copy.36
  23.7 0.0 copy-done.4
  23.7 0.7 fusion.26
  24.4 0.0 collective-permute-done
  24.4 0.0 collective-permute-done.1
  24.4 1.0 constant_dynamic-update-slice_fusion.2
  25.4 0.0 collective-permute-done.2
  25.4 1.0 constant_dynamic-update-slice_fusion.1
  26.4 4.3 %collective-permute-done.3 = bf16[3,256,128]{2,1,0:T(8,128)(2,1)S(1)} collective-permute-done((bf16[3,256,128]{2,1,0:T(8,128)(2,1)S(1)}, bf16[3,256,128]{2,1,0:T(8,128)(2,1)S(1)}, u32[]{:S(2)}, u32[]{:S(2)}) %collective-permute-start.3) | collective-permute-done | bytes 196640 | tf_op jit(solution)/shard_map/ppermute | solution.py:12
  30.7 5.7 %gather_fusion.4 = bf16[80,256,128]{2,1,0:T(8,128)(2,1)} fusion(bf16[28,256,128]{2,1,0:T(8,128)(2,1)S(1)} %constant_dynamic-update-slice_fusion, s32[1024]{0:T(1024)S(1)} %pad_clamp_fusion), kind=kCustom, calls=%fused_computation.1.clone | custom fusion | bytes 10486080 | tf_op jit(solution)/shard_map/jit(_take)/gather | solution.py:33
  36.4 6.2 %constant_dynamic-update-slice_fusion.9 = (bf16[28,256,128]{2,1,0:T(8,128)(2,1)S(1)}, bf16[16,256,128]{2,1,0:T(8,128)(2,1)}, bf16[16,256,128]{2,1,0:T(8,128)(2,1)}) fusion(f32[16,128]{1,0:T(8,128)S(1)} %get-tuple-element.17, bf16[16,5,128,128]{3,2,1,0:T(8,128)(2,1)} %param.11, bf16[16,5,256,128]{3,2,1,0:T(8,128)(2,1)} %bitcast.65, ...), kind=kOutput, calls=%fused_computation.53 | convolution fusion | flops 676331520 | bytes 11026512 | tf_op jit(solution)/shard_map/bjrm,bjnm->brn/dot_general | solution.py:34
  42.6 1.8 gather_fusion.5
  44.4 1.8 gather_fusion.6
  46.2 1.8 gather_fusion.7
  48.0 1.8 gather_fusion.8
  49.9 0.1 broadcast_select_fusion.6
  50.0 2.8 %collective-permute-start.4 = (bf16[3,256,128]{2,1,0:T(8,128)(2,1)S(1)}, bf16[3,256,128]{2,1,0:T(8,128)(2,1)S(1)}, u32[]{:S(2)}, u32[]{:S(2)}) collective-permute-start(bf16[3,256,128]{2,1,0:T(8,128)(2,1)S(1)} %broadcast_select_fusion.6), channel_id=1, source_target_pairs={{0,32},{16,48},{32,64},{48,80},{64,96},{80,112},{96,128},{112,144}... | collective-permute-start | bytes 589832 | tf_op jit(solution)/shard_map/ppermute | solution.py:12
  52.7 0.1 broadcast_select_fusion.4
  52.8 4.6 %collective-permute-start.5 = (bf16[3,256,128]{2,1,0:T(8,128)(2,1)S(1)}, bf16[3,256,128]{2,1,0:T(8,128)(2,1)S(1)}, u32[]{:S(2)}, u32[]{:S(2)}) collective-permute-start(bf16[3,256,128]{2,1,0:T(8,128)(2,1)S(1)} %broadcast_select_fusion.4), channel_id=1, source_target_pairs={{0,16},{16,32},{32,48},{48,64},{64,80},{80,96},{96,112},{112,128},... | collective-permute-start | bytes 589832 | tf_op jit(solution)/shard_map/ppermute | solution.py:12
  57.5 0.1 broadcast_select_fusion.2
  57.6 1.9 collective-permute-start.6
  59.5 0.1 broadcast_select_fusion
  59.6 5.0 %collective-permute-start.7 = (bf16[3,256,128]{2,1,0:T(8,128)(2,1)S(1)}, bf16[3,256,128]{2,1,0:T(8,128)(2,1)S(1)}, u32[]{:S(2)}, u32[]{:S(2)}) collective-permute-start(bf16[3,256,128]{2,1,0:T(8,128)(2,1)S(1)} %broadcast_select_fusion), channel_id=1, source_target_pairs={{32,0},{48,16},{64,32},{80,48},{96,64},{112,80},{128,96},{144,112}... | collective-permute-start | bytes 589832 | tf_op jit(solution)/shard_map/ppermute | solution.py:12
  64.6 0.0 collective-permute-done.4
  64.7 0.0 collective-permute-done.5
  64.7 2.3 %collective-permute-done.6 = bf16[3,256,128]{2,1,0:T(8,128)(2,1)S(1)} collective-permute-done((bf16[3,256,128]{2,1,0:T(8,128)(2,1)S(1)}, bf16[3,256,128]{2,1,0:T(8,128)(2,1)S(1)}, u32[]{:S(2)}, u32[]{:S(2)}) %collective-permute-start.6) | collective-permute-done | bytes 196640 | tf_op jit(solution)/shard_map/ppermute | solution.py:12
  67.0 5.7 %collective-permute-done.7 = bf16[3,256,128]{2,1,0:T(8,128)(2,1)S(1)} collective-permute-done((bf16[3,256,128]{2,1,0:T(8,128)(2,1)S(1)}, bf16[3,256,128]{2,1,0:T(8,128)(2,1)S(1)}, u32[]{:S(2)}, u32[]{:S(2)}) %collective-permute-start.7) | collective-permute-done | bytes 196640 | tf_op jit(solution)/shard_map/ppermute | solution.py:12
  72.8 5.7 %gather_fusion.9 = bf16[80,256,128]{2,1,0:T(8,128)(2,1)} fusion(bf16[28,256,128]{2,1,0:T(8,128)(2,1)S(1)} %constant_dynamic-update-slice_fusion.5, s32[1024]{0:T(1024)S(1)} %pad_clamp_fusion), kind=kCustom, calls=%fused_computation.9.clone | custom fusion | bytes 10486080 | tf_op jit(solution)/shard_map/jit(_take)/gather | solution.py:33
  78.5 8.2 %fusion.11 = bf16[256,16,128]{2,0,1:T(8,128)(2,1)S(1)} fusion(bf16[16,256,128]{2,1,0:T(8,128)(2,1)} %get-tuple-element.21, f32[256,16,128]{2,1,0:T(8,128)} %bitcast.63, bf16[16,5,128,128]{3,2,1,0:T(8,128)(2,1)} %param.11, bf16[16,5,256,128]{3,2,1,0:T(8,128)(2,1)} %bitcast.64, pred[16,5]{1,0:T(8,128)(4,1)S(1)} %copy.36, ...), kind=kOutput, calls=%fused_computation.24 | convolution fusion | flops 679477248 | bytes 12066908 | tf_op jit(solution)/shard_map/bjrm,bjnm->brn/dot_general | solution.py:34
  86.7 0.5 copy.53
  87.2 3.4 %reshape.158 = bf16[8,32,2048]{1,0,2:T(8,128)(2,1)} reshape(bf16[256,16,128]{0,2,1:T(8,128)(2,1)S(1)} %copy.53) | data formatting | bytes 2097152 | tf_op jit(solution)/shard_map/reshape | solution.py:48
  90.6 7.4 %reshape.163 = bf16[16,2,16384]{2,1,0:T(2,128)(2,1)} reshape(bf16[2048,8,32]{2,1,0:T(8,128)(2,1)} %bitcast.60) | data formatting | bytes 2097152
  98.0 11.3 %all-to-all-start = ((bf16[16,2,16384]{2,1,0:T(2,128)(2,1)}), bf16[16,2,16384]{2,1,0:T(2,128)(2,1)S(1)}, u32[]{:S(2)}, u32[]{:S(2)}) async-start(bf16[16,2,16384]{2,1,0:T(2,128)(2,1)} %reshape.163), calls=%async_computation | async-start | bytes 2097152 | tf_op jit(solution)/shard_map/all_to_all | solution.py:47
  109.4 38.6 %all_gather.3 = bf16[512,512]{1,0:T(8,128)(2,1)S(1)} all-gather(bf16[32,512]{1,0:T(8,128)(2,1)S(1)} %copy-done.2), channel_id=1, replica_groups=mesh['dom'=32,'tm'=16] {'tm'}, dimensions={0}, use_global_device_ids=true | all-gather | bytes 557056 | tf_op jit(solution)/shard_map/all_gather | solution.py:56
  148.0 0.0 all-to-all-done
  148.0 3.5 %reshape.164 = bf16[2048,8,32]{2,1,0:T(8,128)(2,1)} reshape(bf16[16,2,16384]{2,1,0:T(2,128)(2,1)S(1)} %all-to-all-done) | data formatting | bytes 2097152
  151.5 4.5 %copy.45 = bf16[8,16,32,128]{3,2,1,0:T(8,128)(2,1)S(1)} copy(bf16[8,16,32,128]{2,0,3,1:T(8,128)(2,1)} %bitcast.61) | data formatting | bytes 2097152 | tf_op jit(solution)/shard_map/all_to_all | solution.py:47
  156.1 0.8 fusion.19
  156.8 0.8 copy.47
  157.6 34.3 %all_to_all.36 = bf16[8,512,128]{2,0,1:T(8,128)(2,1)S(1)} all-to-all(bf16[8,512,128]{2,0,1:T(8,128)(2,1)S(1)} %copy.47), channel_id=1, replica_groups=mesh['dom'=32,'tm'=16] {'tm'}, dimensions={1} | all-to-all | bytes 2097152 | tf_op jit(solution)/shard_map/all_to_all | solution.py:60
  191.9 0.7 copy.49
  192.6 1.3 all_to_all.33
  (25 shorter events, 0.3 us)
Async XLA Ops:
  0.0 3.4 %copy-start.1 = (bf16[8,32,2048]{2,1,0:T(8,128)(2,1)S(1)}, bf16[8,32,2048]{2,1,0:T(8,128)(2,1)}, u32[]{:S(2)}) copy-start(bf16[8,32,2048]{2,1,0:T(8,128)(2,1)} %param.10) | copy-start | bytes 3145732
  3.7 1.4 copy-start
  5.1 18.3 %copy-start.3 = (s32[16,5]{0,1:T(8,128)S(1)}, s32[16,5]{0,1:T(8,128)}, u32[]{:S(2)}) copy-start(s32[16,5]{0,1:T(8,128)} %param.13) | copy-start | bytes 964
  5.1 18.7 %copy-start.4 = (f32[3]{0:T(128)S(1)}, f32[3]{0:T(128)}, u32[]{:S(2)}) copy-start(f32[3]{0:T(128)} %param.15) | copy-start | bytes 40
  5.7 18.6 %collective-permute-start = (bf16[3,256,128]{2,1,0:T(8,128)(2,1)S(1)}, bf16[3,256,128]{2,1,0:T(8,128)(2,1)S(1)}, u32[]{:S(2)}, u32[]{:S(2)}) collective-permute-start(bf16[3,256,128]{2,1,0:T(8,128)(2,1)S(1)} %broadcast_select_fusion.7), channel_id=1, source_target_pairs={{0,32},{16,48},{32,64},{48,80},{64,96},{80,112},{96,128},{112,144}... | collective-permute-start | bytes 589832 | tf_op jit(solution)/shard_map/ppermute | solution.py:12
  11.1 13.4 %collective-permute-start.1 = (bf16[3,256,128]{2,1,0:T(8,128)(2,1)}, bf16[3,256,128]{2,1,0:T(8,128)(2,1)}, u32[]{:S(2)}, u32[]{:S(2)}) collective-permute-start(bf16[3,256,128]{2,1,0:T(8,128)(2,1)} %broadcast_select_fusion.5), channel_id=1, source_target_pairs={{0,16},{16,32},{32,48},{48,64},{64,80},{80,96},{96,112},{112,128},... | collective-permute-start | bytes 589832 | tf_op jit(solution)/shard_map/ppermute | solution.py:12
  16.2 9.2 %collective-permute-start.2 = (bf16[3,256,128]{2,1,0:T(8,128)(2,1)}, bf16[3,256,128]{2,1,0:T(8,128)(2,1)}, u32[]{:S(2)}, u32[]{:S(2)}) collective-permute-start(bf16[3,256,128]{2,1,0:T(8,128)(2,1)} %broadcast_select_fusion.3), channel_id=1, source_target_pairs={{16,0},{32,16},{48,32},{64,48},{80,64},{96,80},{112,96},{128,112},... | collective-permute-start | bytes 589832 | tf_op jit(solution)/shard_map/ppermute | solution.py:12
  18.8 11.9 %collective-permute-start.3 = (bf16[3,256,128]{2,1,0:T(8,128)(2,1)S(1)}, bf16[3,256,128]{2,1,0:T(8,128)(2,1)S(1)}, u32[]{:S(2)}, u32[]{:S(2)}) collective-permute-start(bf16[3,256,128]{2,1,0:T(8,128)(2,1)S(1)} %broadcast_select_fusion.1), channel_id=1, source_target_pairs={{32,0},{48,16},{64,32},{80,48},{96,64},{112,80},{128,96},{144,112}... | collective-permute-start | bytes 589832 | tf_op jit(solution)/shard_map/ppermute | solution.py:12
  50.0 14.7 %collective-permute-start.4 = (bf16[3,256,128]{2,1,0:T(8,128)(2,1)S(1)}, bf16[3,256,128]{2,1,0:T(8,128)(2,1)S(1)}, u32[]{:S(2)}, u32[]{:S(2)}) collective-permute-start(bf16[3,256,128]{2,1,0:T(8,128)(2,1)S(1)} %broadcast_select_fusion.6), channel_id=1, source_target_pairs={{0,32},{16,48},{32,64},{48,80},{64,96},{80,112},{96,128},{112,144}... | collective-permute-start | bytes 589832 | tf_op jit(solution)/shard_map/ppermute | solution.py:12
  52.8 11.8 %collective-permute-start.5 = (bf16[3,256,128]{2,1,0:T(8,128)(2,1)S(1)}, bf16[3,256,128]{2,1,0:T(8,128)(2,1)S(1)}, u32[]{:S(2)}, u32[]{:S(2)}) collective-permute-start(bf16[3,256,128]{2,1,0:T(8,128)(2,1)S(1)} %broadcast_select_fusion.4), channel_id=1, source_target_pairs={{0,16},{16,32},{32,48},{48,64},{64,80},{80,96},{96,112},{112,128},... | collective-permute-start | bytes 589832 | tf_op jit(solution)/shard_map/ppermute | solution.py:12
  57.6 9.4 %collective-permute-start.6 = (bf16[3,256,128]{2,1,0:T(8,128)(2,1)S(1)}, bf16[3,256,128]{2,1,0:T(8,128)(2,1)S(1)}, u32[]{:S(2)}, u32[]{:S(2)}) collective-permute-start(bf16[3,256,128]{2,1,0:T(8,128)(2,1)S(1)} %broadcast_select_fusion.2), channel_id=1, source_target_pairs={{16,0},{32,16},{48,32},{64,48},{80,64},{96,80},{112,96},{128,112},... | collective-permute-start | bytes 589832 | tf_op jit(solution)/shard_map/ppermute | solution.py:12
  59.6 13.2 %collective-permute-start.7 = (bf16[3,256,128]{2,1,0:T(8,128)(2,1)S(1)}, bf16[3,256,128]{2,1,0:T(8,128)(2,1)S(1)}, u32[]{:S(2)}, u32[]{:S(2)}) collective-permute-start(bf16[3,256,128]{2,1,0:T(8,128)(2,1)S(1)} %broadcast_select_fusion), channel_id=1, source_target_pairs={{32,0},{48,16},{64,32},{80,48},{96,64},{112,80},{128,96},{144,112}... | collective-permute-start | bytes 589832 | tf_op jit(solution)/shard_map/ppermute | solution.py:12
  98.0 11.3 %copy-start.2 = (bf16[32,512]{1,0:T(8,128)(2,1)S(1)}, bf16[32,512]{1,0:T(8,128)(2,1)}, u32[]{:S(2)}) copy-start(bf16[32,512]{1,0:T(8,128)(2,1)} %param.14) | copy-start | bytes 98308
  98.0 50.0 %all-to-all-start = ((bf16[16,2,16384]{2,1,0:T(2,128)(2,1)}), bf16[16,2,16384]{2,1,0:T(2,128)(2,1)S(1)}, u32[]{:S(2)}, u32[]{:S(2)}) async-start(bf16[16,2,16384]{2,1,0:T(2,128)(2,1)} %reshape.163), calls=%async_computation | async-start | bytes 2097152 | tf_op jit(solution)/shard_map/all_to_all | solution.py:47
where the time goes:
time: 195 us; the launch traced here: 194 us
  blocking collectives  73 us (37%)
  local copies, waits for them, and re-layouts  48 us (25%)
  starting transfers between devices  39.9 us (20%)
  matrix products  15.2 us (8%)
  waiting for transfers between devices  12.4 us (6%)
  other arithmetic  5.12 us (3%)
    all_gather x1, blocking collectives, body(): lax.all_gather(kernel, 'tm', axis=0, tiled=True)  38.6 us
    all_to_all x1, blocking collectives, body(): lax.all_to_all(filtered_whole, 'tm', split_axis=1, concat_axis=2, tiled=T...  34.3 us
    ppermute x8, starting transfers between devices, from_behind(): return lax.ppermute(block, axis, route)  28.5 us
    dot_general x2, matrix products, neighbour_product(): jnp.einsum('bjrm,bjnm->brn', picked, weights, preferred_element_type=jnp....  14.4 us
    unnamed x19, local copies, waits for them, and re-layouts  13.8 us
    ppermute x8, waiting for transfers between devices, from_behind(): return lax.ppermute(block, axis, route)  12.4 us
    all_to_all x1, starting transfers between devices, body(): lax.all_to_all(combined_field.transpose(1, 0, 2).reshape(probes, t_loc, n...  11.3 us
    gather x2, local copies, waits for them, and re-layouts, neighbour_product(): picked = jnp.take(source, col_ref, axis=0)  11.3 us
  transfers between devices with their start and end apart: 9, of which 3 were waited for; matrix products, arithmetic and copies ran while one was open for 3% of the time, Pallas kernels for 0%

commit v1 on v0

v1 whole, which is shorter than its diff:
```python
import functools

import jax
import jax.numpy as jnp
from jax import lax
from jax.experimental import pallas as pl
from jax.experimental.pallas import tpu as pltpu
from jax.sharding import PartitionSpec as P

REACH = 2
OFFSETS = tuple(range(-REACH, 0)) + tuple(range(1, REACH + 1))
F32, BF16 = jnp.float32, jnp.bfloat16
VMEM = pl.BlockSpec(memory_space=pltpu.VMEM)
SMEM = pl.BlockSpec(memory_space=pltpu.SMEM)
LIMIT = 24 * 2**20


def call(kernel, outs, ins, scratch=(), flops=0, name=None):
    size = sum(a.size * a.dtype.itemsize for a in (*ins, *outs))
    specs = [SMEM if a.dtype == jnp.int32 or a.size < 8 else VMEM for a in ins]
    return pl.pallas_call(
        kernel,
        out_shape=outs,
        in_specs=specs,
        out_specs=[VMEM] * len(outs),
        scratch_shapes=list(scratch),
        compiler_params=pltpu.CompilerParams(vmem_limit_bytes=LIMIT),
        cost_estimate=pl.CostEstimate(flops=flops, bytes_accessed=size, transcendentals=0),
        name=name,
    )(*ins)


def array(*shape, dtype=BF16):
    return jax.ShapeDtypeStruct(shape, dtype)


def times_transposed(a, b):
    return lax.dot_general(a, b, (((1,), (1,)), ((), ())), preferred_element_type=F32)


def pack(send_ref, field_ref, packs):
    for way, out in enumerate(packs):
        for slot in range(out.shape[0]):
            out[slot] = field_ref[send_ref[0, way, slot]]


def first_scale(signal_ref, weights_ref, send_ref, scaled_ref, inv_ref, *packs):
    blocks, per_row, width, _ = weights_ref.shape
    ones = jnp.ones((16, width), BF16)
    for g in range(blocks):
        degree = times_transposed(ones, weights_ref[g, 0])
        for j in range(1, per_row):
            degree += times_transposed(ones, weights_ref[g, j])
        inv = lax.rsqrt(degree[:1])
        inv_ref[g : g + 1, :] = inv
        x = signal_ref[:, g * width : (g + 1) * width].astype(F32)
        scaled_ref[g] = (x * inv).astype(BF16)
    pack(send_ref, scaled_ref, packs)


def gather_sources(scaled_ref, received, source):
    blocks = scaled_ref.shape[0]
    source[:blocks] = scaled_ref[...]
    for way, ref in enumerate(received):
        slots = ref.shape[0]
        source[blocks + way * slots : blocks + (way + 1) * slots] = ref[...]


def block_product(g, col_ref, weights_ref, source):
    per_row = weights_ref.shape[1]
    picked = jnp.concatenate([source[col_ref[g, j]] for j in range(per_row)], axis=1)
    edges = jnp.concatenate([weights_ref[g, j] for j in range(per_row)], axis=1)
    return times_transposed(picked, edges)


def first_product(scaled_ref, r0, r1, r2, r3, weights_ref, inv_ref, col_ref, send_ref, term_ref, next_ref, *rest):
    *packs, source = rest
    gather_sources(scaled_ref, (r0, r1, r2, r3), source)
    for g in range(weights_ref.shape[0]):
        inv = inv_ref[g : g + 1, :]
        term = (-inv * block_product(g, col_ref, weights_ref, source)).astype(BF16)
        term_ref[g] = term
        next_ref[g] = (inv * term.astype(F32)).astype(BF16)
    pack(send_ref, next_ref, packs)


def second_product(next_ref, r0, r1, r2, r3, weights_ref, inv_ref, col_ref, coef_ref, signal_ref, term_ref, mixed_ref, source):
    width = weights_ref.shape[2]
    gather_sources(next_ref, (r0, r1, r2, r3), source)
    for g in range(weights_ref.shape[0]):
        inv = inv_ref[g : g + 1, :]
        total = block_product(g, col_ref, weights_ref, source)
        x = signal_ref[:, g * width : (g + 1) * width].astype(F32)
        two = (-2.0 * inv * total - x).astype(BF16).astype(F32)
        one = term_ref[g].astype(F32)
        mixed_ref[g] = (coef_ref[0] * x + coef_ref[1] * one + coef_ref[2] * two).astype(BF16)


def temporal(t_loc, field_ref, kernel_ref, out_ref, whole):
    owners, rows, width = field_ref.shape
    mix = kernel_ref[...].astype(BF16)
    for p in range(rows // t_loc):
        part = slice(p * t_loc, (p + 1) * t_loc)
        for i in range(owners):
            whole[i * t_loc : (i + 1) * t_loc, p * width : (p + 1) * width] = field_ref[i, part]
    step = 2 * width
    for c in range(whole.shape[1] // step):
        out = jnp.dot(mix, whole[:, c * step : (c + 1) * step], preferred_element_type=F32).astype(BF16)
        for q in range(step // width):
            p = c * (step // width) + q
            for i in range(owners):
                out_ref[i, p * t_loc : (p + 1) * t_loc] = out[i * t_loc : (i + 1) * t_loc, q * width : (q + 1) * width]


def unblock(field_ref, out_ref):
    blocks, _, width = field_ref.shape
    for g in range(blocks):
        out_ref[:, g * width : (g + 1) * width] = field_ref[g]


def halo(packs):
    count = lax.axis_size("dom")
    return [
        lax.ppermute(block, "dom", [(i, (i - distance) % count) for i in range(count)])
        for block, distance in zip(packs, OFFSETS)
    ]


def exchange(field):
    return lax.all_to_all(field, "tm", split_axis=0, concat_axis=0, tiled=True)


def body(signal, weights, send_list, col_ref, kernel, cheb_coef):
    probes, t_loc, n_loc = signal.shape
    blocks, per_row, width, _ = weights.shape
    rows = probes * t_loc
    slots = send_list.shape[2]
    owners = lax.axis_size("tm")
    time = kernel.shape[1]
    xs = signal.reshape(rows, n_loc)
    field = array(blocks, rows, width)
    packed = [array(slots, rows, width)] * len(OFFSETS)
    source = pltpu.VMEM((blocks + len(OFFSETS) * slots, rows, width), BF16)
    work = 2 * rows * per_row * n_loc * width

    mix = lax.all_gather(kernel.astype(F32), "tm", axis=0, tiled=True)
    scaled, inv, *packs = call(
        first_scale, [field, array(blocks, width, dtype=F32), *packed], (xs, weights, send_list), flops=work // 16
    )
    term, nxt, *packs = call(
        first_product,
        [field, field, *packed],
        (scaled, *halo(packs), weights, inv, col_ref, send_list),
        [source],
        flops=work,
    )
    (mixed,) = call(
        second_product, [field], (nxt, *halo(packs), weights, inv, col_ref, cheb_coef, xs, term), [source], flops=work
    )
    (filtered,) = call(
        functools.partial(temporal, t_loc),
        [array(owners, rows, width)],
        (exchange(mixed), mix),
        [pltpu.VMEM((time, probes * width), BF16)],
        flops=2 * time * time * probes * width,
    )
    (out,) = call(unblock, [array(rows, n_loc)], (exchange(filtered),))
    return out.reshape(probes, t_loc, n_loc)


def solution(mesh):
    in_specs = (
        P(None, "tm", "dom"),
        P("dom", None, None, None),
        P("dom", None, None),
        P("dom", None),
        P("tm", None),
        P(),
    )
    out_specs = P(None, "tm", "dom")
    return jax.shard_map(body, mesh=mesh, in_specs=in_specs, out_specs=out_specs, check_vma=False)
```

time: 195 us -> 160 us (0.82)
  the two profiles are of different devices: /device:TPU:133 before, /device:TPU:1 now
where the time goes in v1:
time: 160 us; the launch traced here: 159 us
  starting transfers between devices  46 us (29%)
  waiting for transfers between devices  41 us (26%)
  blocking collectives  33.3 us (21%)
  local copies, waits for them, and re-layouts  13.8 us (9%)
  between operations  13.5 us (8%)
  Pallas kernels  10.6 us (7%)
    ppermute x8, starting transfers between devices, halo(): lax.ppermute(block, 'dom', [(i, (i - distance) % count) for i in range(co...  36.9 us
    all_to_all x1, blocking collectives, exchange(): return lax.all_to_all(field, 'tm', split_axis=0, concat_axis=0, tiled=True)  33.3 us
    all_gather x1, waiting for transfers between devices, body(): mix = lax.all_gather(kernel.astype(F32), 'tm', axis=0, tiled=True)  31 us
    unnamed x32, local copies, waits for them, and re-layouts  13.8 us
    pallas_call x5, Pallas kernels, call(): pl.pallas_call(kernel, out_shape=outs, in_specs=specs, out_specs=[VMEM] *...  10.6 us
    ppermute x8, waiting for transfers between devices, halo(): lax.ppermute(block, 'dom', [(i, (i - distance) % count) for i in range(co...  9.81 us
    all_to_all x1, starting transfers between devices, exchange(): return lax.all_to_all(field, 'tm', split_axis=0, concat_axis=0, tiled=True)  9.18 us
  transfers between devices with their start and end apart: 10, of which 6 were waited for; matrix products, arithmetic and copies ran while one was open for 0% of the time, Pallas kernels for 1%

profile of v1, /device:TPU:1, one launch (start us, length us, event | category | flops | bytes accessed | tf_op | source)
XLA Modules:
  0.0 158.9 jit_solution(14672837190156402278)
XLA Ops:
  6.5 0.0 copy-start.14
  6.5 0.0 all-gather.2.cloned.1.call-start
  6.5 0.8 copy.7.send_ref
  7.3 0.0 copy-start
  7.3 1.7 %copy-done = bf16[16,5,128,128]{3,2,1,0:T(8,128)(2,1)S(1)} copy-done((bf16[16,5,128,128]{3,2,1,0:T(8,128)(2,1)S(1)}, bf16[16,5,128,128]{3,2,1,0:T(8,128)(2,1)}, u32[]{:S(2)}) %copy-start) | copy-done | bytes 2621464
  9.1 0.0 copy-start.2
  9.1 1.2 copy-done.2
  10.3 0.0 copy-start.1
  10.3 0.0 copy-start.13
  10.3 3.0 %shard_map.64 = (bf16[16,256,128]{2,1,0:T(8,128)(2,1)S(1)}, f32[16,128]{1,0:T(8,128)S(1)}, bf16[3,256,128]{2,1,0:T(8,128)(2,1)}, bf16[3,256,128]{2,1,0:T(8,128)(...) custom-call(bf16[256,2048]{1,0:T(8,128)(2,1)S(1)} %bitcast.2, bf16[16,5,128,128]{3,2,1,0:T(8,128)(2,1)S(1)} %copy-done, ...), custom_call_target="tpu_custom_call" | custom-call | flops 41943040 | bytes 5513264 | tf_op jit(solution)/shard_map/pallas_call | solution.py:21
  13.3 0.0 copy-start.10
  13.3 1.0 copy-done.10
  14.2 0.0 copy-start.12
  14.2 5.6 %collective-permute-start = (bf16[3,256,128]{2,1,0:T(8,128)(2,1)}, bf16[3,256,128]{2,1,0:T(8,128)(2,1)S(1)}, u32[]{:S(2)}, u32[]{:S(2)}) collective-permute-start(bf16[3,256,128]{2,1,0:T(8,128)(2,1)} %get-tuple-element.18), channel_id=1, source_target_pairs={{0,32},{16,48},{32,64},{48,80},{64,96},{80,112},{96,128},{112,144}... | collective-permute-start | bytes 589832 | tf_op jit(solution)/shard_map/ppermute | solution.py:124
  19.9 2.2 %collective-permute-start.1 = (bf16[3,256,128]{2,1,0:T(8,128)(2,1)}, bf16[3,256,128]{2,1,0:T(8,128)(2,1)S(1)}, u32[]{:S(2)}, u32[]{:S(2)}) collective-permute-start(bf16[3,256,128]{2,1,0:T(8,128)(2,1)} %get-tuple-element.19), channel_id=1, source_target_pairs={{0,16},{16,32},{32,48},{48,64},{64,80},{80,96},{96,112},{112,128},... | collective-permute-start | bytes 589832 | tf_op jit(solution)/shard_map/ppermute | solution.py:124
  22.1 9.8 %collective-permute-start.2 = (bf16[3,256,128]{2,1,0:T(8,128)(2,1)}, bf16[3,256,128]{2,1,0:T(8,128)(2,1)S(1)}, u32[]{:S(2)}, u32[]{:S(2)}) collective-permute-start(bf16[3,256,128]{2,1,0:T(8,128)(2,1)} %get-tuple-element.20), channel_id=1, source_target_pairs={{0,496},{16,0},{32,16},{48,32},{64,48},{80,64},{96,80},{112,96},{1... | collective-permute-start | bytes 589832 | tf_op jit(solution)/shard_map/ppermute | solution.py:124
  31.9 4.3 %collective-permute-start.3 = (bf16[3,256,128]{2,1,0:T(8,128)(2,1)}, bf16[3,256,128]{2,1,0:T(8,128)(2,1)S(1)}, u32[]{:S(2)}, u32[]{:S(2)}) collective-permute-start(bf16[3,256,128]{2,1,0:T(8,128)(2,1)} %get-tuple-element.21), channel_id=1, source_target_pairs={{0,480},{16,496},{32,0},{48,16},{64,32},{80,48},{96,64},{112,80},{... | collective-permute-start | bytes 589832 | tf_op jit(solution)/shard_map/ppermute | solution.py:124
  36.2 0.0 copy-done.14
  36.2 0.1 copy.8.col_ref
  36.3 0.0 collective-permute-done.r0
  36.3 1.1 collective-permute-done.1.r1
  37.4 0.0 collective-permute-done.2.r2
  37.4 3.6 %collective-permute-done.3.r3 = bf16[3,256,128]{2,1,0:T(8,128)(2,1)S(1)} collective-permute-done((bf16[3,256,128]{2,1,0:T(8,128)(2,1)}, bf16[3,256,128]{2,1,0:T(8,128)(2,1)S(1)}, u32[]{:S(2)}, u32[]{:S(2)}) %collective-permute-start.3) | collective-permute-done | bytes 196640 | tf_op jit(solution)/shard_map/ppermute | solution.py:124
  41.0 0.0 copy-done.1
  41.0 0.0 copy-start.11
  41.0 1.2 copy-done.11
  42.2 3.2 %shard_map.65 = (bf16[16,256,128]{2,1,0:T(8,128)(2,1)S(1)}, bf16[16,256,128]{2,1,0:T(8,128)(2,1)S(1)}, bf16[3,256,128]{2,1,0:T(8,128)(2,1)}, bf16[3,256,128]{2,1...) custom-call(bf16[16,256,128]{2,1,0:T(8,128)(2,1)S(1)} %copy-done.11, ...), custom_call_target="tpu_custom_call" | custom-call | flops 671088640 | bytes 7348592 | tf_op jit(solution)/shard_map/pallas_call | solution.py:21
  45.4 0.0 copy-start.6
  45.4 1.0 copy-done.6
  46.4 0.0 copy-start.8
  46.4 1.0 copy-done.8
  47.4 1.9 %collective-permute-start.4 = (bf16[3,256,128]{2,1,0:T(8,128)(2,1)}, bf16[3,256,128]{2,1,0:T(8,128)(2,1)S(1)}, u32[]{:S(2)}, u32[]{:S(2)}) collective-permute-start(bf16[3,256,128]{2,1,0:T(8,128)(2,1)} %get-tuple-element.24), channel_id=1, source_target_pairs={{0,32},{16,48},{32,64},{48,80},{64,96},{80,112},{96,128},{112,144}... | collective-permute-start | bytes 589832 | tf_op jit(solution)/shard_map/ppermute | solution.py:124
  49.3 3.5 %collective-permute-start.5 = (bf16[3,256,128]{2,1,0:T(8,128)(2,1)}, bf16[3,256,128]{2,1,0:T(8,128)(2,1)S(1)}, u32[]{:S(2)}, u32[]{:S(2)}) collective-permute-start(bf16[3,256,128]{2,1,0:T(8,128)(2,1)} %get-tuple-element.25), channel_id=1, source_target_pairs={{0,16},{16,32},{32,48},{48,64},{64,80},{80,96},{96,112},{112,128},... | collective-permute-start | bytes 589832 | tf_op jit(solution)/shard_map/ppermute | solution.py:124
  52.8 6.4 %collective-permute-start.6 = (bf16[3,256,128]{2,1,0:T(8,128)(2,1)}, bf16[3,256,128]{2,1,0:T(8,128)(2,1)S(1)}, u32[]{:S(2)}, u32[]{:S(2)}) collective-permute-start(bf16[3,256,128]{2,1,0:T(8,128)(2,1)} %get-tuple-element.26), channel_id=1, source_target_pairs={{0,496},{16,0},{32,16},{48,32},{64,48},{80,64},{96,80},{112,96},{1... | collective-permute-start | bytes 589832 | tf_op jit(solution)/shard_map/ppermute | solution.py:124
  59.2 3.1 %collective-permute-start.7 = (bf16[3,256,128]{2,1,0:T(8,128)(2,1)}, bf16[3,256,128]{2,1,0:T(8,128)(2,1)S(1)}, u32[]{:S(2)}, u32[]{:S(2)}) collective-permute-start(bf16[3,256,128]{2,1,0:T(8,128)(2,1)} %get-tuple-element.27), channel_id=1, source_target_pairs={{0,480},{16,496},{32,0},{48,16},{64,32},{80,48},{96,64},{112,80},{... | collective-permute-start | bytes 589832 | tf_op jit(solution)/shard_map/ppermute | solution.py:124
  62.3 0.0 copy-done.13
  62.3 0.6 convert_element_type.3
  63.0 0.0 all-gather.2.cloned.1.call-update
  63.0 0.0 collective-permute-done.4.r0
  63.0 1.3 collective-permute-done.5.r1
  64.3 0.0 collective-permute-done.6.r2
  64.3 3.8 %collective-permute-done.7.r3 = bf16[3,256,128]{2,1,0:T(8,128)(2,1)S(1)} collective-permute-done((bf16[3,256,128]{2,1,0:T(8,128)(2,1)}, bf16[3,256,128]{2,1,0:T(8,128)(2,1)S(1)}, u32[]{:S(2)}, u32[]{:S(2)}) %collective-permute-start.7) | collective-permute-done | bytes 196640 | tf_op jit(solution)/shard_map/ppermute | solution.py:124
  68.1 0.0 copy-done.12
  68.1 0.0 copy-start.3
  68.1 1.2 copy-done.3
  69.3 0.0 copy-start.7
  69.3 1.2 copy-done.7
  70.6 0.0 copy-start.9
  70.6 1.2 copy-done.9
  71.8 2.3 %shard_map.66 = bf16[16,256,128]{2,1,0:T(8,128)(2,1)S(1)} custom-call(bf16[16,256,128]{2,1,0:T(8,128)(2,1)S(1)} %copy-done.9, bf16[3,256,128]{2,1,0:T(8,128)(2,1)S(1)} %collective-permute-done.4.r0, bf16[3,256,128]{2,1,0:T(8,128)(2,1)S(1)} %collective-permute-done.5.r1, bf16[3,256,128]{2,1,0:T(8,128)(2,1)S(1)} %collective-permute-done.6.r2, ...), custom_call_target="tpu_custom_call" | custom-call | flops 671088640 | bytes 7610700 | tf_op jit(solution)/shard_map/pallas_call | solution.py:21
  74.1 0.0 copy-start.4
  74.1 1.0 copy-done.4
  75.1 9.2 %all-to-all-start = ((bf16[16,256,128]{2,1,0:T(8,128)(2,1)}), bf16[16,256,128]{2,1,0:T(8,128)(2,1)S(1)}, u32[]{:S(2)}, u32[]{:S(2)}) async-start(bf16[16,256,128]{2,1,0:T(8,128)(2,1)} %copy-done.4), calls=%async_computation | async-start | bytes 2097152 | tf_op jit(solution)/shard_map/all_to_all | solution.py:130
  84.3 31.0 %all-gather.2.cloned.1.call-done.kernel_ref = f32[512,512]{1,0:T(8,128)} async-done(((f32[32,512]{1,0:T(8,128)}), f32[512,512]{1,0:T(8,128)}) %all-gather.2.cloned.1.call-update) | async-done | bytes 1048592 | tf_op jit(solution)/shard_map/all_gather | solution.py:146
  115.3 0.2 all-to-all-done.field_ref
  115.5 0.0 copy-start.5
  115.5 1.2 copy-done.5
  116.7 0.8 shard_map.67
  117.5 33.3 %all_to_all.10.field_ref = bf16[16,256,128]{2,1,0:T(8,128)(2,1)S(1)} all-to-all(bf16[16,256,128]{2,1,0:T(8,128)(2,1)S(1)} %shard_map.67), channel_id=1, replica_groups=mesh['dom'=32,'tm'=16] {'tm'}, dimensions={0} | all-to-all | bytes 2097152 | tf_op jit(solution)/shard_map/all_to_all | solution.py:130
  150.8 1.3 shard_map.68
Async XLA Ops:
  6.5 29.7 %copy-start.14 = (s32[16,5]{0,1:T(8,128)S(1)}, s32[16,5]{0,1:T(8,128)}, u32[]{:S(2)}) copy-start(s32[16,5]{0,1:T(8,128)} %param.9) | copy-start | bytes 964
  6.5 108.8 %all-gather.2.cloned.1.call-start = ((), (), s32[]{:S(2)}) async-start(), calls=%async_computation.2 | async-start | bytes 1114112 | tf_op jit(solution)/shard_map/all_gather | solution.py:146
  7.3 1.7 %copy-start = (bf16[16,5,128,128]{3,2,1,0:T(8,128)(2,1)S(1)}, bf16[16,5,128,128]{3,2,1,0:T(8,128)(2,1)}, u32[]{:S(2)}) copy-start(bf16[16,5,128,128]{3,2,1,0:T(8,128)(2,1)} %weights_ref.5) | copy-start | bytes 7864324
  9.1 1.2 copy-start.2
  10.3 30.7 %copy-start.1 = (bf16[16,5,128,128]{3,2,1,0:T(8,128)(2,1)S(1)}, bf16[16,5,128,128]{3,2,1,0:T(8,128)(2,1)}, u32[]{:S(2)}) copy-start(bf16[16,5,128,128]{3,2,1,0:T(8,128)(2,1)} %weights_ref.5) | copy-start | bytes 7864324
  10.3 52.1 %copy-start.13 = (bf16[32,512]{1,0:T(8,128)(2,1)S(1)}, bf16[32,512]{1,0:T(8,128)(2,1)}, u32[]{:S(2)}) copy-start(bf16[32,512]{1,0:T(8,128)(2,1)} %param.10) | copy-start | bytes 98308
  13.3 1.0 copy-start.10
  14.2 53.9 %copy-start.12 = (f32[3]{0:T(128)S(1)}, f32[3]{0:T(128)}, u32[]{:S(2)}) copy-start(f32[3]{0:T(128)} %coef_ref.1) | copy-start | bytes 40
  14.2 22.0 %collective-permute-start = (bf16[3,256,128]{2,1,0:T(8,128)(2,1)}, bf16[3,256,128]{2,1,0:T(8,128)(2,1)S(1)}, u32[]{:S(2)}, u32[]{:S(2)}) collective-permute-start(bf16[3,256,128]{2,1,0:T(8,128)(2,1)} %get-tuple-element.18), channel_id=1, source_target_pairs={{0,32},{16,48},{32,64},{48,80},{64,96},{80,112},{96,128},{112,144}... | collective-permute-start | bytes 589832 | tf_op jit(solution)/shard_map/ppermute | solution.py:124
  19.9 17.6 %collective-permute-start.1 = (bf16[3,256,128]{2,1,0:T(8,128)(2,1)}, bf16[3,256,128]{2,1,0:T(8,128)(2,1)S(1)}, u32[]{:S(2)}, u32[]{:S(2)}) collective-permute-start(bf16[3,256,128]{2,1,0:T(8,128)(2,1)} %get-tuple-element.19), channel_id=1, source_target_pairs={{0,16},{16,32},{32,48},{48,64},{64,80},{80,96},{96,112},{112,128},... | collective-permute-start | bytes 589832 | tf_op jit(solution)/shard_map/ppermute | solution.py:124
  22.1 15.3 %collective-permute-start.2 = (bf16[3,256,128]{2,1,0:T(8,128)(2,1)}, bf16[3,256,128]{2,1,0:T(8,128)(2,1)S(1)}, u32[]{:S(2)}, u32[]{:S(2)}) collective-permute-start(bf16[3,256,128]{2,1,0:T(8,128)(2,1)} %get-tuple-element.20), channel_id=1, source_target_pairs={{0,496},{16,0},{32,16},{48,32},{64,48},{80,64},{96,80},{112,96},{1... | collective-permute-start | bytes 589832 | tf_op jit(solution)/shard_map/ppermute | solution.py:124
  31.9 9.1 %collective-permute-start.3 = (bf16[3,256,128]{2,1,0:T(8,128)(2,1)}, bf16[3,256,128]{2,1,0:T(8,128)(2,1)S(1)}, u32[]{:S(2)}, u32[]{:S(2)}) collective-permute-start(bf16[3,256,128]{2,1,0:T(8,128)(2,1)} %get-tuple-element.21), channel_id=1, source_target_pairs={{0,480},{16,496},{32,0},{48,16},{64,32},{80,48},{96,64},{112,80},{... | collective-permute-start | bytes 589832 | tf_op jit(solution)/shard_map/ppermute | solution.py:124
  41.0 1.2 copy-start.11
  45.4 1.0 copy-start.6
  46.4 1.0 copy-start.8
  47.4 15.6 %collective-permute-start.4 = (bf16[3,256,128]{2,1,0:T(8,128)(2,1)}, bf16[3,256,128]{2,1,0:T(8,128)(2,1)S(1)}, u32[]{:S(2)}, u32[]{:S(2)}) collective-permute-start(bf16[3,256,128]{2,1,0:T(8,128)(2,1)} %get-tuple-element.24), channel_id=1, source_target_pairs={{0,32},{16,48},{32,64},{48,80},{64,96},{80,112},{96,128},{112,144}... | collective-permute-start | bytes 589832 | tf_op jit(solution)/shard_map/ppermute | solution.py:124
  49.3 15.0 %collective-permute-start.5 = (bf16[3,256,128]{2,1,0:T(8,128)(2,1)}, bf16[3,256,128]{2,1,0:T(8,128)(2,1)S(1)}, u32[]{:S(2)}, u32[]{:S(2)}) collective-permute-start(bf16[3,256,128]{2,1,0:T(8,128)(2,1)} %get-tuple-element.25), channel_id=1, source_target_pairs={{0,16},{16,32},{32,48},{48,64},{64,80},{80,96},{96,112},{112,128},... | collective-permute-start | bytes 589832 | tf_op jit(solution)/shard_map/ppermute | solution.py:124
  52.8 11.5 %collective-permute-start.6 = (bf16[3,256,128]{2,1,0:T(8,128)(2,1)}, bf16[3,256,128]{2,1,0:T(8,128)(2,1)S(1)}, u32[]{:S(2)}, u32[]{:S(2)}) collective-permute-start(bf16[3,256,128]{2,1,0:T(8,128)(2,1)} %get-tuple-element.26), channel_id=1, source_target_pairs={{0,496},{16,0},{32,16},{48,32},{64,48},{80,64},{96,80},{112,96},{1... | collective-permute-start | bytes 589832 | tf_op jit(solution)/shard_map/ppermute | solution.py:124
  59.2 8.9 %collective-permute-start.7 = (bf16[3,256,128]{2,1,0:T(8,128)(2,1)}, bf16[3,256,128]{2,1,0:T(8,128)(2,1)S(1)}, u32[]{:S(2)}, u32[]{:S(2)}) collective-permute-start(bf16[3,256,128]{2,1,0:T(8,128)(2,1)} %get-tuple-element.27), channel_id=1, source_target_pairs={{0,480},{16,496},{32,0},{48,16},{64,32},{80,48},{96,64},{112,80},{... | collective-permute-start | bytes 589832 | tf_op jit(solution)/shard_map/ppermute | solution.py:124
  68.1 1.2 copy-start.3
  69.3 1.2 copy-start.7
  70.6 1.2 copy-start.9
  74.1 1.0 copy-start.4
  75.1 40.4 %all-to-all-start = ((bf16[16,256,128]{2,1,0:T(8,128)(2,1)}), bf16[16,256,128]{2,1,0:T(8,128)(2,1)S(1)}, u32[]{:S(2)}, u32[]{:S(2)}) async-start(bf16[16,256,128]{2,1,0:T(8,128)(2,1)} %copy-done.4), calls=%async_computation | async-start | bytes 2097152 | tf_op jit(solution)/shard_map/all_to_all | solution.py:130
  115.5 1.2 copy-start.5
Sparse Core Ops, SparseCore 0:
  63.1 52.1 all-gather.1

commit v2 on v1

v2 whole, which is shorter than its diff:
```python
import functools

import jax
import jax.numpy as jnp
from jax import lax
from jax.experimental import pallas as pl
from jax.experimental.pallas import tpu as pltpu
from jax.sharding import PartitionSpec as P

REACH = 2
OFFSETS = tuple(range(-REACH, 0)) + tuple(range(1, REACH + 1))
F32, BF16 = jnp.float32, jnp.bfloat16
LIMIT = 24 * 2**20


def whole(a):
    return pl.BlockSpec(a.shape, lambda i: (0,) * len(a.shape))


def half(a, part):
    return pl.BlockSpec((a.shape[0] // 2, a.shape[1]), lambda i: (part, 0))


SMEM = pl.BlockSpec(memory_space=pltpu.SMEM)


def call(kernel, outs, ins, scratch=(), flops=0, in_specs=None, out_specs=None, aliases=None):
    size = sum(a.size * a.dtype.itemsize for a in (*ins, *outs))
    specs = [SMEM if a.dtype == jnp.int32 or a.size < 8 else whole(a) for a in ins]
    for i, spec in (in_specs or {}).items():
        specs[i] = spec
    results = [whole(a) for a in outs]
    for i, spec in (out_specs or {}).items():
        results[i] = spec
    return pl.pallas_call(
        kernel,
        grid=(1,),
        out_shape=outs,
        in_specs=specs,
        out_specs=results,
        scratch_shapes=list(scratch),
        compiler_params=pltpu.CompilerParams(vmem_limit_bytes=LIMIT),
        cost_estimate=pl.CostEstimate(flops=flops, bytes_accessed=size, transcendentals=0),
        input_output_aliases=aliases or {},
    )(*ins)


def array(*shape, dtype=BF16):
    return jax.ShapeDtypeStruct(shape, dtype)


def times_transposed(a, b):
    return lax.dot_general(a, b, (((1,), (1,)), ((), ())), preferred_element_type=F32)


def block_of(ref, g, width):
    if len(ref.shape) == 3:
        return ref[g]
    start = g * width
    return ref[:, pl.ds(start if isinstance(g, int) else pl.multiple_of(start, width), width)]


def scaled_block(ref, inv_ref, g, width):
    return (block_of(ref, g, width).astype(F32) * inv_ref[pl.ds(g, 1), :]).astype(BF16)


def pack(send_ref, field_ref, inv_ref, packs):
    width = inv_ref.shape[1]
    for way, out in enumerate(packs):
        for slot in range(out.shape[0]):
            out[slot] = scaled_block(field_ref, inv_ref, send_ref[0, way, slot], width)


def lay_out(signal_ref, kernel_ref, out_ref):
    owners, _, width = out_ref.shape
    rows, t_loc = signal_ref.shape[0], kernel_ref.shape[0]
    for i in range(owners):
        out_ref[i, :rows] = signal_ref[:, i * width : (i + 1) * width]
        for q in range(kernel_ref.shape[1] // width):
            out_ref[i, rows + q * t_loc : rows + (q + 1) * t_loc] = kernel_ref[:, q * width : (q + 1) * width]


def first_scale(signal_ref, weights_ref, send_ref, inv_ref, *packs):
    blocks, per_row, width, _ = weights_ref.shape
    ones = jnp.ones((16, width), BF16)
    for g in range(blocks):
        degree = times_transposed(ones, weights_ref[g, 0])
        for j in range(1, per_row):
            degree += times_transposed(ones, weights_ref[g, j])
        inv_ref[g : g + 1, :] = lax.rsqrt(degree[:1])
    pack(send_ref, signal_ref, inv_ref, packs)


def scale(field_ref, inv_ref, send_ref, *packs):
    pack(send_ref, field_ref, inv_ref, packs)


def gather_sources(field_ref, inv_ref, received, source):
    blocks, width = inv_ref.shape
    for g in range(blocks):
        source[g] = scaled_block(field_ref, inv_ref, g, width)
    for way, ref in enumerate(received):
        slots = ref.shape[0]
        source[blocks + way * slots : blocks + (way + 1) * slots] = ref[...]


def block_product(g, col_ref, weights_ref, source):
    per_row = weights_ref.shape[1]
    picked = jnp.concatenate([source[col_ref[g, j]] for j in range(per_row)], axis=1)
    edges = jnp.concatenate([weights_ref[g, j] for j in range(per_row)], axis=1)
    return times_transposed(picked, edges)


def first_product(field_ref, r0, r1, r2, r3, weights_ref, inv_ref, col_ref, send_ref, term_ref, *rest):
    *packs, source = rest
    gather_sources(field_ref, inv_ref, (r0, r1, r2, r3), source)
    for g in range(weights_ref.shape[0]):
        total = block_product(g, col_ref, weights_ref, source)
        term_ref[g] = (-inv_ref[g : g + 1, :] * total).astype(BF16)
    pack(send_ref, term_ref, inv_ref, packs)


def second_product(field_ref, r0, r1, r2, r3, weights_ref, inv_ref, col_ref, coef_ref, term_ref, out_ref, source):
    width = weights_ref.shape[2]
    gather_sources(term_ref, inv_ref, (r0, r1, r2, r3), source)
    for g in range(weights_ref.shape[0]):
        total = block_product(g, col_ref, weights_ref, source)
        x = block_of(field_ref, g, width).astype(F32)
        two = (-2.0 * inv_ref[g : g + 1, :] * total - x).astype(BF16).astype(F32)
        one = term_ref[g].astype(F32)
        mixed = (coef_ref[0] * x + coef_ref[1] * one + coef_ref[2] * two).astype(BF16)
        if len(out_ref.shape) == 3:
            out_ref[g] = mixed
        else:
            out_ref[:, g * width : (g + 1) * width] = mixed


def mix_times(t_loc, rows, mix, field_ref, out_ref, columns):
    owners, _, width = field_ref.shape
    for p in range(rows // t_loc):
        part = slice(p * t_loc, (p + 1) * t_loc)
        for i in range(owners):
            columns[i * t_loc : (i + 1) * t_loc, p * width : (p + 1) * width] = field_ref[i, part]
    step = 2 * width
    for c in range(columns.shape[1] // step):
        out = jnp.dot(mix, columns[:, c * step : (c + 1) * step], preferred_element_type=F32).astype(BF16)
        for q in range(step // width):
            p = c * (step // width) + q
            for i in range(owners):
                out_ref[i, p * t_loc : (p + 1) * t_loc] = out[i * t_loc : (i + 1) * t_loc, q * width : (q + 1) * width]


def first_temporal(t_loc, field_ref, out_ref, mix_ref, columns):
    owners, _, width = field_ref.shape
    rows = out_ref.shape[1]
    for i in range(owners):
        for q in range(mix_ref.shape[1] // width):
            mix_ref[i * t_loc : (i + 1) * t_loc, q * width : (q + 1) * width] = field_ref[
                i, rows + q * t_loc : rows + (q + 1) * t_loc
            ]
    mix_times(t_loc, rows, mix_ref[...], field_ref, out_ref, columns)


def second_temporal(t_loc, field_ref, mix_ref, out_ref, columns):
    mix_times(t_loc, out_ref.shape[1], mix_ref[...], field_ref, out_ref, columns)


def unblock(_, field_ref, out_ref):
    blocks, _, width = field_ref.shape
    for g in range(blocks):
        out_ref[:, g * width : (g + 1) * width] = field_ref[g]


def halo(packs):
    count = lax.axis_size("dom")
    return [
        lax.ppermute(block, "dom", [(i, (i - distance) % count) for i in range(count)])
        for block, distance in zip(packs, OFFSETS)
    ]


def exchange(field):
    return lax.all_to_all(field, "tm", split_axis=0, concat_axis=0, tiled=True)


def body(signal, weights, send_list, col_ref, kernel, cheb_coef):
    probes, t_loc, n_loc = signal.shape
    blocks, per_row, width, _ = weights.shape
    rows = probes * t_loc // 2
    slots = send_list.shape[2]
    owners = lax.axis_size("tm")
    time = kernel.shape[1]
    xs = signal.reshape(2 * rows, n_loc)
    front, back = half(xs, 0), half(xs, 1)
    field = array(blocks, rows, width)
    packed = [array(slots, rows, width)] * len(OFFSETS)
    source = pltpu.VMEM((blocks + len(OFFSETS) * slots, rows, width), BF16)
    columns = pltpu.VMEM((time, rows // t_loc * width), BF16)
    work = 2 * rows * per_row * n_loc * width
    mixing = 2 * time * time * rows // t_loc * width
    shared = (weights,)

    def one(x, packs, inv, spec):
        term, *packs = call(
            first_product,
            [field, *packed],
            (x, *halo(packs), *shared, inv, col_ref, send_list),
            [source],
            flops=work,
            in_specs=spec,
        )
        return term, packs

    def two(x, packs, inv, term, out, spec, out_spec):
        return call(
            second_product,
            [out],
            (x, *halo(packs), *shared, inv, col_ref, cheb_coef, term),
            [source],
            flops=work,
            in_specs=spec,
            out_specs=out_spec,
        )[0]

    chunk = rows + time * t_loc // width
    (laid,) = call(lay_out, [array(owners, chunk, width)], (xs, kernel), in_specs={0: front})
    arrived = exchange(laid)
    inv, *packs = call(
        first_scale,
        [array(blocks, width, dtype=F32), *packed],
        (xs, weights, send_list),
        flops=work // 8,
        in_specs={0: back},
    )
    term, packs = one(xs, packs, inv, {0: back})
    early, mix = call(
        functools.partial(first_temporal, t_loc), [field, array(time, time)], (arrived,), [columns], flops=mixing
    )
    early, *packs = lax.optimization_barrier((early, *packs))
    early = exchange(early)
    late = two(xs, packs, inv, term, field, {0: back}, {})
    late, early = lax.optimization_barrier((late, early))
    late = exchange(late)
    packs = call(scale, packed, (early, inv, send_list))
    term, packs = one(early, packs, inv, {})
    (late,) = call(functools.partial(second_temporal, t_loc), [field], (late, mix), [columns], flops=mixing)
    late, *packs = lax.optimization_barrier((late, *packs))
    late = exchange(late)
    out = array(2 * rows, n_loc)
    done = two(early, packs, inv, term, out, {}, {0: half(out, 0)})
    (done,) = call(
        unblock,
        [out],
        (done, late),
        in_specs={0: pl.BlockSpec(memory_space=pl.ANY)},
        out_specs={0: half(out, 1)},
        aliases={0: 0},
    )
    return done.reshape(probes, t_loc, n_loc)


def solution(mesh):
    in_specs = (
        P(None, "tm", "dom"),
        P("dom", None, None, None),
        P("dom", None, None),
        P("dom", None),
        P("tm", None),
        P(),
    )
    out_specs = P(None, "tm", "dom")
    return jax.shard_map(body, mesh=mesh, in_specs=in_specs, out_specs=out_specs, check_vma=False)
```

time: 160 us -> 151 us (0.944)
  the two profiles are of different devices: /device:TPU:1 before, /device:TPU:136 now
where the time goes in v2:
time: 151 us; the launch traced here: 150 us
  starting transfers between devices  89.5 us (59%)
  waiting for transfers between devices  24.1 us (16%)
  local copies, waits for them, and re-layouts  19.4 us (13%)
  Pallas kernels  16.2 us (11%)
    ppermute x16, starting transfers between devices, halo(): lax.ppermute(block, 'dom', [(i, (i - distance) % count) for i in range(co...  60.2 us
    all_to_all x4, starting transfers between devices, exchange(): return lax.all_to_all(field, 'tm', split_axis=0, concat_axis=0, tiled=True)  29.4 us
    ppermute x16, waiting for transfers between devices, halo(): lax.ppermute(block, 'dom', [(i, (i - distance) % count) for i in range(co...  24.1 us
    unnamed x58, local copies, waits for them, and re-layouts  19.4 us
    pallas_call x10, Pallas kernels, call(): pl.pallas_call(kernel, grid=(1,), out_shape=outs, in_specs=specs, out_spe...  16.2 us
  transfers between devices with their start and end apart: 20, of which 8 were waited for; matrix products, arithmetic and copies ran while one was open for 0% of the time, Pallas kernels for 7%

profile of v2, /device:TPU:136, one launch (start us, length us, event | category | flops | bytes accessed | tf_op | source)
XLA Modules:
  0.0 149.5 jit_solution(10040029886589460303)
XLA Ops:
  0.0 1.4 copy-done.1
  1.4 0.8 copy-done.18
  2.1 0.1 shard_map.64
  2.3 0.0 copy-start.5
  2.3 1.0 copy-done.5
  3.3 7.7 %all-to-all-start = ((bf16[16,256,128]{2,1,0:T(8,128)(2,1)}), bf16[16,256,128]{2,1,0:T(8,128)(2,1)}, u32[]{:S(2)}, u32[]{:S(2)}) async-start(bf16[16,256,128]{2,1,0:T(8,128)(2,1)} %copy-done.5), calls=%async_computation | async-start | bytes 2097152 | tf_op jit(solution)/shard_map/all_to_all | solution.py:183
  11.0 0.1 copy.8.send_ref
  11.1 1.2 copy-done.2
  12.3 2.1 %shard_map.66 = (f32[16,128]{1,0:T(8,128)S(1)}, bf16[3,128,128]{2,1,0:T(8,128)(2,1)S(1)}, bf16[3,128,128]{2,1,0:T(8,128)(2,1)S(1)}, bf16[3,128,128]{2,1,0:T(8,128)(2,1)S(1)}, bf16[3,128,128]{2,1,0:T(8,128)(2,1)S(1)}) custom-call(bf16[256,2048]{1,0:T(8,128)(2,1)S(1)} %bitcast.3, bf16[16,5,128,128]{3,2,1,0:T(8,128)(2,1)S(1)} %copy-done, ...), custom_call_target="tpu_custom_call" | custom-call | flops 41943040 | bytes 4071472 | tf_op jit(solution)/shard_map/pallas_call | solution.py:35
  14.4 4.9 %collective-permute-start = (bf16[3,128,128]{2,1,0:T(8,128)(2,1)S(1)}, bf16[3,128,128]{2,1,0:T(8,128)(2,1)S(1)}, u32[]{:S(2)}, u32[]{:S(2)}) collective-permute-start(bf16[3,128,128]{2,1,0:T(8,128)(2,1)S(1)} %get-tuple-element.39), channel_id=1, source_target_pairs={{0,32},{16,48},{32,64},{48,80},{64,96},{80,112},{96,128},{112,144}... | collective-permute-start | bytes 294920 | tf_op jit(solution)/shard_map/ppermute | solution.py:177
  19.3 2.5 %collective-permute-start.1 = (bf16[3,128,128]{2,1,0:T(8,128)(2,1)S(1)}, bf16[3,128,128]{2,1,0:T(8,128)(2,1)S(1)}, u32[]{:S(2)}, u32[]{:S(2)}) collective-permute-start(bf16[3,128,128]{2,1,0:T(8,128)(2,1)S(1)} %get-tuple-element.40), channel_id=1, source_target_pairs={{0,16},{16,32},{32,48},{48,64},{64,80},{80,96},{96,112},{112,128},... | collective-permute-start | bytes 294920 | tf_op jit(solution)/shard_map/ppermute | solution.py:177
  21.8 5.5 %collective-permute-start.2 = (bf16[3,128,128]{2,1,0:T(8,128)(2,1)S(1)}, bf16[3,128,128]{2,1,0:T(8,128)(2,1)S(1)}, u32[]{:S(2)}, u32[]{:S(2)}) collective-permute-start(bf16[3,128,128]{2,1,0:T(8,128)(2,1)S(1)} %get-tuple-element.41), channel_id=1, source_target_pairs={{0,496},{16,0},{32,16},{48,32},{64,48},{80,64},{96,80},{112,96},{1... | collective-permute-start | bytes 294920 | tf_op jit(solution)/shard_map/ppermute | solution.py:177
  27.3 1.9 %collective-permute-start.3 = (bf16[3,128,128]{2,1,0:T(8,128)(2,1)S(1)}, bf16[3,128,128]{2,1,0:T(8,128)(2,1)S(1)}, u32[]{:S(2)}, u32[]{:S(2)}) collective-permute-start(bf16[3,128,128]{2,1,0:T(8,128)(2,1)S(1)} %get-tuple-element.42), channel_id=1, source_target_pairs={{0,480},{16,496},{32,0},{48,16},{64,32},{80,48},{96,64},{112,80},{... | collective-permute-start | bytes 294920 | tf_op jit(solution)/shard_map/ppermute | solution.py:177
  29.2 0.1 copy.9.col_ref
  29.3 0.7 collective-permute-done.2.r2
  30.0 5.3 %collective-permute-done.3.r3 = bf16[3,128,128]{2,1,0:T(8,128)(2,1)S(1)} collective-permute-done((bf16[3,128,128]{2,1,0:T(8,128)(2,1)S(1)}, bf16[3,128,128]{2,1,0:T(8,128)(2,1)S(1)}, u32[]{:S(2)}, u32[]{:S(2)}) %collective-permute-start.3) | collective-permute-done | bytes 98336 | tf_op jit(solution)/shard_map/ppermute | solution.py:177
  35.3 1.2 copy-done.3
  36.6 0.7 copy-done.16
  37.2 1.9 %shard_map.67 = (bf16[16,128,128]{2,1,0:T(8,128)(2,1)S(1)}, bf16[3,128,128]{2,1,0:T(8,128)(2,1)S(1)}, bf16[3,128,128]{2,1,0:T(8,128)(2,1)S(1)}, bf16[3,128,128]{2,1,0:T(8,128)(2,1)S(1)}, bf16[3,128,128]{2,1,0:T(8,128)(2,1)S(1)}) custom-call(bf16[256,2048]{1,0:T(8,128)(2,1)S(1)} %bitcast.4, bf16[3,128,128]{2,1,0:T(8,128)(2,1)S(1)} %collective-permute-done.r0, ...), custom_call_target="tpu_custom_call" | custom-call | flops 335544320 | bytes 4989296 | tf_op jit(solution)/shard_map/pallas_call | solution.py:35
  39.1 0.8 copy-done.13
  39.9 0.6 copy-done.21
  40.6 0.6 copy-done.22
  41.2 0.6 copy-done.23
  41.8 0.6 copy-done.25
  42.5 1.7 %shard_map.65 = (bf16[16,128,128]{2,1,0:T(8,128)(2,1)S(1)}, bf16[512,512]{1,0:T(8,128)(2,1)S(1)}) custom-call(bf16[16,256,128]{2,1,0:T(8,128)(2,1)} %all-to-all-done.field_ref), custom_call_target="tpu_custom_call" | custom-call | flops 268435456 | bytes 2097152 | tf_op jit(solution)/shard_map/pallas_call | solution.py:35
  44.2 0.8 copy-done.8
  45.0 0.8 copy-done.10
  45.8 7.2 %all-to-all-start.1 = ((bf16[16,128,128]{2,1,0:T(8,128)(2,1)}), bf16[16,128,128]{2,1,0:T(8,128)(2,1)S(1)}, u32[]{:S(2)}, u32[]{:S(2)}) async-start(bf16[16,128,128]{2,1,0:T(8,128)(2,1)} %copy-done.10), calls=%async_computation.1 | async-start | bytes 1048576 | tf_op jit(solution)/shard_map/all_to_all | solution.py:183
  53.0 3.9 %collective-permute-start.4 = (bf16[3,128,128]{2,1,0:T(8,128)(2,1)}, bf16[3,128,128]{2,1,0:T(8,128)(2,1)S(1)}, u32[]{:S(2)}, u32[]{:S(2)}) collective-permute-start(bf16[3,128,128]{2,1,0:T(8,128)(2,1)} %copy-done.25), channel_id=1, source_target_pairs={{0,32},{16,48},{32,64},{48,80},{64,96},{80,112},{96,128},{112,144}... | collective-permute-start | bytes 294920 | tf_op jit(solution)/shard_map/ppermute | solution.py:177
  56.9 2.7 %collective-permute-start.5 = (bf16[3,128,128]{2,1,0:T(8,128)(2,1)}, bf16[3,128,128]{2,1,0:T(8,128)(2,1)S(1)}, u32[]{:S(2)}, u32[]{:S(2)}) collective-permute-start(bf16[3,128,128]{2,1,0:T(8,128)(2,1)} %copy-done.23), channel_id=1, source_target_pairs={{0,16},{16,32},{32,48},{48,64},{64,80},{80,96},{96,112},{112,128},... | collective-permute-start | bytes 294920 | tf_op jit(solution)/shard_map/ppermute | solution.py:177
  59.6 5.3 %collective-permute-start.6 = (bf16[3,128,128]{2,1,0:T(8,128)(2,1)}, bf16[3,128,128]{2,1,0:T(8,128)(2,1)S(1)}, u32[]{:S(2)}, u32[]{:S(2)}) collective-permute-start(bf16[3,128,128]{2,1,0:T(8,128)(2,1)} %copy-done.22), channel_id=1, source_target_pairs={{0,496},{16,0},{32,16},{48,32},{64,48},{80,64},{96,80},{112,96},{1... | collective-permute-start | bytes 294920 | tf_op jit(solution)/shard_map/ppermute | solution.py:177
  64.9 2.2 %collective-permute-start.7 = (bf16[3,128,128]{2,1,0:T(8,128)(2,1)}, bf16[3,128,128]{2,1,0:T(8,128)(2,1)S(1)}, u32[]{:S(2)}, u32[]{:S(2)}) collective-permute-start(bf16[3,128,128]{2,1,0:T(8,128)(2,1)} %copy-done.21), channel_id=1, source_target_pairs={{0,480},{16,496},{32,0},{48,16},{64,32},{80,48},{96,64},{112,80},{... | collective-permute-start | bytes 294920 | tf_op jit(solution)/shard_map/ppermute | solution.py:177
  67.2 0.7 collective-permute-done.6.r2
  67.8 5.3 %collective-permute-done.7.r3 = bf16[3,128,128]{2,1,0:T(8,128)(2,1)S(1)} collective-permute-done((bf16[3,128,128]{2,1,0:T(8,128)(2,1)}, bf16[3,128,128]{2,1,0:T(8,128)(2,1)S(1)}, u32[]{:S(2)}, u32[]{:S(2)}) %collective-permute-start.7) | collective-permute-done | bytes 98336 | tf_op jit(solution)/shard_map/ppermute | solution.py:177
  73.1 1.2 copy-done.4
  74.3 1.0 copy-done.14
  75.4 0.7 copy-done.19
  76.0 1.8 %shard_map.68 = bf16[16,128,128]{2,1,0:T(8,128)(2,1)S(1)} custom-call(bf16[256,2048]{1,0:T(8,128)(2,1)S(1)} %bitcast.5, bf16[3,128,128]{2,1,0:T(8,128)(2,1)S(1)} %collective-permute-done.4.r0, bf16[3,128,128]{2,1,0:T(8,128)(2,1)S(1)} %collective-permute-done.5.r1, bf16[3,128,128]{2,1,0:T(8,128)(2,1)S(1)} %collective-permute-done.6.r2, ...), custom_call_target="tpu_custom_call" | custom-call | flops 335544320 | bytes 5120332 | tf_op jit(solution)/shard_map/pallas_call | solution.py:35
  77.8 0.8 copy-done.7
  78.6 7.2 %all-to-all-start.2 = ((bf16[16,128,128]{2,1,0:T(8,128)(2,1)}), bf16[16,128,128]{2,1,0:T(8,128)(2,1)}, u32[]{:S(2)}, u32[]{:S(2)}) async-start(bf16[16,128,128]{2,1,0:T(8,128)(2,1)} %copy-done.7), calls=%async_computation.2 | async-start | bytes 1048576 | tf_op jit(solution)/shard_map/all_to_all | solution.py:183
  85.9 0.6 shard_map.70
  86.5 6.3 %collective-permute-start.8 = (bf16[3,128,128]{2,1,0:T(8,128)(2,1)S(1)}, bf16[3,128,128]{2,1,0:T(8,128)(2,1)S(1)}, u32[]{:S(2)}, u32[]{:S(2)}) collective-permute-start(bf16[3,128,128]{2,1,0:T(8,128)(2,1)S(1)} %get-tuple-element.57), channel_id=1, source_target_pairs={{0,32},{16,48},{32,64},{48,80},{64,96},{80,112},{96,128},{112,144}... | collective-permute-start | bytes 294920 | tf_op jit(solution)/shard_map/ppermute | solution.py:177
  92.9 2.6 %collective-permute-start.9 = (bf16[3,128,128]{2,1,0:T(8,128)(2,1)S(1)}, bf16[3,128,128]{2,1,0:T(8,128)(2,1)S(1)}, u32[]{:S(2)}, u32[]{:S(2)}) collective-permute-start(bf16[3,128,128]{2,1,0:T(8,128)(2,1)S(1)} %get-tuple-element.58), channel_id=1, source_target_pairs={{0,16},{16,32},{32,48},{48,64},{64,80},{80,96},{96,112},{112,128},... | collective-permute-start | bytes 294920 | tf_op jit(solution)/shard_map/ppermute | solution.py:177
  95.5 5.3 %collective-permute-start.10 = (bf16[3,128,128]{2,1,0:T(8,128)(2,1)S(1)}, bf16[3,128,128]{2,1,0:T(8,128)(2,1)S(1)}, u32[]{:S(2)}, u32[]{:S(2)}) collective-permute-start(bf16[3,128,128]{2,1,0:T(8,128)(2,1)S(1)} %get-tuple-element.59), channel_id=1, source_target_pairs={{0,496},{16,0},{32,16},{48,32},{64,48},{80,64},{96,80},{112,96},{1... | collective-permute-start | bytes 294920 | tf_op jit(solution)/shard_map/ppermute | solution.py:177
  100.8 1.9 %collective-permute-start.11 = (bf16[3,128,128]{2,1,0:T(8,128)(2,1)S(1)}, bf16[3,128,128]{2,1,0:T(8,128)(2,1)S(1)}, u32[]{:S(2)}, u32[]{:S(2)}) collective-permute-start(bf16[3,128,128]{2,1,0:T(8,128)(2,1)S(1)} %get-tuple-element.60), channel_id=1, source_target_pairs={{0,480},{16,496},{32,0},{48,16},{64,32},{80,48},{96,64},{112,80},{... | collective-permute-start | bytes 294920 | tf_op jit(solution)/shard_map/ppermute | solution.py:177
  102.8 0.7 collective-permute-done.10.r2
  103.5 5.4 %collective-permute-done.11.r3 = bf16[3,128,128]{2,1,0:T(8,128)(2,1)S(1)} collective-permute-done((bf16[3,128,128]{2,1,0:T(8,128)(2,1)S(1)}, bf16[3,128,128]{2,1,0:T(8,128)(2,1)S(1)}, u32[]{:S(2)}, u32[]{:S(2)}) %collective-permute-start.11) | collective-permute-done | bytes 98336 | tf_op jit(solution)/shard_map/ppermute | solution.py:177
  108.9 1.9 %shard_map.71 = (bf16[16,128,128]{2,1,0:T(8,128)(2,1)S(1)}, bf16[3,128,128]{2,1,0:T(8,128)(2,1)S(1)}, bf16[3,128,128]{2,1,0:T(8,128)(2,1)S(1)}, bf16[3,128,128]{2,1,0:T(8,128)(2,1)S(1)}, bf16[3,128,128]{2,1,0:T(8,128)(2,1)S(1)}) custom-call(bf16[16,128,128]{2,1,0:T(8,128)(2,1)S(1)} %all-to-all-done.1.field_ref, ...), custom_call_target="tpu_custom_call" | custom-call | flops 335544320 | bytes 4465008 | tf_op jit(solution)/shard_map/pallas_call | solution.py:35
  110.7 0.0 copy-start.11
  110.7 0.8 copy-done.11
  111.5 0.6 copy-done.24
  112.2 1.0 copy-done.9
  113.2 1.5 %shard_map.69 = bf16[16,128,128]{2,1,0:T(8,128)(2,1)S(1)} custom-call(bf16[16,128,128]{2,1,0:T(8,128)(2,1)} %all-to-all-done.2.field_ref, bf16[512,512]{1,0:T(8,128)(2,1)S(1)} %copy-done.9), custom_call_target="tpu_custom_call" | custom-call | flops 268435456 | bytes 1572864 | tf_op jit(solution)/shard_map/pallas_call | solution.py:35
  114.8 0.8 copy-done.6
  115.5 7.2 %all-to-all-start.3 = ((bf16[16,128,128]{2,1,0:T(8,128)(2,1)}), bf16[16,128,128]{2,1,0:T(8,128)(2,1)}, u32[]{:S(2)}, u32[]{:S(2)}) async-start(bf16[16,128,128]{2,1,0:T(8,128)(2,1)} %copy-done.6), calls=%async_computation.3 | async-start | bytes 1048576 | tf_op jit(solution)/shard_map/all_to_all | solution.py:183
  122.8 5.2 %collective-permute-start.12 = (bf16[3,128,128]{2,1,0:T(8,128)(2,1)}, bf16[3,128,128]{2,1,0:T(8,128)(2,1)S(1)}, u32[]{:S(2)}, u32[]{:S(2)}) collective-permute-start(bf16[3,128,128]{2,1,0:T(8,128)(2,1)} %copy-done.24), channel_id=1, source_target_pairs={{0,32},{16,48},{32,64},{48,80},{64,96},{80,112},{96,128},{112,144}... | collective-permute-start | bytes 294920 | tf_op jit(solution)/shard_map/ppermute | solution.py:177
  128.0 2.6 %collective-permute-start.13 = (bf16[3,128,128]{2,1,0:T(8,128)(2,1)S(1)}, bf16[3,128,128]{2,1,0:T(8,128)(2,1)S(1)}, u32[]{:S(2)}, u32[]{:S(2)}) collective-permute-start(bf16[3,128,128]{2,1,0:T(8,128)(2,1)S(1)} %get-tuple-element.66), channel_id=1, source_target_pairs={{0,16},{16,32},{32,48},{48,64},{64,80},{80,96},{96,112},{112,128},... | collective-permute-start | bytes 294920 | tf_op jit(solution)/shard_map/ppermute | solution.py:177
  130.6 5.3 %collective-permute-start.14 = (bf16[3,128,128]{2,1,0:T(8,128)(2,1)S(1)}, bf16[3,128,128]{2,1,0:T(8,128)(2,1)S(1)}, u32[]{:S(2)}, u32[]{:S(2)}) collective-permute-start(bf16[3,128,128]{2,1,0:T(8,128)(2,1)S(1)} %get-tuple-element.67), channel_id=1, source_target_pairs={{0,496},{16,0},{32,16},{48,32},{64,48},{80,64},{96,80},{112,96},{1... | collective-permute-start | bytes 294920 | tf_op jit(solution)/shard_map/ppermute | solution.py:177
  135.9 1.9 %collective-permute-start.15 = (bf16[3,128,128]{2,1,0:T(8,128)(2,1)S(1)}, bf16[3,128,128]{2,1,0:T(8,128)(2,1)S(1)}, u32[]{:S(2)}, u32[]{:S(2)}) collective-permute-start(bf16[3,128,128]{2,1,0:T(8,128)(2,1)S(1)} %get-tuple-element.68), channel_id=1, source_target_pairs={{0,480},{16,496},{32,0},{48,16},{64,32},{80,48},{96,64},{112,80},{... | collective-permute-start | bytes 294920 | tf_op jit(solution)/shard_map/ppermute | solution.py:177
  137.9 0.7 collective-permute-done.14.r2
  138.6 5.3 %collective-permute-done.15.r3 = bf16[3,128,128]{2,1,0:T(8,128)(2,1)S(1)} collective-permute-done((bf16[3,128,128]{2,1,0:T(8,128)(2,1)S(1)}, bf16[3,128,128]{2,1,0:T(8,128)(2,1)S(1)}, u32[]{:S(2)}, u32[]{:S(2)}) %collective-permute-start.15) | collective-permute-done | bytes 98336 | tf_op jit(solution)/shard_map/ppermute | solution.py:177
  144.0 1.0 copy-done.12
  145.0 2.6 %shard_map.72._ = bf16[256,2048]{1,0:T(8,128)(2,1)} custom-call(bf16[16,128,128]{2,1,0:T(8,128)(2,1)S(1)} %all-to-all-done.1.field_ref, bf16[3,128,128]{2,1,0:T(8,128)(2,1)S(1)} %collective-permute-done.12.r0, bf16[3,128,128]{2,1,0:T(8,128)(2,1)S(1)} %collective-permute-done.13.r1, bf16[3,128,128]{2,1,0:T(8,128)(2,1)S(1)} %collective-permute-done.14.r2, ...), custom_call_target="tpu_custom_call" | custom-call | flops 335544320 | bytes 5120332 | tf_op jit(solution)/shard_map/pallas_call | solution.py:35
  147.6 2.0 %shard_map.73 = bf16[256,2048]{1,0:T(8,128)(2,1)} custom-call(bf16[256,2048]{1,0:T(8,128)(2,1)} %shard_map.72._, bf16[16,128,128]{2,1,0:T(8,128)(2,1)} %all-to-all-done.3.field_ref), custom_call_target="tpu_custom_call", output_to_operand_aliasing={{}: (0, {})} | custom-call | bytes 2621440 | tf_op jit(solution)/shard_map/pallas_call | solution.py:35
  (44 shorter events, 0.1 us)
Async XLA Ops:
  0.0 11.1 %copy-start = (bf16[16,5,128,128]{3,2,1,0:T(8,128)(2,1)S(1)}, bf16[16,5,128,128]{3,2,1,0:T(8,128)(2,1)}, u32[]{:S(2)}) copy-start(bf16[16,5,128,128]{3,2,1,0:T(8,128)(2,1)} %weights_ref.9) | copy-start | bytes 7864324
  0.0 1.4 copy-start.1
  1.4 0.8 copy-start.18
  2.1 8.8 %copy-start.27 = (s32[1,4,3]{1,0,2:T(1,128)S(1)}, s32[1,4,3]{1,0,2:T(1,128)}, u32[]{:S(2)}) copy-start(s32[1,4,3]{1,0,2:T(1,128)} %param.8) | copy-start | bytes 148
  2.3 1.0 copy-start.5
  3.3 26.0 %copy-start.26 = (s32[16,5]{0,1:T(8,128)S(1)}, s32[16,5]{0,1:T(8,128)}, u32[]{:S(2)}) copy-start(s32[16,5]{0,1:T(8,128)} %param.9) | copy-start | bytes 964
  3.3 39.2 %all-to-all-start = ((bf16[16,256,128]{2,1,0:T(8,128)(2,1)}), bf16[16,256,128]{2,1,0:T(8,128)(2,1)}, u32[]{:S(2)}, u32[]{:S(2)}) async-start(bf16[16,256,128]{2,1,0:T(8,128)(2,1)} %copy-done.5), calls=%async_computation | async-start | bytes 2097152 | tf_op jit(solution)/shard_map/all_to_all | solution.py:183
  11.1 1.2 copy-start.2
  12.3 23.0 %copy-start.15 = (s32[1,4,3]{2,1,0:T(4,128)}, s32[1,4,3]{2,1,0:T(4,128)S(1)}, u32[]{:S(2)}) copy-start(s32[1,4,3]{2,1,0:T(4,128)S(1)} %copy.8.send_ref) | copy-start | bytes 148
  14.4 14.9 %collective-permute-start = (bf16[3,128,128]{2,1,0:T(8,128)(2,1)S(1)}, bf16[3,128,128]{2,1,0:T(8,128)(2,1)S(1)}, u32[]{:S(2)}, u32[]{:S(2)}) collective-permute-start(bf16[3,128,128]{2,1,0:T(8,128)(2,1)S(1)} %get-tuple-element.39), channel_id=1, source_target_pairs={{0,32},{16,48},{32,64},{48,80},{64,96},{80,112},{96,128},{112,144}... | collective-permute-start | bytes 294920 | tf_op jit(solution)/shard_map/ppermute | solution.py:177
  19.3 10.0 %collective-permute-start.1 = (bf16[3,128,128]{2,1,0:T(8,128)(2,1)S(1)}, bf16[3,128,128]{2,1,0:T(8,128)(2,1)S(1)}, u32[]{:S(2)}, u32[]{:S(2)}) collective-permute-start(bf16[3,128,128]{2,1,0:T(8,128)(2,1)S(1)} %get-tuple-element.40), channel_id=1, source_target_pairs={{0,16},{16,32},{32,48},{48,64},{64,80},{80,96},{96,112},{112,128},... | collective-permute-start | bytes 294920 | tf_op jit(solution)/shard_map/ppermute | solution.py:177
  21.8 8.1 %collective-permute-start.2 = (bf16[3,128,128]{2,1,0:T(8,128)(2,1)S(1)}, bf16[3,128,128]{2,1,0:T(8,128)(2,1)S(1)}, u32[]{:S(2)}, u32[]{:S(2)}) collective-permute-start(bf16[3,128,128]{2,1,0:T(8,128)(2,1)S(1)} %get-tuple-element.41), channel_id=1, source_target_pairs={{0,496},{16,0},{32,16},{48,32},{64,48},{80,64},{96,80},{112,96},{1... | collective-permute-start | bytes 294920 | tf_op jit(solution)/shard_map/ppermute | solution.py:177
  27.3 8.0 %collective-permute-start.3 = (bf16[3,128,128]{2,1,0:T(8,128)(2,1)S(1)}, bf16[3,128,128]{2,1,0:T(8,128)(2,1)S(1)}, u32[]{:S(2)}, u32[]{:S(2)}) collective-permute-start(bf16[3,128,128]{2,1,0:T(8,128)(2,1)S(1)} %get-tuple-element.42), channel_id=1, source_target_pairs={{0,480},{16,496},{32,0},{48,16},{64,32},{80,48},{96,64},{112,80},{... | collective-permute-start | bytes 294920 | tf_op jit(solution)/shard_map/ppermute | solution.py:177
  35.3 1.2 copy-start.3
  36.6 0.7 copy-start.16
  39.1 0.8 copy-start.13
  39.9 0.6 copy-start.21
  40.6 0.6 copy-start.22
  41.2 0.6 copy-start.23
  41.8 0.6 copy-start.25
  44.2 0.8 copy-start.8
  45.0 0.8 copy-start.10
  45.8 32.8 %all-to-all-start.1 = ((bf16[16,128,128]{2,1,0:T(8,128)(2,1)}), bf16[16,128,128]{2,1,0:T(8,128)(2,1)S(1)}, u32[]{:S(2)}, u32[]{:S(2)}) async-start(bf16[16,128,128]{2,1,0:T(8,128)(2,1)} %copy-done.10), calls=%async_computation.1 | async-start | bytes 1048576 | tf_op jit(solution)/shard_map/all_to_all | solution.py:183
  53.0 14.1 %collective-permute-start.4 = (bf16[3,128,128]{2,1,0:T(8,128)(2,1)}, bf16[3,128,128]{2,1,0:T(8,128)(2,1)S(1)}, u32[]{:S(2)}, u32[]{:S(2)}) collective-permute-start(bf16[3,128,128]{2,1,0:T(8,128)(2,1)} %copy-done.25), channel_id=1, source_target_pairs={{0,32},{16,48},{32,64},{48,80},{64,96},{80,112},{96,128},{112,144}... | collective-permute-start | bytes 294920 | tf_op jit(solution)/shard_map/ppermute | solution.py:177
  56.9 10.2 %collective-permute-start.5 = (bf16[3,128,128]{2,1,0:T(8,128)(2,1)}, bf16[3,128,128]{2,1,0:T(8,128)(2,1)S(1)}, u32[]{:S(2)}, u32[]{:S(2)}) collective-permute-start(bf16[3,128,128]{2,1,0:T(8,128)(2,1)} %copy-done.23), channel_id=1, source_target_pairs={{0,16},{16,32},{32,48},{48,64},{64,80},{80,96},{96,112},{112,128},... | collective-permute-start | bytes 294920 | tf_op jit(solution)/shard_map/ppermute | solution.py:177
  59.6 8.3 %collective-permute-start.6 = (bf16[3,128,128]{2,1,0:T(8,128)(2,1)}, bf16[3,128,128]{2,1,0:T(8,128)(2,1)S(1)}, u32[]{:S(2)}, u32[]{:S(2)}) collective-permute-start(bf16[3,128,128]{2,1,0:T(8,128)(2,1)} %copy-done.22), channel_id=1, source_target_pairs={{0,496},{16,0},{32,16},{48,32},{64,48},{80,64},{96,80},{112,96},{1... | collective-permute-start | bytes 294920 | tf_op jit(solution)/shard_map/ppermute | solution.py:177
  64.9 8.2 %collective-permute-start.7 = (bf16[3,128,128]{2,1,0:T(8,128)(2,1)}, bf16[3,128,128]{2,1,0:T(8,128)(2,1)S(1)}, u32[]{:S(2)}, u32[]{:S(2)}) collective-permute-start(bf16[3,128,128]{2,1,0:T(8,128)(2,1)} %copy-done.21), channel_id=1, source_target_pairs={{0,480},{16,496},{32,0},{48,16},{64,32},{80,48},{96,64},{112,80},{... | collective-permute-start | bytes 294920 | tf_op jit(solution)/shard_map/ppermute | solution.py:177
  73.1 1.2 copy-start.4
  74.3 1.0 copy-start.14
  75.4 0.7 copy-start.19
  76.0 9.8 %copy-start.17 = (s32[1,4,3]{2,1,0:T(4,128)S(1)}, s32[1,4,3]{2,1,0:T(4,128)}, u32[]{:S(2)}) copy-start(s32[1,4,3]{2,1,0:T(4,128)} %copy-done.15) | copy-start | bytes 148
  77.8 0.8 copy-start.7
  78.6 33.5 %all-to-all-start.2 = ((bf16[16,128,128]{2,1,0:T(8,128)(2,1)}), bf16[16,128,128]{2,1,0:T(8,128)(2,1)}, u32[]{:S(2)}, u32[]{:S(2)}) async-start(bf16[16,128,128]{2,1,0:T(8,128)(2,1)} %copy-done.7), calls=%async_computation.2 | async-start | bytes 1048576 | tf_op jit(solution)/shard_map/all_to_all | solution.py:183
  86.5 16.3 %collective-permute-start.8 = (bf16[3,128,128]{2,1,0:T(8,128)(2,1)S(1)}, bf16[3,128,128]{2,1,0:T(8,128)(2,1)S(1)}, u32[]{:S(2)}, u32[]{:S(2)}) collective-permute-start(bf16[3,128,128]{2,1,0:T(8,128)(2,1)S(1)} %get-tuple-element.57), channel_id=1, source_target_pairs={{0,32},{16,48},{32,64},{48,80},{64,96},{80,112},{96,128},{112,144}... | collective-permute-start | bytes 294920 | tf_op jit(solution)/shard_map/ppermute | solution.py:177
  92.9 9.9 %collective-permute-start.9 = (bf16[3,128,128]{2,1,0:T(8,128)(2,1)S(1)}, bf16[3,128,128]{2,1,0:T(8,128)(2,1)S(1)}, u32[]{:S(2)}, u32[]{:S(2)}) collective-permute-start(bf16[3,128,128]{2,1,0:T(8,128)(2,1)S(1)} %get-tuple-element.58), channel_id=1, source_target_pairs={{0,16},{16,32},{32,48},{48,64},{64,80},{80,96},{96,112},{112,128},... | collective-permute-start | bytes 294920 | tf_op jit(solution)/shard_map/ppermute | solution.py:177
  95.5 8.0 %collective-permute-start.10 = (bf16[3,128,128]{2,1,0:T(8,128)(2,1)S(1)}, bf16[3,128,128]{2,1,0:T(8,128)(2,1)S(1)}, u32[]{:S(2)}, u32[]{:S(2)}) collective-permute-start(bf16[3,128,128]{2,1,0:T(8,128)(2,1)S(1)} %get-tuple-element.59), channel_id=1, source_target_pairs={{0,496},{16,0},{32,16},{48,32},{64,48},{80,64},{96,80},{112,96},{1... | collective-permute-start | bytes 294920 | tf_op jit(solution)/shard_map/ppermute | solution.py:177
  100.8 43.1 %copy-start.20 = (f32[3]{0:T(128)S(1)}, f32[3]{0:T(128)}, u32[]{:S(2)}) copy-start(f32[3]{0:T(128)} %coef_ref.3) | copy-start | bytes 40
  100.8 8.0 %collective-permute-start.11 = (bf16[3,128,128]{2,1,0:T(8,128)(2,1)S(1)}, bf16[3,128,128]{2,1,0:T(8,128)(2,1)S(1)}, u32[]{:S(2)}, u32[]{:S(2)}) collective-permute-start(bf16[3,128,128]{2,1,0:T(8,128)(2,1)S(1)} %get-tuple-element.60), channel_id=1, source_target_pairs={{0,480},{16,496},{32,0},{48,16},{64,32},{80,48},{96,64},{112,80},{... | collective-permute-start | bytes 294920 | tf_op jit(solution)/shard_map/ppermute | solution.py:177
  110.7 0.8 copy-start.11
  111.5 0.6 copy-start.24
  112.2 1.0 copy-start.9
  114.7 0.8 copy-start.6
  115.5 32.0 %all-to-all-start.3 = ((bf16[16,128,128]{2,1,0:T(8,128)(2,1)}), bf16[16,128,128]{2,1,0:T(8,128)(2,1)}, u32[]{:S(2)}, u32[]{:S(2)}) async-start(bf16[16,128,128]{2,1,0:T(8,128)(2,1)} %copy-done.6), calls=%async_computation.3 | async-start | bytes 1048576 | tf_op jit(solution)/shard_map/all_to_all | solution.py:183
  122.8 15.1 %collective-permute-start.12 = (bf16[3,128,128]{2,1,0:T(8,128)(2,1)}, bf16[3,128,128]{2,1,0:T(8,128)(2,1)S(1)}, u32[]{:S(2)}, u32[]{:S(2)}) collective-permute-start(bf16[3,128,128]{2,1,0:T(8,128)(2,1)} %copy-done.24), channel_id=1, source_target_pairs={{0,32},{16,48},{32,64},{48,80},{64,96},{80,112},{96,128},{112,144}... | collective-permute-start | bytes 294920 | tf_op jit(solution)/shard_map/ppermute | solution.py:177
  128.0 9.9 %collective-permute-start.13 = (bf16[3,128,128]{2,1,0:T(8,128)(2,1)S(1)}, bf16[3,128,128]{2,1,0:T(8,128)(2,1)S(1)}, u32[]{:S(2)}, u32[]{:S(2)}) collective-permute-start(bf16[3,128,128]{2,1,0:T(8,128)(2,1)S(1)} %get-tuple-element.66), channel_id=1, source_target_pairs={{0,16},{16,32},{32,48},{48,64},{64,80},{80,96},{96,112},{112,128},... | collective-permute-start | bytes 294920 | tf_op jit(solution)/shard_map/ppermute | solution.py:177
  130.6 8.0 %collective-permute-start.14 = (bf16[3,128,128]{2,1,0:T(8,128)(2,1)S(1)}, bf16[3,128,128]{2,1,0:T(8,128)(2,1)S(1)}, u32[]{:S(2)}, u32[]{:S(2)}) collective-permute-start(bf16[3,128,128]{2,1,0:T(8,128)(2,1)S(1)} %get-tuple-element.67), channel_id=1, source_target_pairs={{0,496},{16,0},{32,16},{48,32},{64,48},{80,64},{96,80},{112,96},{1... | collective-permute-start | bytes 294920 | tf_op jit(solution)/shard_map/ppermute | solution.py:177
  135.9 8.0 %collective-permute-start.15 = (bf16[3,128,128]{2,1,0:T(8,128)(2,1)S(1)}, bf16[3,128,128]{2,1,0:T(8,128)(2,1)S(1)}, u32[]{:S(2)}, u32[]{:S(2)}) collective-permute-start(bf16[3,128,128]{2,1,0:T(8,128)(2,1)S(1)} %get-tuple-element.68), channel_id=1, source_target_pairs={{0,480},{16,496},{32,0},{48,16},{64,32},{80,48},{96,64},{112,80},{... | collective-permute-start | bytes 294920 | tf_op jit(solution)/shard_map/ppermute | solution.py:177
  144.0 1.0 copy-start.12

commit v3 on v2

v3 whole, which is shorter than its diff:
```python
import functools

import jax
import jax.numpy as jnp
from jax import lax
from jax.experimental import pallas as pl
from jax.experimental.pallas import tpu as pltpu
from jax.sharding import PartitionSpec as P

REACH = 2
OFFSETS = tuple(range(-REACH, 0)) + tuple(range(1, REACH + 1))
F32, BF16 = jnp.float32, jnp.bfloat16
LIMIT = 24 * 2**20
SMEM = pl.BlockSpec(memory_space=pltpu.SMEM)
VMEM = pl.BlockSpec(memory_space=pltpu.VMEM)
HBM = pl.BlockSpec(memory_space=pltpu.HBM)
ANY = pl.BlockSpec(memory_space=pl.ANY)
DMA = pltpu.SemaphoreType.DMA


def call(kernel, outs, ins, scratch, flops=0, aliases=None):
    arrays, specs = zip(*ins)
    shapes, results = zip(*outs)
    size = sum(a.size * a.dtype.itemsize for a in (*arrays, *shapes))
    arrays = [pltpu.with_memory_space_constraint(a, pltpu.HBM) if spec is HBM else a for a, spec in ins]
    shapes = [pltpu.HBM(a.shape, a.dtype) if spec is HBM else a for a, spec in outs]
    return pl.pallas_call(
        kernel,
        out_shape=shapes,
        in_specs=specs,
        out_specs=results,
        scratch_shapes=scratch,
        compiler_params=pltpu.CompilerParams(vmem_limit_bytes=LIMIT),
        cost_estimate=pl.CostEstimate(flops=flops, bytes_accessed=size, transcendentals=0),
        input_output_aliases=aliases or {},
    )(*arrays)


def array(*shape, dtype=BF16):
    return jax.ShapeDtypeStruct(shape, dtype)


def start(source, target, sem):
    copy = pltpu.make_async_copy(source, target, sem)
    copy.start()
    return copy


def wait(copies):
    for copy in copies:
        copy.wait()


def times_transposed(a, b):
    return lax.dot_general(a, b, (((1,), (1,)), ((), ())), preferred_element_type=F32)


def block_of(ref, g, width):
    if len(ref.shape) == 3:
        return ref[g]
    at = g * width
    return ref[:, pl.ds(at if isinstance(g, int) else pl.multiple_of(at, width), width)]


def scaled_block(ref, inv_ref, g, width):
    return (block_of(ref, g, width).astype(F32) * inv_ref[pl.ds(g, 1), :]).astype(BF16)


def pack(send_ref, field_ref, inv_ref, packs, held, sems):
    width = inv_ref.shape[1]
    copies = []
    for way, out in enumerate(packs):
        for slot in range(out.shape[0]):
            held[way, slot] = scaled_block(field_ref, inv_ref, send_ref[0, way, slot], width)
        copies.append(start(held.at[way], out, sems.at[way]))
    return copies


def lay_out(signal_ref, kernel_ref, out_ref, held, mix, in_sems, out_sems, mix_sem):
    owners, chunk, width = out_ref.shape
    t_loc, time = kernel_ref.shape
    rows = chunk - time * t_loc // width
    mixing = start(kernel_ref, mix, mix_sem)
    loads = [
        start(signal_ref.at[:rows, i * width : (i + 1) * width], held.at[i, :rows], in_sems.at[i])
        for i in range(owners)
    ]
    mixing.wait()
    copies = []
    for i in range(owners):
        for q in range(time // width):
            held[i, rows + q * t_loc : rows + (q + 1) * t_loc] = mix[:, q * width : (q + 1) * width]
        loads[i].wait()
        copies.append(start(held.at[i], out_ref.at[i], out_sems.at[i]))
    wait(copies)


def first_scale(signal_ref, weights_ref, send_ref, coef_ref, inv_ref, *rest):
    *packs, field, held, sems, load_sem = rest
    blocks, per_row, width, _ = weights_ref.shape
    rows = field.shape[0]
    load = start(signal_ref.at[rows:], field, load_sem)
    ones = jnp.ones((16, width), BF16)
    for g in range(blocks):
        degree = times_transposed(ones, weights_ref[g, 0])
        for j in range(1, per_row):
            degree += times_transposed(ones, weights_ref[g, j])
        inv_ref[g : g + 1, :] = lax.rsqrt(degree[:1])
    for term in range(coef_ref.shape[0]):
        inv_ref[blocks + term : blocks + term + 1, :] = jnp.full((1, width), coef_ref[term], F32)
    load.wait()
    wait(pack(send_ref, field, inv_ref, packs, held, sems))


def scale(field_ref, inv_ref, send_ref, *rest):
    *packs, held, sems = rest
    wait(pack(send_ref, field_ref, inv_ref, packs, held, sems))


def gather_sources(blocks, field_ref, inv_ref, received, source):
    width = inv_ref.shape[1]
    for g in range(blocks):
        source[g] = scaled_block(field_ref, inv_ref, g, width)
    for way, ref in enumerate(received):
        slots = ref.shape[0]
        source[blocks + way * slots : blocks + (way + 1) * slots] = ref[...]


def block_product(g, col_ref, weights_ref, source):
    per_row = weights_ref.shape[1]
    picked = jnp.concatenate([source[col_ref[g, j]] for j in range(per_row)], axis=1)
    edges = jnp.concatenate([weights_ref[g, j] for j in range(per_row)], axis=1)
    return times_transposed(picked, edges)


def load_half(field_ref, field, sem):
    return [start(field_ref.at[field.shape[0] :], field, sem)]


def first_product(in_hbm, field_ref, r0, r1, r2, r3, weights_ref, inv_ref, col_ref, send_ref, term_ref, *rest):
    *packs, source, term, held, sems, pack_sems = rest[: len(OFFSETS) + 5]
    if in_hbm:
        field, load_sem = rest[len(OFFSETS) + 5 :]
        wait(load_half(field_ref, field, load_sem))
        field_ref = field
    blocks = weights_ref.shape[0]
    gather_sources(blocks, field_ref, inv_ref, (r0, r1, r2, r3), source)
    copies = []
    for g in range(blocks):
        total = block_product(g, col_ref, weights_ref, source)
        term[g] = (-inv_ref[g : g + 1, :] * total).astype(BF16)
        copies.append(start(term.at[g], term_ref.at[g], sems.at[g]))
    wait(copies + pack(send_ref, term, inv_ref, packs, held, pack_sems))


def second_product(in_hbm, field_ref, r0, r1, r2, r3, weights_ref, inv_ref, col_ref, term_ref, out_ref, *rest):
    source, term, held, sems, term_sem = rest[:5]
    loads = [start(term_ref, term, term_sem)]
    if in_hbm:
        field, load_sem = rest[5:]
        loads += load_half(field_ref, field, load_sem)
        field_ref = field
    wait(loads)
    blocks, _, width, _ = weights_ref.shape
    rows = term.shape[1]
    gather_sources(blocks, term, inv_ref, (r0, r1, r2, r3), source)
    coef = [inv_ref[blocks + i : blocks + i + 1, :] for i in range(3)]
    copies = []
    for g in range(blocks):
        total = block_product(g, col_ref, weights_ref, source)
        x = block_of(field_ref, g, width).astype(F32)
        two = (-2.0 * inv_ref[g : g + 1, :] * total - x).astype(BF16).astype(F32)
        one = term[g].astype(F32)
        held[g] = (coef[0] * x + coef[1] * one + coef[2] * two).astype(BF16)
        if len(out_ref.shape) == 3:
            target = out_ref.at[g]
        else:
            target = out_ref.at[:rows, g * width : (g + 1) * width]
        copies.append(start(held.at[g], target, sems.at[g]))
    wait(copies)


def mix_times(t_loc, mix, field_ref, out_ref, columns, held, sems):
    owners, rows, width = out_ref.shape
    for p in range(rows // t_loc):
        part = slice(p * t_loc, (p + 1) * t_loc)
        for i in range(owners):
            columns[i * t_loc : (i + 1) * t_loc, p * width : (p + 1) * width] = field_ref[i, part]
    step = 2 * width
    pieces = columns.shape[1] // step
    depth = rows // pieces
    copies = []
    for c in range(pieces):
        out = jnp.dot(mix, columns[:, c * step : (c + 1) * step], preferred_element_type=F32).astype(BF16)
        for q in range(step // width):
            at = c * depth + q * t_loc
            for i in range(owners):
                held[i, at : at + t_loc] = out[i * t_loc : (i + 1) * t_loc, q * width : (q + 1) * width]
        part = slice(c * depth, (c + 1) * depth)
        copies.append(start(held.at[:, part], out_ref.at[:, part], sems.at[c]))
    return copies


def first_temporal(t_loc, field_ref, out_ref, mix_ref, columns, held, mix, sems, mix_sem):
    owners, rows, width = out_ref.shape
    for i in range(owners):
        for q in range(mix.shape[1] // width):
            mix[i * t_loc : (i + 1) * t_loc, q * width : (q + 1) * width] = field_ref[
                i, rows + q * t_loc : rows + (q + 1) * t_loc
            ]
    keep = start(mix, mix_ref, mix_sem)
    wait(mix_times(t_loc, mix[...], field_ref, out_ref, columns, held, sems) + [keep])


def second_temporal(t_loc, field_ref, mix_ref, out_ref, columns, held, mix, sems, mix_sem):
    start(mix_ref, mix, mix_sem).wait()
    wait(mix_times(t_loc, mix[...], field_ref, out_ref, columns, held, sems))


def unblock(_, field_ref, out_ref, sems):
    blocks, rows, width = field_ref.shape
    wait(
        [
            start(field_ref.at[g], out_ref.at[rows:, g * width : (g + 1) * width], sems.at[g])
            for g in range(blocks)
        ]
    )


def take(block, way):
    count = lax.axis_size("dom")
    return lax.ppermute(block, "dom", [(i, (i - OFFSETS[way]) % count) for i in range(count)])


def exchange(field):
    return lax.all_to_all(field, "tm", split_axis=0, concat_axis=0, tiled=True)


def body(signal, weights, send_list, col_ref, kernel, cheb_coef):
    probes, t_loc, n_loc = signal.shape
    blocks, per_row, width, _ = weights.shape
    rows = probes * t_loc // 2
    slots = send_list.shape[2]
    owners = lax.axis_size("tm")
    time = kernel.shape[1]
    ways = len(OFFSETS)
    pieces = rows // t_loc // 2
    xs = signal.reshape(2 * rows, n_loc)
    field = array(blocks, rows, width)
    packed = [(array(slots, rows, width), HBM)] * ways
    vm = pltpu.VMEM
    source = vm((blocks + ways * slots, rows, width), BF16)
    whole = vm((blocks, rows, width), BF16)
    held = vm((ways, slots, rows, width), BF16)
    second_half = [vm((rows, n_loc), BF16), DMA]
    mixer = [vm((time, rows // t_loc * width), BF16), whole, vm((time, time), BF16), DMA((pieces,)), DMA]
    work = 2 * rows * per_row * n_loc * width
    mixing = 2 * time * time * rows // t_loc * width
    barrier = lax.optimization_barrier

    def one(x, received, inv, in_hbm):
        term, *packs = call(
            functools.partial(first_product, in_hbm),
            [(field, HBM), *packed],
            [
                (x, HBM if in_hbm else VMEM),
                *((r, VMEM) for r in received),
                (weights, VMEM),
                (inv, VMEM),
                (col_ref, SMEM),
                (send_list, SMEM),
            ],
            [source, whole, held, DMA((blocks,)), DMA((ways,))] + (second_half if in_hbm else []),
            flops=work,
        )
        return term, packs

    def two(x, received, inv, term, out, in_hbm):
        return call(
            functools.partial(second_product, in_hbm),
            [(out, HBM)],
            [
                (x, HBM if in_hbm else VMEM),
                *((r, VMEM) for r in received),
                (weights, VMEM),
                (inv, VMEM),
                (col_ref, SMEM),
                (term, HBM),
            ],
            [source, whole, whole, DMA((blocks,)), DMA] + (second_half if in_hbm else []),
            flops=work,
        )[0]

    chunk = rows + time * t_loc // width
    (laid,) = call(
        lay_out,
        [(array(owners, chunk, width), HBM)],
        [(xs, HBM), (kernel, HBM)],
        [vm((owners, chunk, width), BF16), vm(kernel.shape, BF16), DMA((owners,)), DMA((owners,)), DMA],
    )
    arrived = exchange(laid)
    inv, *packs = call(
        first_scale,
        [(array(blocks + 8, width, dtype=F32), VMEM), *packed],
        [(xs, HBM), (weights, VMEM), (send_list, SMEM), (cheb_coef, SMEM)],
        [vm((rows, n_loc), BF16), held, DMA((ways,)), DMA],
        flops=work // 8,
    )
    received = [take(block, way) for way, block in enumerate(packs)]
    term, packs = one(xs, received, inv, True)

    received = [take(packs[way], way) for way in range(ways // 2)]
    early, mix = call(
        functools.partial(first_temporal, t_loc),
        [(field, HBM), (array(time, time), HBM)],
        [(arrived, VMEM)],
        mixer,
        flops=mixing,
    )
    early, *rest = barrier((early, *packs[ways // 2 :]))
    early = exchange(early)
    received += [take(block, ways // 2 + i) for i, block in enumerate(rest)]

    packs = call(scale, packed, [(early, VMEM), (inv, VMEM), (send_list, SMEM)], [held, DMA((ways,))])
    term, *packs = barrier((term, *packs))
    later = [take(packs[way], way) for way in range(ways // 2)]
    late = two(xs, received, inv, term, field, True)
    late, *rest = barrier((late, *packs[ways // 2 :]))
    late = exchange(late)
    received = later + [take(block, ways // 2 + i) for i, block in enumerate(rest)]
    term, packs = one(early, received, inv, False)

    received = [take(packs[way], way) for way in range(ways // 2)]
    (late,) = call(
        functools.partial(second_temporal, t_loc), [(field, HBM)], [(late, VMEM), (mix, HBM)], mixer, flops=mixing
    )
    late, *rest = barrier((late, *packs[ways // 2 :]))
    late = exchange(late)
    received += [take(block, ways // 2 + i) for i, block in enumerate(rest)]
    out = array(2 * rows, n_loc)
    done = two(early, received, inv, term, out, False)
    (done,) = call(unblock, [(out, HBM)], [(done, HBM), (late, ANY)], [DMA((blocks,))], aliases={0: 0})
    return done.reshape(probes, t_loc, n_loc)


def solution(mesh):
    in_specs = (
        P(None, "tm", "dom"),
        P("dom", None, None, None),
        P("dom", None, None),
        P("dom", None),
        P("tm", None),
        P(),
    )
    out_specs = P(None, "tm", "dom")
    return jax.shard_map(body, mesh=mesh, in_specs=in_specs, out_specs=out_specs, check_vma=False)
```

time: 151 us -> 158 us (1.046)
  Pallas kernels: 16.2 us -> 44 us
  local copies, waits for them, and re-layouts: 19.4 us -> 0.21 us
    pallas_call x10, Pallas kernels: 16.2 us -> 44 us  [call(): pl.pallas_call(kernel, out_shape=shapes, in_specs=specs, out_specs=result...]
    unnamed x58 -> x16, local copies, waits for them, and re-layouts: 19.4 us -> 0.21 us
  transfers between devices with their start and end apart: 20 -> 20, of which waited for: 8 -> 8; matrix products, arithmetic and copies ran while one was open for 0% -> 0% of each run, Pallas kernels for 7% -> 9%
where the time goes in v3:
time: 158 us; the launch traced here: 157 us
  starting transfers between devices  89.5 us (57%)
  Pallas kernels  44 us (28%)
  waiting for transfers between devices  23.2 us (15%)
    ppermute x16, starting transfers between devices, take(): lax.ppermute(block, 'dom', [(i, (i - OFFSETS[way]) % count) for i in rang...  60.2 us
    pallas_call x10, Pallas kernels, call(): pl.pallas_call(kernel, out_shape=shapes, in_specs=specs, out_specs=result...  44 us
    all_to_all x4, starting transfers between devices, exchange(): return lax.all_to_all(field, 'tm', split_axis=0, concat_axis=0, tiled=True)  29.3 us
    ppermute x16, waiting for transfers between devices, take(): lax.ppermute(block, 'dom', [(i, (i - OFFSETS[way]) % count) for i in rang...  23 us
  transfers between devices with their start and end apart: 20, of which 8 were waited for; matrix products, arithmetic and copies ran while one was open for 0% of the time, Pallas kernels for 9%

profile of v3, /device:TPU:136, one launch (start us, length us, event | category | flops | bytes accessed | tf_op | source)
XLA Modules:
  0.0 157.3 jit_solution(650078588478293270)
XLA Ops:
  0.0 0.0 copy-start.3
  0.0 2.4 %shard_map.64 = bf16[16,256,128]{2,1,0:T(8,128)(2,1)} custom-call(bf16[256,2048]{1,0:T(8,128)(2,1)} %bitcast.2, bf16[32,512]{1,0:T(8,128)(2,1)} %kernel_ref.1), custom_call_target="tpu_custom_call" | custom-call | bytes 2129920 | tf_op jit(solution)/shard_map/pallas_call | solution.py:27
  2.4 0.0 copy-start.2
  2.4 7.6 %all-to-all-start = ((bf16[16,256,128]{2,1,0:T(8,128)(2,1)}), bf16[16,256,128]{2,1,0:T(8,128)(2,1)}, u32[]{:S(2)}, u32[]{:S(2)}) async-start(bf16[16,256,128]{2,1,0:T(8,128)(2,1)} %shard_map.64), calls=%async_computation | async-start | bytes 2097152 | tf_op jit(solution)/shard_map/all_to_all | solution.py:236
  10.0 0.0 copy-done.3
  10.0 0.1 copy.8.send_ref
  10.1 0.0 copy-done
  10.1 0.0 copy-done.1
  10.1 2.9 %shard_map.66 = (f32[24,128]{1,0:T(8,128)S(1)}, bf16[3,128,128]{2,1,0:T(8,128)(2,1)}, bf16[3,128,128]{2,1,0:T(8,128)(2,1)}, bf16[3,128,128]{2,1,0:T(8,128)(2,1)}, bf16[3,128,128]{2,1,0:T(8,128)(2,1)}) custom-call(bf16[256,2048]{1,0:T(8,128)(2,1)} %bitcast.3, bf16[16,5,128,128]{3,2,1,0:T(8,128)(2,1)S(1)} %copy-done, s32[1,4,3]{2,1,0:T(4,128)S(1)} %copy.8.send_ref, ...), custom_call_target="tpu_custom_call" | custom-call | flops 41943040 | bytes 4075580 | tf_op jit(solution)/shard_map/pallas_call | solution.py:27
  13.0 4.9 %collective-permute-start = (bf16[3,128,128]{2,1,0:T(8,128)(2,1)}, bf16[3,128,128]{2,1,0:T(8,128)(2,1)S(1)}, u32[]{:S(2)}, u32[]{:S(2)}) collective-permute-start(bf16[3,128,128]{2,1,0:T(8,128)(2,1)} %get-tuple-element.41), channel_id=1, source_target_pairs={{0,32},{16,48},{32,64},{48,80},{64,96},{80,112},{96,128},{112,144}... | collective-permute-start | bytes 294920 | tf_op jit(solution)/shard_map/ppermute | solution.py:232
  17.9 2.5 %collective-permute-start.1 = (bf16[3,128,128]{2,1,0:T(8,128)(2,1)}, bf16[3,128,128]{2,1,0:T(8,128)(2,1)S(1)}, u32[]{:S(2)}, u32[]{:S(2)}) collective-permute-start(bf16[3,128,128]{2,1,0:T(8,128)(2,1)} %get-tuple-element.42), channel_id=1, source_target_pairs={{0,16},{16,32},{32,48},{48,64},{64,80},{80,96},{96,112},{112,128},... | collective-permute-start | bytes 294920 | tf_op jit(solution)/shard_map/ppermute | solution.py:232
  20.4 5.5 %collective-permute-start.2 = (bf16[3,128,128]{2,1,0:T(8,128)(2,1)}, bf16[3,128,128]{2,1,0:T(8,128)(2,1)S(1)}, u32[]{:S(2)}, u32[]{:S(2)}) collective-permute-start(bf16[3,128,128]{2,1,0:T(8,128)(2,1)} %get-tuple-element.43), channel_id=1, source_target_pairs={{0,496},{16,0},{32,16},{48,32},{64,48},{80,64},{96,80},{112,96},{1... | collective-permute-start | bytes 294920 | tf_op jit(solution)/shard_map/ppermute | solution.py:232
  25.9 1.9 %collective-permute-start.3 = (bf16[3,128,128]{2,1,0:T(8,128)(2,1)}, bf16[3,128,128]{2,1,0:T(8,128)(2,1)S(1)}, u32[]{:S(2)}, u32[]{:S(2)}) collective-permute-start(bf16[3,128,128]{2,1,0:T(8,128)(2,1)} %get-tuple-element.44), channel_id=1, source_target_pairs={{0,480},{16,496},{32,0},{48,16},{64,32},{80,48},{96,64},{112,80},{... | collective-permute-start | bytes 294920 | tf_op jit(solution)/shard_map/ppermute | solution.py:232
  27.8 0.0 copy-done.2
  27.8 0.1 copy.9.col_ref
  27.9 0.0 collective-permute-done.r0
  27.9 0.0 collective-permute-done.1.r1
  27.9 1.0 collective-permute-done.2.r2
  28.9 5.2 %collective-permute-done.3.r3 = bf16[3,128,128]{2,1,0:T(8,128)(2,1)S(1)} collective-permute-done((bf16[3,128,128]{2,1,0:T(8,128)(2,1)}, bf16[3,128,128]{2,1,0:T(8,128)(2,1)S(1)}, u32[]{:S(2)}, u32[]{:S(2)}) %collective-permute-start.3) | collective-permute-done | bytes 98336 | tf_op jit(solution)/shard_map/ppermute | solution.py:232
  34.1 3.8 %shard_map.67 = (bf16[16,128,128]{2,1,0:T(8,128)(2,1)}, bf16[3,128,128]{2,1,0:T(8,128)(2,1)}, bf16[3,128,128]{2,1,0:T(8,128)(2,1)}, bf16[3,128,128]{2,1,0:T(8,128)(2,1)}, bf16[3,128,128]{2,1,0:T(8,128)(2,1)}) custom-call(bf16[256,2048]{1,0:T(8,128)(2,1)} %bitcast.4, bf16[3,128,128]{2,1,0:T(8,128)(2,1)S(1)} %collective-permute-done.r0, ...), custom_call_target="tpu_custom_call" | custom-call | flops 335544320 | bytes 4993392 | tf_op jit(solution)/shard_map/pallas_call | solution.py:27
  37.9 0.0 all-to-all-done.field_ref
  38.0 2.6 %shard_map.65 = (bf16[16,128,128]{2,1,0:T(8,128)(2,1)}, bf16[512,512]{1,0:T(8,128)(2,1)}) custom-call(bf16[16,256,128]{2,1,0:T(8,128)(2,1)} %all-to-all-done.field_ref), custom_call_target="tpu_custom_call" | custom-call | flops 268435456 | bytes 2097152 | tf_op jit(solution)/shard_map/pallas_call | solution.py:27
  40.5 7.2 %all-to-all-start.1 = ((bf16[16,128,128]{2,1,0:T(8,128)(2,1)}), bf16[16,128,128]{2,1,0:T(8,128)(2,1)S(1)}, u32[]{:S(2)}, u32[]{:S(2)}) async-start(bf16[16,128,128]{2,1,0:T(8,128)(2,1)} %get-tuple-element.48), calls=%async_computation.1 | async-start | bytes 1048576 | tf_op jit(solution)/shard_map/all_to_all | solution.py:236
  47.8 3.9 %collective-permute-start.6 = (bf16[3,128,128]{2,1,0:T(8,128)(2,1)}, bf16[3,128,128]{2,1,0:T(8,128)(2,1)S(1)}, u32[]{:S(2)}, u32[]{:S(2)}) collective-permute-start(bf16[3,128,128]{2,1,0:T(8,128)(2,1)} %get-tuple-element.56), channel_id=1, source_target_pairs={{0,32},{16,48},{32,64},{48,80},{64,96},{80,112},{96,128},{112,144}... | collective-permute-start | bytes 294920 | tf_op jit(solution)/shard_map/ppermute | solution.py:232
  51.7 2.7 %collective-permute-start.7 = (bf16[3,128,128]{2,1,0:T(8,128)(2,1)}, bf16[3,128,128]{2,1,0:T(8,128)(2,1)S(1)}, u32[]{:S(2)}, u32[]{:S(2)}) collective-permute-start(bf16[3,128,128]{2,1,0:T(8,128)(2,1)} %get-tuple-element.57), channel_id=1, source_target_pairs={{0,16},{16,32},{32,48},{48,64},{64,80},{80,96},{96,112},{112,128},... | collective-permute-start | bytes 294920 | tf_op jit(solution)/shard_map/ppermute | solution.py:232
  54.3 5.3 %collective-permute-start.8 = (bf16[3,128,128]{2,1,0:T(8,128)(2,1)}, bf16[3,128,128]{2,1,0:T(8,128)(2,1)S(1)}, u32[]{:S(2)}, u32[]{:S(2)}) collective-permute-start(bf16[3,128,128]{2,1,0:T(8,128)(2,1)} %get-tuple-element.58), channel_id=1, source_target_pairs={{0,496},{16,0},{32,16},{48,32},{64,48},{80,64},{96,80},{112,96},{1... | collective-permute-start | bytes 294920 | tf_op jit(solution)/shard_map/ppermute | solution.py:232
  59.6 2.2 %collective-permute-start.9 = (bf16[3,128,128]{2,1,0:T(8,128)(2,1)}, bf16[3,128,128]{2,1,0:T(8,128)(2,1)}, u32[]{:S(2)}, u32[]{:S(2)}) collective-permute-start(bf16[3,128,128]{2,1,0:T(8,128)(2,1)} %get-tuple-element.59), channel_id=1, source_target_pairs={{0,480},{16,496},{32,0},{48,16},{64,32},{80,48},{96,64},{112,80},{... | collective-permute-start | bytes 294920 | tf_op jit(solution)/shard_map/ppermute | solution.py:232
  61.9 0.3 all-to-all-done.1.field_ref
  62.1 1.4 shard_map.68
  63.5 0.0 collective-permute-done.6.r0
  63.5 0.0 collective-permute-done.7.r1
  63.5 0.0 collective-permute-done.8.r2
  63.5 4.4 %collective-permute-done.9.r3 = bf16[3,128,128]{2,1,0:T(8,128)(2,1)} collective-permute-done((bf16[3,128,128]{2,1,0:T(8,128)(2,1)}, bf16[3,128,128]{2,1,0:T(8,128)(2,1)}, u32[]{:S(2)}, u32[]{:S(2)}) %collective-permute-start.9) | collective-permute-done | bytes 98336 | tf_op jit(solution)/shard_map/ppermute | solution.py:232
  68.0 4.0 %shard_map.69 = bf16[16,128,128]{2,1,0:T(8,128)(2,1)} custom-call(bf16[256,2048]{1,0:T(8,128)(2,1)} %bitcast.5, bf16[3,128,128]{2,1,0:T(8,128)(2,1)S(1)} %collective-permute-done.6.r0, bf16[3,128,128]{2,1,0:T(8,128)(2,1)S(1)} %collective-permute-done.7.r1, bf16[3,128,128]{2,1,0:T(8,128)(2,1)S(1)} %collective-permute-done.8.r2, ...), custom_call_target="tpu_custom_call" | custom-call | flops 335544320 | bytes 5124416 | tf_op jit(solution)/shard_map/pallas_call | solution.py:27
  72.0 7.2 %all-to-all-start.2 = ((bf16[16,128,128]{2,1,0:T(8,128)(2,1)}), bf16[16,128,128]{2,1,0:T(8,128)(2,1)}, u32[]{:S(2)}, u32[]{:S(2)}) async-start(bf16[16,128,128]{2,1,0:T(8,128)(2,1)} %shard_map.69), calls=%async_computation.2 | async-start | bytes 1048576 | tf_op jit(solution)/shard_map/all_to_all | solution.py:236
  79.2 6.3 %collective-permute-start.4 = (bf16[3,128,128]{2,1,0:T(8,128)(2,1)}, bf16[3,128,128]{2,1,0:T(8,128)(2,1)S(1)}, u32[]{:S(2)}, u32[]{:S(2)}) collective-permute-start(bf16[3,128,128]{2,1,0:T(8,128)(2,1)} %get-tuple-element.54), channel_id=1, source_target_pairs={{0,32},{16,48},{32,64},{48,80},{64,96},{80,112},{96,128},{112,144}... | collective-permute-start | bytes 294920 | tf_op jit(solution)/shard_map/ppermute | solution.py:232
  85.6 2.6 %collective-permute-start.5 = (bf16[3,128,128]{2,1,0:T(8,128)(2,1)}, bf16[3,128,128]{2,1,0:T(8,128)(2,1)S(1)}, u32[]{:S(2)}, u32[]{:S(2)}) collective-permute-start(bf16[3,128,128]{2,1,0:T(8,128)(2,1)} %get-tuple-element.55), channel_id=1, source_target_pairs={{0,16},{16,32},{32,48},{48,64},{64,80},{80,96},{96,112},{112,128},... | collective-permute-start | bytes 294920 | tf_op jit(solution)/shard_map/ppermute | solution.py:232
  88.2 5.3 %collective-permute-start.10 = (bf16[3,128,128]{2,1,0:T(8,128)(2,1)}, bf16[3,128,128]{2,1,0:T(8,128)(2,1)S(1)}, u32[]{:S(2)}, u32[]{:S(2)}) collective-permute-start(bf16[3,128,128]{2,1,0:T(8,128)(2,1)} %get-tuple-element.63), channel_id=1, source_target_pairs={{0,496},{16,0},{32,16},{48,32},{64,48},{80,64},{96,80},{112,96},{1... | collective-permute-start | bytes 294920 | tf_op jit(solution)/shard_map/ppermute | solution.py:232
  93.5 1.9 %collective-permute-start.11 = (bf16[3,128,128]{2,1,0:T(8,128)(2,1)}, bf16[3,128,128]{2,1,0:T(8,128)(2,1)S(1)}, u32[]{:S(2)}, u32[]{:S(2)}) collective-permute-start(bf16[3,128,128]{2,1,0:T(8,128)(2,1)} %get-tuple-element.64), channel_id=1, source_target_pairs={{0,480},{16,496},{32,0},{48,16},{64,32},{80,48},{96,64},{112,80},{... | collective-permute-start | bytes 294920 | tf_op jit(solution)/shard_map/ppermute | solution.py:232
  95.4 0.0 collective-permute-done.4.r0
  95.5 0.0 collective-permute-done.5.r1
  95.5 1.1 collective-permute-done.10.r2
  96.5 5.2 %collective-permute-done.11.r3 = bf16[3,128,128]{2,1,0:T(8,128)(2,1)S(1)} collective-permute-done((bf16[3,128,128]{2,1,0:T(8,128)(2,1)}, bf16[3,128,128]{2,1,0:T(8,128)(2,1)S(1)}, u32[]{:S(2)}, u32[]{:S(2)}) %collective-permute-start.11) | collective-permute-done | bytes 98336 | tf_op jit(solution)/shard_map/ppermute | solution.py:232
  101.7 2.8 %shard_map.70 = (bf16[16,128,128]{2,1,0:T(8,128)(2,1)}, bf16[3,128,128]{2,1,0:T(8,128)(2,1)}, bf16[3,128,128]{2,1,0:T(8,128)(2,1)}, bf16[3,128,128]{2,1,0:T(8,128)(2,1)}, bf16[3,128,128]{2,1,0:T(8,128)(2,1)}) custom-call(bf16[16,128,128]{2,1,0:T(8,128)(2,1)S(1)} %all-to-all-done.1.field_ref, bf16[3,128,128]{2,1,0:T(8,128)(2,1)S(1)} %collective-permute-done.4.r0, ...), custom_call_target="tpu_custom_call" | custom-call | flops 335544320 | bytes 4469104 | tf_op jit(solution)/shard_map/pallas_call | solution.py:27
  104.5 0.0 copy-start.6
  104.5 0.0 copy-start.5
  104.5 0.0 copy-start.4
  104.5 0.0 all-to-all-done.2.field_ref
  104.6 3.4 %shard_map.71 = bf16[16,128,128]{2,1,0:T(8,128)(2,1)} custom-call(bf16[16,128,128]{2,1,0:T(8,128)(2,1)} %all-to-all-done.2.field_ref, bf16[512,512]{1,0:T(8,128)(2,1)} %get-tuple-element.68.mix_ref), custom_call_target="tpu_custom_call" | custom-call | flops 268435456 | bytes 1572864 | tf_op jit(solution)/shard_map/pallas_call | solution.py:27
  108.0 7.2 %all-to-all-start.3 = ((bf16[16,128,128]{2,1,0:T(8,128)(2,1)}), bf16[16,128,128]{2,1,0:T(8,128)(2,1)}, u32[]{:S(2)}, u32[]{:S(2)}) async-start(bf16[16,128,128]{2,1,0:T(8,128)(2,1)} %shard_map.71), calls=%async_computation.3 | async-start | bytes 1048576 | tf_op jit(solution)/shard_map/all_to_all | solution.py:236
  115.2 5.2 %collective-permute-start.12 = (bf16[3,128,128]{2,1,0:T(8,128)(2,1)}, bf16[3,128,128]{2,1,0:T(8,128)(2,1)S(1)}, u32[]{:S(2)}, u32[]{:S(2)}) collective-permute-start(bf16[3,128,128]{2,1,0:T(8,128)(2,1)} %get-tuple-element.65), channel_id=1, source_target_pairs={{0,32},{16,48},{32,64},{48,80},{64,96},{80,112},{96,128},{112,144}... | collective-permute-start | bytes 294920 | tf_op jit(solution)/shard_map/ppermute | solution.py:232
  120.5 0.0 copy-done.6
  120.5 2.7 %collective-permute-start.13 = (bf16[3,128,128]{2,1,0:T(8,128)(2,1)S(1)}, bf16[3,128,128]{2,1,0:T(8,128)(2,1)S(1)}, u32[]{:S(2)}, u32[]{:S(2)}) collective-permute-start(bf16[3,128,128]{2,1,0:T(8,128)(2,1)S(1)} %copy-done.6), channel_id=1, source_target_pairs={{0,16},{16,32},{32,48},{48,64},{64,80},{80,96},{96,112},{112,128},... | collective-permute-start | bytes 294920 | tf_op jit(solution)/shard_map/ppermute | solution.py:232
  123.2 0.0 copy-done.5
  123.2 5.3 %collective-permute-start.14 = (bf16[3,128,128]{2,1,0:T(8,128)(2,1)S(1)}, bf16[3,128,128]{2,1,0:T(8,128)(2,1)S(1)}, u32[]{:S(2)}, u32[]{:S(2)}) collective-permute-start(bf16[3,128,128]{2,1,0:T(8,128)(2,1)S(1)} %copy-done.5), channel_id=1, source_target_pairs={{0,496},{16,0},{32,16},{48,32},{64,48},{80,64},{96,80},{112,96},{1... | collective-permute-start | bytes 294920 | tf_op jit(solution)/shard_map/ppermute | solution.py:232
  128.5 0.0 copy-done.4
  128.5 1.9 %collective-permute-start.15 = (bf16[3,128,128]{2,1,0:T(8,128)(2,1)S(1)}, bf16[3,128,128]{2,1,0:T(8,128)(2,1)S(1)}, u32[]{:S(2)}, u32[]{:S(2)}) collective-permute-start(bf16[3,128,128]{2,1,0:T(8,128)(2,1)S(1)} %copy-done.4), channel_id=1, source_target_pairs={{0,480},{16,496},{32,0},{48,16},{64,32},{80,48},{96,64},{112,80},{... | collective-permute-start | bytes 294920 | tf_op jit(solution)/shard_map/ppermute | solution.py:232
  130.4 0.0 collective-permute-done.12.r0
  130.4 0.0 collective-permute-done.13.r1
  130.4 0.7 collective-permute-done.14.r2
  131.1 5.4 %collective-permute-done.15.r3 = bf16[3,128,128]{2,1,0:T(8,128)(2,1)S(1)} collective-permute-done((bf16[3,128,128]{2,1,0:T(8,128)(2,1)S(1)}, bf16[3,128,128]{2,1,0:T(8,128)(2,1)S(1)}, u32[]{:S(2)}, u32[]{:S(2)}) %collective-permute-start.15) | collective-permute-done | bytes 98336 | tf_op jit(solution)/shard_map/ppermute | solution.py:232
  136.5 3.6 %shard_map.72._ = bf16[256,2048]{1,0:T(8,128)(2,1)} custom-call(bf16[16,128,128]{2,1,0:T(8,128)(2,1)S(1)} %all-to-all-done.1.field_ref, bf16[3,128,128]{2,1,0:T(8,128)(2,1)S(1)} %collective-permute-done.12.r0, bf16[3,128,128]{2,1,0:T(8,128)(2,1)S(1)} %collective-permute-done.13.r1, bf16[3,128,128]{2,1,0:T(8,128)(2,1)S(1)} %collective-permute-done.14.r2, ...), custom_call_target="tpu_custom_call" | custom-call | flops 335544320 | bytes 5124416 | tf_op jit(solution)/shard_map/pallas_call | solution.py:27
  140.1 0.0 all-to-all-done.3.field_ref
  140.1 17.1 %shard_map.73 = bf16[256,2048]{1,0:T(8,128)(2,1)} custom-call(bf16[256,2048]{1,0:T(8,128)(2,1)} %shard_map.72._, bf16[16,128,128]{2,1,0:T(8,128)(2,1)} %all-to-all-done.3.field_ref), custom_call_target="tpu_custom_call", output_to_operand_aliasing={{}: (0, {})} | custom-call | bytes 2621440 | tf_op jit(solution)/shard_map/pallas_call | solution.py:27
  (2 shorter events, 0.0 us)
Async XLA Ops:
  0.0 10.0 %copy-start.3 = (s32[1,4,3]{1,0,2:T(1,128)S(1)}, s32[1,4,3]{1,0,2:T(1,128)}, u32[]{:S(2)}) copy-start(s32[1,4,3]{1,0,2:T(1,128)} %param.8) | copy-start | bytes 148
  0.0 10.1 %copy-start = (bf16[16,5,128,128]{3,2,1,0:T(8,128)(2,1)S(1)}, bf16[16,5,128,128]{3,2,1,0:T(8,128)(2,1)}, u32[]{:S(2)}) copy-start(bf16[16,5,128,128]{3,2,1,0:T(8,128)(2,1)} %weights_ref.9) | copy-start | bytes 7864324
  0.0 10.1 %copy-start.1 = (f32[3]{0:T(128)S(1)}, f32[3]{0:T(128)}, u32[]{:S(2)}) copy-start(f32[3]{0:T(128)} %coef_ref.1) | copy-start | bytes 40
  2.4 25.4 %copy-start.2 = (s32[16,5]{0,1:T(8,128)S(1)}, s32[16,5]{0,1:T(8,128)}, u32[]{:S(2)}) copy-start(s32[16,5]{0,1:T(8,128)} %param.9) | copy-start | bytes 964
  2.4 35.5 %all-to-all-start = ((bf16[16,256,128]{2,1,0:T(8,128)(2,1)}), bf16[16,256,128]{2,1,0:T(8,128)(2,1)}, u32[]{:S(2)}, u32[]{:S(2)}) async-start(bf16[16,256,128]{2,1,0:T(8,128)(2,1)} %shard_map.64), calls=%async_computation | async-start | bytes 2097152 | tf_op jit(solution)/shard_map/all_to_all | solution.py:236
  13.0 14.9 %collective-permute-start = (bf16[3,128,128]{2,1,0:T(8,128)(2,1)}, bf16[3,128,128]{2,1,0:T(8,128)(2,1)S(1)}, u32[]{:S(2)}, u32[]{:S(2)}) collective-permute-start(bf16[3,128,128]{2,1,0:T(8,128)(2,1)} %get-tuple-element.41), channel_id=1, source_target_pairs={{0,32},{16,48},{32,64},{48,80},{64,96},{80,112},{96,128},{112,144}... | collective-permute-start | bytes 294920 | tf_op jit(solution)/shard_map/ppermute | solution.py:232
  17.9 10.0 %collective-permute-start.1 = (bf16[3,128,128]{2,1,0:T(8,128)(2,1)}, bf16[3,128,128]{2,1,0:T(8,128)(2,1)S(1)}, u32[]{:S(2)}, u32[]{:S(2)}) collective-permute-start(bf16[3,128,128]{2,1,0:T(8,128)(2,1)} %get-tuple-element.42), channel_id=1, source_target_pairs={{0,16},{16,32},{32,48},{48,64},{64,80},{80,96},{96,112},{112,128},... | collective-permute-start | bytes 294920 | tf_op jit(solution)/shard_map/ppermute | solution.py:232
  20.4 8.5 %collective-permute-start.2 = (bf16[3,128,128]{2,1,0:T(8,128)(2,1)}, bf16[3,128,128]{2,1,0:T(8,128)(2,1)S(1)}, u32[]{:S(2)}, u32[]{:S(2)}) collective-permute-start(bf16[3,128,128]{2,1,0:T(8,128)(2,1)} %get-tuple-element.43), channel_id=1, source_target_pairs={{0,496},{16,0},{32,16},{48,32},{64,48},{80,64},{96,80},{112,96},{1... | collective-permute-start | bytes 294920 | tf_op jit(solution)/shard_map/ppermute | solution.py:232
  25.9 8.2 %collective-permute-start.3 = (bf16[3,128,128]{2,1,0:T(8,128)(2,1)}, bf16[3,128,128]{2,1,0:T(8,128)(2,1)S(1)}, u32[]{:S(2)}, u32[]{:S(2)}) collective-permute-start(bf16[3,128,128]{2,1,0:T(8,128)(2,1)} %get-tuple-element.44), channel_id=1, source_target_pairs={{0,480},{16,496},{32,0},{48,16},{64,32},{80,48},{96,64},{112,80},{... | collective-permute-start | bytes 294920 | tf_op jit(solution)/shard_map/ppermute | solution.py:232
  40.5 21.6 %all-to-all-start.1 = ((bf16[16,128,128]{2,1,0:T(8,128)(2,1)}), bf16[16,128,128]{2,1,0:T(8,128)(2,1)S(1)}, u32[]{:S(2)}, u32[]{:S(2)}) async-start(bf16[16,128,128]{2,1,0:T(8,128)(2,1)} %get-tuple-element.48), calls=%async_computation.1 | async-start | bytes 1048576 | tf_op jit(solution)/shard_map/all_to_all | solution.py:236
  47.8 15.7 %collective-permute-start.6 = (bf16[3,128,128]{2,1,0:T(8,128)(2,1)}, bf16[3,128,128]{2,1,0:T(8,128)(2,1)S(1)}, u32[]{:S(2)}, u32[]{:S(2)}) collective-permute-start(bf16[3,128,128]{2,1,0:T(8,128)(2,1)} %get-tuple-element.56), channel_id=1, source_target_pairs={{0,32},{16,48},{32,64},{48,80},{64,96},{80,112},{96,128},{112,144}... | collective-permute-start | bytes 294920 | tf_op jit(solution)/shard_map/ppermute | solution.py:232
  51.7 11.9 %collective-permute-start.7 = (bf16[3,128,128]{2,1,0:T(8,128)(2,1)}, bf16[3,128,128]{2,1,0:T(8,128)(2,1)S(1)}, u32[]{:S(2)}, u32[]{:S(2)}) collective-permute-start(bf16[3,128,128]{2,1,0:T(8,128)(2,1)} %get-tuple-element.57), channel_id=1, source_target_pairs={{0,16},{16,32},{32,48},{48,64},{64,80},{80,96},{96,112},{112,128},... | collective-permute-start | bytes 294920 | tf_op jit(solution)/shard_map/ppermute | solution.py:232
  54.3 9.2 %collective-permute-start.8 = (bf16[3,128,128]{2,1,0:T(8,128)(2,1)}, bf16[3,128,128]{2,1,0:T(8,128)(2,1)S(1)}, u32[]{:S(2)}, u32[]{:S(2)}) collective-permute-start(bf16[3,128,128]{2,1,0:T(8,128)(2,1)} %get-tuple-element.58), channel_id=1, source_target_pairs={{0,496},{16,0},{32,16},{48,32},{64,48},{80,64},{96,80},{112,96},{1... | collective-permute-start | bytes 294920 | tf_op jit(solution)/shard_map/ppermute | solution.py:232
  59.6 8.3 %collective-permute-start.9 = (bf16[3,128,128]{2,1,0:T(8,128)(2,1)}, bf16[3,128,128]{2,1,0:T(8,128)(2,1)}, u32[]{:S(2)}, u32[]{:S(2)}) collective-permute-start(bf16[3,128,128]{2,1,0:T(8,128)(2,1)} %get-tuple-element.59), channel_id=1, source_target_pairs={{0,480},{16,496},{32,0},{48,16},{64,32},{80,48},{96,64},{112,80},{... | collective-permute-start | bytes 294920 | tf_op jit(solution)/shard_map/ppermute | solution.py:232
  72.0 32.6 %all-to-all-start.2 = ((bf16[16,128,128]{2,1,0:T(8,128)(2,1)}), bf16[16,128,128]{2,1,0:T(8,128)(2,1)}, u32[]{:S(2)}, u32[]{:S(2)}) async-start(bf16[16,128,128]{2,1,0:T(8,128)(2,1)} %shard_map.69), calls=%async_computation.2 | async-start | bytes 1048576 | tf_op jit(solution)/shard_map/all_to_all | solution.py:236
  79.2 16.2 %collective-permute-start.4 = (bf16[3,128,128]{2,1,0:T(8,128)(2,1)}, bf16[3,128,128]{2,1,0:T(8,128)(2,1)S(1)}, u32[]{:S(2)}, u32[]{:S(2)}) collective-permute-start(bf16[3,128,128]{2,1,0:T(8,128)(2,1)} %get-tuple-element.54), channel_id=1, source_target_pairs={{0,32},{16,48},{32,64},{48,80},{64,96},{80,112},{96,128},{112,144}... | collective-permute-start | bytes 294920 | tf_op jit(solution)/shard_map/ppermute | solution.py:232
  85.6 9.9 %collective-permute-start.5 = (bf16[3,128,128]{2,1,0:T(8,128)(2,1)}, bf16[3,128,128]{2,1,0:T(8,128)(2,1)S(1)}, u32[]{:S(2)}, u32[]{:S(2)}) collective-permute-start(bf16[3,128,128]{2,1,0:T(8,128)(2,1)} %get-tuple-element.55), channel_id=1, source_target_pairs={{0,16},{16,32},{32,48},{48,64},{64,80},{80,96},{96,112},{112,128},... | collective-permute-start | bytes 294920 | tf_op jit(solution)/shard_map/ppermute | solution.py:232
  88.2 8.3 %collective-permute-start.10 = (bf16[3,128,128]{2,1,0:T(8,128)(2,1)}, bf16[3,128,128]{2,1,0:T(8,128)(2,1)S(1)}, u32[]{:S(2)}, u32[]{:S(2)}) collective-permute-start(bf16[3,128,128]{2,1,0:T(8,128)(2,1)} %get-tuple-element.63), channel_id=1, source_target_pairs={{0,496},{16,0},{32,16},{48,32},{64,48},{80,64},{96,80},{112,96},{1... | collective-permute-start | bytes 294920 | tf_op jit(solution)/shard_map/ppermute | solution.py:232
  93.5 8.2 %collective-permute-start.11 = (bf16[3,128,128]{2,1,0:T(8,128)(2,1)}, bf16[3,128,128]{2,1,0:T(8,128)(2,1)S(1)}, u32[]{:S(2)}, u32[]{:S(2)}) collective-permute-start(bf16[3,128,128]{2,1,0:T(8,128)(2,1)} %get-tuple-element.64), channel_id=1, source_target_pairs={{0,480},{16,496},{32,0},{48,16},{64,32},{80,48},{96,64},{112,80},{... | collective-permute-start | bytes 294920 | tf_op jit(solution)/shard_map/ppermute | solution.py:232
  104.5 16.0 %copy-start.6 = (bf16[3,128,128]{2,1,0:T(8,128)(2,1)S(1)}, bf16[3,128,128]{2,1,0:T(8,128)(2,1)}, u32[]{:S(2)}) copy-start(bf16[3,128,128]{2,1,0:T(8,128)(2,1)} %get-tuple-element.66) | copy-start | bytes 294916
  104.5 18.6 %copy-start.5 = (bf16[3,128,128]{2,1,0:T(8,128)(2,1)S(1)}, bf16[3,128,128]{2,1,0:T(8,128)(2,1)}, u32[]{:S(2)}) copy-start(bf16[3,128,128]{2,1,0:T(8,128)(2,1)} %get-tuple-element.71) | copy-start | bytes 294916
  104.5 23.9 %copy-start.4 = (bf16[3,128,128]{2,1,0:T(8,128)(2,1)S(1)}, bf16[3,128,128]{2,1,0:T(8,128)(2,1)}, u32[]{:S(2)}) copy-start(bf16[3,128,128]{2,1,0:T(8,128)(2,1)} %get-tuple-element.72) | copy-start | bytes 294916
  108.0 32.1 %all-to-all-start.3 = ((bf16[16,128,128]{2,1,0:T(8,128)(2,1)}), bf16[16,128,128]{2,1,0:T(8,128)(2,1)}, u32[]{:S(2)}, u32[]{:S(2)}) async-start(bf16[16,128,128]{2,1,0:T(8,128)(2,1)} %shard_map.71), calls=%async_computation.3 | async-start | bytes 1048576 | tf_op jit(solution)/shard_map/all_to_all | solution.py:236
  115.2 15.2 %collective-permute-start.12 = (bf16[3,128,128]{2,1,0:T(8,128)(2,1)}, bf16[3,128,128]{2,1,0:T(8,128)(2,1)S(1)}, u32[]{:S(2)}, u32[]{:S(2)}) collective-permute-start(bf16[3,128,128]{2,1,0:T(8,128)(2,1)} %get-tuple-element.65), channel_id=1, source_target_pairs={{0,32},{16,48},{32,64},{48,80},{64,96},{80,112},{96,128},{112,144}... | collective-permute-start | bytes 294920 | tf_op jit(solution)/shard_map/ppermute | solution.py:232
  120.5 9.9 %collective-permute-start.13 = (bf16[3,128,128]{2,1,0:T(8,128)(2,1)S(1)}, bf16[3,128,128]{2,1,0:T(8,128)(2,1)S(1)}, u32[]{:S(2)}, u32[]{:S(2)}) collective-permute-start(bf16[3,128,128]{2,1,0:T(8,128)(2,1)S(1)} %copy-done.6), channel_id=1, source_target_pairs={{0,16},{16,32},{32,48},{48,64},{64,80},{80,96},{96,112},{112,128},... | collective-permute-start | bytes 294920 | tf_op jit(solution)/shard_map/ppermute | solution.py:232
  123.2 8.0 %collective-permute-start.14 = (bf16[3,128,128]{2,1,0:T(8,128)(2,1)S(1)}, bf16[3,128,128]{2,1,0:T(8,128)(2,1)S(1)}, u32[]{:S(2)}, u32[]{:S(2)}) collective-permute-start(bf16[3,128,128]{2,1,0:T(8,128)(2,1)S(1)} %copy-done.5), channel_id=1, source_target_pairs={{0,496},{16,0},{32,16},{48,32},{64,48},{80,64},{96,80},{112,96},{1... | collective-permute-start | bytes 294920 | tf_op jit(solution)/shard_map/ppermute | solution.py:232
  128.5 8.0 %collective-permute-start.15 = (bf16[3,128,128]{2,1,0:T(8,128)(2,1)S(1)}, bf16[3,128,128]{2,1,0:T(8,128)(2,1)S(1)}, u32[]{:S(2)}, u32[]{:S(2)}) collective-permute-start(bf16[3,128,128]{2,1,0:T(8,128)(2,1)S(1)} %copy-done.4), channel_id=1, source_target_pairs={{0,480},{16,496},{32,0},{48,16},{64,32},{80,48},{96,64},{112,80},{... | collective-permute-start | bytes 294920 | tf_op jit(solution)/shard_map/ppermute | solution.py:232

commit v4 on v3

--- a/solution.py
+++ b/solution.py
@@ -14,7 +14,6 @@
 SMEM = pl.BlockSpec(memory_space=pltpu.SMEM)
 VMEM = pl.BlockSpec(memory_space=pltpu.VMEM)
 HBM = pl.BlockSpec(memory_space=pltpu.HBM)
-ANY = pl.BlockSpec(memory_space=pl.ANY)
 DMA = pltpu.SemaphoreType.DMA
 
 
@@ -234,6 +233,24 @@
 
 def exchange(field):
     return lax.all_to_all(field, "tm", split_axis=0, concat_axis=0, tiled=True)
+
+
+def begin(packs, first):
+    ways = len(packs)
+    ahead = [(first + i) % ways for i in range(ways // 2)]
+    behind = [(first + ways // 2 + i) % ways for i in range(ways // 2)]
+    got = {way: take(packs[way], way) for way in ahead}
+
+    def finish(field):
+        field, *rest = lax.optimization_barrier(
+            (field, *(got[way] for way in ahead), *(packs[way] for way in behind))
+        )
+        field = exchange(field)
+        got.update(zip(ahead, rest[: len(ahead)]))
+        got.update((way, take(block, way)) for way, block in zip(behind, rest[len(ahead) :]))
+        return field, [got[way] for way in range(ways)]
+
+    return finish
 
 
 def body(signal, weights, send_list, col_ref, kernel, cheb_coef):
@@ -256,7 +273,6 @@
     mixer = [vm((time, rows // t_loc * width), BF16), whole, vm((time, time), BF16), DMA((pieces,)), DMA]
     work = 2 * rows * per_row * n_loc * width
     mixing = 2 * time * time * rows // t_loc * width
-    barrier = lax.optimization_barrier
 
     def one(x, received, inv, in_hbm):
         term, *packs = call(
@@ -309,7 +325,7 @@
     received = [take(block, way) for way, block in enumerate(packs)]
     term, packs = one(xs, received, inv, True)
 
-    received = [take(packs[way], way) for way in range(ways // 2)]
+    finish = begin(packs, ways // 2)
     early, mix = call(
         functools.partial(first_temporal, t_loc),
         [(field, HBM), (array(time, time), HBM)],
@@ -317,29 +333,23 @@
         mixer,
         flops=mixing,
     )
-    early, *rest = barrier((early, *packs[ways // 2 :]))
-    early = exchange(early)
-    received += [take(block, ways // 2 + i) for i, block in enumerate(rest)]
+    early, received = finish(early)
 
     packs = call(scale, packed, [(early, VMEM), (inv, VMEM), (send_list, SMEM)], [held, DMA((ways,))])
-    term, *packs = barrier((term, *packs))
-    later = [take(packs[way], way) for way in range(ways // 2)]
+    term, *packs = lax.optimization_barrier((term, *packs))
+    finish = begin(packs, 0)
     late = two(xs, received, inv, term, field, True)
-    late, *rest = barrier((late, *packs[ways // 2 :]))
-    late = exchange(late)
-    received = later + [take(block, ways // 2 + i) for i, block in enumerate(rest)]
+    late, received = finish(late)
     term, packs = one(early, received, inv, False)
 
-    received = [take(packs[way], way) for way in range(ways // 2)]
+    finish = begin(packs, ways // 2)
     (late,) = call(
         functools.partial(second_temporal, t_loc), [(field, HBM)], [(late, VMEM), (mix, HBM)], mixer, flops=mixing
     )
-    late, *rest = barrier((late, *packs[ways // 2 :]))
-    late = exchange(late)
-    received += [take(block, ways // 2 + i) for i, block in enumerate(rest)]
+    late, received = finish(late)
     out = array(2 * rows, n_loc)
     done = two(early, received, inv, term, out, False)
-    (done,) = call(unblock, [(out, HBM)], [(done, HBM), (late, ANY)], [DMA((blocks,))], aliases={0: 0})
+    (done,) = call(unblock, [(out, HBM)], [(done, HBM), (late, VMEM)], [DMA((blocks,))], aliases={0: 0})
     return done.reshape(probes, t_loc, n_loc)
 
 

time: 158 us -> 156 us (0.987)
  the two profiles are of different devices: /device:TPU:136 before, /device:TPU:1 now
where the time goes in v4:
time: 156 us; the launch traced here: 155 us
  starting transfers between devices  88.2 us (57%)
  waiting for transfers between devices  36.1 us (23%)
  Pallas kernels  28.8 us (18%)
  local copies, waits for them, and re-layouts  1.72 us (1%)
    ppermute x16, starting transfers between devices, take(): lax.ppermute(block, 'dom', [(i, (i - OFFSETS[way]) % count) for i in rang...  52.9 us
    all_to_all x4, starting transfers between devices, exchange(): return lax.all_to_all(field, 'tm', split_axis=0, concat_axis=0, tiled=True)  35.3 us
    pallas_call x10, Pallas kernels, call(): pl.pallas_call(kernel, out_shape=shapes, in_specs=specs, out_specs=result...  28.8 us
    ppermute x16, waiting for transfers between devices, take(): lax.ppermute(block, 'dom', [(i, (i - OFFSETS[way]) % count) for i in rang...  20.3 us
    all_to_all x4, waiting for transfers between devices, exchange(): return lax.all_to_all(field, 'tm', split_axis=0, concat_axis=0, tiled=True)  15.8 us
  transfers between devices with their start and end apart: 20, of which 11 were waited for; matrix products, arithmetic and copies ran while one was open for 0% of the time, Pallas kernels for 16%

profile of v4, /device:TPU:1, one launch (start us, length us, event | category | flops | bytes accessed | tf_op | source)
XLA Modules:
  0.0 155.0 jit_solution(10756622739937152485)
XLA Ops:
  0.0 0.0 copy-start.5
  0.0 0.0 copy-start
  0.0 0.0 copy-start.3
  0.0 2.4 %shard_map.64 = bf16[16,256,128]{2,1,0:T(8,128)(2,1)} custom-call(bf16[256,2048]{1,0:T(8,128)(2,1)} %bitcast.2, bf16[32,512]{1,0:T(8,128)(2,1)} %kernel_ref.1), custom_call_target="tpu_custom_call" | custom-call | bytes 2129920 | tf_op jit(solution)/shard_map/pallas_call | solution.py:26
  2.4 0.0 copy-start.4
  2.4 10.9 %all-to-all-start = ((bf16[16,256,128]{2,1,0:T(8,128)(2,1)}), bf16[16,256,128]{2,1,0:T(8,128)(2,1)}, u32[]{:S(2)}, u32[]{:S(2)}) async-start(bf16[16,256,128]{2,1,0:T(8,128)(2,1)} %shard_map.64), calls=%async_computation | async-start | bytes 2097152 | tf_op jit(solution)/shard_map/all_to_all | solution.py:235
  13.4 0.0 copy-done.5
  13.4 0.1 copy.8.send_ref
  13.5 0.0 copy-done
  13.5 0.0 copy-done.3
  13.5 2.9 %shard_map.66 = (f32[24,128]{1,0:T(8,128)S(1)}, bf16[3,128,128]{2,1,0:T(8,128)(2,1)}, bf16[3,128,128]{2,1,0:T(8,128)(2,1)}, bf16[3,128,128]{2,1,0:T(8,128)(2,1)}, bf16[3,128,128]{2,1,0:T(8,128)(2,1)}) custom-call(bf16[256,2048]{1,0:T(8,128)(2,1)} %bitcast.3, bf16[16,5,128,128]{3,2,1,0:T(8,128)(2,1)S(1)} %copy-done, s32[1,4,3]{2,1,0:T(4,128)S(1)} %copy.8.send_ref, ...), custom_call_target="tpu_custom_call" | custom-call | flops 41943040 | bytes 4075580 | tf_op jit(solution)/shard_map/pallas_call | solution.py:26
  16.4 2.3 %collective-permute-start = (bf16[3,128,128]{2,1,0:T(8,128)(2,1)}, bf16[3,128,128]{2,1,0:T(8,128)(2,1)S(1)}, u32[]{:S(2)}, u32[]{:S(2)}) collective-permute-start(bf16[3,128,128]{2,1,0:T(8,128)(2,1)} %get-tuple-element.47), channel_id=1, source_target_pairs={{0,32},{16,48},{32,64},{48,80},{64,96},{80,112},{96,128},{112,144}... | collective-permute-start | bytes 294920 | tf_op jit(solution)/shard_map/ppermute | solution.py:231
  18.7 2.2 %collective-permute-start.1 = (bf16[3,128,128]{2,1,0:T(8,128)(2,1)}, bf16[3,128,128]{2,1,0:T(8,128)(2,1)S(1)}, u32[]{:S(2)}, u32[]{:S(2)}) collective-permute-start(bf16[3,128,128]{2,1,0:T(8,128)(2,1)} %get-tuple-element.48), channel_id=1, source_target_pairs={{0,16},{16,32},{32,48},{48,64},{64,80},{80,96},{96,112},{112,128},... | collective-permute-start | bytes 294920 | tf_op jit(solution)/shard_map/ppermute | solution.py:231
  20.9 9.8 %collective-permute-start.2 = (bf16[3,128,128]{2,1,0:T(8,128)(2,1)}, bf16[3,128,128]{2,1,0:T(8,128)(2,1)S(1)}, u32[]{:S(2)}, u32[]{:S(2)}) collective-permute-start(bf16[3,128,128]{2,1,0:T(8,128)(2,1)} %get-tuple-element.49), channel_id=1, source_target_pairs={{0,496},{16,0},{32,16},{48,32},{64,48},{80,64},{96,80},{112,96},{1... | collective-permute-start | bytes 294920 | tf_op jit(solution)/shard_map/ppermute | solution.py:231
  30.8 4.3 %collective-permute-start.3 = (bf16[3,128,128]{2,1,0:T(8,128)(2,1)}, bf16[3,128,128]{2,1,0:T(8,128)(2,1)S(1)}, u32[]{:S(2)}, u32[]{:S(2)}) collective-permute-start(bf16[3,128,128]{2,1,0:T(8,128)(2,1)} %get-tuple-element.50), channel_id=1, source_target_pairs={{0,480},{16,496},{32,0},{48,16},{64,32},{80,48},{96,64},{112,80},{... | collective-permute-start | bytes 294920 | tf_op jit(solution)/shard_map/ppermute | solution.py:231
  35.0 0.0 copy-done.4
  35.0 0.1 copy.9.col_ref
  35.1 0.0 collective-permute-done.r0
  35.1 0.0 collective-permute-done.1.r1
  35.1 0.0 collective-permute-done.2.r2
  35.1 3.3 %collective-permute-done.3.r3 = bf16[3,128,128]{2,1,0:T(8,128)(2,1)S(1)} collective-permute-done((bf16[3,128,128]{2,1,0:T(8,128)(2,1)}, bf16[3,128,128]{2,1,0:T(8,128)(2,1)S(1)}, u32[]{:S(2)}, u32[]{:S(2)}) %collective-permute-start.3) | collective-permute-done | bytes 98336 | tf_op jit(solution)/shard_map/ppermute | solution.py:231
  38.4 3.8 %shard_map.67 = (bf16[16,128,128]{2,1,0:T(8,128)(2,1)}, bf16[3,128,128]{2,1,0:T(8,128)(2,1)}, bf16[3,128,128]{2,1,0:T(8,128)(2,1)}, bf16[3,128,128]{2,1,0:T(8,128)(2,1)}, bf16[3,128,128]{2,1,0:T(8,128)(2,1)}) custom-call(bf16[256,2048]{1,0:T(8,128)(2,1)} %bitcast.4, bf16[3,128,128]{2,1,0:T(8,128)(2,1)S(1)} %collective-permute-done.r0, ...), custom_call_target="tpu_custom_call" | custom-call | flops 335544320 | bytes 4993392 | tf_op jit(solution)/shard_map/pallas_call | solution.py:26
  42.2 4.9 %collective-permute-start.4 = (bf16[3,128,128]{2,1,0:T(8,128)(2,1)}, bf16[3,128,128]{2,1,0:T(8,128)(2,1)S(1)}, u32[]{:S(2)}, u32[]{:S(2)}) collective-permute-start(bf16[3,128,128]{2,1,0:T(8,128)(2,1)} %get-tuple-element.52), channel_id=1, source_target_pairs={{0,496},{16,0},{32,16},{48,32},{64,48},{80,64},{96,80},{112,96},{1... | collective-permute-start | bytes 294920 | tf_op jit(solution)/shard_map/ppermute | solution.py:231
  47.1 3.2 %collective-permute-start.5 = (bf16[3,128,128]{2,1,0:T(8,128)(2,1)}, bf16[3,128,128]{2,1,0:T(8,128)(2,1)S(1)}, u32[]{:S(2)}, u32[]{:S(2)}) collective-permute-start(bf16[3,128,128]{2,1,0:T(8,128)(2,1)} %get-tuple-element.53), channel_id=1, source_target_pairs={{0,480},{16,496},{32,0},{48,16},{64,32},{80,48},{96,64},{112,80},{... | collective-permute-start | bytes 294920 | tf_op jit(solution)/shard_map/ppermute | solution.py:231
  50.4 0.0 all-to-all-done.field_ref
  50.4 2.6 %shard_map.65 = (bf16[16,128,128]{2,1,0:T(8,128)(2,1)}, bf16[512,512]{1,0:T(8,128)(2,1)}) custom-call(bf16[16,256,128]{2,1,0:T(8,128)(2,1)} %all-to-all-done.field_ref), custom_call_target="tpu_custom_call" | custom-call | flops 268435456 | bytes 2097152 | tf_op jit(solution)/shard_map/pallas_call | solution.py:26
  52.9 0.0 collective-permute-done.4.r2
  53.0 1.3 collective-permute-done.5.r3
  54.2 10.4 %all-to-all-start.1 = ((bf16[16,128,128]{2,1,0:T(8,128)(2,1)}), bf16[16,128,128]{2,1,0:T(8,128)(2,1)S(1)}, u32[]{:S(2)}, u32[]{:S(2)}) async-start(bf16[16,128,128]{2,1,0:T(8,128)(2,1)} %get-tuple-element.56), calls=%async_computation.1 | async-start | bytes 1048576 | tf_op jit(solution)/shard_map/all_to_all | solution.py:235
  64.6 1.9 %collective-permute-start.6 = (bf16[3,128,128]{2,1,0:T(8,128)(2,1)}, bf16[3,128,128]{2,1,0:T(8,128)(2,1)}, u32[]{:S(2)}, u32[]{:S(2)}) collective-permute-start(bf16[3,128,128]{2,1,0:T(8,128)(2,1)} %get-tuple-element.57), channel_id=1, source_target_pairs={{0,32},{16,48},{32,64},{48,80},{64,96},{80,112},{96,128},{112,144}... | collective-permute-start | bytes 294920 | tf_op jit(solution)/shard_map/ppermute | solution.py:231
  66.5 1.9 %collective-permute-start.7 = (bf16[3,128,128]{2,1,0:T(8,128)(2,1)}, bf16[3,128,128]{2,1,0:T(8,128)(2,1)}, u32[]{:S(2)}, u32[]{:S(2)}) collective-permute-start(bf16[3,128,128]{2,1,0:T(8,128)(2,1)} %get-tuple-element.58), channel_id=1, source_target_pairs={{0,16},{16,32},{32,48},{48,64},{64,80},{80,96},{96,112},{112,128},... | collective-permute-start | bytes 294920 | tf_op jit(solution)/shard_map/ppermute | solution.py:231
  68.4 13.5 %all-to-all-done.1.field_ref = bf16[16,128,128]{2,1,0:T(8,128)(2,1)S(1)} async-done(((bf16[16,128,128]{2,1,0:T(8,128)(2,1)}), bf16[16,128,128]{2,1,0:T(8,128)(2,1)S(1)}, u32[]{:S(2)}, u32[]{:S(2)}) %all-to-all-start.1) | async-done | bytes 524320 | tf_op jit(solution)/shard_map/all_to_all | solution.py:235
  81.9 1.4 shard_map.68
  83.3 1.9 %collective-permute-start.8 = (bf16[3,128,128]{2,1,0:T(8,128)(2,1)}, bf16[3,128,128]{2,1,0:T(8,128)(2,1)S(1)}, u32[]{:S(2)}, u32[]{:S(2)}) collective-permute-start(bf16[3,128,128]{2,1,0:T(8,128)(2,1)} %get-tuple-element.67), channel_id=1, source_target_pairs={{0,32},{16,48},{32,64},{48,80},{64,96},{80,112},{96,128},{112,144}... | collective-permute-start | bytes 294920 | tf_op jit(solution)/shard_map/ppermute | solution.py:231
  85.2 1.9 %collective-permute-start.9 = (bf16[3,128,128]{2,1,0:T(8,128)(2,1)}, bf16[3,128,128]{2,1,0:T(8,128)(2,1)S(1)}, u32[]{:S(2)}, u32[]{:S(2)}) collective-permute-start(bf16[3,128,128]{2,1,0:T(8,128)(2,1)} %get-tuple-element.68), channel_id=1, source_target_pairs={{0,16},{16,32},{32,48},{48,64},{64,80},{80,96},{96,112},{112,128},... | collective-permute-start | bytes 294920 | tf_op jit(solution)/shard_map/ppermute | solution.py:231
  87.2 0.0 collective-permute-done.6.r0
  87.2 0.0 collective-permute-done.7.r1
  87.2 4.1 %shard_map.69 = bf16[16,128,128]{2,1,0:T(8,128)(2,1)} custom-call(bf16[256,2048]{1,0:T(8,128)(2,1)} %bitcast.5, bf16[3,128,128]{2,1,0:T(8,128)(2,1)} %collective-permute-done.6.r0, bf16[3,128,128]{2,1,0:T(8,128)(2,1)} %collective-permute-done.7.r1, bf16[3,128,128]{2,1,0:T(8,128)(2,1)S(1)} %collective-permute-done.4.r2, ...), custom_call_target="tpu_custom_call" | custom-call | flops 335544320 | bytes 5124416 | tf_op jit(solution)/shard_map/pallas_call | solution.py:26
  91.2 2.0 %collective-permute-done.8.r0 = bf16[3,128,128]{2,1,0:T(8,128)(2,1)S(1)} collective-permute-done((bf16[3,128,128]{2,1,0:T(8,128)(2,1)}, bf16[3,128,128]{2,1,0:T(8,128)(2,1)S(1)}, u32[]{:S(2)}, u32[]{:S(2)}) %collective-permute-start.8) | collective-permute-done | bytes 98336 | tf_op jit(solution)/shard_map/ppermute | solution.py:231
  93.3 1.6 %collective-permute-done.9.r1 = bf16[3,128,128]{2,1,0:T(8,128)(2,1)S(1)} collective-permute-done((bf16[3,128,128]{2,1,0:T(8,128)(2,1)}, bf16[3,128,128]{2,1,0:T(8,128)(2,1)S(1)}, u32[]{:S(2)}, u32[]{:S(2)}) %collective-permute-start.9) | collective-permute-done | bytes 98336 | tf_op jit(solution)/shard_map/ppermute | solution.py:231
  94.9 0.6 copy-done.1
  95.5 4.1 %all-to-all-start.2 = ((bf16[16,128,128]{2,1,0:T(8,128)(2,1)}), bf16[16,128,128]{2,1,0:T(8,128)(2,1)}, u32[]{:S(2)}, u32[]{:S(2)}) async-start(bf16[16,128,128]{2,1,0:T(8,128)(2,1)} %shard_map.69), calls=%async_computation.2 | async-start | bytes 1048576 | tf_op jit(solution)/shard_map/all_to_all | solution.py:235
  99.7 3.0 %collective-permute-start.10 = (bf16[3,128,128]{2,1,0:T(8,128)(2,1)}, bf16[3,128,128]{2,1,0:T(8,128)(2,1)S(1)}, u32[]{:S(2)}, u32[]{:S(2)}) collective-permute-start(bf16[3,128,128]{2,1,0:T(8,128)(2,1)} %get-tuple-element.75), channel_id=1, source_target_pairs={{0,496},{16,0},{32,16},{48,32},{64,48},{80,64},{96,80},{112,96},{1... | collective-permute-start | bytes 294920 | tf_op jit(solution)/shard_map/ppermute | solution.py:231
  102.7 3.7 %collective-permute-start.11 = (bf16[3,128,128]{2,1,0:T(8,128)(2,1)}, bf16[3,128,128]{2,1,0:T(8,128)(2,1)S(1)}, u32[]{:S(2)}, u32[]{:S(2)}) collective-permute-start(bf16[3,128,128]{2,1,0:T(8,128)(2,1)} %get-tuple-element.76), channel_id=1, source_target_pairs={{0,480},{16,496},{32,0},{48,16},{64,32},{80,48},{96,64},{112,80},{... | collective-permute-start | bytes 294920 | tf_op jit(solution)/shard_map/ppermute | solution.py:231
  106.4 2.1 %collective-permute-done.10.r2 = bf16[3,128,128]{2,1,0:T(8,128)(2,1)S(1)} collective-permute-done((bf16[3,128,128]{2,1,0:T(8,128)(2,1)}, bf16[3,128,128]{2,1,0:T(8,128)(2,1)S(1)}, u32[]{:S(2)}, u32[]{:S(2)}) %collective-permute-start.10) | collective-permute-done | bytes 98336 | tf_op jit(solution)/shard_map/ppermute | solution.py:231
  108.5 2.5 %collective-permute-done.11.r3 = bf16[3,128,128]{2,1,0:T(8,128)(2,1)S(1)} collective-permute-done((bf16[3,128,128]{2,1,0:T(8,128)(2,1)}, bf16[3,128,128]{2,1,0:T(8,128)(2,1)S(1)}, u32[]{:S(2)}, u32[]{:S(2)}) %collective-permute-start.11) | collective-permute-done | bytes 98336 | tf_op jit(solution)/shard_map/ppermute | solution.py:231
  111.0 0.9 copy-done.2
  111.9 2.8 %shard_map.71 = (bf16[16,128,128]{2,1,0:T(8,128)(2,1)}, bf16[3,128,128]{2,1,0:T(8,128)(2,1)}, bf16[3,128,128]{2,1,0:T(8,128)(2,1)}, bf16[3,128,128]{2,1,0:T(8,128)(2,1)}, bf16[3,128,128]{2,1,0:T(8,128)(2,1)}) custom-call(bf16[16,128,128]{2,1,0:T(8,128)(2,1)S(1)} %all-to-all-done.1.field_ref, bf16[3,128,128]{2,1,0:T(8,128)(2,1)S(1)} %collective-permute-done.8.r0, ...), custom_call_target="tpu_custom_call" | custom-call | flops 335544320 | bytes 4469104 | tf_op jit(solution)/shard_map/pallas_call | solution.py:26
  114.7 0.0 copy-start.6
  114.7 4.1 %collective-permute-start.12 = (bf16[3,128,128]{2,1,0:T(8,128)(2,1)}, bf16[3,128,128]{2,1,0:T(8,128)(2,1)S(1)}, u32[]{:S(2)}, u32[]{:S(2)}) collective-permute-start(bf16[3,128,128]{2,1,0:T(8,128)(2,1)} %get-tuple-element.77), channel_id=1, source_target_pairs={{0,496},{16,0},{32,16},{48,32},{64,48},{80,64},{96,80},{112,96},{1... | collective-permute-start | bytes 294920 | tf_op jit(solution)/shard_map/ppermute | solution.py:231
  118.8 3.5 %collective-permute-start.13 = (bf16[3,128,128]{2,1,0:T(8,128)(2,1)}, bf16[3,128,128]{2,1,0:T(8,128)(2,1)S(1)}, u32[]{:S(2)}, u32[]{:S(2)}) collective-permute-start(bf16[3,128,128]{2,1,0:T(8,128)(2,1)} %get-tuple-element.78), channel_id=1, source_target_pairs={{0,480},{16,496},{32,0},{48,16},{64,32},{80,48},{96,64},{112,80},{... | collective-permute-start | bytes 294920 | tf_op jit(solution)/shard_map/ppermute | solution.py:231
  122.3 0.0 all-to-all-done.2.field_ref
  122.3 3.4 %shard_map.70 = bf16[16,128,128]{2,1,0:T(8,128)(2,1)} custom-call(bf16[16,128,128]{2,1,0:T(8,128)(2,1)} %all-to-all-done.2.field_ref, bf16[512,512]{1,0:T(8,128)(2,1)} %get-tuple-element.72.mix_ref), custom_call_target="tpu_custom_call" | custom-call | flops 268435456 | bytes 1572864 | tf_op jit(solution)/shard_map/pallas_call | solution.py:26
  125.7 0.0 collective-permute-done.12.r2
  125.7 0.1 collective-permute-done.13.r3
  125.8 9.8 %all-to-all-start.3 = ((bf16[16,128,128]{2,1,0:T(8,128)(2,1)}), bf16[16,128,128]{2,1,0:T(8,128)(2,1)}, u32[]{:S(2)}, u32[]{:S(2)}) async-start(bf16[16,128,128]{2,1,0:T(8,128)(2,1)} %shard_map.70), calls=%async_computation.3 | async-start | bytes 1048576 | tf_op jit(solution)/shard_map/all_to_all | solution.py:235
  135.7 2.3 %collective-permute-start.14 = (bf16[3,128,128]{2,1,0:T(8,128)(2,1)}, bf16[3,128,128]{2,1,0:T(8,128)(2,1)S(1)}, u32[]{:S(2)}, u32[]{:S(2)}) collective-permute-start(bf16[3,128,128]{2,1,0:T(8,128)(2,1)} %get-tuple-element.81), channel_id=1, source_target_pairs={{0,32},{16,48},{32,64},{48,80},{64,96},{80,112},{96,128},{112,144}... | collective-permute-start | bytes 294920 | tf_op jit(solution)/shard_map/ppermute | solution.py:231
  137.9 0.0 copy-done.6
  137.9 1.9 %collective-permute-start.15 = (bf16[3,128,128]{2,1,0:T(8,128)(2,1)S(1)}, bf16[3,128,128]{2,1,0:T(8,128)(2,1)S(1)}, u32[]{:S(2)}, u32[]{:S(2)}) collective-permute-start(bf16[3,128,128]{2,1,0:T(8,128)(2,1)S(1)} %copy-done.6), channel_id=1, source_target_pairs={{0,16},{16,32},{32,48},{48,64},{64,80},{80,96},{96,112},{112,128},... | collective-permute-start | bytes 294920 | tf_op jit(solution)/shard_map/ppermute | solution.py:231
  139.9 5.7 %collective-permute-done.14.r0 = bf16[3,128,128]{2,1,0:T(8,128)(2,1)S(1)} collective-permute-done((bf16[3,128,128]{2,1,0:T(8,128)(2,1)}, bf16[3,128,128]{2,1,0:T(8,128)(2,1)S(1)}, u32[]{:S(2)}, u32[]{:S(2)}) %collective-permute-start.14) | collective-permute-done | bytes 98336 | tf_op jit(solution)/shard_map/ppermute | solution.py:231
  145.6 1.6 %collective-permute-done.15.r1 = bf16[3,128,128]{2,1,0:T(8,128)(2,1)S(1)} collective-permute-done((bf16[3,128,128]{2,1,0:T(8,128)(2,1)S(1)}, bf16[3,128,128]{2,1,0:T(8,128)(2,1)S(1)}, u32[]{:S(2)}, u32[]{:S(2)}) %collective-permute-start.15) | collective-permute-done | bytes 98336 | tf_op jit(solution)/shard_map/ppermute | solution.py:231
  147.2 3.6 %shard_map.72._ = bf16[256,2048]{1,0:T(8,128)(2,1)} custom-call(bf16[16,128,128]{2,1,0:T(8,128)(2,1)S(1)} %all-to-all-done.1.field_ref, bf16[3,128,128]{2,1,0:T(8,128)(2,1)S(1)} %collective-permute-done.14.r0, bf16[3,128,128]{2,1,0:T(8,128)(2,1)S(1)} %collective-permute-done.15.r1, bf16[3,128,128]{2,1,0:T(8,128)(2,1)S(1)} %collective-permute-done.12.r2, ...), custom_call_target="tpu_custom_call" | custom-call | flops 335544320 | bytes 5124416 | tf_op jit(solution)/shard_map/pallas_call | solution.py:26
  150.8 2.3 %all-to-all-done.3.field_ref = bf16[16,128,128]{2,1,0:T(8,128)(2,1)} async-done(((bf16[16,128,128]{2,1,0:T(8,128)(2,1)}), bf16[16,128,128]{2,1,0:T(8,128)(2,1)}, u32[]{:S(2)}, u32[]{:S(2)}) %all-to-all-start.3) | async-done | bytes 524320 | tf_op jit(solution)/shard_map/all_to_all | solution.py:235
  153.1 2.0 %shard_map.73 = bf16[256,2048]{1,0:T(8,128)(2,1)} custom-call(bf16[256,2048]{1,0:T(8,128)(2,1)} %shard_map.72._, bf16[16,128,128]{2,1,0:T(8,128)(2,1)} %all-to-all-done.3.field_ref), custom_call_target="tpu_custom_call", output_to_operand_aliasing={{}: (0, {})} | custom-call | bytes 2621440 | tf_op jit(solution)/shard_map/pallas_call | solution.py:26
  (2 shorter events, 0.0 us)
Async XLA Ops:
  0.0 13.4 %copy-start.5 = (s32[1,4,3]{1,0,2:T(1,128)S(1)}, s32[1,4,3]{1,0,2:T(1,128)}, u32[]{:S(2)}) copy-start(s32[1,4,3]{1,0,2:T(1,128)} %param.8) | copy-start | bytes 148
  0.0 13.5 %copy-start = (bf16[16,5,128,128]{3,2,1,0:T(8,128)(2,1)S(1)}, bf16[16,5,128,128]{3,2,1,0:T(8,128)(2,1)}, u32[]{:S(2)}) copy-start(bf16[16,5,128,128]{3,2,1,0:T(8,128)(2,1)} %weights_ref.9) | copy-start | bytes 7864324
  0.0 13.5 %copy-start.3 = (f32[3]{0:T(128)S(1)}, f32[3]{0:T(128)}, u32[]{:S(2)}) copy-start(f32[3]{0:T(128)} %coef_ref.1) | copy-start | bytes 40
  2.4 32.6 %copy-start.4 = (s32[16,5]{0,1:T(8,128)S(1)}, s32[16,5]{0,1:T(8,128)}, u32[]{:S(2)}) copy-start(s32[16,5]{0,1:T(8,128)} %param.9) | copy-start | bytes 964
  2.4 47.9 %all-to-all-start = ((bf16[16,256,128]{2,1,0:T(8,128)(2,1)}), bf16[16,256,128]{2,1,0:T(8,128)(2,1)}, u32[]{:S(2)}, u32[]{:S(2)}) async-start(bf16[16,256,128]{2,1,0:T(8,128)(2,1)} %shard_map.64), calls=%async_computation | async-start | bytes 2097152 | tf_op jit(solution)/shard_map/all_to_all | solution.py:235
  16.4 18.8 %collective-permute-start = (bf16[3,128,128]{2,1,0:T(8,128)(2,1)}, bf16[3,128,128]{2,1,0:T(8,128)(2,1)S(1)}, u32[]{:S(2)}, u32[]{:S(2)}) collective-permute-start(bf16[3,128,128]{2,1,0:T(8,128)(2,1)} %get-tuple-element.47), channel_id=1, source_target_pairs={{0,32},{16,48},{32,64},{48,80},{64,96},{80,112},{96,128},{112,144}... | collective-permute-start | bytes 294920 | tf_op jit(solution)/shard_map/ppermute | solution.py:231
  18.7 16.4 %collective-permute-start.1 = (bf16[3,128,128]{2,1,0:T(8,128)(2,1)}, bf16[3,128,128]{2,1,0:T(8,128)(2,1)S(1)}, u32[]{:S(2)}, u32[]{:S(2)}) collective-permute-start(bf16[3,128,128]{2,1,0:T(8,128)(2,1)} %get-tuple-element.48), channel_id=1, source_target_pairs={{0,16},{16,32},{32,48},{48,64},{64,80},{80,96},{96,112},{112,128},... | collective-permute-start | bytes 294920 | tf_op jit(solution)/shard_map/ppermute | solution.py:231
  20.9 14.2 %collective-permute-start.2 = (bf16[3,128,128]{2,1,0:T(8,128)(2,1)}, bf16[3,128,128]{2,1,0:T(8,128)(2,1)S(1)}, u32[]{:S(2)}, u32[]{:S(2)}) collective-permute-start(bf16[3,128,128]{2,1,0:T(8,128)(2,1)} %get-tuple-element.49), channel_id=1, source_target_pairs={{0,496},{16,0},{32,16},{48,32},{64,48},{80,64},{96,80},{112,96},{1... | collective-permute-start | bytes 294920 | tf_op jit(solution)/shard_map/ppermute | solution.py:231
  30.8 7.6 %collective-permute-start.3 = (bf16[3,128,128]{2,1,0:T(8,128)(2,1)}, bf16[3,128,128]{2,1,0:T(8,128)(2,1)S(1)}, u32[]{:S(2)}, u32[]{:S(2)}) collective-permute-start(bf16[3,128,128]{2,1,0:T(8,128)(2,1)} %get-tuple-element.50), channel_id=1, source_target_pairs={{0,480},{16,496},{32,0},{48,16},{64,32},{80,48},{96,64},{112,80},{... | collective-permute-start | bytes 294920 | tf_op jit(solution)/shard_map/ppermute | solution.py:231
  42.2 10.7 %collective-permute-start.4 = (bf16[3,128,128]{2,1,0:T(8,128)(2,1)}, bf16[3,128,128]{2,1,0:T(8,128)(2,1)S(1)}, u32[]{:S(2)}, u32[]{:S(2)}) collective-permute-start(bf16[3,128,128]{2,1,0:T(8,128)(2,1)} %get-tuple-element.52), channel_id=1, source_target_pairs={{0,496},{16,0},{32,16},{48,32},{64,48},{80,64},{96,80},{112,96},{1... | collective-permute-start | bytes 294920 | tf_op jit(solution)/shard_map/ppermute | solution.py:231
  47.1 7.1 %collective-permute-start.5 = (bf16[3,128,128]{2,1,0:T(8,128)(2,1)}, bf16[3,128,128]{2,1,0:T(8,128)(2,1)S(1)}, u32[]{:S(2)}, u32[]{:S(2)}) collective-permute-start(bf16[3,128,128]{2,1,0:T(8,128)(2,1)} %get-tuple-element.53), channel_id=1, source_target_pairs={{0,480},{16,496},{32,0},{48,16},{64,32},{80,48},{96,64},{112,80},{... | collective-permute-start | bytes 294920 | tf_op jit(solution)/shard_map/ppermute | solution.py:231
  54.2 27.7 %all-to-all-start.1 = ((bf16[16,128,128]{2,1,0:T(8,128)(2,1)}), bf16[16,128,128]{2,1,0:T(8,128)(2,1)S(1)}, u32[]{:S(2)}, u32[]{:S(2)}) async-start(bf16[16,128,128]{2,1,0:T(8,128)(2,1)} %get-tuple-element.56), calls=%async_computation.1 | async-start | bytes 1048576 | tf_op jit(solution)/shard_map/all_to_all | solution.py:235
  64.6 22.6 %collective-permute-start.6 = (bf16[3,128,128]{2,1,0:T(8,128)(2,1)}, bf16[3,128,128]{2,1,0:T(8,128)(2,1)}, u32[]{:S(2)}, u32[]{:S(2)}) collective-permute-start(bf16[3,128,128]{2,1,0:T(8,128)(2,1)} %get-tuple-element.57), channel_id=1, source_target_pairs={{0,32},{16,48},{32,64},{48,80},{64,96},{80,112},{96,128},{112,144}... | collective-permute-start | bytes 294920 | tf_op jit(solution)/shard_map/ppermute | solution.py:231
  66.5 20.7 %collective-permute-start.7 = (bf16[3,128,128]{2,1,0:T(8,128)(2,1)}, bf16[3,128,128]{2,1,0:T(8,128)(2,1)}, u32[]{:S(2)}, u32[]{:S(2)}) collective-permute-start(bf16[3,128,128]{2,1,0:T(8,128)(2,1)} %get-tuple-element.58), channel_id=1, source_target_pairs={{0,16},{16,32},{32,48},{48,64},{64,80},{80,96},{96,112},{112,128},... | collective-permute-start | bytes 294920 | tf_op jit(solution)/shard_map/ppermute | solution.py:231
  83.3 10.0 %collective-permute-start.8 = (bf16[3,128,128]{2,1,0:T(8,128)(2,1)}, bf16[3,128,128]{2,1,0:T(8,128)(2,1)S(1)}, u32[]{:S(2)}, u32[]{:S(2)}) collective-permute-start(bf16[3,128,128]{2,1,0:T(8,128)(2,1)} %get-tuple-element.67), channel_id=1, source_target_pairs={{0,32},{16,48},{32,64},{48,80},{64,96},{80,112},{96,128},{112,144}... | collective-permute-start | bytes 294920 | tf_op jit(solution)/shard_map/ppermute | solution.py:231
  85.2 9.7 %collective-permute-start.9 = (bf16[3,128,128]{2,1,0:T(8,128)(2,1)}, bf16[3,128,128]{2,1,0:T(8,128)(2,1)S(1)}, u32[]{:S(2)}, u32[]{:S(2)}) collective-permute-start(bf16[3,128,128]{2,1,0:T(8,128)(2,1)} %get-tuple-element.68), channel_id=1, source_target_pairs={{0,16},{16,32},{32,48},{48,64},{64,80},{80,96},{96,112},{112,128},... | collective-permute-start | bytes 294920 | tf_op jit(solution)/shard_map/ppermute | solution.py:231
  94.9 0.6 copy-start.1
  95.5 26.8 %all-to-all-start.2 = ((bf16[16,128,128]{2,1,0:T(8,128)(2,1)}), bf16[16,128,128]{2,1,0:T(8,128)(2,1)}, u32[]{:S(2)}, u32[]{:S(2)}) async-start(bf16[16,128,128]{2,1,0:T(8,128)(2,1)} %shard_map.69), calls=%async_computation.2 | async-start | bytes 1048576 | tf_op jit(solution)/shard_map/all_to_all | solution.py:235
  99.7 8.8 %collective-permute-start.10 = (bf16[3,128,128]{2,1,0:T(8,128)(2,1)}, bf16[3,128,128]{2,1,0:T(8,128)(2,1)S(1)}, u32[]{:S(2)}, u32[]{:S(2)}) collective-permute-start(bf16[3,128,128]{2,1,0:T(8,128)(2,1)} %get-tuple-element.75), channel_id=1, source_target_pairs={{0,496},{16,0},{32,16},{48,32},{64,48},{80,64},{96,80},{112,96},{1... | collective-permute-start | bytes 294920 | tf_op jit(solution)/shard_map/ppermute | solution.py:231
  102.7 8.3 %collective-permute-start.11 = (bf16[3,128,128]{2,1,0:T(8,128)(2,1)}, bf16[3,128,128]{2,1,0:T(8,128)(2,1)S(1)}, u32[]{:S(2)}, u32[]{:S(2)}) collective-permute-start(bf16[3,128,128]{2,1,0:T(8,128)(2,1)} %get-tuple-element.76), channel_id=1, source_target_pairs={{0,480},{16,496},{32,0},{48,16},{64,32},{80,48},{96,64},{112,80},{... | collective-permute-start | bytes 294920 | tf_op jit(solution)/shard_map/ppermute | solution.py:231
  111.0 0.9 copy-start.2
  114.7 23.2 %copy-start.6 = (bf16[3,128,128]{2,1,0:T(8,128)(2,1)S(1)}, bf16[3,128,128]{2,1,0:T(8,128)(2,1)}, u32[]{:S(2)}) copy-start(bf16[3,128,128]{2,1,0:T(8,128)(2,1)} %get-tuple-element.82) | copy-start | bytes 294916
  114.7 11.0 %collective-permute-start.12 = (bf16[3,128,128]{2,1,0:T(8,128)(2,1)}, bf16[3,128,128]{2,1,0:T(8,128)(2,1)S(1)}, u32[]{:S(2)}, u32[]{:S(2)}) collective-permute-start(bf16[3,128,128]{2,1,0:T(8,128)(2,1)} %get-tuple-element.77), channel_id=1, source_target_pairs={{0,496},{16,0},{32,16},{48,32},{64,48},{80,64},{96,80},{112,96},{1... | collective-permute-start | bytes 294920 | tf_op jit(solution)/shard_map/ppermute | solution.py:231
  118.8 7.1 %collective-permute-start.13 = (bf16[3,128,128]{2,1,0:T(8,128)(2,1)}, bf16[3,128,128]{2,1,0:T(8,128)(2,1)S(1)}, u32[]{:S(2)}, u32[]{:S(2)}) collective-permute-start(bf16[3,128,128]{2,1,0:T(8,128)(2,1)} %get-tuple-element.78), channel_id=1, source_target_pairs={{0,480},{16,496},{32,0},{48,16},{64,32},{80,48},{96,64},{112,80},{... | collective-permute-start | bytes 294920 | tf_op jit(solution)/shard_map/ppermute | solution.py:231
  125.8 27.2 %all-to-all-start.3 = ((bf16[16,128,128]{2,1,0:T(8,128)(2,1)}), bf16[16,128,128]{2,1,0:T(8,128)(2,1)}, u32[]{:S(2)}, u32[]{:S(2)}) async-start(bf16[16,128,128]{2,1,0:T(8,128)(2,1)} %shard_map.70), calls=%async_computation.3 | async-start | bytes 1048576 | tf_op jit(solution)/shard_map/all_to_all | solution.py:235
  135.7 9.9 %collective-permute-start.14 = (bf16[3,128,128]{2,1,0:T(8,128)(2,1)}, bf16[3,128,128]{2,1,0:T(8,128)(2,1)S(1)}, u32[]{:S(2)}, u32[]{:S(2)}) collective-permute-start(bf16[3,128,128]{2,1,0:T(8,128)(2,1)} %get-tuple-element.81), channel_id=1, source_target_pairs={{0,32},{16,48},{32,64},{48,80},{64,96},{80,112},{96,128},{112,144}... | collective-permute-start | bytes 294920 | tf_op jit(solution)/shard_map/ppermute | solution.py:231
  137.9 9.2 %collective-permute-start.15 = (bf16[3,128,128]{2,1,0:T(8,128)(2,1)S(1)}, bf16[3,128,128]{2,1,0:T(8,128)(2,1)S(1)}, u32[]{:S(2)}, u32[]{:S(2)}) collective-permute-start(bf16[3,128,128]{2,1,0:T(8,128)(2,1)S(1)} %copy-done.6), channel_id=1, source_target_pairs={{0,16},{16,32},{32,48},{48,64},{64,80},{80,96},{96,112},{112,128},... | collective-permute-start | bytes 294920 | tf_op jit(solution)/shard_map/ppermute | solution.py:231

commit v5 on v1

v5 whole, which is shorter than its diff:
```python
import functools

import jax
import jax.numpy as jnp
from jax import lax
from jax.experimental import pallas as pl
from jax.experimental.pallas import tpu as pltpu
from jax.sharding import PartitionSpec as P

REACH = 2
OFFSETS = tuple(range(-REACH, 0)) + tuple(range(1, REACH + 1))
F32, BF16 = jnp.float32, jnp.bfloat16
LIMIT = 24 * 2**20
SMEM = pl.BlockSpec(memory_space=pltpu.SMEM)
VMEM = pl.BlockSpec(memory_space=pltpu.VMEM)
HBM = pl.BlockSpec(memory_space=pltpu.HBM)
DMA = pltpu.SemaphoreType.DMA


def call(kernel, outs, ins, scratch, flops=0, aliases=None):
    arrays, specs = zip(*ins)
    shapes, results = zip(*outs)
    size = sum(a.size * a.dtype.itemsize for a in (*arrays, *shapes))
    arrays = [pltpu.with_memory_space_constraint(a, pltpu.HBM) if spec is HBM else a for a, spec in ins]
    shapes = [pltpu.HBM(a.shape, a.dtype) if spec is HBM else a for a, spec in outs]
    return pl.pallas_call(
        kernel,
        out_shape=shapes,
        in_specs=specs,
        out_specs=results,
        scratch_shapes=scratch,
        compiler_params=pltpu.CompilerParams(vmem_limit_bytes=LIMIT),
        cost_estimate=pl.CostEstimate(flops=flops, bytes_accessed=size, transcendentals=0),
        input_output_aliases=aliases or {},
    )(*arrays)


def array(*shape, dtype=BF16):
    return jax.ShapeDtypeStruct(shape, dtype)


def start(source, target, sem):
    copy = pltpu.make_async_copy(source, target, sem)
    copy.start()
    return copy


def wait(copies):
    for copy in copies:
        copy.wait()


def times_transposed(a, b):
    return lax.dot_general(a, b, (((1,), (1,)), ((), ())), preferred_element_type=F32)


def block_of(ref, g, width):
    if len(ref.shape) == 3:
        return ref[g]
    at = g * width
    return ref[:, pl.ds(at if isinstance(g, int) else pl.multiple_of(at, width), width)]


def scaled_block(ref, inv_ref, g, width):
    return (block_of(ref, g, width).astype(F32) * inv_ref[pl.ds(g, 1), :]).astype(BF16)


def partner_ways():
    place = lax.axis_index("dom")
    odd = lax.rem(place, 2)
    upper = lax.div(lax.rem(place, 4), 2)
    return [2 - odd, 1 + odd, 3 * (1 - upper), 3 * upper]


def partners(index, count):
    reach = 1 + index // 2
    down = [(p // reach) % 2 != index % 2 for p in range(count)]
    return [(p, (p - reach if down[p] else p + reach) % count) for p in range(count)]


def pack(send_ref, field_ref, inv_ref, packs, held, sems):
    width = inv_ref.shape[1]
    copies = []
    ways = partner_ways()
    for i in reversed(range(len(packs))):
        out = packs[i]
        way = len(OFFSETS) - 1 - ways[i]
        for slot in range(out.shape[0]):
            held[i, slot] = scaled_block(field_ref, inv_ref, send_ref[0, way, slot], width)
        copies.append(start(held.at[i], out, sems.at[i]))
    return copies


def spread(kernel_ref, out_ref, mix, held, sems, mix_sem):
    owners, _, width = out_ref.shape
    t_loc, time = kernel_ref.shape
    start(kernel_ref, mix, mix_sem).wait()
    for q in range(time // width):
        held[q * t_loc : (q + 1) * t_loc] = mix[:, q * width : (q + 1) * width]
    wait([start(held, out_ref.at[i], sems.at[i]) for i in range(owners)])


def first_scale(signal_ref, weights_ref, send_ref, coef_ref, inv_ref, *rest):
    *packs, field, edges, inv, held, sems, edge_sems, load_sem = rest
    blocks, per_row, width, _ = weights_ref.shape
    loads = [start(weights_ref.at[g], edges.at[g], edge_sems.at[g]) for g in range(blocks)]
    load = start(signal_ref, field, load_sem)
    for term in range(coef_ref.shape[0]):
        inv[blocks + term : blocks + term + 1, :] = jnp.full((1, width), coef_ref[term], F32)
    ones = jnp.ones((16, width), BF16)
    for g in range(blocks):
        loads[g].wait()
        degree = times_transposed(ones, edges[g, 0])
        for j in range(1, per_row):
            degree += times_transposed(ones, edges[g, j])
        inv[g : g + 1, :] = lax.rsqrt(degree[:1])
    load.wait()
    copies = pack(send_ref, field, inv, packs, held, sems)
    wait([start(inv, inv_ref, load_sem), *copies])


def place_received(blocks, received, source):
    for way, ref in zip(partner_ways(), received):
        slots = ref.shape[0]
        for slot in range(slots):
            source[blocks + way * slots + slot] = ref[slot]


def place_own(blocks, field_ref, inv_ref, source):
    for g in range(blocks):
        source[g] = scaled_block(field_ref, inv_ref, g, inv_ref.shape[1])


def block_product(g, col_ref, weights_ref, source):
    per_row = weights_ref.shape[1]
    picked = jnp.concatenate([source[col_ref[g, j]] for j in range(per_row)], axis=1)
    edges = jnp.concatenate([weights_ref[g, j] for j in range(per_row)], axis=1)
    return times_transposed(picked, edges)


def first_product(field_ref, r0, r1, r2, r3, weights_ref, inv_ref, col_ref, send_ref, term_ref, *rest):
    *packs, source, term, held, sems, pack_sems, field, load_sem, inv, inv_sem = rest
    load = start(field_ref, field, load_sem)
    scales = start(inv_ref, inv, inv_sem)
    blocks = weights_ref.shape[0]
    place_received(blocks, (r0, r1, r2, r3), source)
    load.wait()
    scales.wait()
    place_own(blocks, field, inv, source)
    copies = []
    for g in range(blocks):
        total = block_product(g, col_ref, weights_ref, source)
        term[g] = (-inv[g : g + 1, :] * total).astype(BF16)
        copies.append(start(term.at[g], term_ref.at[g], sems.at[g]))
    wait(copies + pack(send_ref, term, inv, packs, held, pack_sems))


def second_product(field_ref, r0, r1, r2, r3, weights_ref, inv_ref, col_ref, term_ref, out_ref, *rest):
    source, term, held, sems, term_sem, field, load_sem, inv, inv_sem = rest
    scales = start(inv_ref, inv, inv_sem)
    first = start(term_ref, term, term_sem)
    load = start(field_ref, field, load_sem)
    blocks, _, width, _ = weights_ref.shape
    place_received(blocks, (r0, r1, r2, r3), source)
    first.wait()
    scales.wait()
    place_own(blocks, term, inv, source)
    coef = [inv[blocks + i : blocks + i + 1, :] for i in range(3)]
    load.wait()
    copies = []
    for g in range(blocks):
        total = block_product(g, col_ref, weights_ref, source)
        x = block_of(field, g, width).astype(F32)
        two = (-2.0 * inv[g : g + 1, :] * total - x).astype(BF16).astype(F32)
        one = term[g].astype(F32)
        held[g] = (coef[0] * x + coef[1] * one + coef[2] * two).astype(BF16)
        copies.append(start(held.at[g], out_ref.at[g], sems.at[g]))
    wait(copies)


def mix_times(t_loc, mix, field_ref, out_ref, columns, held, sems):
    owners, rows, width = out_ref.shape
    for p in range(rows // t_loc):
        part = slice(p * t_loc, (p + 1) * t_loc)
        for i in range(owners):
            columns[i * t_loc : (i + 1) * t_loc, p * width : (p + 1) * width] = field_ref[i, part]
    step = 2 * width
    pieces = columns.shape[1] // step
    depth = rows // pieces
    copies = []
    for c in range(pieces):
        out = jnp.dot(mix, columns[:, c * step : (c + 1) * step], preferred_element_type=F32).astype(BF16)
        for q in range(step // width):
            at = c * depth + q * t_loc
            for i in range(owners):
                held[i, at : at + t_loc] = out[i * t_loc : (i + 1) * t_loc, q * width : (q + 1) * width]
        part = slice(c * depth, (c + 1) * depth)
        copies.append(start(held.at[:, part], out_ref.at[:, part], sems.at[c]))
    return copies


def temporal(t_loc, field_ref, spread_ref, out_ref, columns, held, mix, sems):
    owners = out_ref.shape[0]
    width = out_ref.shape[2]
    for i in range(owners):
        for q in range(mix.shape[1] // width):
            mix[i * t_loc : (i + 1) * t_loc, q * width : (q + 1) * width] = spread_ref[i, q * t_loc : (q + 1) * t_loc]
    wait(mix_times(t_loc, mix[...], field_ref, out_ref, columns, held, sems))


def unblock(field_ref, out_ref, sems):
    blocks, _, width = field_ref.shape
    wait([start(field_ref.at[g], out_ref.at[:, g * width : (g + 1) * width], sems.at[g]) for g in range(blocks)])


def swap(packs):
    count = lax.axis_size("dom")
    return [lax.ppermute(block, "dom", partners(i, count)) for i, block in enumerate(packs)]


def exchange(field):
    return lax.all_to_all(field, "tm", split_axis=0, concat_axis=0, tiled=True)


def body(signal, weights, send_list, col_ref, kernel, cheb_coef):
    probes, t_loc, n_loc = signal.shape
    blocks, per_row, width, _ = weights.shape
    rows = probes * t_loc
    slots = send_list.shape[2]
    owners = lax.axis_size("tm")
    time = kernel.shape[1]
    ways = len(OFFSETS)
    pieces = probes // 2
    xs = signal.reshape(rows, n_loc)
    field = array(blocks, rows, width)
    packed = [(array(slots, rows, width), HBM)] * ways
    vm = pltpu.VMEM
    source = vm((blocks + ways * slots, rows, width), BF16)
    whole = vm((blocks, rows, width), BF16)
    held = vm((ways, slots, rows, width), BF16)
    scales = array(blocks + 8, width, dtype=F32)
    loaded = [vm((rows, n_loc), BF16), DMA, vm(scales.shape, F32), DMA]
    work = 2 * rows * per_row * n_loc * width

    depth = time * t_loc // width
    (mix,) = call(
        spread,
        [(array(owners, depth, width), HBM)],
        [(kernel, HBM)],
        [vm(kernel.shape, BF16), vm((depth, width), BF16), DMA((owners,)), DMA],
    )
    mix = exchange(mix)
    inv, *packs = call(
        first_scale,
        [(scales, HBM), *packed],
        [(xs, HBM), (weights, HBM), (send_list, SMEM), (cheb_coef, SMEM)],
        [loaded[0], vm(weights.shape, BF16), loaded[2], held, DMA((ways,)), DMA((blocks,)), DMA],
        flops=work // 8,
    )
    received = swap(packs)
    term, *packs = call(
        first_product,
        [(field, HBM), *packed],
        [
            (xs, HBM),
            *((r, VMEM) for r in received),
            (weights, VMEM),
            (inv, HBM),
            (col_ref, SMEM),
            (send_list, SMEM),
        ],
        [source, whole, held, DMA((blocks,)), DMA((ways,)), *loaded],
        flops=work,
    )
    (mixed,) = call(
        second_product,
        [(field, HBM)],
        [
            (xs, HBM),
            *((r, VMEM) for r in swap(packs)),
            (weights, VMEM),
            (inv, HBM),
            (col_ref, SMEM),
            (term, HBM),
        ],
        [source, whole, whole, DMA((blocks,)), DMA, *loaded],
        flops=work,
    )
    (filtered,) = call(
        functools.partial(temporal, t_loc),
        [(array(owners, rows, width), HBM)],
        [(exchange(mixed), VMEM), (mix, VMEM)],
        [vm((time, probes * width), BF16), whole, vm((time, time), BF16), DMA((pieces,))],
        flops=2 * time * time * probes * width,
    )
    (out,) = call(unblock, [(array(rows, n_loc), HBM)], [(exchange(filtered), VMEM)], [DMA((blocks,))])
    return out.reshape(probes, t_loc, n_loc)


def solution(mesh):
    in_specs = (
        P(None, "tm", "dom"),
        P("dom", None, None, None),
        P("dom", None, None),
        P("dom", None),
        P("tm", None),
        P(),
    )
    out_specs = P(None, "tm", "dom")
    return jax.shard_map(body, mesh=mesh, in_specs=in_specs, out_specs=out_specs, check_vma=False)
```

time: 160 us -> 151 us (0.944)
  blocking collectives: 33.3 us -> 70.9 us
  waiting for transfers between devices: 41 us -> 12.4 us
  between operations: 13.5 us -> 0.14 us
  local copies, waits for them, and re-layouts: 13.8 us -> 1.51 us
  Pallas kernels: 10.6 us -> 21.4 us
  starting transfers between devices: 46 us -> 44.4 us
    all_to_all x1 -> x2, blocking collectives: 33.3 us -> 70.9 us  [exchange(): return lax.all_to_all(field, 'tm', split_axis=0, concat_axis=0, tiled=True)]
    all_gather x1 -> x0, waiting for transfers between devices: 31 us -> none  [body(): mix = lax.all_gather(kernel.astype(F32), 'tm', axis=0, tiled=True)]
    unnamed x32 -> x8, local copies, waits for them, and re-layouts: 13.8 us -> 1.51 us
    pallas_call x5 -> x6, Pallas kernels: 10.6 us -> 21.4 us  [call(): pl.pallas_call(kernel, out_shape=shapes, in_specs=specs, out_specs=result...]
    ppermute x8, starting transfers between devices: 36.9 us -> 34.1 us  [swap(): lax.ppermute(block, 'dom', partners(i, count))]
    ppermute x8, waiting for transfers between devices: 9.81 us -> 12.4 us  [swap(): lax.ppermute(block, 'dom', partners(i, count))]
  transfers between devices with their start and end apart: 10 -> 9, of which waited for: 6 -> 4; matrix products, arithmetic and copies ran while one was open for 0% -> 1% of each run, Pallas kernels for 1% -> 11%
where the time goes in v5:
time: 151 us
  blocking collectives  70.9 us (47%)
  starting transfers between devices  44.4 us (29%)
  Pallas kernels  21.4 us (14%)
  waiting for transfers between devices  12.4 us (8%)
  local copies, waits for them, and re-layouts  1.51 us (1%)
    all_to_all x2, blocking collectives, exchange(): return lax.all_to_all(field, 'tm', split_axis=0, concat_axis=0, tiled=True)  70.9 us
    ppermute x8, starting transfers between devices, swap(): lax.ppermute(block, 'dom', partners(i, count))  34.1 us
    pallas_call x6, Pallas kernels, call(): pl.pallas_call(kernel, out_shape=shapes, in_specs=specs, out_specs=result...  21.4 us
    ppermute x8, waiting for transfers between devices, swap(): lax.ppermute(block, 'dom', partners(i, count))  12.4 us
    all_to_all x1, starting transfers between devices, exchange(): return lax.all_to_all(field, 'tm', split_axis=0, concat_axis=0, tiled=True)  10.2 us
  transfers between devices with their start and end apart: 9, of which 4 were waited for; matrix products, arithmetic and copies ran while one was open for 1% of the time, Pallas kernels for 11%

profile of v5, /device:TPU:1, one launch (start us, length us, event | category | flops | bytes accessed | tf_op | source)
XLA Modules:
  0.0 150.7 jit_solution(11359729832213226947)
XLA Ops:
  0.0 0.0 copy-start
  0.0 1.9 %shard_map.67 = bf16[16,128,128]{2,1,0:T(8,128)(2,1)} custom-call(bf16[32,512]{1,0:T(8,128)(2,1)} %kernel_ref.1), custom_call_target="tpu_custom_call" | custom-call | bytes 557056 | tf_op jit(solution)/shard_map/pallas_call | solution.py:26
  1.9 10.2 %all-to-all-start.1 = ((bf16[16,128,128]{2,1,0:T(8,128)(2,1)}), bf16[16,128,128]{2,1,0:T(8,128)(2,1)S(1)}, u32[]{:S(2)}, u32[]{:S(2)}) async-start(bf16[16,128,128]{2,1,0:T(8,128)(2,1)} %shard_map.67), calls=%async_computation.1 | async-start | bytes 1048576 | tf_op jit(solution)/shard_map/all_to_all | solution.py:222
  12.1 0.8 copy.7.send_ref
  12.9 0.0 copy-start.1
  12.9 0.7 copy-done.1
  13.5 0.0 copy-start.2
  13.5 7.2 %shard_map.64 = (f32[24,128]{1,0:T(8,128)}, bf16[3,256,128]{2,1,0:T(8,128)(2,1)}, bf16[3,256,128]{2,1,0:T(8,128)(2,1)}, bf16[3,256,128]{2,1,0:T(8,128)(2,1)}, bf16[3,256,128]{2,1,0:T(8,128)(2,1)}) custom-call(bf16[256,2048]{1,0:T(8,128)(2,1)} %bitcast.2, bf16[16,5,128,128]{3,2,1,0:T(8,128)(2,1)} %weights_ref.5, s32[1,4,3]{2,1,0:T(4,128)S(1)} %copy.7.send_ref, ...), custom_call_target="tpu_custom_call" | custom-call | flops 83886080 | bytes 4468796 | tf_op jit(solution)/shard_map/pallas_call | solution.py:26
  20.8 1.9 %collective-permute-start = (bf16[3,256,128]{2,1,0:T(8,128)(2,1)}, bf16[3,256,128]{2,1,0:T(8,128)(2,1)S(1)}, u32[]{:S(2)}, u32[]{:S(2)}) collective-permute-start(bf16[3,256,128]{2,1,0:T(8,128)(2,1)} %get-tuple-element.15), channel_id=1, source_target_pairs={{0,16},{16,0},{32,48},{48,32},{64,80},{80,64},{96,112},{112,96},{1... | collective-permute-start | bytes 589832 | tf_op jit(solution)/shard_map/ppermute | solution.py:218
  22.7 11.8 %collective-permute-start.1 = (bf16[3,256,128]{2,1,0:T(8,128)(2,1)}, bf16[3,256,128]{2,1,0:T(8,128)(2,1)S(1)}, u32[]{:S(2)}, u32[]{:S(2)}) collective-permute-start(bf16[3,256,128]{2,1,0:T(8,128)(2,1)} %get-tuple-element.16), channel_id=1, source_target_pairs={{0,496},{16,32},{32,16},{48,64},{64,48},{80,96},{96,80},{112,128},... | collective-permute-start | bytes 589832 | tf_op jit(solution)/shard_map/ppermute | solution.py:218
  34.5 1.9 %collective-permute-start.2 = (bf16[3,256,128]{2,1,0:T(8,128)(2,1)}, bf16[3,256,128]{2,1,0:T(8,128)(2,1)}, u32[]{:S(2)}, u32[]{:S(2)}) collective-permute-start(bf16[3,256,128]{2,1,0:T(8,128)(2,1)} %get-tuple-element.17), channel_id=1, source_target_pairs={{0,32},{16,48},{32,0},{48,16},{64,96},{80,112},{96,64},{112,80},{1... | collective-permute-start | bytes 589832 | tf_op jit(solution)/shard_map/ppermute | solution.py:218
  36.4 4.9 %collective-permute-start.3 = (bf16[3,256,128]{2,1,0:T(8,128)(2,1)}, bf16[3,256,128]{2,1,0:T(8,128)(2,1)}, u32[]{:S(2)}, u32[]{:S(2)}) collective-permute-start(bf16[3,256,128]{2,1,0:T(8,128)(2,1)} %get-tuple-element.18), channel_id=1, source_target_pairs={{0,480},{16,496},{32,64},{48,80},{64,32},{80,48},{96,128},{112,144... | collective-permute-start | bytes 589832 | tf_op jit(solution)/shard_map/ppermute | solution.py:218
  41.3 0.0 copy-done.2
  41.3 0.1 copy.8.col_ref
  41.4 0.0 collective-permute-done.r0
  41.4 0.0 collective-permute-done.1.r1
  41.4 2.6 %collective-permute-done.2.r2 = bf16[3,256,128]{2,1,0:T(8,128)(2,1)} collective-permute-done((bf16[3,256,128]{2,1,0:T(8,128)(2,1)}, bf16[3,256,128]{2,1,0:T(8,128)(2,1)}, u32[]{:S(2)}, u32[]{:S(2)}) %collective-permute-start.2) | collective-permute-done | bytes 196640 | tf_op jit(solution)/shard_map/ppermute | solution.py:218
  44.0 4.1 %collective-permute-done.3.r3 = bf16[3,256,128]{2,1,0:T(8,128)(2,1)} collective-permute-done((bf16[3,256,128]{2,1,0:T(8,128)(2,1)}, bf16[3,256,128]{2,1,0:T(8,128)(2,1)}, u32[]{:S(2)}, u32[]{:S(2)}) %collective-permute-start.3) | collective-permute-done | bytes 196640 | tf_op jit(solution)/shard_map/ppermute | solution.py:218
  48.1 0.0 copy-done
  48.1 5.1 %shard_map.65 = (bf16[16,256,128]{2,1,0:T(8,128)(2,1)}, bf16[3,256,128]{2,1,0:T(8,128)(2,1)}, bf16[3,256,128]{2,1,0:T(8,128)(2,1)}, bf16[3,256,128]{2,1,0:T(8,128)(2,1)}, bf16[3,256,128]{2,1,0:T(8,128)(2,1)}) custom-call(bf16[256,2048]{1,0:T(8,128)(2,1)} %bitcast.3, bf16[3,256,128]{2,1,0:T(8,128)(2,1)S(1)} %collective-permute-done.r0, ...), custom_call_target="tpu_custom_call" | custom-call | flops 671088640 | bytes 6304112 | tf_op jit(solution)/shard_map/pallas_call | solution.py:26
  53.2 1.9 %collective-permute-start.4 = (bf16[3,256,128]{2,1,0:T(8,128)(2,1)}, bf16[3,256,128]{2,1,0:T(8,128)(2,1)S(1)}, u32[]{:S(2)}, u32[]{:S(2)}) collective-permute-start(bf16[3,256,128]{2,1,0:T(8,128)(2,1)} %get-tuple-element.20), channel_id=1, source_target_pairs={{0,16},{16,0},{32,48},{48,32},{64,80},{80,64},{96,112},{112,96},{1... | collective-permute-start | bytes 589832 | tf_op jit(solution)/shard_map/ppermute | solution.py:218
  55.1 5.0 %collective-permute-start.5 = (bf16[3,256,128]{2,1,0:T(8,128)(2,1)}, bf16[3,256,128]{2,1,0:T(8,128)(2,1)S(1)}, u32[]{:S(2)}, u32[]{:S(2)}) collective-permute-start(bf16[3,256,128]{2,1,0:T(8,128)(2,1)} %get-tuple-element.21), channel_id=1, source_target_pairs={{0,496},{16,32},{32,16},{48,64},{64,48},{80,96},{96,80},{112,128},... | collective-permute-start | bytes 589832 | tf_op jit(solution)/shard_map/ppermute | solution.py:218
  60.1 2.0 %collective-permute-start.6 = (bf16[3,256,128]{2,1,0:T(8,128)(2,1)}, bf16[3,256,128]{2,1,0:T(8,128)(2,1)S(1)}, u32[]{:S(2)}, u32[]{:S(2)}) collective-permute-start(bf16[3,256,128]{2,1,0:T(8,128)(2,1)} %get-tuple-element.22), channel_id=1, source_target_pairs={{0,32},{16,48},{32,0},{48,16},{64,96},{80,112},{96,64},{112,80},{1... | collective-permute-start | bytes 589832 | tf_op jit(solution)/shard_map/ppermute | solution.py:218
  62.2 4.7 %collective-permute-start.7 = (bf16[3,256,128]{2,1,0:T(8,128)(2,1)}, bf16[3,256,128]{2,1,0:T(8,128)(2,1)S(1)}, u32[]{:S(2)}, u32[]{:S(2)}) collective-permute-start(bf16[3,256,128]{2,1,0:T(8,128)(2,1)} %get-tuple-element.23), channel_id=1, source_target_pairs={{0,480},{16,496},{32,64},{48,80},{64,32},{80,48},{96,128},{112,144... | collective-permute-start | bytes 589832 | tf_op jit(solution)/shard_map/ppermute | solution.py:218
  66.9 0.0 collective-permute-done.4.r0
  66.9 0.0 collective-permute-done.5.r1
  66.9 2.4 %collective-permute-done.6.r2 = bf16[3,256,128]{2,1,0:T(8,128)(2,1)S(1)} collective-permute-done((bf16[3,256,128]{2,1,0:T(8,128)(2,1)}, bf16[3,256,128]{2,1,0:T(8,128)(2,1)S(1)}, u32[]{:S(2)}, u32[]{:S(2)}) %collective-permute-start.6) | collective-permute-done | bytes 196640 | tf_op jit(solution)/shard_map/ppermute | solution.py:218
  69.3 3.3 %collective-permute-done.7.r3 = bf16[3,256,128]{2,1,0:T(8,128)(2,1)S(1)} collective-permute-done((bf16[3,256,128]{2,1,0:T(8,128)(2,1)}, bf16[3,256,128]{2,1,0:T(8,128)(2,1)S(1)}, u32[]{:S(2)}, u32[]{:S(2)}) %collective-permute-start.7) | collective-permute-done | bytes 196640 | tf_op jit(solution)/shard_map/ppermute | solution.py:218
  72.5 4.5 %shard_map.66 = bf16[16,256,128]{2,1,0:T(8,128)(2,1)} custom-call(bf16[256,2048]{1,0:T(8,128)(2,1)} %bitcast.4, bf16[3,256,128]{2,1,0:T(8,128)(2,1)S(1)} %collective-permute-done.4.r0, bf16[3,256,128]{2,1,0:T(8,128)(2,1)S(1)} %collective-permute-done.5.r1, bf16[3,256,128]{2,1,0:T(8,128)(2,1)S(1)} %collective-permute-done.6.r2, ...), custom_call_target="tpu_custom_call" | custom-call | flops 671088640 | bytes 6566208 | tf_op jit(solution)/shard_map/pallas_call | solution.py:26
  77.1 0.0 all-to-all-done.1.spread_ref
  77.1 39.4 %all_to_all.15.field_ref = bf16[16,256,128]{2,1,0:T(8,128)(2,1)S(1)} all-to-all(bf16[16,256,128]{2,1,0:T(8,128)(2,1)} %shard_map.66), channel_id=1, replica_groups=mesh['dom'=32,'tm'=16] {'tm'}, dimensions={0} | all-to-all | bytes 2097152 | tf_op jit(solution)/shard_map/all_to_all | solution.py:222
  116.5 1.7 %shard_map.68 = bf16[16,256,128]{2,1,0:T(8,128)(2,1)} custom-call(bf16[16,256,128]{2,1,0:T(8,128)(2,1)S(1)} %all_to_all.15.field_ref, bf16[16,128,128]{2,1,0:T(8,128)(2,1)S(1)} %all-to-all-done.1.spread_ref), custom_call_target="tpu_custom_call" | custom-call | flops 536870912 | bytes 2621440 | tf_op jit(solution)/shard_map/pallas_call | solution.py:26
  118.2 31.4 %all_to_all.16.field_ref = bf16[16,256,128]{2,1,0:T(8,128)(2,1)S(1)} all-to-all(bf16[16,256,128]{2,1,0:T(8,128)(2,1)} %shard_map.68), channel_id=1, replica_groups=mesh['dom'=32,'tm'=16] {'tm'}, dimensions={0} | all-to-all | bytes 2097152 | tf_op jit(solution)/shard_map/all_to_all | solution.py:222
  149.6 1.1 shard_map.69
Async XLA Ops:
  0.0 48.1 %copy-start = (bf16[16,5,128,128]{3,2,1,0:T(8,128)(2,1)S(1)}, bf16[16,5,128,128]{3,2,1,0:T(8,128)(2,1)}, u32[]{:S(2)}) copy-start(bf16[16,5,128,128]{3,2,1,0:T(8,128)(2,1)} %weights_ref.5) | copy-start | bytes 7864324
  1.9 75.2 %all-to-all-start.1 = ((bf16[16,128,128]{2,1,0:T(8,128)(2,1)}), bf16[16,128,128]{2,1,0:T(8,128)(2,1)S(1)}, u32[]{:S(2)}, u32[]{:S(2)}) async-start(bf16[16,128,128]{2,1,0:T(8,128)(2,1)} %shard_map.67), calls=%async_computation.1 | async-start | bytes 1048576 | tf_op jit(solution)/shard_map/all_to_all | solution.py:222
  12.9 0.7 copy-start.1
  13.5 27.7 %copy-start.2 = (s32[16,5]{0,1:T(8,128)S(1)}, s32[16,5]{0,1:T(8,128)}, u32[]{:S(2)}) copy-start(s32[16,5]{0,1:T(8,128)} %param.9) | copy-start | bytes 964
  20.8 20.6 %collective-permute-start = (bf16[3,256,128]{2,1,0:T(8,128)(2,1)}, bf16[3,256,128]{2,1,0:T(8,128)(2,1)S(1)}, u32[]{:S(2)}, u32[]{:S(2)}) collective-permute-start(bf16[3,256,128]{2,1,0:T(8,128)(2,1)} %get-tuple-element.15), channel_id=1, source_target_pairs={{0,16},{16,0},{32,48},{48,32},{64,80},{80,64},{96,112},{112,96},{1... | collective-permute-start | bytes 589832 | tf_op jit(solution)/shard_map/ppermute | solution.py:218
  22.7 18.7 %collective-permute-start.1 = (bf16[3,256,128]{2,1,0:T(8,128)(2,1)}, bf16[3,256,128]{2,1,0:T(8,128)(2,1)S(1)}, u32[]{:S(2)}, u32[]{:S(2)}) collective-permute-start(bf16[3,256,128]{2,1,0:T(8,128)(2,1)} %get-tuple-element.16), channel_id=1, source_target_pairs={{0,496},{16,32},{32,16},{48,64},{64,48},{80,96},{96,80},{112,128},... | collective-permute-start | bytes 589832 | tf_op jit(solution)/shard_map/ppermute | solution.py:218
  34.5 9.5 %collective-permute-start.2 = (bf16[3,256,128]{2,1,0:T(8,128)(2,1)}, bf16[3,256,128]{2,1,0:T(8,128)(2,1)}, u32[]{:S(2)}, u32[]{:S(2)}) collective-permute-start(bf16[3,256,128]{2,1,0:T(8,128)(2,1)} %get-tuple-element.17), channel_id=1, source_target_pairs={{0,32},{16,48},{32,0},{48,16},{64,96},{80,112},{96,64},{112,80},{1... | collective-permute-start | bytes 589832 | tf_op jit(solution)/shard_map/ppermute | solution.py:218
  36.4 11.7 %collective-permute-start.3 = (bf16[3,256,128]{2,1,0:T(8,128)(2,1)}, bf16[3,256,128]{2,1,0:T(8,128)(2,1)}, u32[]{:S(2)}, u32[]{:S(2)}) collective-permute-start(bf16[3,256,128]{2,1,0:T(8,128)(2,1)} %get-tuple-element.18), channel_id=1, source_target_pairs={{0,480},{16,496},{32,64},{48,80},{64,32},{80,48},{96,128},{112,144... | collective-permute-start | bytes 589832 | tf_op jit(solution)/shard_map/ppermute | solution.py:218
  53.2 13.7 %collective-permute-start.4 = (bf16[3,256,128]{2,1,0:T(8,128)(2,1)}, bf16[3,256,128]{2,1,0:T(8,128)(2,1)S(1)}, u32[]{:S(2)}, u32[]{:S(2)}) collective-permute-start(bf16[3,256,128]{2,1,0:T(8,128)(2,1)} %get-tuple-element.20), channel_id=1, source_target_pairs={{0,16},{16,0},{32,48},{48,32},{64,80},{80,64},{96,112},{112,96},{1... | collective-permute-start | bytes 589832 | tf_op jit(solution)/shard_map/ppermute | solution.py:218
  55.1 11.8 %collective-permute-start.5 = (bf16[3,256,128]{2,1,0:T(8,128)(2,1)}, bf16[3,256,128]{2,1,0:T(8,128)(2,1)S(1)}, u32[]{:S(2)}, u32[]{:S(2)}) collective-permute-start(bf16[3,256,128]{2,1,0:T(8,128)(2,1)} %get-tuple-element.21), channel_id=1, source_target_pairs={{0,496},{16,32},{32,16},{48,64},{64,48},{80,96},{96,80},{112,128},... | collective-permute-start | bytes 589832 | tf_op jit(solution)/shard_map/ppermute | solution.py:218
  60.1 9.1 %collective-permute-start.6 = (bf16[3,256,128]{2,1,0:T(8,128)(2,1)}, bf16[3,256,128]{2,1,0:T(8,128)(2,1)S(1)}, u32[]{:S(2)}, u32[]{:S(2)}) collective-permute-start(bf16[3,256,128]{2,1,0:T(8,128)(2,1)} %get-tuple-element.22), channel_id=1, source_target_pairs={{0,32},{16,48},{32,0},{48,16},{64,96},{80,112},{96,64},{112,80},{1... | collective-permute-start | bytes 589832 | tf_op jit(solution)/shard_map/ppermute | solution.py:218
  62.2 10.3 %collective-permute-start.7 = (bf16[3,256,128]{2,1,0:T(8,128)(2,1)}, bf16[3,256,128]{2,1,0:T(8,128)(2,1)S(1)}, u32[]{:S(2)}, u32[]{:S(2)}) collective-permute-start(bf16[3,256,128]{2,1,0:T(8,128)(2,1)} %get-tuple-element.23), channel_id=1, source_target_pairs={{0,480},{16,496},{32,64},{48,80},{64,32},{80,48},{96,128},{112,144... | collective-permute-start | bytes 589832 | tf_op jit(solution)/shard_map/ppermute | solution.py:218

commit v6 on v4

--- a/solution.py
+++ b/solution.py
@@ -65,13 +65,28 @@
     return (block_of(ref, g, width).astype(F32) * inv_ref[pl.ds(g, 1), :]).astype(BF16)
 
 
+def partner_ways():
+    place = lax.axis_index("dom")
+    odd = lax.rem(place, 2)
+    upper = lax.div(lax.rem(place, 4), 2)
+    return [2 - odd, 1 + odd, 3 * (1 - upper), 3 * upper]
+
+
+def partners(index, count):
+    reach = 1 + index // 2
+    down = [(p // reach) % 2 != index % 2 for p in range(count)]
+    return [(p, (p - reach if down[p] else p + reach) % count) for p in range(count)]
+
+
 def pack(send_ref, field_ref, inv_ref, packs, held, sems):
     width = inv_ref.shape[1]
     copies = []
-    for way, out in enumerate(packs):
+    ways = partner_ways()
+    for i, out in enumerate(packs):
+        way = len(OFFSETS) - 1 - ways[i]
         for slot in range(out.shape[0]):
-            held[way, slot] = scaled_block(field_ref, inv_ref, send_ref[0, way, slot], width)
-        copies.append(start(held.at[way], out, sems.at[way]))
+            held[i, slot] = scaled_block(field_ref, inv_ref, send_ref[0, way, slot], width)
+        copies.append(start(held.at[i], out, sems.at[i]))
     return copies
 
 
@@ -116,13 +131,16 @@
     wait(pack(send_ref, field_ref, inv_ref, packs, held, sems))
 
 
-def gather_sources(blocks, field_ref, inv_ref, received, source):
-    width = inv_ref.shape[1]
+def place_received(blocks, received, source):
+    for way, ref in zip(partner_ways(), received):
+        slots = ref.shape[0]
+        for slot in range(slots):
+            source[blocks + way * slots + slot] = ref[slot]
+
+
+def place_own(blocks, field_ref, inv_ref, source):
     for g in range(blocks):
-        source[g] = scaled_block(field_ref, inv_ref, g, width)
-    for way, ref in enumerate(received):
-        slots = ref.shape[0]
-        source[blocks + way * slots : blocks + (way + 1) * slots] = ref[...]
+        source[g] = scaled_block(field_ref, inv_ref, g, inv_ref.shape[1])
 
 
 def block_product(g, col_ref, weights_ref, source):
@@ -138,12 +156,15 @@
 
 def first_product(in_hbm, field_ref, r0, r1, r2, r3, weights_ref, inv_ref, col_ref, send_ref, term_ref, *rest):
     *packs, source, term, held, sems, pack_sems = rest[: len(OFFSETS) + 5]
+    loads = []
     if in_hbm:
         field, load_sem = rest[len(OFFSETS) + 5 :]
-        wait(load_half(field_ref, field, load_sem))
+        loads = load_half(field_ref, field, load_sem)
         field_ref = field
     blocks = weights_ref.shape[0]
-    gather_sources(blocks, field_ref, inv_ref, (r0, r1, r2, r3), source)
+    place_received(blocks, (r0, r1, r2, r3), source)
+    wait(loads)
+    place_own(blocks, field_ref, inv_ref, source)
     copies = []
     for g in range(blocks):
         total = block_product(g, col_ref, weights_ref, source)
@@ -159,10 +180,11 @@
         field, load_sem = rest[5:]
         loads += load_half(field_ref, field, load_sem)
         field_ref = field
-    wait(loads)
     blocks, _, width, _ = weights_ref.shape
     rows = term.shape[1]
-    gather_sources(blocks, term, inv_ref, (r0, r1, r2, r3), source)
+    place_received(blocks, (r0, r1, r2, r3), source)
+    wait(loads)
+    place_own(blocks, term, inv_ref, source)
     coef = [inv_ref[blocks + i : blocks + i + 1, :] for i in range(3)]
     copies = []
     for g in range(blocks):
@@ -226,29 +248,21 @@
     )
 
 
-def take(block, way):
-    count = lax.axis_size("dom")
-    return lax.ppermute(block, "dom", [(i, (i - OFFSETS[way]) % count) for i in range(count)])
+def swap(block, index):
+    return lax.ppermute(block, "dom", partners(index, lax.axis_size("dom")))
 
 
 def exchange(field):
     return lax.all_to_all(field, "tm", split_axis=0, concat_axis=0, tiled=True)
 
 
-def begin(packs, first):
-    ways = len(packs)
-    ahead = [(first + i) % ways for i in range(ways // 2)]
-    behind = [(first + ways // 2 + i) % ways for i in range(ways // 2)]
-    got = {way: take(packs[way], way) for way in ahead}
+def begin(packs):
+    near = [swap(packs[i], i) for i in range(2)]
 
     def finish(field):
-        field, *rest = lax.optimization_barrier(
-            (field, *(got[way] for way in ahead), *(packs[way] for way in behind))
-        )
+        field, *rest = lax.optimization_barrier((field, *near, *packs[2:]))
         field = exchange(field)
-        got.update(zip(ahead, rest[: len(ahead)]))
-        got.update((way, take(block, way)) for way, block in zip(behind, rest[len(ahead) :]))
-        return field, [got[way] for way in range(ways)]
+        return field, rest[:2] + [swap(block, 2 + i) for i, block in enumerate(rest[2:])]
 
     return finish
 
@@ -322,10 +336,10 @@
         [vm((rows, n_loc), BF16), held, DMA((ways,)), DMA],
         flops=work // 8,
     )
-    received = [take(block, way) for way, block in enumerate(packs)]
+    received = [swap(block, i) for i, block in enumerate(packs)]
     term, packs = one(xs, received, inv, True)
 
-    finish = begin(packs, ways // 2)
+    finish = begin(packs)
     early, mix = call(
         functools.partial(first_temporal, t_loc),
         [(field, HBM), (array(time, time), HBM)],
@@ -336,13 +350,12 @@
     early, received = finish(early)
 
     packs = call(scale, packed, [(early, VMEM), (inv, VMEM), (send_list, SMEM)], [held, DMA((ways,))])
-    term, *packs = lax.optimization_barrier((term, *packs))
-    finish = begin(packs, 0)
+    finish = begin(packs)
     late = two(xs, received, inv, term, field, True)
     late, received = finish(late)
     term, packs = one(early, received, inv, False)
 
-    finish = begin(packs, ways // 2)
+    finish = begin(packs)
     (late,) = call(
         functools.partial(second_temporal, t_loc), [(field, HBM)], [(late, VMEM), (mix, HBM)], mixer, flops=mixing
     )

time: 156 us -> 157 us (level)
  starting transfers between devices: 88.2 us -> 93.7 us
  waiting for transfers between devices: 36.1 us -> 31.1 us
    ppermute x16, starting transfers between devices: 52.9 us -> 59.7 us  [swap(): return lax.ppermute(block, 'dom', partners(index, lax.axis_size('dom')))]
    ppermute x16, waiting for transfers between devices: 20.3 us -> 16.9 us  [swap(): return lax.ppermute(block, 'dom', partners(index, lax.axis_size('dom')))]
  transfers between devices with their start and end apart: 20 -> 20, of which waited for: 11 -> 9; matrix products, arithmetic and copies ran while one was open for 0% -> 0% of each run, Pallas kernels for 16% -> 16%
where the time goes in v6:
time: 157 us; the launch traced here: 156 us
  starting transfers between devices  93.7 us (60%)
  waiting for transfers between devices  31.1 us (20%)
  Pallas kernels  28.7 us (18%)
  local copies, waits for them, and re-layouts  1.71 us (1%)
    ppermute x16, starting transfers between devices, swap(): return lax.ppermute(block, 'dom', partners(index, lax.axis_size('dom')))  59.7 us
    all_to_all x4, starting transfers between devices, exchange(): return lax.all_to_all(field, 'tm', split_axis=0, concat_axis=0, tiled=True)  34 us
    pallas_call x10, Pallas kernels, call(): pl.pallas_call(kernel, out_shape=shapes, in_specs=specs, out_specs=result...  28.7 us
    ppermute x16, waiting for transfers between devices, swap(): return lax.ppermute(block, 'dom', partners(index, lax.axis_size('dom')))  16.9 us
    all_to_all x4, waiting for transfers between devices, exchange(): return lax.all_to_all(field, 'tm', split_axis=0, concat_axis=0, tiled=True)  14.2 us
  transfers between devices with their start and end apart: 20, of which 9 were waited for; matrix products, arithmetic and copies ran while one was open for 0% of the time, Pallas kernels for 16%

profile of v6, /device:TPU:1, one launch (start us, length us, event | category | flops | bytes accessed | tf_op | source)
XLA Modules:
  0.0 155.6 jit_solution(14962843500088896705)
XLA Ops:
  0.0 0.0 copy-start.5
  0.0 0.0 copy-start
  0.0 2.4 %shard_map.64 = bf16[16,256,128]{2,1,0:T(8,128)(2,1)} custom-call(bf16[256,2048]{1,0:T(8,128)(2,1)} %bitcast.2, bf16[32,512]{1,0:T(8,128)(2,1)} %kernel_ref.1), custom_call_target="tpu_custom_call" | custom-call | bytes 2129920 | tf_op jit(solution)/shard_map/pallas_call | solution.py:26
  2.4 0.0 copy-start.4
  2.4 10.9 %all-to-all-start = ((bf16[16,256,128]{2,1,0:T(8,128)(2,1)}), bf16[16,256,128]{2,1,0:T(8,128)(2,1)}, u32[]{:S(2)}, u32[]{:S(2)}) async-start(bf16[16,256,128]{2,1,0:T(8,128)(2,1)} %shard_map.64), calls=%async_computation | async-start | bytes 2097152 | tf_op jit(solution)/shard_map/all_to_all | solution.py:256
  13.4 0.0 copy-done.5
  13.4 0.1 copy.8.send_ref
  13.5 0.0 copy-done
  13.5 0.0 copy-done.3
  13.5 2.9 %shard_map.66 = (f32[24,128]{1,0:T(8,128)S(1)}, bf16[3,128,128]{2,1,0:T(8,128)(2,1)}, bf16[3,128,128]{2,1,0:T(8,128)(2,1)}, bf16[3,128,128]{2,1,0:T(8,128)(2,1)}, bf16[3,128,128]{2,1,0:T(8,128)(2,1)}) custom-call(bf16[256,2048]{1,0:T(8,128)(2,1)} %bitcast.3, bf16[16,5,128,128]{3,2,1,0:T(8,128)(2,1)S(1)} %copy-done, s32[1,4,3]{2,1,0:T(4,128)S(1)} %copy.8.send_ref, ...), custom_call_target="tpu_custom_call" | custom-call | flops 41943040 | bytes 4075580 | tf_op jit(solution)/shard_map/pallas_call | solution.py:26
  16.4 1.9 %collective-permute-start = (bf16[3,128,128]{2,1,0:T(8,128)(2,1)}, bf16[3,128,128]{2,1,0:T(8,128)(2,1)S(1)}, u32[]{:S(2)}, u32[]{:S(2)}) collective-permute-start(bf16[3,128,128]{2,1,0:T(8,128)(2,1)} %get-tuple-element.42), channel_id=1, source_target_pairs={{0,16},{16,0},{32,48},{48,32},{64,80},{80,64},{96,112},{112,96},{1... | collective-permute-start | bytes 294920 | tf_op jit(solution)/shard_map/ppermute | solution.py:252
  18.3 11.1 %collective-permute-start.1 = (bf16[3,128,128]{2,1,0:T(8,128)(2,1)}, bf16[3,128,128]{2,1,0:T(8,128)(2,1)S(1)}, u32[]{:S(2)}, u32[]{:S(2)}) collective-permute-start(bf16[3,128,128]{2,1,0:T(8,128)(2,1)} %get-tuple-element.43), channel_id=1, source_target_pairs={{0,496},{16,32},{32,16},{48,64},{64,48},{80,96},{96,80},{112,128},... | collective-permute-start | bytes 294920 | tf_op jit(solution)/shard_map/ppermute | solution.py:252
  29.4 1.9 %collective-permute-start.2 = (bf16[3,128,128]{2,1,0:T(8,128)(2,1)}, bf16[3,128,128]{2,1,0:T(8,128)(2,1)S(1)}, u32[]{:S(2)}, u32[]{:S(2)}) collective-permute-start(bf16[3,128,128]{2,1,0:T(8,128)(2,1)} %get-tuple-element.44), channel_id=1, source_target_pairs={{0,32},{16,48},{32,0},{48,16},{64,96},{80,112},{96,64},{112,80},{1... | collective-permute-start | bytes 294920 | tf_op jit(solution)/shard_map/ppermute | solution.py:252
  31.3 4.9 %collective-permute-start.3 = (bf16[3,128,128]{2,1,0:T(8,128)(2,1)}, bf16[3,128,128]{2,1,0:T(8,128)(2,1)S(1)}, u32[]{:S(2)}, u32[]{:S(2)}) collective-permute-start(bf16[3,128,128]{2,1,0:T(8,128)(2,1)} %get-tuple-element.45), channel_id=1, source_target_pairs={{0,480},{16,496},{32,64},{48,80},{64,32},{80,48},{96,128},{112,144... | collective-permute-start | bytes 294920 | tf_op jit(solution)/shard_map/ppermute | solution.py:252
  36.2 0.0 copy-done.4
  36.2 0.1 copy.9.col_ref
  36.3 0.0 collective-permute-done.r0
  36.3 0.0 collective-permute-done.1.r1
  36.3 0.2 collective-permute-done.2.r2
  36.5 4.0 %collective-permute-done.3.r3 = bf16[3,128,128]{2,1,0:T(8,128)(2,1)S(1)} collective-permute-done((bf16[3,128,128]{2,1,0:T(8,128)(2,1)}, bf16[3,128,128]{2,1,0:T(8,128)(2,1)S(1)}, u32[]{:S(2)}, u32[]{:S(2)}) %collective-permute-start.3) | collective-permute-done | bytes 98336 | tf_op jit(solution)/shard_map/ppermute | solution.py:252
  40.5 3.8 %shard_map.67 = (bf16[16,128,128]{2,1,0:T(8,128)(2,1)}, bf16[3,128,128]{2,1,0:T(8,128)(2,1)}, bf16[3,128,128]{2,1,0:T(8,128)(2,1)}, bf16[3,128,128]{2,1,0:T(8,128)(2,1)}, bf16[3,128,128]{2,1,0:T(8,128)(2,1)}) custom-call(bf16[256,2048]{1,0:T(8,128)(2,1)} %bitcast.4, bf16[3,128,128]{2,1,0:T(8,128)(2,1)S(1)} %collective-permute-done.r0, ...), custom_call_target="tpu_custom_call" | custom-call | flops 335544320 | bytes 4993392 | tf_op jit(solution)/shard_map/pallas_call | solution.py:26
  44.3 1.9 %collective-permute-start.4 = (bf16[3,128,128]{2,1,0:T(8,128)(2,1)}, bf16[3,128,128]{2,1,0:T(8,128)(2,1)S(1)}, u32[]{:S(2)}, u32[]{:S(2)}) collective-permute-start(bf16[3,128,128]{2,1,0:T(8,128)(2,1)} %get-tuple-element.47), channel_id=1, source_target_pairs={{0,16},{16,0},{32,48},{48,32},{64,80},{80,64},{96,112},{112,96},{1... | collective-permute-start | bytes 294920 | tf_op jit(solution)/shard_map/ppermute | solution.py:252
  46.2 5.1 %collective-permute-start.5 = (bf16[3,128,128]{2,1,0:T(8,128)(2,1)}, bf16[3,128,128]{2,1,0:T(8,128)(2,1)S(1)}, u32[]{:S(2)}, u32[]{:S(2)}) collective-permute-start(bf16[3,128,128]{2,1,0:T(8,128)(2,1)} %get-tuple-element.48), channel_id=1, source_target_pairs={{0,496},{16,32},{32,16},{48,64},{64,48},{80,96},{96,80},{112,128},... | collective-permute-start | bytes 294920 | tf_op jit(solution)/shard_map/ppermute | solution.py:252
  51.3 0.0 all-to-all-done.field_ref
  51.4 2.6 %shard_map.65 = (bf16[16,128,128]{2,1,0:T(8,128)(2,1)}, bf16[512,512]{1,0:T(8,128)(2,1)}) custom-call(bf16[16,256,128]{2,1,0:T(8,128)(2,1)} %all-to-all-done.field_ref), custom_call_target="tpu_custom_call" | custom-call | flops 268435456 | bytes 2097152 | tf_op jit(solution)/shard_map/pallas_call | solution.py:26
  53.9 0.0 collective-permute-done.4.r0
  53.9 1.2 collective-permute-done.5.r1
  55.1 10.1 %all-to-all-start.1 = ((bf16[16,128,128]{2,1,0:T(8,128)(2,1)}), bf16[16,128,128]{2,1,0:T(8,128)(2,1)S(1)}, u32[]{:S(2)}, u32[]{:S(2)}) async-start(bf16[16,128,128]{2,1,0:T(8,128)(2,1)} %get-tuple-element.51), calls=%async_computation.1 | async-start | bytes 1048576 | tf_op jit(solution)/shard_map/all_to_all | solution.py:256
  65.2 1.9 %collective-permute-start.6 = (bf16[3,128,128]{2,1,0:T(8,128)(2,1)}, bf16[3,128,128]{2,1,0:T(8,128)(2,1)}, u32[]{:S(2)}, u32[]{:S(2)}) collective-permute-start(bf16[3,128,128]{2,1,0:T(8,128)(2,1)} %get-tuple-element.54), channel_id=1, source_target_pairs={{0,32},{16,48},{32,0},{48,16},{64,96},{80,112},{96,64},{112,80},{1... | collective-permute-start | bytes 294920 | tf_op jit(solution)/shard_map/ppermute | solution.py:252
  67.1 3.3 %collective-permute-start.7 = (bf16[3,128,128]{2,1,0:T(8,128)(2,1)}, bf16[3,128,128]{2,1,0:T(8,128)(2,1)}, u32[]{:S(2)}, u32[]{:S(2)}) collective-permute-start(bf16[3,128,128]{2,1,0:T(8,128)(2,1)} %get-tuple-element.55), channel_id=1, source_target_pairs={{0,480},{16,496},{32,64},{48,80},{64,32},{80,48},{96,128},{112,144... | collective-permute-start | bytes 294920 | tf_op jit(solution)/shard_map/ppermute | solution.py:252
  70.4 12.1 %all-to-all-done.1.field_ref = bf16[16,128,128]{2,1,0:T(8,128)(2,1)S(1)} async-done(((bf16[16,128,128]{2,1,0:T(8,128)(2,1)}), bf16[16,128,128]{2,1,0:T(8,128)(2,1)S(1)}, u32[]{:S(2)}, u32[]{:S(2)}) %all-to-all-start.1) | async-done | bytes 524320 | tf_op jit(solution)/shard_map/all_to_all | solution.py:256
  82.5 1.4 shard_map.69
  83.9 1.9 %collective-permute-start.8 = (bf16[3,128,128]{2,1,0:T(8,128)(2,1)}, bf16[3,128,128]{2,1,0:T(8,128)(2,1)S(1)}, u32[]{:S(2)}, u32[]{:S(2)}) collective-permute-start(bf16[3,128,128]{2,1,0:T(8,128)(2,1)} %get-tuple-element.57), channel_id=1, source_target_pairs={{0,16},{16,0},{32,48},{48,32},{64,80},{80,64},{96,112},{112,96},{1... | collective-permute-start | bytes 294920 | tf_op jit(solution)/shard_map/ppermute | solution.py:252
  85.8 5.7 %collective-permute-start.9 = (bf16[3,128,128]{2,1,0:T(8,128)(2,1)}, bf16[3,128,128]{2,1,0:T(8,128)(2,1)S(1)}, u32[]{:S(2)}, u32[]{:S(2)}) collective-permute-start(bf16[3,128,128]{2,1,0:T(8,128)(2,1)} %get-tuple-element.58), channel_id=1, source_target_pairs={{0,496},{16,32},{32,16},{48,64},{64,48},{80,96},{96,80},{112,128},... | collective-permute-start | bytes 294920 | tf_op jit(solution)/shard_map/ppermute | solution.py:252
  91.5 0.0 collective-permute-done.6.r2
  91.5 0.0 collective-permute-done.7.r3
  91.6 4.0 %shard_map.68 = bf16[16,128,128]{2,1,0:T(8,128)(2,1)} custom-call(bf16[256,2048]{1,0:T(8,128)(2,1)} %bitcast.5, bf16[3,128,128]{2,1,0:T(8,128)(2,1)S(1)} %collective-permute-done.4.r0, bf16[3,128,128]{2,1,0:T(8,128)(2,1)S(1)} %collective-permute-done.5.r1, bf16[3,128,128]{2,1,0:T(8,128)(2,1)} %collective-permute-done.6.r2, ...), custom_call_target="tpu_custom_call" | custom-call | flops 335544320 | bytes 5124416 | tf_op jit(solution)/shard_map/pallas_call | solution.py:26
  95.6 0.0 collective-permute-done.8.r0
  95.6 0.0 collective-permute-done.9.r1
  95.6 0.0 copy-start.1
  95.6 0.6 copy-done.1
  96.2 4.1 %all-to-all-start.2 = ((bf16[16,128,128]{2,1,0:T(8,128)(2,1)}), bf16[16,128,128]{2,1,0:T(8,128)(2,1)}, u32[]{:S(2)}, u32[]{:S(2)}) async-start(bf16[16,128,128]{2,1,0:T(8,128)(2,1)} %shard_map.68), calls=%async_computation.2 | async-start | bytes 1048576 | tf_op jit(solution)/shard_map/all_to_all | solution.py:256
  100.4 1.9 %collective-permute-start.10 = (bf16[3,128,128]{2,1,0:T(8,128)(2,1)}, bf16[3,128,128]{2,1,0:T(8,128)(2,1)S(1)}, u32[]{:S(2)}, u32[]{:S(2)}) collective-permute-start(bf16[3,128,128]{2,1,0:T(8,128)(2,1)} %get-tuple-element.65), channel_id=1, source_target_pairs={{0,32},{16,48},{32,0},{48,16},{64,96},{80,112},{96,64},{112,80},{1... | collective-permute-start | bytes 294920 | tf_op jit(solution)/shard_map/ppermute | solution.py:252
  102.3 3.4 %collective-permute-start.11 = (bf16[3,128,128]{2,1,0:T(8,128)(2,1)}, bf16[3,128,128]{2,1,0:T(8,128)(2,1)S(1)}, u32[]{:S(2)}, u32[]{:S(2)}) collective-permute-start(bf16[3,128,128]{2,1,0:T(8,128)(2,1)} %get-tuple-element.66), channel_id=1, source_target_pairs={{0,480},{16,496},{32,64},{48,80},{64,32},{80,48},{96,128},{112,144... | collective-permute-start | bytes 294920 | tf_op jit(solution)/shard_map/ppermute | solution.py:252
  105.7 3.2 %collective-permute-done.10.r2 = bf16[3,128,128]{2,1,0:T(8,128)(2,1)S(1)} collective-permute-done((bf16[3,128,128]{2,1,0:T(8,128)(2,1)}, bf16[3,128,128]{2,1,0:T(8,128)(2,1)S(1)}, u32[]{:S(2)}, u32[]{:S(2)}) %collective-permute-start.10) | collective-permute-done | bytes 98336 | tf_op jit(solution)/shard_map/ppermute | solution.py:252
  108.9 3.9 %collective-permute-done.11.r3 = bf16[3,128,128]{2,1,0:T(8,128)(2,1)S(1)} collective-permute-done((bf16[3,128,128]{2,1,0:T(8,128)(2,1)}, bf16[3,128,128]{2,1,0:T(8,128)(2,1)S(1)}, u32[]{:S(2)}, u32[]{:S(2)}) %collective-permute-start.11) | collective-permute-done | bytes 98336 | tf_op jit(solution)/shard_map/ppermute | solution.py:252
  112.8 0.9 copy-done.2
  113.7 2.8 %shard_map.71 = (bf16[16,128,128]{2,1,0:T(8,128)(2,1)}, bf16[3,128,128]{2,1,0:T(8,128)(2,1)}, bf16[3,128,128]{2,1,0:T(8,128)(2,1)}, bf16[3,128,128]{2,1,0:T(8,128)(2,1)}, bf16[3,128,128]{2,1,0:T(8,128)(2,1)}) custom-call(bf16[16,128,128]{2,1,0:T(8,128)(2,1)S(1)} %all-to-all-done.1.field_ref, bf16[3,128,128]{2,1,0:T(8,128)(2,1)S(1)} %collective-permute-done.8.r0, ...), custom_call_target="tpu_custom_call" | custom-call | flops 335544320 | bytes 4469104 | tf_op jit(solution)/shard_map/pallas_call | solution.py:26
  116.5 0.0 copy-start.6
  116.5 2.1 %collective-permute-start.12 = (bf16[3,128,128]{2,1,0:T(8,128)(2,1)}, bf16[3,128,128]{2,1,0:T(8,128)(2,1)S(1)}, u32[]{:S(2)}, u32[]{:S(2)}) collective-permute-start(bf16[3,128,128]{2,1,0:T(8,128)(2,1)} %get-tuple-element.67), channel_id=1, source_target_pairs={{0,16},{16,0},{32,48},{48,32},{64,80},{80,64},{96,112},{112,96},{1... | collective-permute-start | bytes 294920 | tf_op jit(solution)/shard_map/ppermute | solution.py:252
  118.5 4.7 %collective-permute-start.13 = (bf16[3,128,128]{2,1,0:T(8,128)(2,1)}, bf16[3,128,128]{2,1,0:T(8,128)(2,1)S(1)}, u32[]{:S(2)}, u32[]{:S(2)}) collective-permute-start(bf16[3,128,128]{2,1,0:T(8,128)(2,1)} %get-tuple-element.68), channel_id=1, source_target_pairs={{0,496},{16,32},{32,16},{48,64},{64,48},{80,96},{96,80},{112,128},... | collective-permute-start | bytes 294920 | tf_op jit(solution)/shard_map/ppermute | solution.py:252
  123.3 0.0 all-to-all-done.2.field_ref
  123.3 3.4 %shard_map.70 = bf16[16,128,128]{2,1,0:T(8,128)(2,1)} custom-call(bf16[16,128,128]{2,1,0:T(8,128)(2,1)} %all-to-all-done.2.field_ref, bf16[512,512]{1,0:T(8,128)(2,1)} %get-tuple-element.62.mix_ref), custom_call_target="tpu_custom_call" | custom-call | flops 268435456 | bytes 1572864 | tf_op jit(solution)/shard_map/pallas_call | solution.py:26
  126.7 0.0 collective-permute-done.12.r0
  126.7 0.7 collective-permute-done.13.r1
  127.4 8.8 %all-to-all-start.3 = ((bf16[16,128,128]{2,1,0:T(8,128)(2,1)}), bf16[16,128,128]{2,1,0:T(8,128)(2,1)}, u32[]{:S(2)}, u32[]{:S(2)}) async-start(bf16[16,128,128]{2,1,0:T(8,128)(2,1)} %shard_map.70), calls=%async_computation.3 | async-start | bytes 1048576 | tf_op jit(solution)/shard_map/all_to_all | solution.py:256
  136.2 1.9 %collective-permute-start.14 = (bf16[3,128,128]{2,1,0:T(8,128)(2,1)}, bf16[3,128,128]{2,1,0:T(8,128)(2,1)S(1)}, u32[]{:S(2)}, u32[]{:S(2)}) collective-permute-start(bf16[3,128,128]{2,1,0:T(8,128)(2,1)} %get-tuple-element.73), channel_id=1, source_target_pairs={{0,32},{16,48},{32,0},{48,16},{64,96},{80,112},{96,64},{112,80},{1... | collective-permute-start | bytes 294920 | tf_op jit(solution)/shard_map/ppermute | solution.py:252
  138.1 0.0 copy-done.6
  138.1 6.1 %collective-permute-start.15 = (bf16[3,128,128]{2,1,0:T(8,128)(2,1)S(1)}, bf16[3,128,128]{2,1,0:T(8,128)(2,1)S(1)}, u32[]{:S(2)}, u32[]{:S(2)}) collective-permute-start(bf16[3,128,128]{2,1,0:T(8,128)(2,1)S(1)} %copy-done.6), channel_id=1, source_target_pairs={{0,480},{16,496},{32,64},{48,80},{64,32},{80,48},{96,128},{112,144... | collective-permute-start | bytes 294920 | tf_op jit(solution)/shard_map/ppermute | solution.py:252
  144.2 0.0 collective-permute-done.14.r2
  144.2 3.7 %collective-permute-done.15.r3 = bf16[3,128,128]{2,1,0:T(8,128)(2,1)S(1)} collective-permute-done((bf16[3,128,128]{2,1,0:T(8,128)(2,1)S(1)}, bf16[3,128,128]{2,1,0:T(8,128)(2,1)S(1)}, u32[]{:S(2)}, u32[]{:S(2)}) %collective-permute-start.15) | collective-permute-done | bytes 98336 | tf_op jit(solution)/shard_map/ppermute | solution.py:252
  147.9 3.6 %shard_map.72._ = bf16[256,2048]{1,0:T(8,128)(2,1)} custom-call(bf16[16,128,128]{2,1,0:T(8,128)(2,1)S(1)} %all-to-all-done.1.field_ref, bf16[3,128,128]{2,1,0:T(8,128)(2,1)S(1)} %collective-permute-done.12.r0, bf16[3,128,128]{2,1,0:T(8,128)(2,1)S(1)} %collective-permute-done.13.r1, bf16[3,128,128]{2,1,0:T(8,128)(2,1)S(1)} %collective-permute-done.14.r2, ...), custom_call_target="tpu_custom_call" | custom-call | flops 335544320 | bytes 5124416 | tf_op jit(solution)/shard_map/pallas_call | solution.py:26
  151.5 2.1 %all-to-all-done.3.field_ref = bf16[16,128,128]{2,1,0:T(8,128)(2,1)} async-done(((bf16[16,128,128]{2,1,0:T(8,128)(2,1)}), bf16[16,128,128]{2,1,0:T(8,128)(2,1)}, u32[]{:S(2)}, u32[]{:S(2)}) %all-to-all-start.3) | async-done | bytes 524320 | tf_op jit(solution)/shard_map/all_to_all | solution.py:256
  153.6 2.0 %shard_map.73 = bf16[256,2048]{1,0:T(8,128)(2,1)} custom-call(bf16[256,2048]{1,0:T(8,128)(2,1)} %shard_map.72._, bf16[16,128,128]{2,1,0:T(8,128)(2,1)} %all-to-all-done.3.field_ref), custom_call_target="tpu_custom_call", output_to_operand_aliasing={{}: (0, {})} | custom-call | bytes 2621440 | tf_op jit(solution)/shard_map/pallas_call | solution.py:26
  (2 shorter events, 0.0 us)
Async XLA Ops:
  0.0 13.4 %copy-start.5 = (s32[1,4,3]{1,0,2:T(1,128)S(1)}, s32[1,4,3]{1,0,2:T(1,128)}, u32[]{:S(2)}) copy-start(s32[1,4,3]{1,0,2:T(1,128)} %param.8) | copy-start | bytes 148
  0.0 13.5 %copy-start = (bf16[16,5,128,128]{3,2,1,0:T(8,128)(2,1)S(1)}, bf16[16,5,128,128]{3,2,1,0:T(8,128)(2,1)}, u32[]{:S(2)}) copy-start(bf16[16,5,128,128]{3,2,1,0:T(8,128)(2,1)} %weights_ref.9) | copy-start | bytes 7864324
  0.0 13.5 %copy-start.3 = (f32[3]{0:T(128)S(1)}, f32[3]{0:T(128)}, u32[]{:S(2)}) copy-start(f32[3]{0:T(128)} %coef_ref.1) | copy-start | bytes 40
  2.4 33.8 %copy-start.4 = (s32[16,5]{0,1:T(8,128)S(1)}, s32[16,5]{0,1:T(8,128)}, u32[]{:S(2)}) copy-start(s32[16,5]{0,1:T(8,128)} %param.9) | copy-start | bytes 964
  2.4 48.9 %all-to-all-start = ((bf16[16,256,128]{2,1,0:T(8,128)(2,1)}), bf16[16,256,128]{2,1,0:T(8,128)(2,1)}, u32[]{:S(2)}, u32[]{:S(2)}) async-start(bf16[16,256,128]{2,1,0:T(8,128)(2,1)} %shard_map.64), calls=%async_computation | async-start | bytes 2097152 | tf_op jit(solution)/shard_map/all_to_all | solution.py:256
  16.4 19.9 %collective-permute-start = (bf16[3,128,128]{2,1,0:T(8,128)(2,1)}, bf16[3,128,128]{2,1,0:T(8,128)(2,1)S(1)}, u32[]{:S(2)}, u32[]{:S(2)}) collective-permute-start(bf16[3,128,128]{2,1,0:T(8,128)(2,1)} %get-tuple-element.42), channel_id=1, source_target_pairs={{0,16},{16,0},{32,48},{48,32},{64,80},{80,64},{96,112},{112,96},{1... | collective-permute-start | bytes 294920 | tf_op jit(solution)/shard_map/ppermute | solution.py:252
  18.3 18.0 %collective-permute-start.1 = (bf16[3,128,128]{2,1,0:T(8,128)(2,1)}, bf16[3,128,128]{2,1,0:T(8,128)(2,1)S(1)}, u32[]{:S(2)}, u32[]{:S(2)}) collective-permute-start(bf16[3,128,128]{2,1,0:T(8,128)(2,1)} %get-tuple-element.43), channel_id=1, source_target_pairs={{0,496},{16,32},{32,16},{48,64},{64,48},{80,96},{96,80},{112,128},... | collective-permute-start | bytes 294920 | tf_op jit(solution)/shard_map/ppermute | solution.py:252
  29.4 7.1 %collective-permute-start.2 = (bf16[3,128,128]{2,1,0:T(8,128)(2,1)}, bf16[3,128,128]{2,1,0:T(8,128)(2,1)S(1)}, u32[]{:S(2)}, u32[]{:S(2)}) collective-permute-start(bf16[3,128,128]{2,1,0:T(8,128)(2,1)} %get-tuple-element.44), channel_id=1, source_target_pairs={{0,32},{16,48},{32,0},{48,16},{64,96},{80,112},{96,64},{112,80},{1... | collective-permute-start | bytes 294920 | tf_op jit(solution)/shard_map/ppermute | solution.py:252
  31.3 9.2 %collective-permute-start.3 = (bf16[3,128,128]{2,1,0:T(8,128)(2,1)}, bf16[3,128,128]{2,1,0:T(8,128)(2,1)S(1)}, u32[]{:S(2)}, u32[]{:S(2)}) collective-permute-start(bf16[3,128,128]{2,1,0:T(8,128)(2,1)} %get-tuple-element.45), channel_id=1, source_target_pairs={{0,480},{16,496},{32,64},{48,80},{64,32},{80,48},{96,128},{112,144... | collective-permute-start | bytes 294920 | tf_op jit(solution)/shard_map/ppermute | solution.py:252
  44.3 9.6 %collective-permute-start.4 = (bf16[3,128,128]{2,1,0:T(8,128)(2,1)}, bf16[3,128,128]{2,1,0:T(8,128)(2,1)S(1)}, u32[]{:S(2)}, u32[]{:S(2)}) collective-permute-start(bf16[3,128,128]{2,1,0:T(8,128)(2,1)} %get-tuple-element.47), channel_id=1, source_target_pairs={{0,16},{16,0},{32,48},{48,32},{64,80},{80,64},{96,112},{112,96},{1... | collective-permute-start | bytes 294920 | tf_op jit(solution)/shard_map/ppermute | solution.py:252
  46.2 8.9 %collective-permute-start.5 = (bf16[3,128,128]{2,1,0:T(8,128)(2,1)}, bf16[3,128,128]{2,1,0:T(8,128)(2,1)S(1)}, u32[]{:S(2)}, u32[]{:S(2)}) collective-permute-start(bf16[3,128,128]{2,1,0:T(8,128)(2,1)} %get-tuple-element.48), channel_id=1, source_target_pairs={{0,496},{16,32},{32,16},{48,64},{64,48},{80,96},{96,80},{112,128},... | collective-permute-start | bytes 294920 | tf_op jit(solution)/shard_map/ppermute | solution.py:252
  55.1 27.4 %all-to-all-start.1 = ((bf16[16,128,128]{2,1,0:T(8,128)(2,1)}), bf16[16,128,128]{2,1,0:T(8,128)(2,1)S(1)}, u32[]{:S(2)}, u32[]{:S(2)}) async-start(bf16[16,128,128]{2,1,0:T(8,128)(2,1)} %get-tuple-element.51), calls=%async_computation.1 | async-start | bytes 1048576 | tf_op jit(solution)/shard_map/all_to_all | solution.py:256
  65.2 26.3 %collective-permute-start.6 = (bf16[3,128,128]{2,1,0:T(8,128)(2,1)}, bf16[3,128,128]{2,1,0:T(8,128)(2,1)}, u32[]{:S(2)}, u32[]{:S(2)}) collective-permute-start(bf16[3,128,128]{2,1,0:T(8,128)(2,1)} %get-tuple-element.54), channel_id=1, source_target_pairs={{0,32},{16,48},{32,0},{48,16},{64,96},{80,112},{96,64},{112,80},{1... | collective-permute-start | bytes 294920 | tf_op jit(solution)/shard_map/ppermute | solution.py:252
  67.1 24.4 %collective-permute-start.7 = (bf16[3,128,128]{2,1,0:T(8,128)(2,1)}, bf16[3,128,128]{2,1,0:T(8,128)(2,1)}, u32[]{:S(2)}, u32[]{:S(2)}) collective-permute-start(bf16[3,128,128]{2,1,0:T(8,128)(2,1)} %get-tuple-element.55), channel_id=1, source_target_pairs={{0,480},{16,496},{32,64},{48,80},{64,32},{80,48},{96,128},{112,144... | collective-permute-start | bytes 294920 | tf_op jit(solution)/shard_map/ppermute | solution.py:252
  83.9 11.7 %collective-permute-start.8 = (bf16[3,128,128]{2,1,0:T(8,128)(2,1)}, bf16[3,128,128]{2,1,0:T(8,128)(2,1)S(1)}, u32[]{:S(2)}, u32[]{:S(2)}) collective-permute-start(bf16[3,128,128]{2,1,0:T(8,128)(2,1)} %get-tuple-element.57), channel_id=1, source_target_pairs={{0,16},{16,0},{32,48},{48,32},{64,80},{80,64},{96,112},{112,96},{1... | collective-permute-start | bytes 294920 | tf_op jit(solution)/shard_map/ppermute | solution.py:252
  85.8 9.8 %collective-permute-start.9 = (bf16[3,128,128]{2,1,0:T(8,128)(2,1)}, bf16[3,128,128]{2,1,0:T(8,128)(2,1)S(1)}, u32[]{:S(2)}, u32[]{:S(2)}) collective-permute-start(bf16[3,128,128]{2,1,0:T(8,128)(2,1)} %get-tuple-element.58), channel_id=1, source_target_pairs={{0,496},{16,32},{32,16},{48,64},{64,48},{80,96},{96,80},{112,128},... | collective-permute-start | bytes 294920 | tf_op jit(solution)/shard_map/ppermute | solution.py:252
  95.6 0.6 copy-start.1
  96.2 27.0 %all-to-all-start.2 = ((bf16[16,128,128]{2,1,0:T(8,128)(2,1)}), bf16[16,128,128]{2,1,0:T(8,128)(2,1)}, u32[]{:S(2)}, u32[]{:S(2)}) async-start(bf16[16,128,128]{2,1,0:T(8,128)(2,1)} %shard_map.68), calls=%async_computation.2 | async-start | bytes 1048576 | tf_op jit(solution)/shard_map/all_to_all | solution.py:256
  100.4 8.5 %collective-permute-start.10 = (bf16[3,128,128]{2,1,0:T(8,128)(2,1)}, bf16[3,128,128]{2,1,0:T(8,128)(2,1)S(1)}, u32[]{:S(2)}, u32[]{:S(2)}) collective-permute-start(bf16[3,128,128]{2,1,0:T(8,128)(2,1)} %get-tuple-element.65), channel_id=1, source_target_pairs={{0,32},{16,48},{32,0},{48,16},{64,96},{80,112},{96,64},{112,80},{1... | collective-permute-start | bytes 294920 | tf_op jit(solution)/shard_map/ppermute | solution.py:252
  102.3 10.5 %collective-permute-start.11 = (bf16[3,128,128]{2,1,0:T(8,128)(2,1)}, bf16[3,128,128]{2,1,0:T(8,128)(2,1)S(1)}, u32[]{:S(2)}, u32[]{:S(2)}) collective-permute-start(bf16[3,128,128]{2,1,0:T(8,128)(2,1)} %get-tuple-element.66), channel_id=1, source_target_pairs={{0,480},{16,496},{32,64},{48,80},{64,32},{80,48},{96,128},{112,144... | collective-permute-start | bytes 294920 | tf_op jit(solution)/shard_map/ppermute | solution.py:252
  112.8 0.9 copy-start.2
  116.5 21.7 %copy-start.6 = (bf16[3,128,128]{2,1,0:T(8,128)(2,1)S(1)}, bf16[3,128,128]{2,1,0:T(8,128)(2,1)}, u32[]{:S(2)}) copy-start(bf16[3,128,128]{2,1,0:T(8,128)(2,1)} %get-tuple-element.74) | copy-start | bytes 294916
  116.5 10.2 %collective-permute-start.12 = (bf16[3,128,128]{2,1,0:T(8,128)(2,1)}, bf16[3,128,128]{2,1,0:T(8,128)(2,1)S(1)}, u32[]{:S(2)}, u32[]{:S(2)}) collective-permute-start(bf16[3,128,128]{2,1,0:T(8,128)(2,1)} %get-tuple-element.67), channel_id=1, source_target_pairs={{0,16},{16,0},{32,48},{48,32},{64,80},{80,64},{96,112},{112,96},{1... | collective-permute-start | bytes 294920 | tf_op jit(solution)/shard_map/ppermute | solution.py:252
  118.5 8.9 %collective-permute-start.13 = (bf16[3,128,128]{2,1,0:T(8,128)(2,1)}, bf16[3,128,128]{2,1,0:T(8,128)(2,1)S(1)}, u32[]{:S(2)}, u32[]{:S(2)}) collective-permute-start(bf16[3,128,128]{2,1,0:T(8,128)(2,1)} %get-tuple-element.68), channel_id=1, source_target_pairs={{0,496},{16,32},{32,16},{48,64},{64,48},{80,96},{96,80},{112,128},... | collective-permute-start | bytes 294920 | tf_op jit(solution)/shard_map/ppermute | solution.py:252
  127.4 26.2 %all-to-all-start.3 = ((bf16[16,128,128]{2,1,0:T(8,128)(2,1)}), bf16[16,128,128]{2,1,0:T(8,128)(2,1)}, u32[]{:S(2)}, u32[]{:S(2)}) async-start(bf16[16,128,128]{2,1,0:T(8,128)(2,1)} %shard_map.70), calls=%async_computation.3 | async-start | bytes 1048576 | tf_op jit(solution)/shard_map/all_to_all | solution.py:256
  136.2 8.0 %collective-permute-start.14 = (bf16[3,128,128]{2,1,0:T(8,128)(2,1)}, bf16[3,128,128]{2,1,0:T(8,128)(2,1)S(1)}, u32[]{:S(2)}, u32[]{:S(2)}) collective-permute-start(bf16[3,128,128]{2,1,0:T(8,128)(2,1)} %get-tuple-element.73), channel_id=1, source_target_pairs={{0,32},{16,48},{32,0},{48,16},{64,96},{80,112},{96,64},{112,80},{1... | collective-permute-start | bytes 294920 | tf_op jit(solution)/shard_map/ppermute | solution.py:252
  138.1 9.8 %collective-permute-start.15 = (bf16[3,128,128]{2,1,0:T(8,128)(2,1)S(1)}, bf16[3,128,128]{2,1,0:T(8,128)(2,1)S(1)}, u32[]{:S(2)}, u32[]{:S(2)}) collective-permute-start(bf16[3,128,128]{2,1,0:T(8,128)(2,1)S(1)} %copy-done.6), channel_id=1, source_target_pairs={{0,480},{16,496},{32,64},{48,80},{64,32},{80,48},{96,128},{112,144... | collective-permute-start | bytes 294920 | tf_op jit(solution)/shard_map/ppermute | solution.py:252

commit v7 on v6

v7 whole, which is shorter than its diff:
```python
import functools

import jax
import jax.numpy as jnp
from jax import lax
from jax.experimental import pallas as pl
from jax.experimental.pallas import tpu as pltpu
from jax.sharding import PartitionSpec as P

REACH = 2
OFFSETS = tuple(range(-REACH, 0)) + tuple(range(1, REACH + 1))
F32, BF16 = jnp.float32, jnp.bfloat16
LIMIT = 24 * 2**20
SMEM = pl.BlockSpec(memory_space=pltpu.SMEM)
VMEM = pl.BlockSpec(memory_space=pltpu.VMEM)
HBM = pl.BlockSpec(memory_space=pltpu.HBM)
DMA = pltpu.SemaphoreType.DMA


def call(kernel, outs, ins, scratch, flops=0, aliases=None):
    arrays, specs = zip(*ins)
    shapes, results = zip(*outs)
    size = sum(a.size * a.dtype.itemsize for a in (*arrays, *shapes))
    arrays = [pltpu.with_memory_space_constraint(a, pltpu.HBM) if spec is HBM else a for a, spec in ins]
    shapes = [pltpu.HBM(a.shape, a.dtype) if spec is HBM else a for a, spec in outs]
    return pl.pallas_call(
        kernel,
        out_shape=shapes,
        in_specs=specs,
        out_specs=results,
        scratch_shapes=scratch,
        compiler_params=pltpu.CompilerParams(vmem_limit_bytes=LIMIT),
        cost_estimate=pl.CostEstimate(flops=flops, bytes_accessed=size, transcendentals=0),
        input_output_aliases=aliases or {},
    )(*arrays)


def array(*shape, dtype=BF16):
    return jax.ShapeDtypeStruct(shape, dtype)


def start(source, target, sem):
    copy = pltpu.make_async_copy(source, target, sem)
    copy.start()
    return copy


def wait(copies):
    for copy in copies:
        copy.wait()


def times_transposed(a, b):
    return lax.dot_general(a, b, (((1,), (1,)), ((), ())), preferred_element_type=F32)


def block_of(ref, g, width):
    if len(ref.shape) == 3:
        return ref[g]
    at = g * width
    return ref[:, pl.ds(at if isinstance(g, int) else pl.multiple_of(at, width), width)]


def scaled_block(ref, inv_ref, g, width):
    return (block_of(ref, g, width).astype(F32) * inv_ref[pl.ds(g, 1), :]).astype(BF16)


def partner_ways():
    place = lax.axis_index("dom")
    return [0, 1, 2, 3]


def partners(index, count):
    return [(i, (i - OFFSETS[index]) % count) for i in range(count)]


def pack(send_ref, field_ref, inv_ref, packs, held, sems):
    width = inv_ref.shape[1]
    copies = []
    ways = partner_ways()
    for i, out in enumerate(packs):
        way = ways[i]
        for slot in range(out.shape[0]):
            held[i, slot] = scaled_block(field_ref, inv_ref, send_ref[0, way, slot], width)
        copies.append(start(held.at[i], out, sems.at[i]))
    return copies


def lay_out(signal_ref, kernel_ref, out_ref, held, mix, in_sems, out_sems, mix_sem):
    owners, chunk, width = out_ref.shape
    t_loc, time = kernel_ref.shape
    rows = chunk - time * t_loc // width
    mixing = start(kernel_ref, mix, mix_sem)
    loads = [
        start(signal_ref.at[:rows, i * width : (i + 1) * width], held.at[i, :rows], in_sems.at[i])
        for i in range(owners)
    ]
    mixing.wait()
    copies = []
    for i in range(owners):
        for q in range(time // width):
            held[i, rows + q * t_loc : rows + (q + 1) * t_loc] = mix[:, q * width : (q + 1) * width]
        loads[i].wait()
        copies.append(start(held.at[i], out_ref.at[i], out_sems.at[i]))
    wait(copies)


def first_scale(signal_ref, weights_ref, send_ref, coef_ref, inv_ref, *rest):
    *packs, field, held, sems, load_sem = rest
    blocks, per_row, width, _ = weights_ref.shape
    rows = field.shape[0]
    load = start(signal_ref.at[rows:], field, load_sem)
    ones = jnp.ones((16, width), BF16)
    for g in range(blocks):
        degree = times_transposed(ones, weights_ref[g, 0])
        for j in range(1, per_row):
            degree += times_transposed(ones, weights_ref[g, j])
        inv_ref[g : g + 1, :] = lax.rsqrt(degree[:1])
    for term in range(coef_ref.shape[0]):
        inv_ref[blocks + term : blocks + term + 1, :] = jnp.full((1, width), coef_ref[term], F32)
    load.wait()
    wait(pack(send_ref, field, inv_ref, packs, held, sems))


def place_received(blocks, received, source):
    for way, ref in zip(partner_ways(), received):
        slots = ref.shape[0]
        for slot in range(slots):
            source[blocks + way * slots + slot] = ref[slot]


def place_own(blocks, field_ref, inv_ref, source):
    for g in range(blocks):
        source[g] = scaled_block(field_ref, inv_ref, g, inv_ref.shape[1])


def block_product(g, col_ref, weights_ref, source):
    per_row = weights_ref.shape[1]
    picked = jnp.concatenate([source[col_ref[g, j]] for j in range(per_row)], axis=1)
    edges = jnp.concatenate([weights_ref[g, j] for j in range(per_row)], axis=1)
    return times_transposed(picked, edges)


def product_one(field, received, weights_ref, inv_ref, col_ref, send_ref, term_ref, packs, scratch, loads):
    source, term, held, sems, pack_sems = scratch
    blocks = weights_ref.shape[0]
    place_received(blocks, received, source)
    wait(loads)
    place_own(blocks, field, inv_ref, source)
    copies = []
    for g in range(blocks):
        total = block_product(g, col_ref, weights_ref, source)
        term[g] = (-inv_ref[g : g + 1, :] * total).astype(BF16)
        copies.append(start(term.at[g], term_ref.at[g], sems.at[g]))
    return copies + pack(send_ref, term, inv_ref, packs, held, pack_sems)


def product_two(field, received, weights_ref, inv_ref, col_ref, term_ref, target, scratch, loads):
    source, term, mixed, sems, term_sem = scratch
    start_term = start(term_ref, term, term_sem)
    blocks, _, width, _ = weights_ref.shape
    place_received(blocks, received, source)
    start_term.wait()
    place_own(blocks, term, inv_ref, source)
    coef = [inv_ref[blocks + i : blocks + i + 1, :] for i in range(3)]
    wait(loads)
    copies = []
    for g in range(blocks):
        total = block_product(g, col_ref, weights_ref, source)
        x = block_of(field, g, width).astype(F32)
        two = (-2.0 * inv_ref[g : g + 1, :] * total - x).astype(BF16).astype(F32)
        one = term[g].astype(F32)
        mixed[g] = (coef[0] * x + coef[1] * one + coef[2] * two).astype(BF16)
        copies.append(start(mixed.at[g], target(g), sems.at[g]))
    return copies


def mix_times(t_loc, mix, field_ref, out_ref, columns, held, sems):
    owners, rows, width = out_ref.shape
    for p in range(rows // t_loc):
        part = slice(p * t_loc, (p + 1) * t_loc)
        for i in range(owners):
            columns[i * t_loc : (i + 1) * t_loc, p * width : (p + 1) * width] = field_ref[i, part]
    step = 2 * width
    pieces = columns.shape[1] // step
    depth = rows // pieces
    copies = []
    for c in range(pieces):
        out = jnp.dot(mix, columns[:, c * step : (c + 1) * step], preferred_element_type=F32).astype(BF16)
        for q in range(step // width):
            at = c * depth + q * t_loc
            for i in range(owners):
                held[i, at : at + t_loc] = out[i * t_loc : (i + 1) * t_loc, q * width : (q + 1) * width]
        part = slice(c * depth, (c + 1) * depth)
        copies.append(start(held.at[:, part], out_ref.at[:, part], sems.at[c]))
    return copies


def rear_one(t_loc, signal_ref, r0, r1, r2, r3, weights_ref, inv_ref, col_ref, send_ref, arrived_ref, term_ref, *rest):
    *packs, out_ref, mix_ref = rest[: len(OFFSETS) + 2]
    *scratch, field, columns, mixed, mix, arrived, load_sems, out_sems = rest[len(OFFSETS) + 2 :]
    owners, rows, width = out_ref.shape
    load = start(signal_ref.at[rows:], field, load_sems.at[0])
    loads = [start(arrived_ref.at[i], arrived.at[i], load_sems.at[2 + i]) for i in range(owners)]
    copies = product_one(
        field, (r0, r1, r2, r3), weights_ref, inv_ref, col_ref, send_ref, term_ref, packs, scratch, [load]
    )
    for i in range(owners):
        loads[i].wait()
        for q in range(mix.shape[1] // width):
            mix[i * t_loc : (i + 1) * t_loc, q * width : (q + 1) * width] = arrived[
                i, rows + q * t_loc : rows + (q + 1) * t_loc
            ]
    copies.append(start(mix, mix_ref, load_sems.at[1]))
    wait(copies + mix_times(t_loc, mix[...], arrived, out_ref, columns, mixed, out_sems))


def front_one(t_loc, field_ref, r0, r1, r2, r3, weights_ref, inv_ref, col_ref, send_ref, arrived_ref, mix_ref, term_ref, *rest):
    *packs, out_ref = rest[: len(OFFSETS) + 1]
    *scratch, field, columns, mixed, mix, arrived, load_sems, out_sems = rest[len(OFFSETS) + 1 :]
    load = start(field_ref, field, load_sems.at[0])
    loads = [start(mix_ref, mix, load_sems.at[1]), start(arrived_ref, arrived, load_sems.at[2])]
    copies = product_one(
        field, (r0, r1, r2, r3), weights_ref, inv_ref, col_ref, send_ref, term_ref, packs, scratch, [load]
    )
    wait(loads)
    wait(copies + mix_times(t_loc, mix[...], arrived, out_ref, columns, mixed, out_sems))


def rear_two(signal_ref, r0, r1, r2, r3, weights_ref, inv_ref, col_ref, term_ref, send_ref, early_ref, out_ref, *rest):
    packs = rest[: len(OFFSETS)]
    *scratch, field, early, held, load_sems, pack_sems = rest[len(OFFSETS) :]
    load = start(signal_ref.at[field.shape[0] :], field, load_sems.at[0])
    start(early_ref, early, load_sems.at[1]).wait()
    copies = pack(send_ref, early, inv_ref, packs, held, pack_sems)
    wait(
        copies
        + product_two(
            field, (r0, r1, r2, r3), weights_ref, inv_ref, col_ref, term_ref, lambda g: out_ref.at[g], scratch, [load]
        )
    )


def front_two(field_ref, r0, r1, r2, r3, weights_ref, inv_ref, col_ref, term_ref, late_ref, out_ref, *rest):
    *scratch, field, late, load_sems, late_sems = rest
    blocks, rows, width = late.shape
    load = start(field_ref, field, load_sems.at[0])
    loads = [start(late_ref, late, load_sems.at[1])]

    def target(g):
        return out_ref.at[:rows, g * width : (g + 1) * width]

    copies = product_two(
        field, (r0, r1, r2, r3), weights_ref, inv_ref, col_ref, term_ref, target, scratch, [load]
    )
    wait(loads)
    copies += [
        start(late.at[g], out_ref.at[rows:, g * width : (g + 1) * width], late_sems.at[g]) for g in range(blocks)
    ]
    wait(copies)


def swap(packs):
    count = lax.axis_size("dom")
    return [lax.ppermute(block, "dom", partners(i, count)) for i, block in enumerate(packs)]


def exchange(field):
    return lax.all_to_all(field, "tm", split_axis=0, concat_axis=0, tiled=True)


def body(signal, weights, send_list, col_ref, kernel, cheb_coef):
    probes, t_loc, n_loc = signal.shape
    blocks, per_row, width, _ = weights.shape
    rows = probes * t_loc // 2
    slots = send_list.shape[2]
    owners = lax.axis_size("tm")
    time = kernel.shape[1]
    ways = len(OFFSETS)
    pieces = rows // t_loc // 2
    xs = signal.reshape(2 * rows, n_loc)
    field = array(blocks, rows, width)
    packed = [(array(slots, rows, width), HBM)] * ways
    vm = pltpu.VMEM
    source = vm((blocks + ways * slots, rows, width), BF16)
    whole = vm((blocks, rows, width), BF16)
    held = vm((ways, slots, rows, width), BF16)
    columns = vm((time, rows // t_loc * width), BF16)
    square = vm((time, time), BF16)
    scratch_one = [source, whole, held, DMA((blocks,)), DMA((ways,))]
    scratch_two = [source, whole, whole, DMA((blocks,)), DMA]
    side_by_side = vm((rows, n_loc), BF16)
    work = 2 * rows * per_row * n_loc * width
    mixing = 2 * time * time * rows // t_loc * width

    def operands(x, packs, inv):
        received = [(r, VMEM) for r in swap(packs)]
        return [(x, HBM), *received, (weights, VMEM), (inv, VMEM), (col_ref, SMEM)]

    chunk = rows + time * t_loc // width
    (laid,) = call(
        lay_out,
        [(array(owners, chunk, width), HBM)],
        [(xs, HBM), (kernel, HBM)],
        [vm((owners, chunk, width), BF16), vm(kernel.shape, BF16), DMA((owners,)), DMA((owners,)), DMA],
    )
    arrived = exchange(laid)
    inv, *packs = call(
        first_scale,
        [(array(blocks + 8, width, dtype=F32), VMEM), *packed],
        [(xs, HBM), (weights, VMEM), (send_list, SMEM), (cheb_coef, SMEM)],
        [side_by_side, held, DMA((ways,)), DMA],
        flops=work // 8,
    )
    term, *packs, early, mix = call(
        functools.partial(rear_one, t_loc),
        [(field, HBM), *packed, (field, HBM), (array(time, time), HBM)],
        [*operands(xs, packs, inv), (send_list, SMEM), (arrived, HBM)],
        [*scratch_one, side_by_side, columns, whole, square, vm(laid.shape, BF16), DMA((2 + owners,)), DMA((pieces,))],
        flops=work + mixing,
    )
    early = exchange(early)
    late, *front = call(
        rear_two,
        [(field, HBM), *packed],
        [*operands(xs, packs, inv), (term, HBM), (send_list, SMEM), (early, HBM)],
        [*scratch_two, side_by_side, whole, held, DMA((2,)), DMA((ways,))],
        flops=work,
    )
    late = exchange(late)
    term, *packs, late = call(
        functools.partial(front_one, t_loc),
        [(field, HBM), *packed, (field, HBM)],
        [*operands(early, front, inv), (send_list, SMEM), (late, HBM), (mix, HBM)],
        [*scratch_one, whole, columns, whole, square, whole, DMA((3,)), DMA((pieces,))],
        flops=work + mixing,
    )
    late = exchange(late)
    (out,) = call(
        front_two,
        [(array(2 * rows, n_loc), HBM)],
        [*operands(early, packs, inv), (term, HBM), (late, HBM)],
        [*scratch_two, whole, whole, DMA((2,)), DMA((blocks,))],
        flops=work,
    )
    return out.reshape(probes, t_loc, n_loc)


def solution(mesh):
    in_specs = (
        P(None, "tm", "dom"),
        P("dom", None, None, None),
        P("dom", None, None),
        P("dom", None),
        P("tm", None),
        P(),
    )
    out_specs = P(None, "tm", "dom")
    return jax.shard_map(body, mesh=mesh, in_specs=in_specs, out_specs=out_specs, check_vma=False)
```

time: 157 us -> 141 us (0.90)
  the two profiles are of different devices: /device:TPU:1 before, /device:TPU:200 now
where the time goes in v7:
time: 141 us; the launch traced here: 139 us
  starting transfers between devices  89.6 us (64%)
  waiting for transfers between devices  25.8 us (18%)
  Pallas kernels  23.6 us (17%)
    ppermute x16, starting transfers between devices, swap(): lax.ppermute(block, 'dom', partners(i, count))  60.9 us
    all_to_all x4, starting transfers between devices, exchange(): return lax.all_to_all(field, 'tm', split_axis=0, concat_axis=0, tiled=True)  28.8 us
    ppermute x16, waiting for transfers between devices, swap(): lax.ppermute(block, 'dom', partners(i, count))  25 us
    pallas_call x6, Pallas kernels, call(): pl.pallas_call(kernel, out_shape=shapes, in_specs=specs, out_specs=result...  23.6 us
  transfers between devices with their start and end apart: 20, of which 9 were waited for; matrix products, arithmetic and copies ran while one was open for 0% of the time, Pallas kernels for 2%

profile of v7, /device:TPU:200, one launch (start us, length us, event | category | flops | bytes accessed | tf_op | source)
XLA Modules:
  0.0 139.5 jit_solution(1291317820594946595)
XLA Ops:
  0.0 0.0 copy-start.3
  0.0 0.0 copy-start
  0.0 0.0 copy-start.1
  0.0 2.4 %shard_map.65 = bf16[16,256,128]{2,1,0:T(8,128)(2,1)} custom-call(bf16[256,2048]{1,0:T(8,128)(2,1)} %bitcast.2, bf16[32,512]{1,0:T(8,128)(2,1)} %kernel_ref.1), custom_call_target="tpu_custom_call" | custom-call | bytes 2129920 | tf_op jit(solution)/shard_map/pallas_call | solution.py:26
  2.4 0.0 copy-start.2
  2.4 7.6 %all-to-all-start = ((bf16[16,256,128]{2,1,0:T(8,128)(2,1)}), bf16[16,256,128]{2,1,0:T(8,128)(2,1)}, u32[]{:S(2)}, u32[]{:S(2)}) async-start(bf16[16,256,128]{2,1,0:T(8,128)(2,1)} %shard_map.65), calls=%async_computation | async-start | bytes 2097152 | tf_op jit(solution)/shard_map/all_to_all | solution.py:269
  10.0 0.0 copy-done.3
  10.0 0.1 copy.7.send_ref
  10.1 0.0 copy-done
  10.1 0.0 copy-done.1
  10.1 2.9 %shard_map.64 = (f32[24,128]{1,0:T(8,128)S(1)}, bf16[3,128,128]{2,1,0:T(8,128)(2,1)}, bf16[3,128,128]{2,1,0:T(8,128)(2,1)}, bf16[3,128,128]{2,1,0:T(8,128)(2,1)}, bf16[3,128,128]{2,1,0:T(8,128)(2,1)}) custom-call(bf16[256,2048]{1,0:T(8,128)(2,1)} %bitcast.3, bf16[16,5,128,128]{3,2,1,0:T(8,128)(2,1)S(1)} %copy-done, s32[1,4,3]{2,1,0:T(4,128)S(1)} %copy.7.send_ref, ...), custom_call_target="tpu_custom_call" | custom-call | flops 41943040 | bytes 4075580 | tf_op jit(solution)/shard_map/pallas_call | solution.py:26
  13.0 4.9 %collective-permute-start = (bf16[3,128,128]{2,1,0:T(8,128)(2,1)}, bf16[3,128,128]{2,1,0:T(8,128)(2,1)S(1)}, u32[]{:S(2)}, u32[]{:S(2)}) collective-permute-start(bf16[3,128,128]{2,1,0:T(8,128)(2,1)} %get-tuple-element.28), channel_id=1, source_target_pairs={{0,32},{16,48},{32,64},{48,80},{64,96},{80,112},{96,128},{112,144}... | collective-permute-start | bytes 294920 | tf_op jit(solution)/shard_map/ppermute | solution.py:265
  17.9 2.5 %collective-permute-start.1 = (bf16[3,128,128]{2,1,0:T(8,128)(2,1)}, bf16[3,128,128]{2,1,0:T(8,128)(2,1)S(1)}, u32[]{:S(2)}, u32[]{:S(2)}) collective-permute-start(bf16[3,128,128]{2,1,0:T(8,128)(2,1)} %get-tuple-element.29), channel_id=1, source_target_pairs={{0,16},{16,32},{32,48},{48,64},{64,80},{80,96},{96,112},{112,128},... | collective-permute-start | bytes 294920 | tf_op jit(solution)/shard_map/ppermute | solution.py:265
  20.4 5.5 %collective-permute-start.2 = (bf16[3,128,128]{2,1,0:T(8,128)(2,1)}, bf16[3,128,128]{2,1,0:T(8,128)(2,1)S(1)}, u32[]{:S(2)}, u32[]{:S(2)}) collective-permute-start(bf16[3,128,128]{2,1,0:T(8,128)(2,1)} %get-tuple-element.30), channel_id=1, source_target_pairs={{0,496},{16,0},{32,16},{48,32},{64,48},{80,64},{96,80},{112,96},{1... | collective-permute-start | bytes 294920 | tf_op jit(solution)/shard_map/ppermute | solution.py:265
  25.9 1.9 %collective-permute-start.3 = (bf16[3,128,128]{2,1,0:T(8,128)(2,1)}, bf16[3,128,128]{2,1,0:T(8,128)(2,1)S(1)}, u32[]{:S(2)}, u32[]{:S(2)}) collective-permute-start(bf16[3,128,128]{2,1,0:T(8,128)(2,1)} %get-tuple-element.31), channel_id=1, source_target_pairs={{0,480},{16,496},{32,0},{48,16},{64,32},{80,48},{96,64},{112,80},{... | collective-permute-start | bytes 294920 | tf_op jit(solution)/shard_map/ppermute | solution.py:265
  27.8 0.0 copy-done.2
  27.8 0.1 copy.8.col_ref
  27.9 0.0 collective-permute-done.r0
  27.9 0.0 collective-permute-done.1.r1
  27.9 1.0 collective-permute-done.2.r2
  28.9 5.2 %collective-permute-done.3.r3 = bf16[3,128,128]{2,1,0:T(8,128)(2,1)S(1)} collective-permute-done((bf16[3,128,128]{2,1,0:T(8,128)(2,1)}, bf16[3,128,128]{2,1,0:T(8,128)(2,1)S(1)}, u32[]{:S(2)}, u32[]{:S(2)}) %collective-permute-start.3) | collective-permute-done | bytes 98336 | tf_op jit(solution)/shard_map/ppermute | solution.py:265
  34.1 0.8 all-to-all-done.arrived_ref
  34.9 4.7 %shard_map.66 = (bf16[16,128,128]{2,1,0:T(8,128)(2,1)}, bf16[3,128,128]{2,1,0:T(8,128)(2,1)}, bf16[3,128,128]{2,1,0:T(8,128)(2,1)}, bf16[3,128,128]{2,1,0:T(8,12...) custom-call(bf16[256,2048]{1,0:T(8,128)(2,1)} %bitcast.4, ...), custom_call_target="tpu_custom_call" | custom-call | flops 603979776 | bytes 7090544 | tf_op jit(solution)/shard_map/pallas_call | solution.py:26
  39.5 6.7 %all-to-all-start.1 = ((bf16[16,128,128]{2,1,0:T(8,128)(2,1)}), bf16[16,128,128]{2,1,0:T(8,128)(2,1)}, u32[]{:S(2)}, u32[]{:S(2)}) async-start(bf16[16,128,128]{2,1,0:T(8,128)(2,1)} %get-tuple-element.33), calls=%async_computation.1 | async-start | bytes 1048576 | tf_op jit(solution)/shard_map/all_to_all | solution.py:269
  46.2 6.1 %collective-permute-start.4 = (bf16[3,128,128]{2,1,0:T(8,128)(2,1)}, bf16[3,128,128]{2,1,0:T(8,128)(2,1)S(1)}, u32[]{:S(2)}, u32[]{:S(2)}) collective-permute-start(bf16[3,128,128]{2,1,0:T(8,128)(2,1)} %get-tuple-element.34), channel_id=1, source_target_pairs={{0,32},{16,48},{32,64},{48,80},{64,96},{80,112},{96,128},{112,144}... | collective-permute-start | bytes 294920 | tf_op jit(solution)/shard_map/ppermute | solution.py:265
  52.3 2.6 %collective-permute-start.5 = (bf16[3,128,128]{2,1,0:T(8,128)(2,1)}, bf16[3,128,128]{2,1,0:T(8,128)(2,1)S(1)}, u32[]{:S(2)}, u32[]{:S(2)}) collective-permute-start(bf16[3,128,128]{2,1,0:T(8,128)(2,1)} %get-tuple-element.35), channel_id=1, source_target_pairs={{0,16},{16,32},{32,48},{48,64},{64,80},{80,96},{96,112},{112,128},... | collective-permute-start | bytes 294920 | tf_op jit(solution)/shard_map/ppermute | solution.py:265
  55.0 5.3 %collective-permute-start.6 = (bf16[3,128,128]{2,1,0:T(8,128)(2,1)}, bf16[3,128,128]{2,1,0:T(8,128)(2,1)S(1)}, u32[]{:S(2)}, u32[]{:S(2)}) collective-permute-start(bf16[3,128,128]{2,1,0:T(8,128)(2,1)} %get-tuple-element.36), channel_id=1, source_target_pairs={{0,496},{16,0},{32,16},{48,32},{64,48},{80,64},{96,80},{112,96},{1... | collective-permute-start | bytes 294920 | tf_op jit(solution)/shard_map/ppermute | solution.py:265
  60.3 1.9 %collective-permute-start.7 = (bf16[3,128,128]{2,1,0:T(8,128)(2,1)}, bf16[3,128,128]{2,1,0:T(8,128)(2,1)S(1)}, u32[]{:S(2)}, u32[]{:S(2)}) collective-permute-start(bf16[3,128,128]{2,1,0:T(8,128)(2,1)} %get-tuple-element.37), channel_id=1, source_target_pairs={{0,480},{16,496},{32,0},{48,16},{64,32},{80,48},{96,64},{112,80},{... | collective-permute-start | bytes 294920 | tf_op jit(solution)/shard_map/ppermute | solution.py:265
  62.2 0.0 collective-permute-done.4.r0
  62.2 0.0 collective-permute-done.5.r1
  62.2 1.1 collective-permute-done.6.r2
  63.3 5.2 %collective-permute-done.7.r3 = bf16[3,128,128]{2,1,0:T(8,128)(2,1)S(1)} collective-permute-done((bf16[3,128,128]{2,1,0:T(8,128)(2,1)}, bf16[3,128,128]{2,1,0:T(8,128)(2,1)S(1)}, u32[]{:S(2)}, u32[]{:S(2)}) %collective-permute-start.7) | collective-permute-done | bytes 98336 | tf_op jit(solution)/shard_map/ppermute | solution.py:265
  68.5 0.0 all-to-all-done.1.early_ref.field_ref
  68.5 5.0 %shard_map.67 = (bf16[16,128,128]{2,1,0:T(8,128)(2,1)}, bf16[3,128,128]{2,1,0:T(8,128)(2,1)}, bf16[3,128,128]{2,1,0:T(8,128)(2,1)}, bf16[3,128,128]{2,1,0:T(8,128)(2,1)}, bf16[3,128,128]{2,1,0:T(8,128)(2,1)}) custom-call(bf16[256,2048]{1,0:T(8,128)(2,1)} %bitcast.5, bf16[3,128,128]{2,1,0:T(8,128)(2,1)S(1)} %collective-permute-done.4.r0, ...), custom_call_target="tpu_custom_call" | custom-call | flops 335544320 | bytes 6041968 | tf_op jit(solution)/shard_map/pallas_call | solution.py:26
  73.6 7.2 %all-to-all-start.2 = ((bf16[16,128,128]{2,1,0:T(8,128)(2,1)}), bf16[16,128,128]{2,1,0:T(8,128)(2,1)}, u32[]{:S(2)}, u32[]{:S(2)}) async-start(bf16[16,128,128]{2,1,0:T(8,128)(2,1)} %get-tuple-element.43), calls=%async_computation.2 | async-start | bytes 1048576 | tf_op jit(solution)/shard_map/all_to_all | solution.py:269
  80.8 5.2 %collective-permute-start.8 = (bf16[3,128,128]{2,1,0:T(8,128)(2,1)}, bf16[3,128,128]{2,1,0:T(8,128)(2,1)S(1)}, u32[]{:S(2)}, u32[]{:S(2)}) collective-permute-start(bf16[3,128,128]{2,1,0:T(8,128)(2,1)} %get-tuple-element.39), channel_id=1, source_target_pairs={{0,32},{16,48},{32,64},{48,80},{64,96},{80,112},{96,128},{112,144}... | collective-permute-start | bytes 294920 | tf_op jit(solution)/shard_map/ppermute | solution.py:265
  86.1 2.6 %collective-permute-start.9 = (bf16[3,128,128]{2,1,0:T(8,128)(2,1)}, bf16[3,128,128]{2,1,0:T(8,128)(2,1)S(1)}, u32[]{:S(2)}, u32[]{:S(2)}) collective-permute-start(bf16[3,128,128]{2,1,0:T(8,128)(2,1)} %get-tuple-element.40), channel_id=1, source_target_pairs={{0,16},{16,32},{32,48},{48,64},{64,80},{80,96},{96,112},{112,128},... | collective-permute-start | bytes 294920 | tf_op jit(solution)/shard_map/ppermute | solution.py:265
  88.6 5.4 %collective-permute-start.10 = (bf16[3,128,128]{2,1,0:T(8,128)(2,1)}, bf16[3,128,128]{2,1,0:T(8,128)(2,1)S(1)}, u32[]{:S(2)}, u32[]{:S(2)}) collective-permute-start(bf16[3,128,128]{2,1,0:T(8,128)(2,1)} %get-tuple-element.41), channel_id=1, source_target_pairs={{0,496},{16,0},{32,16},{48,32},{64,48},{80,64},{96,80},{112,96},{1... | collective-permute-start | bytes 294920 | tf_op jit(solution)/shard_map/ppermute | solution.py:265
  94.0 1.9 %collective-permute-start.11 = (bf16[3,128,128]{2,1,0:T(8,128)(2,1)}, bf16[3,128,128]{2,1,0:T(8,128)(2,1)S(1)}, u32[]{:S(2)}, u32[]{:S(2)}) collective-permute-start(bf16[3,128,128]{2,1,0:T(8,128)(2,1)} %get-tuple-element.42), channel_id=1, source_target_pairs={{0,480},{16,496},{32,0},{48,16},{64,32},{80,48},{96,64},{112,80},{... | collective-permute-start | bytes 294920 | tf_op jit(solution)/shard_map/ppermute | solution.py:265
  95.9 0.0 collective-permute-done.8.r0
  96.0 0.0 collective-permute-done.9.r1
  96.0 1.1 collective-permute-done.10.r2
  97.0 5.2 %collective-permute-done.11.r3 = bf16[3,128,128]{2,1,0:T(8,128)(2,1)S(1)} collective-permute-done((bf16[3,128,128]{2,1,0:T(8,128)(2,1)}, bf16[3,128,128]{2,1,0:T(8,128)(2,1)S(1)}, u32[]{:S(2)}, u32[]{:S(2)}) %collective-permute-start.11) | collective-permute-done | bytes 98336 | tf_op jit(solution)/shard_map/ppermute | solution.py:265
  102.2 0.0 all-to-all-done.2.arrived_ref
  102.2 4.4 %shard_map.68 = (bf16[16,128,128]{2,1,0:T(8,128)(2,1)}, bf16[3,128,128]{2,1,0:T(8,128)(2,1)}, bf16[3,128,128]{2,1,0:T(8,128)(2,1)}, bf16[3,128,128]{2,1,0:T(8,12...) custom-call(bf16[16,128,128]{2,1,0:T(8,128)(2,1)} %all-to-all-done.1.early_ref.field_ref, ...), custom_call_target="tpu_custom_call" | custom-call | flops 603979776 | bytes 6041968 | tf_op jit(solution)/shard_map/pallas_call | solution.py:26
  106.6 7.2 %all-to-all-start.3 = ((bf16[16,128,128]{2,1,0:T(8,128)(2,1)}), bf16[16,128,128]{2,1,0:T(8,128)(2,1)}, u32[]{:S(2)}, u32[]{:S(2)}) async-start(bf16[16,128,128]{2,1,0:T(8,128)(2,1)} %get-tuple-element.50), calls=%async_computation.3 | async-start | bytes 1048576 | tf_op jit(solution)/shard_map/all_to_all | solution.py:269
  113.9 5.2 %collective-permute-start.12 = (bf16[3,128,128]{2,1,0:T(8,128)(2,1)}, bf16[3,128,128]{2,1,0:T(8,128)(2,1)S(1)}, u32[]{:S(2)}, u32[]{:S(2)}) collective-permute-start(bf16[3,128,128]{2,1,0:T(8,128)(2,1)} %get-tuple-element.45), channel_id=1, source_target_pairs={{0,32},{16,48},{32,64},{48,80},{64,96},{80,112},{96,128},{112,144}... | collective-permute-start | bytes 294920 | tf_op jit(solution)/shard_map/ppermute | solution.py:265
  119.0 1.9 %collective-permute-start.13 = (bf16[3,128,128]{2,1,0:T(8,128)(2,1)}, bf16[3,128,128]{2,1,0:T(8,128)(2,1)S(1)}, u32[]{:S(2)}, u32[]{:S(2)}) collective-permute-start(bf16[3,128,128]{2,1,0:T(8,128)(2,1)} %get-tuple-element.46), channel_id=1, source_target_pairs={{0,16},{16,32},{32,48},{48,64},{64,80},{80,96},{96,112},{112,128},... | collective-permute-start | bytes 294920 | tf_op jit(solution)/shard_map/ppermute | solution.py:265
  121.0 6.0 %collective-permute-start.14 = (bf16[3,128,128]{2,1,0:T(8,128)(2,1)}, bf16[3,128,128]{2,1,0:T(8,128)(2,1)S(1)}, u32[]{:S(2)}, u32[]{:S(2)}) collective-permute-start(bf16[3,128,128]{2,1,0:T(8,128)(2,1)} %get-tuple-element.47), channel_id=1, source_target_pairs={{0,496},{16,0},{32,16},{48,32},{64,48},{80,64},{96,80},{112,96},{1... | collective-permute-start | bytes 294920 | tf_op jit(solution)/shard_map/ppermute | solution.py:265
  127.0 1.9 %collective-permute-start.15 = (bf16[3,128,128]{2,1,0:T(8,128)(2,1)}, bf16[3,128,128]{2,1,0:T(8,128)(2,1)S(1)}, u32[]{:S(2)}, u32[]{:S(2)}) collective-permute-start(bf16[3,128,128]{2,1,0:T(8,128)(2,1)} %get-tuple-element.48), channel_id=1, source_target_pairs={{0,480},{16,496},{32,0},{48,16},{64,32},{80,48},{96,64},{112,80},{... | collective-permute-start | bytes 294920 | tf_op jit(solution)/shard_map/ppermute | solution.py:265
  128.9 0.0 collective-permute-done.12.r0
  129.0 0.0 collective-permute-done.13.r1
  129.0 1.1 collective-permute-done.14.r2
  130.0 5.2 %collective-permute-done.15.r3 = bf16[3,128,128]{2,1,0:T(8,128)(2,1)S(1)} collective-permute-done((bf16[3,128,128]{2,1,0:T(8,128)(2,1)}, bf16[3,128,128]{2,1,0:T(8,128)(2,1)S(1)}, u32[]{:S(2)}, u32[]{:S(2)}) %collective-permute-start.15) | collective-permute-done | bytes 98336 | tf_op jit(solution)/shard_map/ppermute | solution.py:265
  135.2 0.0 all-to-all-done.3.late_ref
  135.2 4.3 %shard_map.69 = bf16[256,2048]{1,0:T(8,128)(2,1)} custom-call(bf16[16,128,128]{2,1,0:T(8,128)(2,1)} %all-to-all-done.1.early_ref.field_ref, bf16[3,128,128]{2,1,0:T(8,128)(2,1)S(1)} %collective-permute-done.12.r0, bf16[3,128,128]{2,1,0:T(8,128)(2,1)S(1)} %collective-permute-done.13.r1, bf16[3,128,128]{2,1,0:T(8,128)(2,1)S(1)} %collective-permute-done.14.r2, ...), custom_call_target="tpu_custom_call" | custom-call | flops 335544320 | bytes 5648704 | tf_op jit(solution)/shard_map/pallas_call | solution.py:26
Async XLA Ops:
  0.0 10.0 %copy-start.3 = (s32[1,4,3]{1,0,2:T(1,128)S(1)}, s32[1,4,3]{1,0,2:T(1,128)}, u32[]{:S(2)}) copy-start(s32[1,4,3]{1,0,2:T(1,128)} %param.8) | copy-start | bytes 148
  0.0 10.1 %copy-start = (bf16[16,5,128,128]{3,2,1,0:T(8,128)(2,1)S(1)}, bf16[16,5,128,128]{3,2,1,0:T(8,128)(2,1)}, u32[]{:S(2)}) copy-start(bf16[16,5,128,128]{3,2,1,0:T(8,128)(2,1)} %weights_ref.9) | copy-start | bytes 7864324
  0.0 10.1 %copy-start.1 = (f32[3]{0:T(128)S(1)}, f32[3]{0:T(128)}, u32[]{:S(2)}) copy-start(f32[3]{0:T(128)} %coef_ref.1) | copy-start | bytes 40
  2.4 25.4 %copy-start.2 = (s32[16,5]{0,1:T(8,128)S(1)}, s32[16,5]{0,1:T(8,128)}, u32[]{:S(2)}) copy-start(s32[16,5]{0,1:T(8,128)} %param.9) | copy-start | bytes 964
  2.4 32.4 %all-to-all-start = ((bf16[16,256,128]{2,1,0:T(8,128)(2,1)}), bf16[16,256,128]{2,1,0:T(8,128)(2,1)}, u32[]{:S(2)}, u32[]{:S(2)}) async-start(bf16[16,256,128]{2,1,0:T(8,128)(2,1)} %shard_map.65), calls=%async_computation | async-start | bytes 2097152 | tf_op jit(solution)/shard_map/all_to_all | solution.py:269
  13.0 14.9 %collective-permute-start = (bf16[3,128,128]{2,1,0:T(8,128)(2,1)}, bf16[3,128,128]{2,1,0:T(8,128)(2,1)S(1)}, u32[]{:S(2)}, u32[]{:S(2)}) collective-permute-start(bf16[3,128,128]{2,1,0:T(8,128)(2,1)} %get-tuple-element.28), channel_id=1, source_target_pairs={{0,32},{16,48},{32,64},{48,80},{64,96},{80,112},{96,128},{112,144}... | collective-permute-start | bytes 294920 | tf_op jit(solution)/shard_map/ppermute | solution.py:265
  17.9 10.0 %collective-permute-start.1 = (bf16[3,128,128]{2,1,0:T(8,128)(2,1)}, bf16[3,128,128]{2,1,0:T(8,128)(2,1)S(1)}, u32[]{:S(2)}, u32[]{:S(2)}) collective-permute-start(bf16[3,128,128]{2,1,0:T(8,128)(2,1)} %get-tuple-element.29), channel_id=1, source_target_pairs={{0,16},{16,32},{32,48},{48,64},{64,80},{80,96},{96,112},{112,128},... | collective-permute-start | bytes 294920 | tf_op jit(solution)/shard_map/ppermute | solution.py:265
  20.4 8.5 %collective-permute-start.2 = (bf16[3,128,128]{2,1,0:T(8,128)(2,1)}, bf16[3,128,128]{2,1,0:T(8,128)(2,1)S(1)}, u32[]{:S(2)}, u32[]{:S(2)}) collective-permute-start(bf16[3,128,128]{2,1,0:T(8,128)(2,1)} %get-tuple-element.30), channel_id=1, source_target_pairs={{0,496},{16,0},{32,16},{48,32},{64,48},{80,64},{96,80},{112,96},{1... | collective-permute-start | bytes 294920 | tf_op jit(solution)/shard_map/ppermute | solution.py:265
  25.9 8.2 %collective-permute-start.3 = (bf16[3,128,128]{2,1,0:T(8,128)(2,1)}, bf16[3,128,128]{2,1,0:T(8,128)(2,1)S(1)}, u32[]{:S(2)}, u32[]{:S(2)}) collective-permute-start(bf16[3,128,128]{2,1,0:T(8,128)(2,1)} %get-tuple-element.31), channel_id=1, source_target_pairs={{0,480},{16,496},{32,0},{48,16},{64,32},{80,48},{96,64},{112,80},{... | collective-permute-start | bytes 294920 | tf_op jit(solution)/shard_map/ppermute | solution.py:265
  39.5 29.0 %all-to-all-start.1 = ((bf16[16,128,128]{2,1,0:T(8,128)(2,1)}), bf16[16,128,128]{2,1,0:T(8,128)(2,1)}, u32[]{:S(2)}, u32[]{:S(2)}) async-start(bf16[16,128,128]{2,1,0:T(8,128)(2,1)} %get-tuple-element.33), calls=%async_computation.1 | async-start | bytes 1048576 | tf_op jit(solution)/shard_map/all_to_all | solution.py:269
  46.2 16.0 %collective-permute-start.4 = (bf16[3,128,128]{2,1,0:T(8,128)(2,1)}, bf16[3,128,128]{2,1,0:T(8,128)(2,1)S(1)}, u32[]{:S(2)}, u32[]{:S(2)}) collective-permute-start(bf16[3,128,128]{2,1,0:T(8,128)(2,1)} %get-tuple-element.34), channel_id=1, source_target_pairs={{0,32},{16,48},{32,64},{48,80},{64,96},{80,112},{96,128},{112,144}... | collective-permute-start | bytes 294920 | tf_op jit(solution)/shard_map/ppermute | solution.py:265
  52.3 9.9 %collective-permute-start.5 = (bf16[3,128,128]{2,1,0:T(8,128)(2,1)}, bf16[3,128,128]{2,1,0:T(8,128)(2,1)S(1)}, u32[]{:S(2)}, u32[]{:S(2)}) collective-permute-start(bf16[3,128,128]{2,1,0:T(8,128)(2,1)} %get-tuple-element.35), channel_id=1, source_target_pairs={{0,16},{16,32},{32,48},{48,64},{64,80},{80,96},{96,112},{112,128},... | collective-permute-start | bytes 294920 | tf_op jit(solution)/shard_map/ppermute | solution.py:265
  55.0 8.3 %collective-permute-start.6 = (bf16[3,128,128]{2,1,0:T(8,128)(2,1)}, bf16[3,128,128]{2,1,0:T(8,128)(2,1)S(1)}, u32[]{:S(2)}, u32[]{:S(2)}) collective-permute-start(bf16[3,128,128]{2,1,0:T(8,128)(2,1)} %get-tuple-element.36), channel_id=1, source_target_pairs={{0,496},{16,0},{32,16},{48,32},{64,48},{80,64},{96,80},{112,96},{1... | collective-permute-start | bytes 294920 | tf_op jit(solution)/shard_map/ppermute | solution.py:265
  60.3 8.2 %collective-permute-start.7 = (bf16[3,128,128]{2,1,0:T(8,128)(2,1)}, bf16[3,128,128]{2,1,0:T(8,128)(2,1)S(1)}, u32[]{:S(2)}, u32[]{:S(2)}) collective-permute-start(bf16[3,128,128]{2,1,0:T(8,128)(2,1)} %get-tuple-element.37), channel_id=1, source_target_pairs={{0,480},{16,496},{32,0},{48,16},{64,32},{80,48},{96,64},{112,80},{... | collective-permute-start | bytes 294920 | tf_op jit(solution)/shard_map/ppermute | solution.py:265
  73.6 28.7 %all-to-all-start.2 = ((bf16[16,128,128]{2,1,0:T(8,128)(2,1)}), bf16[16,128,128]{2,1,0:T(8,128)(2,1)}, u32[]{:S(2)}, u32[]{:S(2)}) async-start(bf16[16,128,128]{2,1,0:T(8,128)(2,1)} %get-tuple-element.43), calls=%async_computation.2 | async-start | bytes 1048576 | tf_op jit(solution)/shard_map/all_to_all | solution.py:269
  80.8 15.1 %collective-permute-start.8 = (bf16[3,128,128]{2,1,0:T(8,128)(2,1)}, bf16[3,128,128]{2,1,0:T(8,128)(2,1)S(1)}, u32[]{:S(2)}, u32[]{:S(2)}) collective-permute-start(bf16[3,128,128]{2,1,0:T(8,128)(2,1)} %get-tuple-element.39), channel_id=1, source_target_pairs={{0,32},{16,48},{32,64},{48,80},{64,96},{80,112},{96,128},{112,144}... | collective-permute-start | bytes 294920 | tf_op jit(solution)/shard_map/ppermute | solution.py:265
  86.1 9.9 %collective-permute-start.9 = (bf16[3,128,128]{2,1,0:T(8,128)(2,1)}, bf16[3,128,128]{2,1,0:T(8,128)(2,1)S(1)}, u32[]{:S(2)}, u32[]{:S(2)}) collective-permute-start(bf16[3,128,128]{2,1,0:T(8,128)(2,1)} %get-tuple-element.40), channel_id=1, source_target_pairs={{0,16},{16,32},{32,48},{48,64},{64,80},{80,96},{96,112},{112,128},... | collective-permute-start | bytes 294920 | tf_op jit(solution)/shard_map/ppermute | solution.py:265
  88.6 8.4 %collective-permute-start.10 = (bf16[3,128,128]{2,1,0:T(8,128)(2,1)}, bf16[3,128,128]{2,1,0:T(8,128)(2,1)S(1)}, u32[]{:S(2)}, u32[]{:S(2)}) collective-permute-start(bf16[3,128,128]{2,1,0:T(8,128)(2,1)} %get-tuple-element.41), channel_id=1, source_target_pairs={{0,496},{16,0},{32,16},{48,32},{64,48},{80,64},{96,80},{112,96},{1... | collective-permute-start | bytes 294920 | tf_op jit(solution)/shard_map/ppermute | solution.py:265
  94.0 8.2 %collective-permute-start.11 = (bf16[3,128,128]{2,1,0:T(8,128)(2,1)}, bf16[3,128,128]{2,1,0:T(8,128)(2,1)S(1)}, u32[]{:S(2)}, u32[]{:S(2)}) collective-permute-start(bf16[3,128,128]{2,1,0:T(8,128)(2,1)} %get-tuple-element.42), channel_id=1, source_target_pairs={{0,480},{16,496},{32,0},{48,16},{64,32},{80,48},{96,64},{112,80},{... | collective-permute-start | bytes 294920 | tf_op jit(solution)/shard_map/ppermute | solution.py:265
  106.6 28.6 %all-to-all-start.3 = ((bf16[16,128,128]{2,1,0:T(8,128)(2,1)}), bf16[16,128,128]{2,1,0:T(8,128)(2,1)}, u32[]{:S(2)}, u32[]{:S(2)}) async-start(bf16[16,128,128]{2,1,0:T(8,128)(2,1)} %get-tuple-element.50), calls=%async_computation.3 | async-start | bytes 1048576 | tf_op jit(solution)/shard_map/all_to_all | solution.py:269
  113.9 15.1 %collective-permute-start.12 = (bf16[3,128,128]{2,1,0:T(8,128)(2,1)}, bf16[3,128,128]{2,1,0:T(8,128)(2,1)S(1)}, u32[]{:S(2)}, u32[]{:S(2)}) collective-permute-start(bf16[3,128,128]{2,1,0:T(8,128)(2,1)} %get-tuple-element.45), channel_id=1, source_target_pairs={{0,32},{16,48},{32,64},{48,80},{64,96},{80,112},{96,128},{112,144}... | collective-permute-start | bytes 294920 | tf_op jit(solution)/shard_map/ppermute | solution.py:265
  119.0 9.9 %collective-permute-start.13 = (bf16[3,128,128]{2,1,0:T(8,128)(2,1)}, bf16[3,128,128]{2,1,0:T(8,128)(2,1)S(1)}, u32[]{:S(2)}, u32[]{:S(2)}) collective-permute-start(bf16[3,128,128]{2,1,0:T(8,128)(2,1)} %get-tuple-element.46), channel_id=1, source_target_pairs={{0,16},{16,32},{32,48},{48,64},{64,80},{80,96},{96,112},{112,128},... | collective-permute-start | bytes 294920 | tf_op jit(solution)/shard_map/ppermute | solution.py:265
  121.0 9.0 %collective-permute-start.14 = (bf16[3,128,128]{2,1,0:T(8,128)(2,1)}, bf16[3,128,128]{2,1,0:T(8,128)(2,1)S(1)}, u32[]{:S(2)}, u32[]{:S(2)}) collective-permute-start(bf16[3,128,128]{2,1,0:T(8,128)(2,1)} %get-tuple-element.47), channel_id=1, source_target_pairs={{0,496},{16,0},{32,16},{48,32},{64,48},{80,64},{96,80},{112,96},{1... | collective-permute-start | bytes 294920 | tf_op jit(solution)/shard_map/ppermute | solution.py:265
  127.0 8.2 %collective-permute-start.15 = (bf16[3,128,128]{2,1,0:T(8,128)(2,1)}, bf16[3,128,128]{2,1,0:T(8,128)(2,1)S(1)}, u32[]{:S(2)}, u32[]{:S(2)}) collective-permute-start(bf16[3,128,128]{2,1,0:T(8,128)(2,1)} %get-tuple-element.48), channel_id=1, source_target_pairs={{0,480},{16,496},{32,0},{48,16},{64,32},{80,48},{96,64},{112,80},{... | collective-permute-start | bytes 294920 | tf_op jit(solution)/shard_map/ppermute | solution.py:265

commit v8 on v7

--- a/solution.py
+++ b/solution.py
@@ -215,49 +215,60 @@
     wait(copies + mix_times(t_loc, mix[...], arrived, out_ref, columns, mixed, out_sems))
 
 
-def front_one(t_loc, field_ref, r0, r1, r2, r3, weights_ref, inv_ref, col_ref, send_ref, arrived_ref, mix_ref, term_ref, *rest):
-    *packs, out_ref = rest[: len(OFFSETS) + 1]
-    *scratch, field, columns, mixed, mix, arrived, load_sems, out_sems = rest[len(OFFSETS) + 1 :]
-    load = start(field_ref, field, load_sems.at[0])
-    loads = [start(mix_ref, mix, load_sems.at[1]), start(arrived_ref, arrived, load_sems.at[2])]
-    copies = product_one(
-        field, (r0, r1, r2, r3), weights_ref, inv_ref, col_ref, send_ref, term_ref, packs, scratch, [load]
-    )
-    wait(loads)
-    wait(copies + mix_times(t_loc, mix[...], arrived, out_ref, columns, mixed, out_sems))
-
-
-def rear_two(signal_ref, r0, r1, r2, r3, weights_ref, inv_ref, col_ref, term_ref, send_ref, early_ref, out_ref, *rest):
+def front_one(field_ref, r0, r1, r2, r3, weights_ref, inv_ref, col_ref, send_ref, term_ref, *rest):
     packs = rest[: len(OFFSETS)]
-    *scratch, field, early, held, load_sems, pack_sems = rest[len(OFFSETS) :]
-    load = start(signal_ref.at[field.shape[0] :], field, load_sems.at[0])
-    start(early_ref, early, load_sems.at[1]).wait()
-    copies = pack(send_ref, early, inv_ref, packs, held, pack_sems)
+    *scratch, field, load_sem = rest[len(OFFSETS) :]
+    load = start(field_ref, field, load_sem)
     wait(
-        copies
-        + product_two(
+        product_one(
+            field, (r0, r1, r2, r3), weights_ref, inv_ref, col_ref, send_ref, term_ref, packs, scratch, [load]
+        )
+    )
+
+
+def second_temporal(t_loc, arrived_ref, mix_ref, out_ref, columns, mixed, mix, arrived, load_sems, out_sems):
+    wait([start(arrived_ref, arrived, load_sems.at[0]), start(mix_ref, mix, load_sems.at[1])])
+    wait(mix_times(t_loc, mix[...], arrived, out_ref, columns, mixed, out_sems))
+
+
+def rear_two(signal_ref, r0, r1, r2, r3, weights_ref, inv_ref, col_ref, term_ref, out_ref, *rest):
+    *scratch, field, load_sem = rest
+    load = start(signal_ref.at[field.shape[0] :], field, load_sem)
+    wait(
+        product_two(
             field, (r0, r1, r2, r3), weights_ref, inv_ref, col_ref, term_ref, lambda g: out_ref.at[g], scratch, [load]
         )
     )
 
 
-def front_two(field_ref, r0, r1, r2, r3, weights_ref, inv_ref, col_ref, term_ref, late_ref, out_ref, *rest):
-    *scratch, field, late, load_sems, late_sems = rest
-    blocks, rows, width = late.shape
-    load = start(field_ref, field, load_sems.at[0])
-    loads = [start(late_ref, late, load_sems.at[1])]
+def front_packs(early_ref, inv_ref, send_ref, *rest):
+    packs = rest[: len(OFFSETS)]
+    early, held, load_sem, pack_sems = rest[len(OFFSETS) :]
+    start(early_ref, early, load_sem).wait()
+    wait(pack(send_ref, early, inv_ref, packs, held, pack_sems))
+
+
+def front_two(field_ref, r0, r1, r2, r3, weights_ref, inv_ref, col_ref, term_ref, _, out_ref, *rest):
+    *scratch, field, load_sem = rest
+    rows, width = field.shape[1:]
 
     def target(g):
         return out_ref.at[:rows, g * width : (g + 1) * width]
 
-    copies = product_two(
-        field, (r0, r1, r2, r3), weights_ref, inv_ref, col_ref, term_ref, target, scratch, [load]
-    )
-    wait(loads)
-    copies += [
-        start(late.at[g], out_ref.at[rows:, g * width : (g + 1) * width], late_sems.at[g]) for g in range(blocks)
-    ]
-    wait(copies)
+    load = start(field_ref, field, load_sem)
+    wait(
+        product_two(
+            field, (r0, r1, r2, r3), weights_ref, inv_ref, col_ref, term_ref, target, scratch, [load]
+        )
+    )
+
+
+def unblock(late_ref, out_ref, late, load_sem, sems):
+    blocks, rows, width = late.shape
+    start(late_ref, late, load_sem).wait()
+    wait(
+        [start(late.at[g], out_ref.at[rows:, g * width : (g + 1) * width], sems.at[g]) for g in range(blocks)]
+    )
 
 
 def swap(packs):
@@ -320,28 +331,41 @@
         flops=work + mixing,
     )
     early = exchange(early)
-    late, *front = call(
-        rear_two,
-        [(field, HBM), *packed],
-        [*operands(xs, packs, inv), (term, HBM), (send_list, SMEM), (early, HBM)],
-        [*scratch_two, side_by_side, whole, held, DMA((2,)), DMA((ways,))],
-        flops=work,
-    )
+    takes = operands(xs, packs, inv)
+    front = call(
+        front_packs, packed, [(early, HBM), (inv, VMEM), (send_list, SMEM)], [whole, held, DMA, DMA((ways,))]
+    )
+    term, *front = lax.optimization_barrier((term, *front))
+    (late,) = call(
+        rear_two, [(field, HBM)], [*takes, (term, HBM)], [*scratch_two, side_by_side, DMA], flops=work
+    )
+    late, *front = lax.optimization_barrier((late, *front))
     late = exchange(late)
-    term, *packs, late = call(
-        functools.partial(front_one, t_loc),
-        [(field, HBM), *packed, (field, HBM)],
-        [*operands(early, front, inv), (send_list, SMEM), (late, HBM), (mix, HBM)],
-        [*scratch_one, whole, columns, whole, square, whole, DMA((3,)), DMA((pieces,))],
-        flops=work + mixing,
-    )
+    takes = operands(early, front, inv)
+    (late,) = call(
+        functools.partial(second_temporal, t_loc),
+        [(field, HBM)],
+        [(late, HBM), (mix, HBM)],
+        [columns, whole, square, whole, DMA((2,)), DMA((pieces,))],
+        flops=mixing,
+    )
+    late, term = lax.optimization_barrier((late, takes[0][0]))
+    takes[0] = (term, HBM)
+    term, *packs = call(
+        front_one, [(field, HBM), *packed], [*takes, (send_list, SMEM)], [*scratch_one, whole, DMA], flops=work
+    )
+    late, *packs = lax.optimization_barrier((late, *packs))
     late = exchange(late)
+    takes = operands(early, packs, inv)
+    out = array(2 * rows, n_loc)
+    (rear,) = call(unblock, [(out, HBM)], [(late, HBM)], [whole, DMA, DMA((blocks,))])
     (out,) = call(
         front_two,
-        [(array(2 * rows, n_loc), HBM)],
-        [*operands(early, packs, inv), (term, HBM), (late, HBM)],
-        [*scratch_two, whole, whole, DMA((2,)), DMA((blocks,))],
+        [(out, HBM)],
+        [*takes, (term, HBM), (rear, HBM)],
+        [*scratch_two, whole, DMA],
         flops=work,
+        aliases={9: 0},
     )
     return out.reshape(probes, t_loc, n_loc)
 

time: 141 us -> 138 us (0.979)
  the two profiles are of different devices: /device:TPU:200 before, /device:TPU:1 now
where the time goes in v8:
time: 138 us; the launch traced here: 137 us
  starting transfers between devices  94.1 us (68%)
  Pallas kernels  28.2 us (20%)
  waiting for transfers between devices  14.1 us (10%)
    ppermute x16, starting transfers between devices, swap(): lax.ppermute(block, 'dom', partners(i, count))  64.7 us
    all_to_all x4, starting transfers between devices, exchange(): return lax.all_to_all(field, 'tm', split_axis=0, concat_axis=0, tiled=True)  29.4 us
    pallas_call x9, Pallas kernels, call(): pl.pallas_call(kernel, out_shape=shapes, in_specs=specs, out_specs=result...  28.2 us
    all_to_all x4, waiting for transfers between devices, exchange(): return lax.all_to_all(field, 'tm', split_axis=0, concat_axis=0, tiled=True)  9.46 us
    ppermute x16, waiting for transfers between devices, swap(): lax.ppermute(block, 'dom', partners(i, count))  4.66 us
  transfers between devices with their start and end apart: 20, of which 5 were waited for; matrix products, arithmetic and copies ran while one was open for 0% of the time, Pallas kernels for 7%

profile of v8, /device:TPU:1, one launch (start us, length us, event | category | flops | bytes accessed | tf_op | source)
XLA Modules:
  0.0 137.0 jit_solution(12003349507507284715)
XLA Ops:
  0.0 2.4 %shard_map.65 = bf16[16,256,128]{2,1,0:T(8,128)(2,1)} custom-call(bf16[256,2048]{1,0:T(8,128)(2,1)} %bitcast.2, bf16[32,512]{1,0:T(8,128)(2,1)} %kernel_ref.1), custom_call_target="tpu_custom_call" | custom-call | bytes 2129920 | tf_op jit(solution)/shard_map/pallas_call | solution.py:26
  2.4 0.0 copy-start.2
  2.4 10.9 %all-to-all-start = ((bf16[16,256,128]{2,1,0:T(8,128)(2,1)}), bf16[16,256,128]{2,1,0:T(8,128)(2,1)}, u32[]{:S(2)}, u32[]{:S(2)}) async-start(bf16[16,256,128]{2,1,0:T(8,128)(2,1)} %shard_map.65), calls=%async_computation | async-start | bytes 2097152 | tf_op jit(solution)/shard_map/all_to_all | solution.py:280
  13.4 0.0 copy-done.3
  13.4 0.1 copy.8.send_ref
  13.5 0.0 copy-done
  13.5 0.0 copy-done.1
  13.5 2.9 %shard_map.64 = (f32[24,128]{1,0:T(8,128)S(1)}, bf16[3,128,128]{2,1,0:T(8,128)(2,1)}, bf16[3,128,128]{2,1,0:T(8,128)(2,1)}, bf16[3,128,128]{2,1,0:T(8,128)(2,1)}, bf16[3,128,128]{2,1,0:T(8,128)(2,1)}) custom-call(bf16[256,2048]{1,0:T(8,128)(2,1)} %bitcast.3, bf16[16,5,128,128]{3,2,1,0:T(8,128)(2,1)S(1)} %copy-done, s32[1,4,3]{2,1,0:T(4,128)S(1)} %copy.8.send_ref, ...), custom_call_target="tpu_custom_call" | custom-call | flops 41943040 | bytes 4075580 | tf_op jit(solution)/shard_map/pallas_call | solution.py:26
  16.4 2.3 %collective-permute-start = (bf16[3,128,128]{2,1,0:T(8,128)(2,1)}, bf16[3,128,128]{2,1,0:T(8,128)(2,1)S(1)}, u32[]{:S(2)}, u32[]{:S(2)}) collective-permute-start(bf16[3,128,128]{2,1,0:T(8,128)(2,1)} %get-tuple-element.43), channel_id=1, source_target_pairs={{0,32},{16,48},{32,64},{48,80},{64,96},{80,112},{96,128},{112,144}... | collective-permute-start | bytes 294920 | tf_op jit(solution)/shard_map/ppermute | solution.py:276
  18.7 2.2 %collective-permute-start.1 = (bf16[3,128,128]{2,1,0:T(8,128)(2,1)}, bf16[3,128,128]{2,1,0:T(8,128)(2,1)S(1)}, u32[]{:S(2)}, u32[]{:S(2)}) collective-permute-start(bf16[3,128,128]{2,1,0:T(8,128)(2,1)} %get-tuple-element.44), channel_id=1, source_target_pairs={{0,16},{16,32},{32,48},{48,64},{64,80},{80,96},{96,112},{112,128},... | collective-permute-start | bytes 294920 | tf_op jit(solution)/shard_map/ppermute | solution.py:276
  20.9 9.8 %collective-permute-start.2 = (bf16[3,128,128]{2,1,0:T(8,128)(2,1)}, bf16[3,128,128]{2,1,0:T(8,128)(2,1)S(1)}, u32[]{:S(2)}, u32[]{:S(2)}) collective-permute-start(bf16[3,128,128]{2,1,0:T(8,128)(2,1)} %get-tuple-element.45), channel_id=1, source_target_pairs={{0,496},{16,0},{32,16},{48,32},{64,48},{80,64},{96,80},{112,96},{1... | collective-permute-start | bytes 294920 | tf_op jit(solution)/shard_map/ppermute | solution.py:276
  30.8 4.3 %collective-permute-start.3 = (bf16[3,128,128]{2,1,0:T(8,128)(2,1)}, bf16[3,128,128]{2,1,0:T(8,128)(2,1)S(1)}, u32[]{:S(2)}, u32[]{:S(2)}) collective-permute-start(bf16[3,128,128]{2,1,0:T(8,128)(2,1)} %get-tuple-element.46), channel_id=1, source_target_pairs={{0,480},{16,496},{32,0},{48,16},{64,32},{80,48},{96,64},{112,80},{... | collective-permute-start | bytes 294920 | tf_op jit(solution)/shard_map/ppermute | solution.py:276
  35.0 0.0 copy-done.2
  35.0 0.1 copy.9.col_ref
  35.1 0.0 collective-permute-done.r0
  35.1 0.0 collective-permute-done.1.r1
  35.1 0.0 collective-permute-done.2.r2
  35.1 3.3 %collective-permute-done.3.r3 = bf16[3,128,128]{2,1,0:T(8,128)(2,1)S(1)} collective-permute-done((bf16[3,128,128]{2,1,0:T(8,128)(2,1)}, bf16[3,128,128]{2,1,0:T(8,128)(2,1)S(1)}, u32[]{:S(2)}, u32[]{:S(2)}) %collective-permute-start.3) | collective-permute-done | bytes 98336 | tf_op jit(solution)/shard_map/ppermute | solution.py:276
  38.4 3.0 %all-to-all-done.arrived_ref = bf16[16,256,128]{2,1,0:T(8,128)(2,1)} async-done(((bf16[16,256,128]{2,1,0:T(8,128)(2,1)}), bf16[16,256,128]{2,1,0:T(8,128)(2,1)}, u32[]{:S(2)}, u32[]{:S(2)}) %all-to-all-start) | async-done | bytes 1048608 | tf_op jit(solution)/shard_map/all_to_all | solution.py:280
  41.5 4.7 %shard_map.66 = (bf16[16,128,128]{2,1,0:T(8,128)(2,1)}, bf16[3,128,128]{2,1,0:T(8,128)(2,1)}, bf16[3,128,128]{2,1,0:T(8,128)(2,1)}, bf16[3,128,128]{2,1,0:T(8,12...) custom-call(bf16[256,2048]{1,0:T(8,128)(2,1)} %bitcast.4, ...), custom_call_target="tpu_custom_call" | custom-call | flops 603979776 | bytes 7090544 | tf_op jit(solution)/shard_map/pallas_call | solution.py:26
  46.1 5.0 %all-to-all-start.1 = ((bf16[16,128,128]{2,1,0:T(8,128)(2,1)}), bf16[16,128,128]{2,1,0:T(8,128)(2,1)}, u32[]{:S(2)}, u32[]{:S(2)}) async-start(bf16[16,128,128]{2,1,0:T(8,128)(2,1)} %get-tuple-element.48), calls=%async_computation.1 | async-start | bytes 1048576 | tf_op jit(solution)/shard_map/all_to_all | solution.py:280
  51.2 1.9 %collective-permute-start.4 = (bf16[3,128,128]{2,1,0:T(8,128)(2,1)}, bf16[3,128,128]{2,1,0:T(8,128)(2,1)S(1)}, u32[]{:S(2)}, u32[]{:S(2)}) collective-permute-start(bf16[3,128,128]{2,1,0:T(8,128)(2,1)} %get-tuple-element.49), channel_id=1, source_target_pairs={{0,32},{16,48},{32,64},{48,80},{64,96},{80,112},{96,128},{112,144}... | collective-permute-start | bytes 294920 | tf_op jit(solution)/shard_map/ppermute | solution.py:276
  53.1 1.9 %collective-permute-start.5 = (bf16[3,128,128]{2,1,0:T(8,128)(2,1)}, bf16[3,128,128]{2,1,0:T(8,128)(2,1)S(1)}, u32[]{:S(2)}, u32[]{:S(2)}) collective-permute-start(bf16[3,128,128]{2,1,0:T(8,128)(2,1)} %get-tuple-element.50), channel_id=1, source_target_pairs={{0,16},{16,32},{32,48},{48,64},{64,80},{80,96},{96,112},{112,128},... | collective-permute-start | bytes 294920 | tf_op jit(solution)/shard_map/ppermute | solution.py:276
  55.0 9.6 %collective-permute-start.6 = (bf16[3,128,128]{2,1,0:T(8,128)(2,1)}, bf16[3,128,128]{2,1,0:T(8,128)(2,1)S(1)}, u32[]{:S(2)}, u32[]{:S(2)}) collective-permute-start(bf16[3,128,128]{2,1,0:T(8,128)(2,1)} %get-tuple-element.51), channel_id=1, source_target_pairs={{0,496},{16,0},{32,16},{48,32},{64,48},{80,64},{96,80},{112,96},{1... | collective-permute-start | bytes 294920 | tf_op jit(solution)/shard_map/ppermute | solution.py:276
  64.7 4.3 %collective-permute-start.7 = (bf16[3,128,128]{2,1,0:T(8,128)(2,1)}, bf16[3,128,128]{2,1,0:T(8,128)(2,1)S(1)}, u32[]{:S(2)}, u32[]{:S(2)}) collective-permute-start(bf16[3,128,128]{2,1,0:T(8,128)(2,1)} %get-tuple-element.52), channel_id=1, source_target_pairs={{0,480},{16,496},{32,0},{48,16},{64,32},{80,48},{96,64},{112,80},{... | collective-permute-start | bytes 294920 | tf_op jit(solution)/shard_map/ppermute | solution.py:276
  68.9 0.0 all-to-all-done.1.early_ref.field_ref
  68.9 2.4 %shard_map.67 = (bf16[3,128,128]{2,1,0:T(8,128)(2,1)}, bf16[3,128,128]{2,1,0:T(8,128)(2,1)}, bf16[3,128,128]{2,1,0:T(8,128)(2,1)}, bf16[3,128,128]{2,1,0:T(8,128)(2,1)}) custom-call(bf16[16,128,128]{2,1,0:T(8,128)(2,1)} %all-to-all-done.1.early_ref.field_ref, f32[24,128]{1,0:T(8,128)S(1)} %get-tuple-element.47.inv_ref, s32[1,4,3]{2,1,0:T(4,128)S(1)} %copy.8.send_ref), custom_call_target="tpu_custom_call" | custom-call | bytes 929840 | tf_op jit(solution)/shard_map/pallas_call | solution.py:26
  71.4 0.0 copy-start.7
  71.4 0.0 copy-start.6
  71.4 0.0 copy-start.5
  71.4 0.0 copy-start.4
  71.4 0.0 collective-permute-done.4.r0
  71.4 0.0 collective-permute-done.5.r1
  71.4 0.0 collective-permute-done.6.r2
  71.4 1.4 collective-permute-done.7.r3
  72.8 3.8 %shard_map.68 = bf16[16,128,128]{2,1,0:T(8,128)(2,1)} custom-call(bf16[256,2048]{1,0:T(8,128)(2,1)} %bitcast.5, bf16[3,128,128]{2,1,0:T(8,128)(2,1)S(1)} %collective-permute-done.4.r0, bf16[3,128,128]{2,1,0:T(8,128)(2,1)S(1)} %collective-permute-done.5.r1, bf16[3,128,128]{2,1,0:T(8,128)(2,1)S(1)} %collective-permute-done.6.r2, ...), custom_call_target="tpu_custom_call" | custom-call | flops 335544320 | bytes 5124416 | tf_op jit(solution)/shard_map/pallas_call | solution.py:26
  76.6 7.0 %all-to-all-start.2 = ((bf16[16,128,128]{2,1,0:T(8,128)(2,1)}), bf16[16,128,128]{2,1,0:T(8,128)(2,1)}, u32[]{:S(2)}, u32[]{:S(2)}) async-start(bf16[16,128,128]{2,1,0:T(8,128)(2,1)} %shard_map.68), calls=%async_computation.2 | async-start | bytes 1048576 | tf_op jit(solution)/shard_map/all_to_all | solution.py:280
  83.6 0.0 copy-done.7
  83.6 1.9 %collective-permute-start.8 = (bf16[3,128,128]{2,1,0:T(8,128)(2,1)S(1)}, bf16[3,128,128]{2,1,0:T(8,128)(2,1)S(1)}, u32[]{:S(2)}, u32[]{:S(2)}) collective-permute-start(bf16[3,128,128]{2,1,0:T(8,128)(2,1)S(1)} %copy-done.7), channel_id=1, source_target_pairs={{0,32},{16,48},{32,64},{48,80},{64,96},{80,112},{96,128},{112,144}... | collective-permute-start | bytes 294920 | tf_op jit(solution)/shard_map/ppermute | solution.py:276
  85.5 0.0 copy-done.6
  85.5 1.9 %collective-permute-start.9 = (bf16[3,128,128]{2,1,0:T(8,128)(2,1)S(1)}, bf16[3,128,128]{2,1,0:T(8,128)(2,1)S(1)}, u32[]{:S(2)}, u32[]{:S(2)}) collective-permute-start(bf16[3,128,128]{2,1,0:T(8,128)(2,1)S(1)} %copy-done.6), channel_id=1, source_target_pairs={{0,16},{16,32},{32,48},{48,64},{64,80},{80,96},{96,112},{112,128},... | collective-permute-start | bytes 294920 | tf_op jit(solution)/shard_map/ppermute | solution.py:276
  87.4 0.0 copy-done.5
  87.4 6.7 %collective-permute-start.10 = (bf16[3,128,128]{2,1,0:T(8,128)(2,1)S(1)}, bf16[3,128,128]{2,1,0:T(8,128)(2,1)S(1)}, u32[]{:S(2)}, u32[]{:S(2)}) collective-permute-start(bf16[3,128,128]{2,1,0:T(8,128)(2,1)S(1)} %copy-done.5), channel_id=1, source_target_pairs={{0,496},{16,0},{32,16},{48,32},{64,48},{80,64},{96,80},{112,96},{1... | collective-permute-start | bytes 294920 | tf_op jit(solution)/shard_map/ppermute | solution.py:276
  94.1 0.0 copy-done.4
  94.1 3.7 %collective-permute-start.11 = (bf16[3,128,128]{2,1,0:T(8,128)(2,1)S(1)}, bf16[3,128,128]{2,1,0:T(8,128)(2,1)S(1)}, u32[]{:S(2)}, u32[]{:S(2)}) collective-permute-start(bf16[3,128,128]{2,1,0:T(8,128)(2,1)S(1)} %copy-done.4), channel_id=1, source_target_pairs={{0,480},{16,496},{32,0},{48,16},{64,32},{80,48},{96,64},{112,80},{... | collective-permute-start | bytes 294920 | tf_op jit(solution)/shard_map/ppermute | solution.py:276
  97.8 3.2 %all-to-all-done.2.arrived_ref = bf16[16,128,128]{2,1,0:T(8,128)(2,1)} async-done(((bf16[16,128,128]{2,1,0:T(8,128)(2,1)}), bf16[16,128,128]{2,1,0:T(8,128)(2,1)}, u32[]{:S(2)}, u32[]{:S(2)}) %all-to-all-start.2) | async-done | bytes 524320 | tf_op jit(solution)/shard_map/all_to_all | solution.py:280
  101.0 2.5 %shard_map.69 = bf16[16,128,128]{2,1,0:T(8,128)(2,1)} custom-call(bf16[16,128,128]{2,1,0:T(8,128)(2,1)} %all-to-all-done.2.arrived_ref, bf16[512,512]{1,0:T(8,128)(2,1)} %get-tuple-element.64.mix_ref), custom_call_target="tpu_custom_call" | custom-call | flops 268435456 | bytes 1572864 | tf_op jit(solution)/shard_map/pallas_call | solution.py:26
  103.5 0.0 collective-permute-done.8.r0
  103.5 0.0 collective-permute-done.9.r1
  103.5 0.0 collective-permute-done.10.r2
  103.5 0.0 collective-permute-done.11.r3
  103.5 3.8 %shard_map.70 = (bf16[16,128,128]{2,1,0:T(8,128)(2,1)}, bf16[3,128,128]{2,1,0:T(8,128)(2,1)}, bf16[3,128,128]{2,1,0:T(8,128)(2,1)}, bf16[3,128,128]{2,1,0:T(8,128)(2,1)}, bf16[3,128,128]{2,1,0:T(8,128)(2,1)}) custom-call(bf16[16,128,128]{2,1,0:T(8,128)(2,1)} %all-to-all-done.1.early_ref.field_ref, bf16[3,128,128]{2,1,0:T(8,128)(2,1)S(1)} %collective-permute-done.8.r0, ...), custom_call_target="tpu_custom_call" | custom-call | flops 335544320 | bytes 4469104 | tf_op jit(solution)/shard_map/pallas_call | solution.py:26
  107.3 6.4 %all-to-all-start.3 = ((bf16[16,128,128]{2,1,0:T(8,128)(2,1)}), bf16[16,128,128]{2,1,0:T(8,128)(2,1)}, u32[]{:S(2)}, u32[]{:S(2)}) async-start(bf16[16,128,128]{2,1,0:T(8,128)(2,1)} %shard_map.69), calls=%async_computation.3 | async-start | bytes 1048576 | tf_op jit(solution)/shard_map/all_to_all | solution.py:280
  113.7 1.9 %collective-permute-start.12 = (bf16[3,128,128]{2,1,0:T(8,128)(2,1)}, bf16[3,128,128]{2,1,0:T(8,128)(2,1)S(1)}, u32[]{:S(2)}, u32[]{:S(2)}) collective-permute-start(bf16[3,128,128]{2,1,0:T(8,128)(2,1)} %get-tuple-element.75), channel_id=1, source_target_pairs={{0,32},{16,48},{32,64},{48,80},{64,96},{80,112},{96,128},{112,144}... | collective-permute-start | bytes 294920 | tf_op jit(solution)/shard_map/ppermute | solution.py:276
  115.7 1.9 %collective-permute-start.13 = (bf16[3,128,128]{2,1,0:T(8,128)(2,1)}, bf16[3,128,128]{2,1,0:T(8,128)(2,1)S(1)}, u32[]{:S(2)}, u32[]{:S(2)}) collective-permute-start(bf16[3,128,128]{2,1,0:T(8,128)(2,1)} %get-tuple-element.76), channel_id=1, source_target_pairs={{0,16},{16,32},{32,48},{48,64},{64,80},{80,96},{96,112},{112,128},... | collective-permute-start | bytes 294920 | tf_op jit(solution)/shard_map/ppermute | solution.py:276
  117.6 6.7 %collective-permute-start.14 = (bf16[3,128,128]{2,1,0:T(8,128)(2,1)}, bf16[3,128,128]{2,1,0:T(8,128)(2,1)S(1)}, u32[]{:S(2)}, u32[]{:S(2)}) collective-permute-start(bf16[3,128,128]{2,1,0:T(8,128)(2,1)} %get-tuple-element.77), channel_id=1, source_target_pairs={{0,496},{16,0},{32,16},{48,32},{64,48},{80,64},{96,80},{112,96},{1... | collective-permute-start | bytes 294920 | tf_op jit(solution)/shard_map/ppermute | solution.py:276
  124.3 3.7 %collective-permute-start.15 = (bf16[3,128,128]{2,1,0:T(8,128)(2,1)}, bf16[3,128,128]{2,1,0:T(8,128)(2,1)S(1)}, u32[]{:S(2)}, u32[]{:S(2)}) collective-permute-start(bf16[3,128,128]{2,1,0:T(8,128)(2,1)} %get-tuple-element.78), channel_id=1, source_target_pairs={{0,480},{16,496},{32,0},{48,16},{64,32},{80,48},{96,64},{112,80},{... | collective-permute-start | bytes 294920 | tf_op jit(solution)/shard_map/ppermute | solution.py:276
  127.9 3.2 %all-to-all-done.3.late_ref = bf16[16,128,128]{2,1,0:T(8,128)(2,1)} async-done(((bf16[16,128,128]{2,1,0:T(8,128)(2,1)}), bf16[16,128,128]{2,1,0:T(8,128)(2,1)}, u32[]{:S(2)}, u32[]{:S(2)}) %all-to-all-start.3) | async-done | bytes 524320 | tf_op jit(solution)/shard_map/all_to_all | solution.py:280
  131.2 2.0 %shard_map.71._ = bf16[256,2048]{1,0:T(8,128)(2,1)} custom-call(bf16[16,128,128]{2,1,0:T(8,128)(2,1)} %all-to-all-done.3.late_ref), custom_call_target="tpu_custom_call" | custom-call | bytes 1572864 | tf_op jit(solution)/shard_map/pallas_call | solution.py:26
  133.1 0.0 collective-permute-done.12.r0
  133.1 0.0 collective-permute-done.13.r1
  133.2 0.0 collective-permute-done.14.r2
  133.2 0.0 collective-permute-done.15.r3
  133.2 3.8 %shard_map.72 = bf16[256,2048]{1,0:T(8,128)(2,1)} custom-call(bf16[16,128,128]{2,1,0:T(8,128)(2,1)} %all-to-all-done.1.early_ref.field_ref, bf16[3,128,128]{2,1,0:T(8,128)(2,1)S(1)} %collective-permute-done.12.r0, bf16[3,128,128]{2,1,0:T(8,128)(2,1)S(1)} %collective-permute-done.13.r1, ...), custom_call_target="tpu_custom_call", output_to_operand_aliasing={{}: (9, {})} | custom-call | flops 335544320 | bytes 6172992 | tf_op jit(solution)/shard_map/pallas_call | solution.py:26
  (3 shorter events, 0.0 us)
Async XLA Ops:
  0.0 13.4 %copy-start.3 = (s32[1,4,3]{1,0,2:T(1,128)S(1)}, s32[1,4,3]{1,0,2:T(1,128)}, u32[]{:S(2)}) copy-start(s32[1,4,3]{1,0,2:T(1,128)} %param.8) | copy-start | bytes 148
  0.0 13.5 %copy-start = (bf16[16,5,128,128]{3,2,1,0:T(8,128)(2,1)S(1)}, bf16[16,5,128,128]{3,2,1,0:T(8,128)(2,1)}, u32[]{:S(2)}) copy-start(bf16[16,5,128,128]{3,2,1,0:T(8,128)(2,1)} %weights_ref.9) | copy-start | bytes 7864324
  0.0 13.5 %copy-start.1 = (f32[3]{0:T(128)S(1)}, f32[3]{0:T(128)}, u32[]{:S(2)}) copy-start(f32[3]{0:T(128)} %coef_ref.1) | copy-start | bytes 40
  2.4 32.6 %copy-start.2 = (s32[16,5]{0,1:T(8,128)S(1)}, s32[16,5]{0,1:T(8,128)}, u32[]{:S(2)}) copy-start(s32[16,5]{0,1:T(8,128)} %param.9) | copy-start | bytes 964
  2.4 39.0 %all-to-all-start = ((bf16[16,256,128]{2,1,0:T(8,128)(2,1)}), bf16[16,256,128]{2,1,0:T(8,128)(2,1)}, u32[]{:S(2)}, u32[]{:S(2)}) async-start(bf16[16,256,128]{2,1,0:T(8,128)(2,1)} %shard_map.65), calls=%async_computation | async-start | bytes 2097152 | tf_op jit(solution)/shard_map/all_to_all | solution.py:280
  16.4 18.8 %collective-permute-start = (bf16[3,128,128]{2,1,0:T(8,128)(2,1)}, bf16[3,128,128]{2,1,0:T(8,128)(2,1)S(1)}, u32[]{:S(2)}, u32[]{:S(2)}) collective-permute-start(bf16[3,128,128]{2,1,0:T(8,128)(2,1)} %get-tuple-element.43), channel_id=1, source_target_pairs={{0,32},{16,48},{32,64},{48,80},{64,96},{80,112},{96,128},{112,144}... | collective-permute-start | bytes 294920 | tf_op jit(solution)/shard_map/ppermute | solution.py:276
  18.7 16.4 %collective-permute-start.1 = (bf16[3,128,128]{2,1,0:T(8,128)(2,1)}, bf16[3,128,128]{2,1,0:T(8,128)(2,1)S(1)}, u32[]{:S(2)}, u32[]{:S(2)}) collective-permute-start(bf16[3,128,128]{2,1,0:T(8,128)(2,1)} %get-tuple-element.44), channel_id=1, source_target_pairs={{0,16},{16,32},{32,48},{48,64},{64,80},{80,96},{96,112},{112,128},... | collective-permute-start | bytes 294920 | tf_op jit(solution)/shard_map/ppermute | solution.py:276
  20.9 14.2 %collective-permute-start.2 = (bf16[3,128,128]{2,1,0:T(8,128)(2,1)}, bf16[3,128,128]{2,1,0:T(8,128)(2,1)S(1)}, u32[]{:S(2)}, u32[]{:S(2)}) collective-permute-start(bf16[3,128,128]{2,1,0:T(8,128)(2,1)} %get-tuple-element.45), channel_id=1, source_target_pairs={{0,496},{16,0},{32,16},{48,32},{64,48},{80,64},{96,80},{112,96},{1... | collective-permute-start | bytes 294920 | tf_op jit(solution)/shard_map/ppermute | solution.py:276
  30.8 7.6 %collective-permute-start.3 = (bf16[3,128,128]{2,1,0:T(8,128)(2,1)}, bf16[3,128,128]{2,1,0:T(8,128)(2,1)S(1)}, u32[]{:S(2)}, u32[]{:S(2)}) collective-permute-start(bf16[3,128,128]{2,1,0:T(8,128)(2,1)} %get-tuple-element.46), channel_id=1, source_target_pairs={{0,480},{16,496},{32,0},{48,16},{64,32},{80,48},{96,64},{112,80},{... | collective-permute-start | bytes 294920 | tf_op jit(solution)/shard_map/ppermute | solution.py:276
  46.1 22.8 %all-to-all-start.1 = ((bf16[16,128,128]{2,1,0:T(8,128)(2,1)}), bf16[16,128,128]{2,1,0:T(8,128)(2,1)}, u32[]{:S(2)}, u32[]{:S(2)}) async-start(bf16[16,128,128]{2,1,0:T(8,128)(2,1)} %get-tuple-element.48), calls=%async_computation.1 | async-start | bytes 1048576 | tf_op jit(solution)/shard_map/all_to_all | solution.py:280
  51.2 20.2 %collective-permute-start.4 = (bf16[3,128,128]{2,1,0:T(8,128)(2,1)}, bf16[3,128,128]{2,1,0:T(8,128)(2,1)S(1)}, u32[]{:S(2)}, u32[]{:S(2)}) collective-permute-start(bf16[3,128,128]{2,1,0:T(8,128)(2,1)} %get-tuple-element.49), channel_id=1, source_target_pairs={{0,32},{16,48},{32,64},{48,80},{64,96},{80,112},{96,128},{112,144}... | collective-permute-start | bytes 294920 | tf_op jit(solution)/shard_map/ppermute | solution.py:276
  53.1 18.3 %collective-permute-start.5 = (bf16[3,128,128]{2,1,0:T(8,128)(2,1)}, bf16[3,128,128]{2,1,0:T(8,128)(2,1)S(1)}, u32[]{:S(2)}, u32[]{:S(2)}) collective-permute-start(bf16[3,128,128]{2,1,0:T(8,128)(2,1)} %get-tuple-element.50), channel_id=1, source_target_pairs={{0,16},{16,32},{32,48},{48,64},{64,80},{80,96},{96,112},{112,128},... | collective-permute-start | bytes 294920 | tf_op jit(solution)/shard_map/ppermute | solution.py:276
  55.0 16.4 %collective-permute-start.6 = (bf16[3,128,128]{2,1,0:T(8,128)(2,1)}, bf16[3,128,128]{2,1,0:T(8,128)(2,1)S(1)}, u32[]{:S(2)}, u32[]{:S(2)}) collective-permute-start(bf16[3,128,128]{2,1,0:T(8,128)(2,1)} %get-tuple-element.51), channel_id=1, source_target_pairs={{0,496},{16,0},{32,16},{48,32},{64,48},{80,64},{96,80},{112,96},{1... | collective-permute-start | bytes 294920 | tf_op jit(solution)/shard_map/ppermute | solution.py:276
  64.7 8.1 %collective-permute-start.7 = (bf16[3,128,128]{2,1,0:T(8,128)(2,1)}, bf16[3,128,128]{2,1,0:T(8,128)(2,1)S(1)}, u32[]{:S(2)}, u32[]{:S(2)}) collective-permute-start(bf16[3,128,128]{2,1,0:T(8,128)(2,1)} %get-tuple-element.52), channel_id=1, source_target_pairs={{0,480},{16,496},{32,0},{48,16},{64,32},{80,48},{96,64},{112,80},{... | collective-permute-start | bytes 294920 | tf_op jit(solution)/shard_map/ppermute | solution.py:276
  71.4 12.2 %copy-start.7 = (bf16[3,128,128]{2,1,0:T(8,128)(2,1)S(1)}, bf16[3,128,128]{2,1,0:T(8,128)(2,1)}, u32[]{:S(2)}) copy-start(bf16[3,128,128]{2,1,0:T(8,128)(2,1)} %get-tuple-element.67) | copy-start | bytes 294916
  71.4 14.1 %copy-start.6 = (bf16[3,128,128]{2,1,0:T(8,128)(2,1)S(1)}, bf16[3,128,128]{2,1,0:T(8,128)(2,1)}, u32[]{:S(2)}) copy-start(bf16[3,128,128]{2,1,0:T(8,128)(2,1)} %get-tuple-element.68) | copy-start | bytes 294916
  71.4 16.0 %copy-start.5 = (bf16[3,128,128]{2,1,0:T(8,128)(2,1)S(1)}, bf16[3,128,128]{2,1,0:T(8,128)(2,1)}, u32[]{:S(2)}) copy-start(bf16[3,128,128]{2,1,0:T(8,128)(2,1)} %get-tuple-element.69) | copy-start | bytes 294916
  71.4 22.7 %copy-start.4 = (bf16[3,128,128]{2,1,0:T(8,128)(2,1)S(1)}, bf16[3,128,128]{2,1,0:T(8,128)(2,1)}, u32[]{:S(2)}) copy-start(bf16[3,128,128]{2,1,0:T(8,128)(2,1)} %get-tuple-element.70) | copy-start | bytes 294916
  76.6 24.4 %all-to-all-start.2 = ((bf16[16,128,128]{2,1,0:T(8,128)(2,1)}), bf16[16,128,128]{2,1,0:T(8,128)(2,1)}, u32[]{:S(2)}, u32[]{:S(2)}) async-start(bf16[16,128,128]{2,1,0:T(8,128)(2,1)} %shard_map.68), calls=%async_computation.2 | async-start | bytes 1048576 | tf_op jit(solution)/shard_map/all_to_all | solution.py:280
  83.6 19.9 %collective-permute-start.8 = (bf16[3,128,128]{2,1,0:T(8,128)(2,1)S(1)}, bf16[3,128,128]{2,1,0:T(8,128)(2,1)S(1)}, u32[]{:S(2)}, u32[]{:S(2)}) collective-permute-start(bf16[3,128,128]{2,1,0:T(8,128)(2,1)S(1)} %copy-done.7), channel_id=1, source_target_pairs={{0,32},{16,48},{32,64},{48,80},{64,96},{80,112},{96,128},{112,144}... | collective-permute-start | bytes 294920 | tf_op jit(solution)/shard_map/ppermute | solution.py:276
  85.5 18.0 %collective-permute-start.9 = (bf16[3,128,128]{2,1,0:T(8,128)(2,1)S(1)}, bf16[3,128,128]{2,1,0:T(8,128)(2,1)S(1)}, u32[]{:S(2)}, u32[]{:S(2)}) collective-permute-start(bf16[3,128,128]{2,1,0:T(8,128)(2,1)S(1)} %copy-done.6), channel_id=1, source_target_pairs={{0,16},{16,32},{32,48},{48,64},{64,80},{80,96},{96,112},{112,128},... | collective-permute-start | bytes 294920 | tf_op jit(solution)/shard_map/ppermute | solution.py:276
  87.4 16.1 %collective-permute-start.10 = (bf16[3,128,128]{2,1,0:T(8,128)(2,1)S(1)}, bf16[3,128,128]{2,1,0:T(8,128)(2,1)S(1)}, u32[]{:S(2)}, u32[]{:S(2)}) collective-permute-start(bf16[3,128,128]{2,1,0:T(8,128)(2,1)S(1)} %copy-done.5), channel_id=1, source_target_pairs={{0,496},{16,0},{32,16},{48,32},{64,48},{80,64},{96,80},{112,96},{1... | collective-permute-start | bytes 294920 | tf_op jit(solution)/shard_map/ppermute | solution.py:276
  94.1 9.4 %collective-permute-start.11 = (bf16[3,128,128]{2,1,0:T(8,128)(2,1)S(1)}, bf16[3,128,128]{2,1,0:T(8,128)(2,1)S(1)}, u32[]{:S(2)}, u32[]{:S(2)}) collective-permute-start(bf16[3,128,128]{2,1,0:T(8,128)(2,1)S(1)} %copy-done.4), channel_id=1, source_target_pairs={{0,480},{16,496},{32,0},{48,16},{64,32},{80,48},{96,64},{112,80},{... | collective-permute-start | bytes 294920 | tf_op jit(solution)/shard_map/ppermute | solution.py:276
  107.3 23.8 %all-to-all-start.3 = ((bf16[16,128,128]{2,1,0:T(8,128)(2,1)}), bf16[16,128,128]{2,1,0:T(8,128)(2,1)}, u32[]{:S(2)}, u32[]{:S(2)}) async-start(bf16[16,128,128]{2,1,0:T(8,128)(2,1)} %shard_map.69), calls=%async_computation.3 | async-start | bytes 1048576 | tf_op jit(solution)/shard_map/all_to_all | solution.py:280
  113.7 19.4 %collective-permute-start.12 = (bf16[3,128,128]{2,1,0:T(8,128)(2,1)}, bf16[3,128,128]{2,1,0:T(8,128)(2,1)S(1)}, u32[]{:S(2)}, u32[]{:S(2)}) collective-permute-start(bf16[3,128,128]{2,1,0:T(8,128)(2,1)} %get-tuple-element.75), channel_id=1, source_target_pairs={{0,32},{16,48},{32,64},{48,80},{64,96},{80,112},{96,128},{112,144}... | collective-permute-start | bytes 294920 | tf_op jit(solution)/shard_map/ppermute | solution.py:276
  115.7 17.5 %collective-permute-start.13 = (bf16[3,128,128]{2,1,0:T(8,128)(2,1)}, bf16[3,128,128]{2,1,0:T(8,128)(2,1)S(1)}, u32[]{:S(2)}, u32[]{:S(2)}) collective-permute-start(bf16[3,128,128]{2,1,0:T(8,128)(2,1)} %get-tuple-element.76), channel_id=1, source_target_pairs={{0,16},{16,32},{32,48},{48,64},{64,80},{80,96},{96,112},{112,128},... | collective-permute-start | bytes 294920 | tf_op jit(solution)/shard_map/ppermute | solution.py:276
  117.6 15.6 %collective-permute-start.14 = (bf16[3,128,128]{2,1,0:T(8,128)(2,1)}, bf16[3,128,128]{2,1,0:T(8,128)(2,1)S(1)}, u32[]{:S(2)}, u32[]{:S(2)}) collective-permute-start(bf16[3,128,128]{2,1,0:T(8,128)(2,1)} %get-tuple-element.77), channel_id=1, source_target_pairs={{0,496},{16,0},{32,16},{48,32},{64,48},{80,64},{96,80},{112,96},{1... | collective-permute-start | bytes 294920 | tf_op jit(solution)/shard_map/ppermute | solution.py:276
  124.3 8.9 %collective-permute-start.15 = (bf16[3,128,128]{2,1,0:T(8,128)(2,1)}, bf16[3,128,128]{2,1,0:T(8,128)(2,1)S(1)}, u32[]{:S(2)}, u32[]{:S(2)}) collective-permute-start(bf16[3,128,128]{2,1,0:T(8,128)(2,1)} %get-tuple-element.78), channel_id=1, source_target_pairs={{0,480},{16,496},{32,0},{48,16},{64,32},{80,48},{96,64},{112,80},{... | collective-permute-start | bytes 294920 | tf_op jit(solution)/shard_map/ppermute | solution.py:276

commit v9 on v8

--- a/solution.py
+++ b/solution.py
@@ -50,6 +50,11 @@
         copy.wait()
 
 
+def ended(g, count):
+    size = count // 2
+    return slice(g + 1 - size, g + 1) if (g + 1) % size == 0 else None
+
+
 def times_transposed(a, b):
     return lax.dot_general(a, b, (((1,), (1,)), ((), ())), preferred_element_type=F32)
 
@@ -86,22 +91,22 @@
     return copies
 
 
-def lay_out(signal_ref, kernel_ref, out_ref, held, mix, in_sems, out_sems, mix_sem):
-    owners, chunk, width = out_ref.shape
+def lay_out(signal_ref, kernel_ref, out_ref, field, held, mix, sems):
+    owners, _, width = out_ref.shape
     t_loc, time = kernel_ref.shape
-    rows = chunk - time * t_loc // width
-    mixing = start(kernel_ref, mix, mix_sem)
-    loads = [
-        start(signal_ref.at[:rows, i * width : (i + 1) * width], held.at[i, :rows], in_sems.at[i])
-        for i in range(owners)
-    ]
+    rows = field.shape[0]
+    mixing = start(kernel_ref, mix, sems.at[0])
+    load = start(signal_ref.at[:rows], field, sems.at[1])
     mixing.wait()
-    copies = []
     for i in range(owners):
         for q in range(time // width):
             held[i, rows + q * t_loc : rows + (q + 1) * t_loc] = mix[:, q * width : (q + 1) * width]
-        loads[i].wait()
-        copies.append(start(held.at[i], out_ref.at[i], out_sems.at[i]))
+    load.wait()
+    copies = []
+    for i in range(owners):
+        held[i, :rows] = field[:, i * width : (i + 1) * width]
+        if part := ended(i, owners):
+            copies.append(start(held.at[part], out_ref.at[part], sems.at[len(copies)]))
     wait(copies)
 
 
@@ -151,7 +156,8 @@
     for g in range(blocks):
         total = block_product(g, col_ref, weights_ref, source)
         term[g] = (-inv_ref[g : g + 1, :] * total).astype(BF16)
-        copies.append(start(term.at[g], term_ref.at[g], sems.at[g]))
+        if part := ended(g, blocks):
+            copies.append(start(term.at[part], term_ref.at[part], sems.at[len(copies)]))
     return copies + pack(send_ref, term, inv_ref, packs, held, pack_sems)
 
 
@@ -201,12 +207,12 @@
     *scratch, field, columns, mixed, mix, arrived, load_sems, out_sems = rest[len(OFFSETS) + 2 :]
     owners, rows, width = out_ref.shape
     load = start(signal_ref.at[rows:], field, load_sems.at[0])
-    loads = [start(arrived_ref.at[i], arrived.at[i], load_sems.at[2 + i]) for i in range(owners)]
+    load_arrived = start(arrived_ref, arrived, load_sems.at[2])
     copies = product_one(
         field, (r0, r1, r2, r3), weights_ref, inv_ref, col_ref, send_ref, term_ref, packs, scratch, [load]
     )
+    load_arrived.wait()
     for i in range(owners):
-        loads[i].wait()
         for q in range(mix.shape[1] // width):
             mix[i * t_loc : (i + 1) * t_loc, q * width : (q + 1) * width] = arrived[
                 i, rows + q * t_loc : rows + (q + 1) * t_loc
@@ -313,7 +319,7 @@
         lay_out,
         [(array(owners, chunk, width), HBM)],
         [(xs, HBM), (kernel, HBM)],
-        [vm((owners, chunk, width), BF16), vm(kernel.shape, BF16), DMA((owners,)), DMA((owners,)), DMA],
+        [side_by_side, vm((owners, chunk, width), BF16), vm(kernel.shape, BF16), DMA((2,))],
     )
     arrived = exchange(laid)
     inv, *packs = call(
@@ -327,7 +333,7 @@
         functools.partial(rear_one, t_loc),
         [(field, HBM), *packed, (field, HBM), (array(time, time), HBM)],
         [*operands(xs, packs, inv), (send_list, SMEM), (arrived, HBM)],
-        [*scratch_one, side_by_side, columns, whole, square, vm(laid.shape, BF16), DMA((2 + owners,)), DMA((pieces,))],
+        [*scratch_one, side_by_side, columns, whole, square, vm(laid.shape, BF16), DMA((3,)), DMA((pieces,))],
         flops=work + mixing,
     )
     early = exchange(early)

time: 138 us -> 138 us (level)
  no operation moved by 1% of the time
where the time goes in v9:
time: 138 us; the launch traced here: 137 us
  starting transfers between devices  94.1 us (68%)
  Pallas kernels  27.9 us (20%)
  waiting for transfers between devices  14.1 us (10%)
    ppermute x16, starting transfers between devices, swap(): lax.ppermute(block, 'dom', partners(i, count))  64.7 us
    all_to_all x4, starting transfers between devices, exchange(): return lax.all_to_all(field, 'tm', split_axis=0, concat_axis=0, tiled=True)  29.4 us
    pallas_call x9, Pallas kernels, call(): pl.pallas_call(kernel, out_shape=shapes, in_specs=specs, out_specs=result...  27.9 us
    all_to_all x4, waiting for transfers between devices, exchange(): return lax.all_to_all(field, 'tm', split_axis=0, concat_axis=0, tiled=True)  9.46 us
    ppermute x16, waiting for transfers between devices, swap(): lax.ppermute(block, 'dom', partners(i, count))  4.66 us
  transfers between devices with their start and end apart: 20, of which 5 were waited for; matrix products, arithmetic and copies ran while one was open for 0% of the time, Pallas kernels for 7%

profile of v9, /device:TPU:1, one launch (start us, length us, event | category | flops | bytes accessed | tf_op | source)
XLA Modules:
  0.0 136.7 jit_solution(5170912856585002841)
XLA Ops:
  0.0 2.2 %shard_map.65 = bf16[16,256,128]{2,1,0:T(8,128)(2,1)} custom-call(bf16[256,2048]{1,0:T(8,128)(2,1)} %bitcast.2, bf16[32,512]{1,0:T(8,128)(2,1)} %kernel_ref.1), custom_call_target="tpu_custom_call" | custom-call | bytes 2129920 | tf_op jit(solution)/shard_map/pallas_call | solution.py:26
  2.3 0.0 copy-start.2
  2.3 10.9 %all-to-all-start = ((bf16[16,256,128]{2,1,0:T(8,128)(2,1)}), bf16[16,256,128]{2,1,0:T(8,128)(2,1)}, u32[]{:S(2)}, u32[]{:S(2)}) async-start(bf16[16,256,128]{2,1,0:T(8,128)(2,1)} %shard_map.65), calls=%async_computation | async-start | bytes 2097152 | tf_op jit(solution)/shard_map/all_to_all | solution.py:286
  13.2 0.0 copy-done.3
  13.2 0.1 copy.8.send_ref
  13.3 0.0 copy-done
  13.3 0.0 copy-done.1
  13.3 2.9 %shard_map.64 = (f32[24,128]{1,0:T(8,128)S(1)}, bf16[3,128,128]{2,1,0:T(8,128)(2,1)}, bf16[3,128,128]{2,1,0:T(8,128)(2,1)}, bf16[3,128,128]{2,1,0:T(8,128)(2,1)}, bf16[3,128,128]{2,1,0:T(8,128)(2,1)}) custom-call(bf16[256,2048]{1,0:T(8,128)(2,1)} %bitcast.3, bf16[16,5,128,128]{3,2,1,0:T(8,128)(2,1)S(1)} %copy-done, s32[1,4,3]{2,1,0:T(4,128)S(1)} %copy.8.send_ref, ...), custom_call_target="tpu_custom_call" | custom-call | flops 41943040 | bytes 4075580 | tf_op jit(solution)/shard_map/pallas_call | solution.py:26
  16.2 2.3 %collective-permute-start = (bf16[3,128,128]{2,1,0:T(8,128)(2,1)}, bf16[3,128,128]{2,1,0:T(8,128)(2,1)S(1)}, u32[]{:S(2)}, u32[]{:S(2)}) collective-permute-start(bf16[3,128,128]{2,1,0:T(8,128)(2,1)} %get-tuple-element.43), channel_id=1, source_target_pairs={{0,32},{16,48},{32,64},{48,80},{64,96},{80,112},{96,128},{112,144}... | collective-permute-start | bytes 294920 | tf_op jit(solution)/shard_map/ppermute | solution.py:282
  18.5 2.2 %collective-permute-start.1 = (bf16[3,128,128]{2,1,0:T(8,128)(2,1)}, bf16[3,128,128]{2,1,0:T(8,128)(2,1)S(1)}, u32[]{:S(2)}, u32[]{:S(2)}) collective-permute-start(bf16[3,128,128]{2,1,0:T(8,128)(2,1)} %get-tuple-element.44), channel_id=1, source_target_pairs={{0,16},{16,32},{32,48},{48,64},{64,80},{80,96},{96,112},{112,128},... | collective-permute-start | bytes 294920 | tf_op jit(solution)/shard_map/ppermute | solution.py:282
  20.8 9.8 %collective-permute-start.2 = (bf16[3,128,128]{2,1,0:T(8,128)(2,1)}, bf16[3,128,128]{2,1,0:T(8,128)(2,1)S(1)}, u32[]{:S(2)}, u32[]{:S(2)}) collective-permute-start(bf16[3,128,128]{2,1,0:T(8,128)(2,1)} %get-tuple-element.45), channel_id=1, source_target_pairs={{0,496},{16,0},{32,16},{48,32},{64,48},{80,64},{96,80},{112,96},{1... | collective-permute-start | bytes 294920 | tf_op jit(solution)/shard_map/ppermute | solution.py:282
  30.6 4.3 %collective-permute-start.3 = (bf16[3,128,128]{2,1,0:T(8,128)(2,1)}, bf16[3,128,128]{2,1,0:T(8,128)(2,1)S(1)}, u32[]{:S(2)}, u32[]{:S(2)}) collective-permute-start(bf16[3,128,128]{2,1,0:T(8,128)(2,1)} %get-tuple-element.46), channel_id=1, source_target_pairs={{0,480},{16,496},{32,0},{48,16},{64,32},{80,48},{96,64},{112,80},{... | collective-permute-start | bytes 294920 | tf_op jit(solution)/shard_map/ppermute | solution.py:282
  34.9 0.0 copy-done.2
  34.9 0.1 copy.9.col_ref
  35.0 0.0 collective-permute-done.r0
  35.0 0.0 collective-permute-done.1.r1
  35.0 0.0 collective-permute-done.2.r2
  35.0 3.3 %collective-permute-done.3.r3 = bf16[3,128,128]{2,1,0:T(8,128)(2,1)S(1)} collective-permute-done((bf16[3,128,128]{2,1,0:T(8,128)(2,1)}, bf16[3,128,128]{2,1,0:T(8,128)(2,1)S(1)}, u32[]{:S(2)}, u32[]{:S(2)}) %collective-permute-start.3) | collective-permute-done | bytes 98336 | tf_op jit(solution)/shard_map/ppermute | solution.py:282
  38.3 3.0 %all-to-all-done.arrived_ref = bf16[16,256,128]{2,1,0:T(8,128)(2,1)} async-done(((bf16[16,256,128]{2,1,0:T(8,128)(2,1)}), bf16[16,256,128]{2,1,0:T(8,128)(2,1)}, u32[]{:S(2)}, u32[]{:S(2)}) %all-to-all-start) | async-done | bytes 1048608 | tf_op jit(solution)/shard_map/all_to_all | solution.py:286
  41.3 4.4 %shard_map.66 = (bf16[16,128,128]{2,1,0:T(8,128)(2,1)}, bf16[3,128,128]{2,1,0:T(8,128)(2,1)}, bf16[3,128,128]{2,1,0:T(8,128)(2,1)}, bf16[3,128,128]{2,1,0:T(8,12...) custom-call(bf16[256,2048]{1,0:T(8,128)(2,1)} %bitcast.4, ...), custom_call_target="tpu_custom_call" | custom-call | flops 603979776 | bytes 7090544 | tf_op jit(solution)/shard_map/pallas_call | solution.py:26
  45.7 5.0 %all-to-all-start.1 = ((bf16[16,128,128]{2,1,0:T(8,128)(2,1)}), bf16[16,128,128]{2,1,0:T(8,128)(2,1)}, u32[]{:S(2)}, u32[]{:S(2)}) async-start(bf16[16,128,128]{2,1,0:T(8,128)(2,1)} %get-tuple-element.48), calls=%async_computation.1 | async-start | bytes 1048576 | tf_op jit(solution)/shard_map/all_to_all | solution.py:286
  50.8 1.9 %collective-permute-start.4 = (bf16[3,128,128]{2,1,0:T(8,128)(2,1)}, bf16[3,128,128]{2,1,0:T(8,128)(2,1)S(1)}, u32[]{:S(2)}, u32[]{:S(2)}) collective-permute-start(bf16[3,128,128]{2,1,0:T(8,128)(2,1)} %get-tuple-element.49), channel_id=1, source_target_pairs={{0,32},{16,48},{32,64},{48,80},{64,96},{80,112},{96,128},{112,144}... | collective-permute-start | bytes 294920 | tf_op jit(solution)/shard_map/ppermute | solution.py:282
  52.7 1.9 %collective-permute-start.5 = (bf16[3,128,128]{2,1,0:T(8,128)(2,1)}, bf16[3,128,128]{2,1,0:T(8,128)(2,1)S(1)}, u32[]{:S(2)}, u32[]{:S(2)}) collective-permute-start(bf16[3,128,128]{2,1,0:T(8,128)(2,1)} %get-tuple-element.50), channel_id=1, source_target_pairs={{0,16},{16,32},{32,48},{48,64},{64,80},{80,96},{96,112},{112,128},... | collective-permute-start | bytes 294920 | tf_op jit(solution)/shard_map/ppermute | solution.py:282
  54.6 9.6 %collective-permute-start.6 = (bf16[3,128,128]{2,1,0:T(8,128)(2,1)}, bf16[3,128,128]{2,1,0:T(8,128)(2,1)S(1)}, u32[]{:S(2)}, u32[]{:S(2)}) collective-permute-start(bf16[3,128,128]{2,1,0:T(8,128)(2,1)} %get-tuple-element.51), channel_id=1, source_target_pairs={{0,496},{16,0},{32,16},{48,32},{64,48},{80,64},{96,80},{112,96},{1... | collective-permute-start | bytes 294920 | tf_op jit(solution)/shard_map/ppermute | solution.py:282
  64.3 4.3 %collective-permute-start.7 = (bf16[3,128,128]{2,1,0:T(8,128)(2,1)}, bf16[3,128,128]{2,1,0:T(8,128)(2,1)S(1)}, u32[]{:S(2)}, u32[]{:S(2)}) collective-permute-start(bf16[3,128,128]{2,1,0:T(8,128)(2,1)} %get-tuple-element.52), channel_id=1, source_target_pairs={{0,480},{16,496},{32,0},{48,16},{64,32},{80,48},{96,64},{112,80},{... | collective-permute-start | bytes 294920 | tf_op jit(solution)/shard_map/ppermute | solution.py:282
  68.5 0.0 all-to-all-done.1.early_ref.field_ref
  68.6 2.4 %shard_map.67 = (bf16[3,128,128]{2,1,0:T(8,128)(2,1)}, bf16[3,128,128]{2,1,0:T(8,128)(2,1)}, bf16[3,128,128]{2,1,0:T(8,128)(2,1)}, bf16[3,128,128]{2,1,0:T(8,128)(2,1)}) custom-call(bf16[16,128,128]{2,1,0:T(8,128)(2,1)} %all-to-all-done.1.early_ref.field_ref, f32[24,128]{1,0:T(8,128)S(1)} %get-tuple-element.47.inv_ref, s32[1,4,3]{2,1,0:T(4,128)S(1)} %copy.8.send_ref), custom_call_target="tpu_custom_call" | custom-call | bytes 929840 | tf_op jit(solution)/shard_map/pallas_call | solution.py:26
  71.0 0.0 copy-start.7
  71.0 0.0 copy-start.6
  71.0 0.0 copy-start.5
  71.0 0.0 copy-start.4
  71.0 0.0 collective-permute-done.4.r0
  71.0 0.0 collective-permute-done.5.r1
  71.0 0.0 collective-permute-done.6.r2
  71.1 1.4 collective-permute-done.7.r3
  72.4 3.8 %shard_map.68 = bf16[16,128,128]{2,1,0:T(8,128)(2,1)} custom-call(bf16[256,2048]{1,0:T(8,128)(2,1)} %bitcast.5, bf16[3,128,128]{2,1,0:T(8,128)(2,1)S(1)} %collective-permute-done.4.r0, bf16[3,128,128]{2,1,0:T(8,128)(2,1)S(1)} %collective-permute-done.5.r1, bf16[3,128,128]{2,1,0:T(8,128)(2,1)S(1)} %collective-permute-done.6.r2, ...), custom_call_target="tpu_custom_call" | custom-call | flops 335544320 | bytes 5124416 | tf_op jit(solution)/shard_map/pallas_call | solution.py:26
  76.2 7.0 %all-to-all-start.2 = ((bf16[16,128,128]{2,1,0:T(8,128)(2,1)}), bf16[16,128,128]{2,1,0:T(8,128)(2,1)}, u32[]{:S(2)}, u32[]{:S(2)}) async-start(bf16[16,128,128]{2,1,0:T(8,128)(2,1)} %shard_map.68), calls=%async_computation.2 | async-start | bytes 1048576 | tf_op jit(solution)/shard_map/all_to_all | solution.py:286
  83.2 0.0 copy-done.7
  83.2 1.9 %collective-permute-start.8 = (bf16[3,128,128]{2,1,0:T(8,128)(2,1)S(1)}, bf16[3,128,128]{2,1,0:T(8,128)(2,1)S(1)}, u32[]{:S(2)}, u32[]{:S(2)}) collective-permute-start(bf16[3,128,128]{2,1,0:T(8,128)(2,1)S(1)} %copy-done.7), channel_id=1, source_target_pairs={{0,32},{16,48},{32,64},{48,80},{64,96},{80,112},{96,128},{112,144}... | collective-permute-start | bytes 294920 | tf_op jit(solution)/shard_map/ppermute | solution.py:282
  85.1 0.0 copy-done.6
  85.1 1.9 %collective-permute-start.9 = (bf16[3,128,128]{2,1,0:T(8,128)(2,1)S(1)}, bf16[3,128,128]{2,1,0:T(8,128)(2,1)S(1)}, u32[]{:S(2)}, u32[]{:S(2)}) collective-permute-start(bf16[3,128,128]{2,1,0:T(8,128)(2,1)S(1)} %copy-done.6), channel_id=1, source_target_pairs={{0,16},{16,32},{32,48},{48,64},{64,80},{80,96},{96,112},{112,128},... | collective-permute-start | bytes 294920 | tf_op jit(solution)/shard_map/ppermute | solution.py:282
  87.0 0.0 copy-done.5
  87.0 6.7 %collective-permute-start.10 = (bf16[3,128,128]{2,1,0:T(8,128)(2,1)S(1)}, bf16[3,128,128]{2,1,0:T(8,128)(2,1)S(1)}, u32[]{:S(2)}, u32[]{:S(2)}) collective-permute-start(bf16[3,128,128]{2,1,0:T(8,128)(2,1)S(1)} %copy-done.5), channel_id=1, source_target_pairs={{0,496},{16,0},{32,16},{48,32},{64,48},{80,64},{96,80},{112,96},{1... | collective-permute-start | bytes 294920 | tf_op jit(solution)/shard_map/ppermute | solution.py:282
  93.7 0.0 copy-done.4
  93.7 3.7 %collective-permute-start.11 = (bf16[3,128,128]{2,1,0:T(8,128)(2,1)S(1)}, bf16[3,128,128]{2,1,0:T(8,128)(2,1)S(1)}, u32[]{:S(2)}, u32[]{:S(2)}) collective-permute-start(bf16[3,128,128]{2,1,0:T(8,128)(2,1)S(1)} %copy-done.4), channel_id=1, source_target_pairs={{0,480},{16,496},{32,0},{48,16},{64,32},{80,48},{96,64},{112,80},{... | collective-permute-start | bytes 294920 | tf_op jit(solution)/shard_map/ppermute | solution.py:282
  97.4 3.2 %all-to-all-done.2.arrived_ref = bf16[16,128,128]{2,1,0:T(8,128)(2,1)} async-done(((bf16[16,128,128]{2,1,0:T(8,128)(2,1)}), bf16[16,128,128]{2,1,0:T(8,128)(2,1)}, u32[]{:S(2)}, u32[]{:S(2)}) %all-to-all-start.2) | async-done | bytes 524320 | tf_op jit(solution)/shard_map/all_to_all | solution.py:286
  100.6 2.5 %shard_map.69 = bf16[16,128,128]{2,1,0:T(8,128)(2,1)} custom-call(bf16[16,128,128]{2,1,0:T(8,128)(2,1)} %all-to-all-done.2.arrived_ref, bf16[512,512]{1,0:T(8,128)(2,1)} %get-tuple-element.64.mix_ref), custom_call_target="tpu_custom_call" | custom-call | flops 268435456 | bytes 1572864 | tf_op jit(solution)/shard_map/pallas_call | solution.py:26
  103.1 0.0 collective-permute-done.8.r0
  103.1 0.0 collective-permute-done.9.r1
  103.1 0.0 collective-permute-done.10.r2
  103.1 0.0 collective-permute-done.11.r3
  103.1 3.9 %shard_map.70 = (bf16[16,128,128]{2,1,0:T(8,128)(2,1)}, bf16[3,128,128]{2,1,0:T(8,128)(2,1)}, bf16[3,128,128]{2,1,0:T(8,128)(2,1)}, bf16[3,128,128]{2,1,0:T(8,128)(2,1)}, bf16[3,128,128]{2,1,0:T(8,128)(2,1)}) custom-call(bf16[16,128,128]{2,1,0:T(8,128)(2,1)} %all-to-all-done.1.early_ref.field_ref, bf16[3,128,128]{2,1,0:T(8,128)(2,1)S(1)} %collective-permute-done.8.r0, ...), custom_call_target="tpu_custom_call" | custom-call | flops 335544320 | bytes 4469104 | tf_op jit(solution)/shard_map/pallas_call | solution.py:26
  107.0 6.4 %all-to-all-start.3 = ((bf16[16,128,128]{2,1,0:T(8,128)(2,1)}), bf16[16,128,128]{2,1,0:T(8,128)(2,1)}, u32[]{:S(2)}, u32[]{:S(2)}) async-start(bf16[16,128,128]{2,1,0:T(8,128)(2,1)} %shard_map.69), calls=%async_computation.3 | async-start | bytes 1048576 | tf_op jit(solution)/shard_map/all_to_all | solution.py:286
  113.4 1.9 %collective-permute-start.12 = (bf16[3,128,128]{2,1,0:T(8,128)(2,1)}, bf16[3,128,128]{2,1,0:T(8,128)(2,1)S(1)}, u32[]{:S(2)}, u32[]{:S(2)}) collective-permute-start(bf16[3,128,128]{2,1,0:T(8,128)(2,1)} %get-tuple-element.75), channel_id=1, source_target_pairs={{0,32},{16,48},{32,64},{48,80},{64,96},{80,112},{96,128},{112,144}... | collective-permute-start | bytes 294920 | tf_op jit(solution)/shard_map/ppermute | solution.py:282
  115.3 1.9 %collective-permute-start.13 = (bf16[3,128,128]{2,1,0:T(8,128)(2,1)}, bf16[3,128,128]{2,1,0:T(8,128)(2,1)S(1)}, u32[]{:S(2)}, u32[]{:S(2)}) collective-permute-start(bf16[3,128,128]{2,1,0:T(8,128)(2,1)} %get-tuple-element.76), channel_id=1, source_target_pairs={{0,16},{16,32},{32,48},{48,64},{64,80},{80,96},{96,112},{112,128},... | collective-permute-start | bytes 294920 | tf_op jit(solution)/shard_map/ppermute | solution.py:282
  117.3 6.7 %collective-permute-start.14 = (bf16[3,128,128]{2,1,0:T(8,128)(2,1)}, bf16[3,128,128]{2,1,0:T(8,128)(2,1)S(1)}, u32[]{:S(2)}, u32[]{:S(2)}) collective-permute-start(bf16[3,128,128]{2,1,0:T(8,128)(2,1)} %get-tuple-element.77), channel_id=1, source_target_pairs={{0,496},{16,0},{32,16},{48,32},{64,48},{80,64},{96,80},{112,96},{1... | collective-permute-start | bytes 294920 | tf_op jit(solution)/shard_map/ppermute | solution.py:282
  124.0 3.7 %collective-permute-start.15 = (bf16[3,128,128]{2,1,0:T(8,128)(2,1)}, bf16[3,128,128]{2,1,0:T(8,128)(2,1)S(1)}, u32[]{:S(2)}, u32[]{:S(2)}) collective-permute-start(bf16[3,128,128]{2,1,0:T(8,128)(2,1)} %get-tuple-element.78), channel_id=1, source_target_pairs={{0,480},{16,496},{32,0},{48,16},{64,32},{80,48},{96,64},{112,80},{... | collective-permute-start | bytes 294920 | tf_op jit(solution)/shard_map/ppermute | solution.py:282
  127.6 3.2 %all-to-all-done.3.late_ref = bf16[16,128,128]{2,1,0:T(8,128)(2,1)} async-done(((bf16[16,128,128]{2,1,0:T(8,128)(2,1)}), bf16[16,128,128]{2,1,0:T(8,128)(2,1)}, u32[]{:S(2)}, u32[]{:S(2)}) %all-to-all-start.3) | async-done | bytes 524320 | tf_op jit(solution)/shard_map/all_to_all | solution.py:286
  130.9 2.0 %shard_map.71._ = bf16[256,2048]{1,0:T(8,128)(2,1)} custom-call(bf16[16,128,128]{2,1,0:T(8,128)(2,1)} %all-to-all-done.3.late_ref), custom_call_target="tpu_custom_call" | custom-call | bytes 1572864 | tf_op jit(solution)/shard_map/pallas_call | solution.py:26
  132.8 0.0 collective-permute-done.12.r0
  132.8 0.0 collective-permute-done.13.r1
  132.9 0.0 collective-permute-done.14.r2
  132.9 0.0 collective-permute-done.15.r3
  132.9 3.8 %shard_map.72 = bf16[256,2048]{1,0:T(8,128)(2,1)} custom-call(bf16[16,128,128]{2,1,0:T(8,128)(2,1)} %all-to-all-done.1.early_ref.field_ref, bf16[3,128,128]{2,1,0:T(8,128)(2,1)S(1)} %collective-permute-done.12.r0, bf16[3,128,128]{2,1,0:T(8,128)(2,1)S(1)} %collective-permute-done.13.r1, ...), custom_call_target="tpu_custom_call", output_to_operand_aliasing={{}: (9, {})} | custom-call | flops 335544320 | bytes 6172992 | tf_op jit(solution)/shard_map/pallas_call | solution.py:26
  (3 shorter events, 0.0 us)
Async XLA Ops:
  0.0 13.2 %copy-start.3 = (s32[1,4,3]{1,0,2:T(1,128)S(1)}, s32[1,4,3]{1,0,2:T(1,128)}, u32[]{:S(2)}) copy-start(s32[1,4,3]{1,0,2:T(1,128)} %param.8) | copy-start | bytes 148
  0.0 13.3 %copy-start = (bf16[16,5,128,128]{3,2,1,0:T(8,128)(2,1)S(1)}, bf16[16,5,128,128]{3,2,1,0:T(8,128)(2,1)}, u32[]{:S(2)}) copy-start(bf16[16,5,128,128]{3,2,1,0:T(8,128)(2,1)} %weights_ref.9) | copy-start | bytes 7864324
  0.0 13.3 %copy-start.1 = (f32[3]{0:T(128)S(1)}, f32[3]{0:T(128)}, u32[]{:S(2)}) copy-start(f32[3]{0:T(128)} %coef_ref.1) | copy-start | bytes 40
  2.3 32.6 %copy-start.2 = (s32[16,5]{0,1:T(8,128)S(1)}, s32[16,5]{0,1:T(8,128)}, u32[]{:S(2)}) copy-start(s32[16,5]{0,1:T(8,128)} %param.9) | copy-start | bytes 964
  2.3 39.0 %all-to-all-start = ((bf16[16,256,128]{2,1,0:T(8,128)(2,1)}), bf16[16,256,128]{2,1,0:T(8,128)(2,1)}, u32[]{:S(2)}, u32[]{:S(2)}) async-start(bf16[16,256,128]{2,1,0:T(8,128)(2,1)} %shard_map.65), calls=%async_computation | async-start | bytes 2097152 | tf_op jit(solution)/shard_map/all_to_all | solution.py:286
  16.2 18.8 %collective-permute-start = (bf16[3,128,128]{2,1,0:T(8,128)(2,1)}, bf16[3,128,128]{2,1,0:T(8,128)(2,1)S(1)}, u32[]{:S(2)}, u32[]{:S(2)}) collective-permute-start(bf16[3,128,128]{2,1,0:T(8,128)(2,1)} %get-tuple-element.43), channel_id=1, source_target_pairs={{0,32},{16,48},{32,64},{48,80},{64,96},{80,112},{96,128},{112,144}... | collective-permute-start | bytes 294920 | tf_op jit(solution)/shard_map/ppermute | solution.py:282
  18.5 16.4 %collective-permute-start.1 = (bf16[3,128,128]{2,1,0:T(8,128)(2,1)}, bf16[3,128,128]{2,1,0:T(8,128)(2,1)S(1)}, u32[]{:S(2)}, u32[]{:S(2)}) collective-permute-start(bf16[3,128,128]{2,1,0:T(8,128)(2,1)} %get-tuple-element.44), channel_id=1, source_target_pairs={{0,16},{16,32},{32,48},{48,64},{64,80},{80,96},{96,112},{112,128},... | collective-permute-start | bytes 294920 | tf_op jit(solution)/shard_map/ppermute | solution.py:282
  20.8 14.2 %collective-permute-start.2 = (bf16[3,128,128]{2,1,0:T(8,128)(2,1)}, bf16[3,128,128]{2,1,0:T(8,128)(2,1)S(1)}, u32[]{:S(2)}, u32[]{:S(2)}) collective-permute-start(bf16[3,128,128]{2,1,0:T(8,128)(2,1)} %get-tuple-element.45), channel_id=1, source_target_pairs={{0,496},{16,0},{32,16},{48,32},{64,48},{80,64},{96,80},{112,96},{1... | collective-permute-start | bytes 294920 | tf_op jit(solution)/shard_map/ppermute | solution.py:282
  30.6 7.6 %collective-permute-start.3 = (bf16[3,128,128]{2,1,0:T(8,128)(2,1)}, bf16[3,128,128]{2,1,0:T(8,128)(2,1)S(1)}, u32[]{:S(2)}, u32[]{:S(2)}) collective-permute-start(bf16[3,128,128]{2,1,0:T(8,128)(2,1)} %get-tuple-element.46), channel_id=1, source_target_pairs={{0,480},{16,496},{32,0},{48,16},{64,32},{80,48},{96,64},{112,80},{... | collective-permute-start | bytes 294920 | tf_op jit(solution)/shard_map/ppermute | solution.py:282
  45.7 22.8 %all-to-all-start.1 = ((bf16[16,128,128]{2,1,0:T(8,128)(2,1)}), bf16[16,128,128]{2,1,0:T(8,128)(2,1)}, u32[]{:S(2)}, u32[]{:S(2)}) async-start(bf16[16,128,128]{2,1,0:T(8,128)(2,1)} %get-tuple-element.48), calls=%async_computation.1 | async-start | bytes 1048576 | tf_op jit(solution)/shard_map/all_to_all | solution.py:286
  50.8 20.2 %collective-permute-start.4 = (bf16[3,128,128]{2,1,0:T(8,128)(2,1)}, bf16[3,128,128]{2,1,0:T(8,128)(2,1)S(1)}, u32[]{:S(2)}, u32[]{:S(2)}) collective-permute-start(bf16[3,128,128]{2,1,0:T(8,128)(2,1)} %get-tuple-element.49), channel_id=1, source_target_pairs={{0,32},{16,48},{32,64},{48,80},{64,96},{80,112},{96,128},{112,144}... | collective-permute-start | bytes 294920 | tf_op jit(solution)/shard_map/ppermute | solution.py:282
  52.7 18.3 %collective-permute-start.5 = (bf16[3,128,128]{2,1,0:T(8,128)(2,1)}, bf16[3,128,128]{2,1,0:T(8,128)(2,1)S(1)}, u32[]{:S(2)}, u32[]{:S(2)}) collective-permute-start(bf16[3,128,128]{2,1,0:T(8,128)(2,1)} %get-tuple-element.50), channel_id=1, source_target_pairs={{0,16},{16,32},{32,48},{48,64},{64,80},{80,96},{96,112},{112,128},... | collective-permute-start | bytes 294920 | tf_op jit(solution)/shard_map/ppermute | solution.py:282
  54.6 16.4 %collective-permute-start.6 = (bf16[3,128,128]{2,1,0:T(8,128)(2,1)}, bf16[3,128,128]{2,1,0:T(8,128)(2,1)S(1)}, u32[]{:S(2)}, u32[]{:S(2)}) collective-permute-start(bf16[3,128,128]{2,1,0:T(8,128)(2,1)} %get-tuple-element.51), channel_id=1, source_target_pairs={{0,496},{16,0},{32,16},{48,32},{64,48},{80,64},{96,80},{112,96},{1... | collective-permute-start | bytes 294920 | tf_op jit(solution)/shard_map/ppermute | solution.py:282
  64.3 8.1 %collective-permute-start.7 = (bf16[3,128,128]{2,1,0:T(8,128)(2,1)}, bf16[3,128,128]{2,1,0:T(8,128)(2,1)S(1)}, u32[]{:S(2)}, u32[]{:S(2)}) collective-permute-start(bf16[3,128,128]{2,1,0:T(8,128)(2,1)} %get-tuple-element.52), channel_id=1, source_target_pairs={{0,480},{16,496},{32,0},{48,16},{64,32},{80,48},{96,64},{112,80},{... | collective-permute-start | bytes 294920 | tf_op jit(solution)/shard_map/ppermute | solution.py:282
  71.0 12.2 %copy-start.7 = (bf16[3,128,128]{2,1,0:T(8,128)(2,1)S(1)}, bf16[3,128,128]{2,1,0:T(8,128)(2,1)}, u32[]{:S(2)}) copy-start(bf16[3,128,128]{2,1,0:T(8,128)(2,1)} %get-tuple-element.67) | copy-start | bytes 294916
  71.0 14.1 %copy-start.6 = (bf16[3,128,128]{2,1,0:T(8,128)(2,1)S(1)}, bf16[3,128,128]{2,1,0:T(8,128)(2,1)}, u32[]{:S(2)}) copy-start(bf16[3,128,128]{2,1,0:T(8,128)(2,1)} %get-tuple-element.68) | copy-start | bytes 294916
  71.0 16.0 %copy-start.5 = (bf16[3,128,128]{2,1,0:T(8,128)(2,1)S(1)}, bf16[3,128,128]{2,1,0:T(8,128)(2,1)}, u32[]{:S(2)}) copy-start(bf16[3,128,128]{2,1,0:T(8,128)(2,1)} %get-tuple-element.69) | copy-start | bytes 294916
  71.0 22.7 %copy-start.4 = (bf16[3,128,128]{2,1,0:T(8,128)(2,1)S(1)}, bf16[3,128,128]{2,1,0:T(8,128)(2,1)}, u32[]{:S(2)}) copy-start(bf16[3,128,128]{2,1,0:T(8,128)(2,1)} %get-tuple-element.70) | copy-start | bytes 294916
  76.2 24.4 %all-to-all-start.2 = ((bf16[16,128,128]{2,1,0:T(8,128)(2,1)}), bf16[16,128,128]{2,1,0:T(8,128)(2,1)}, u32[]{:S(2)}, u32[]{:S(2)}) async-start(bf16[16,128,128]{2,1,0:T(8,128)(2,1)} %shard_map.68), calls=%async_computation.2 | async-start | bytes 1048576 | tf_op jit(solution)/shard_map/all_to_all | solution.py:286
  83.2 19.9 %collective-permute-start.8 = (bf16[3,128,128]{2,1,0:T(8,128)(2,1)S(1)}, bf16[3,128,128]{2,1,0:T(8,128)(2,1)S(1)}, u32[]{:S(2)}, u32[]{:S(2)}) collective-permute-start(bf16[3,128,128]{2,1,0:T(8,128)(2,1)S(1)} %copy-done.7), channel_id=1, source_target_pairs={{0,32},{16,48},{32,64},{48,80},{64,96},{80,112},{96,128},{112,144}... | collective-permute-start | bytes 294920 | tf_op jit(solution)/shard_map/ppermute | solution.py:282
  85.1 18.0 %collective-permute-start.9 = (bf16[3,128,128]{2,1,0:T(8,128)(2,1)S(1)}, bf16[3,128,128]{2,1,0:T(8,128)(2,1)S(1)}, u32[]{:S(2)}, u32[]{:S(2)}) collective-permute-start(bf16[3,128,128]{2,1,0:T(8,128)(2,1)S(1)} %copy-done.6), channel_id=1, source_target_pairs={{0,16},{16,32},{32,48},{48,64},{64,80},{80,96},{96,112},{112,128},... | collective-permute-start | bytes 294920 | tf_op jit(solution)/shard_map/ppermute | solution.py:282
  87.0 16.1 %collective-permute-start.10 = (bf16[3,128,128]{2,1,0:T(8,128)(2,1)S(1)}, bf16[3,128,128]{2,1,0:T(8,128)(2,1)S(1)}, u32[]{:S(2)}, u32[]{:S(2)}) collective-permute-start(bf16[3,128,128]{2,1,0:T(8,128)(2,1)S(1)} %copy-done.5), channel_id=1, source_target_pairs={{0,496},{16,0},{32,16},{48,32},{64,48},{80,64},{96,80},{112,96},{1... | collective-permute-start | bytes 294920 | tf_op jit(solution)/shard_map/ppermute | solution.py:282
  93.7 9.4 %collective-permute-start.11 = (bf16[3,128,128]{2,1,0:T(8,128)(2,1)S(1)}, bf16[3,128,128]{2,1,0:T(8,128)(2,1)S(1)}, u32[]{:S(2)}, u32[]{:S(2)}) collective-permute-start(bf16[3,128,128]{2,1,0:T(8,128)(2,1)S(1)} %copy-done.4), channel_id=1, source_target_pairs={{0,480},{16,496},{32,0},{48,16},{64,32},{80,48},{96,64},{112,80},{... | collective-permute-start | bytes 294920 | tf_op jit(solution)/shard_map/ppermute | solution.py:282
  107.0 23.8 %all-to-all-start.3 = ((bf16[16,128,128]{2,1,0:T(8,128)(2,1)}), bf16[16,128,128]{2,1,0:T(8,128)(2,1)}, u32[]{:S(2)}, u32[]{:S(2)}) async-start(bf16[16,128,128]{2,1,0:T(8,128)(2,1)} %shard_map.69), calls=%async_computation.3 | async-start | bytes 1048576 | tf_op jit(solution)/shard_map/all_to_all | solution.py:286
  113.4 19.4 %collective-permute-start.12 = (bf16[3,128,128]{2,1,0:T(8,128)(2,1)}, bf16[3,128,128]{2,1,0:T(8,128)(2,1)S(1)}, u32[]{:S(2)}, u32[]{:S(2)}) collective-permute-start(bf16[3,128,128]{2,1,0:T(8,128)(2,1)} %get-tuple-element.75), channel_id=1, source_target_pairs={{0,32},{16,48},{32,64},{48,80},{64,96},{80,112},{96,128},{112,144}... | collective-permute-start | bytes 294920 | tf_op jit(solution)/shard_map/ppermute | solution.py:282
  115.3 17.5 %collective-permute-start.13 = (bf16[3,128,128]{2,1,0:T(8,128)(2,1)}, bf16[3,128,128]{2,1,0:T(8,128)(2,1)S(1)}, u32[]{:S(2)}, u32[]{:S(2)}) collective-permute-start(bf16[3,128,128]{2,1,0:T(8,128)(2,1)} %get-tuple-element.76), channel_id=1, source_target_pairs={{0,16},{16,32},{32,48},{48,64},{64,80},{80,96},{96,112},{112,128},... | collective-permute-start | bytes 294920 | tf_op jit(solution)/shard_map/ppermute | solution.py:282
  117.3 15.6 %collective-permute-start.14 = (bf16[3,128,128]{2,1,0:T(8,128)(2,1)}, bf16[3,128,128]{2,1,0:T(8,128)(2,1)S(1)}, u32[]{:S(2)}, u32[]{:S(2)}) collective-permute-start(bf16[3,128,128]{2,1,0:T(8,128)(2,1)} %get-tuple-element.77), channel_id=1, source_target_pairs={{0,496},{16,0},{32,16},{48,32},{64,48},{80,64},{96,80},{112,96},{1... | collective-permute-start | bytes 294920 | tf_op jit(solution)/shard_map/ppermute | solution.py:282
  124.0 8.9 %collective-permute-start.15 = (bf16[3,128,128]{2,1,0:T(8,128)(2,1)}, bf16[3,128,128]{2,1,0:T(8,128)(2,1)S(1)}, u32[]{:S(2)}, u32[]{:S(2)}) collective-permute-start(bf16[3,128,128]{2,1,0:T(8,128)(2,1)} %get-tuple-element.78), channel_id=1, source_target_pairs={{0,480},{16,496},{32,0},{48,16},{64,32},{80,48},{96,64},{112,80},{... | collective-permute-start | bytes 294920 | tf_op jit(solution)/shard_map/ppermute | solution.py:282

commit v10 on v9

--- a/solution.py
+++ b/solution.py
@@ -177,7 +177,7 @@
         two = (-2.0 * inv_ref[g : g + 1, :] * total - x).astype(BF16).astype(F32)
         one = term[g].astype(F32)
         mixed[g] = (coef[0] * x + coef[1] * one + coef[2] * two).astype(BF16)
-        copies.append(start(mixed.at[g], target(g), sems.at[g]))
+        copies += target(g, mixed, sems)
     return copies
 
 
@@ -240,9 +240,14 @@
 def rear_two(signal_ref, r0, r1, r2, r3, weights_ref, inv_ref, col_ref, term_ref, out_ref, *rest):
     *scratch, field, load_sem = rest
     load = start(signal_ref.at[field.shape[0] :], field, load_sem)
+
+    def target(g, mixed, sems):
+        part = ended(g, mixed.shape[0])
+        return [start(mixed.at[part], out_ref.at[part], sems.at[g])] if part else []
+
     wait(
         product_two(
-            field, (r0, r1, r2, r3), weights_ref, inv_ref, col_ref, term_ref, lambda g: out_ref.at[g], scratch, [load]
+            field, (r0, r1, r2, r3), weights_ref, inv_ref, col_ref, term_ref, target, scratch, [load]
         )
     )
 
@@ -258,8 +263,8 @@
     *scratch, field, load_sem = rest
     rows, width = field.shape[1:]
 
-    def target(g):
-        return out_ref.at[:rows, g * width : (g + 1) * width]
+    def target(g, mixed, sems):
+        return [start(mixed.at[g], out_ref.at[:rows, g * width : (g + 1) * width], sems.at[g])]
 
     load = start(field_ref, field, load_sem)
     wait(

time: 138 us -> 138 us (level)
  no operation moved by 1% of the time
where the time goes in v10:
time: 138 us; the launch traced here: 137 us
  starting transfers between devices  94.1 us (68%)
  Pallas kernels  28 us (20%)
  waiting for transfers between devices  14.1 us (10%)
    ppermute x16, starting transfers between devices, swap(): lax.ppermute(block, 'dom', partners(i, count))  64.7 us
    all_to_all x4, starting transfers between devices, exchange(): return lax.all_to_all(field, 'tm', split_axis=0, concat_axis=0, tiled=True)  29.4 us
    pallas_call x9, Pallas kernels, call(): pl.pallas_call(kernel, out_shape=shapes, in_specs=specs, out_specs=result...  28 us
    all_to_all x4, waiting for transfers between devices, exchange(): return lax.all_to_all(field, 'tm', split_axis=0, concat_axis=0, tiled=True)  9.46 us
    ppermute x16, waiting for transfers between devices, swap(): lax.ppermute(block, 'dom', partners(i, count))  4.66 us
  transfers between devices with their start and end apart: 20, of which 5 were waited for; matrix products, arithmetic and copies ran while one was open for 0% of the time, Pallas kernels for 7%

profile of v10, /device:TPU:1, one launch (start us, length us, event | category | flops | bytes accessed | tf_op | source)
XLA Modules:
  0.0 136.7 jit_solution(11603221072562465468)
XLA Ops:
  0.0 2.2 %shard_map.65 = bf16[16,256,128]{2,1,0:T(8,128)(2,1)} custom-call(bf16[256,2048]{1,0:T(8,128)(2,1)} %bitcast.2, bf16[32,512]{1,0:T(8,128)(2,1)} %kernel_ref.1), custom_call_target="tpu_custom_call" | custom-call | bytes 2129920 | tf_op jit(solution)/shard_map/pallas_call | solution.py:26
  2.3 0.0 copy-start.2
  2.3 10.9 %all-to-all-start = ((bf16[16,256,128]{2,1,0:T(8,128)(2,1)}), bf16[16,256,128]{2,1,0:T(8,128)(2,1)}, u32[]{:S(2)}, u32[]{:S(2)}) async-start(bf16[16,256,128]{2,1,0:T(8,128)(2,1)} %shard_map.65), calls=%async_computation | async-start | bytes 2097152 | tf_op jit(solution)/shard_map/all_to_all | solution.py:291
  13.2 0.0 copy-done.3
  13.2 0.1 copy.8.send_ref
  13.3 0.0 copy-done
  13.3 0.0 copy-done.1
  13.3 2.9 %shard_map.64 = (f32[24,128]{1,0:T(8,128)S(1)}, bf16[3,128,128]{2,1,0:T(8,128)(2,1)}, bf16[3,128,128]{2,1,0:T(8,128)(2,1)}, bf16[3,128,128]{2,1,0:T(8,128)(2,1)}, bf16[3,128,128]{2,1,0:T(8,128)(2,1)}) custom-call(bf16[256,2048]{1,0:T(8,128)(2,1)} %bitcast.3, bf16[16,5,128,128]{3,2,1,0:T(8,128)(2,1)S(1)} %copy-done, s32[1,4,3]{2,1,0:T(4,128)S(1)} %copy.8.send_ref, ...), custom_call_target="tpu_custom_call" | custom-call | flops 41943040 | bytes 4075580 | tf_op jit(solution)/shard_map/pallas_call | solution.py:26
  16.2 2.3 %collective-permute-start = (bf16[3,128,128]{2,1,0:T(8,128)(2,1)}, bf16[3,128,128]{2,1,0:T(8,128)(2,1)S(1)}, u32[]{:S(2)}, u32[]{:S(2)}) collective-permute-start(bf16[3,128,128]{2,1,0:T(8,128)(2,1)} %get-tuple-element.43), channel_id=1, source_target_pairs={{0,32},{16,48},{32,64},{48,80},{64,96},{80,112},{96,128},{112,144}... | collective-permute-start | bytes 294920 | tf_op jit(solution)/shard_map/ppermute | solution.py:287
  18.5 2.2 %collective-permute-start.1 = (bf16[3,128,128]{2,1,0:T(8,128)(2,1)}, bf16[3,128,128]{2,1,0:T(8,128)(2,1)S(1)}, u32[]{:S(2)}, u32[]{:S(2)}) collective-permute-start(bf16[3,128,128]{2,1,0:T(8,128)(2,1)} %get-tuple-element.44), channel_id=1, source_target_pairs={{0,16},{16,32},{32,48},{48,64},{64,80},{80,96},{96,112},{112,128},... | collective-permute-start | bytes 294920 | tf_op jit(solution)/shard_map/ppermute | solution.py:287
  20.8 9.8 %collective-permute-start.2 = (bf16[3,128,128]{2,1,0:T(8,128)(2,1)}, bf16[3,128,128]{2,1,0:T(8,128)(2,1)S(1)}, u32[]{:S(2)}, u32[]{:S(2)}) collective-permute-start(bf16[3,128,128]{2,1,0:T(8,128)(2,1)} %get-tuple-element.45), channel_id=1, source_target_pairs={{0,496},{16,0},{32,16},{48,32},{64,48},{80,64},{96,80},{112,96},{1... | collective-permute-start | bytes 294920 | tf_op jit(solution)/shard_map/ppermute | solution.py:287
  30.6 4.3 %collective-permute-start.3 = (bf16[3,128,128]{2,1,0:T(8,128)(2,1)}, bf16[3,128,128]{2,1,0:T(8,128)(2,1)S(1)}, u32[]{:S(2)}, u32[]{:S(2)}) collective-permute-start(bf16[3,128,128]{2,1,0:T(8,128)(2,1)} %get-tuple-element.46), channel_id=1, source_target_pairs={{0,480},{16,496},{32,0},{48,16},{64,32},{80,48},{96,64},{112,80},{... | collective-permute-start | bytes 294920 | tf_op jit(solution)/shard_map/ppermute | solution.py:287
  34.9 0.0 copy-done.2
  34.9 0.1 copy.9.col_ref
  35.0 0.0 collective-permute-done.r0
  35.0 0.0 collective-permute-done.1.r1
  35.0 0.0 collective-permute-done.2.r2
  35.0 3.3 %collective-permute-done.3.r3 = bf16[3,128,128]{2,1,0:T(8,128)(2,1)S(1)} collective-permute-done((bf16[3,128,128]{2,1,0:T(8,128)(2,1)}, bf16[3,128,128]{2,1,0:T(8,128)(2,1)S(1)}, u32[]{:S(2)}, u32[]{:S(2)}) %collective-permute-start.3) | collective-permute-done | bytes 98336 | tf_op jit(solution)/shard_map/ppermute | solution.py:287
  38.3 3.0 %all-to-all-done.arrived_ref = bf16[16,256,128]{2,1,0:T(8,128)(2,1)} async-done(((bf16[16,256,128]{2,1,0:T(8,128)(2,1)}), bf16[16,256,128]{2,1,0:T(8,128)(2,1)}, u32[]{:S(2)}, u32[]{:S(2)}) %all-to-all-start) | async-done | bytes 1048608 | tf_op jit(solution)/shard_map/all_to_all | solution.py:291
  41.3 4.4 %shard_map.66 = (bf16[16,128,128]{2,1,0:T(8,128)(2,1)}, bf16[3,128,128]{2,1,0:T(8,128)(2,1)}, bf16[3,128,128]{2,1,0:T(8,128)(2,1)}, bf16[3,128,128]{2,1,0:T(8,12...) custom-call(bf16[256,2048]{1,0:T(8,128)(2,1)} %bitcast.4, ...), custom_call_target="tpu_custom_call" | custom-call | flops 603979776 | bytes 7090544 | tf_op jit(solution)/shard_map/pallas_call | solution.py:26
  45.7 5.0 %all-to-all-start.1 = ((bf16[16,128,128]{2,1,0:T(8,128)(2,1)}), bf16[16,128,128]{2,1,0:T(8,128)(2,1)}, u32[]{:S(2)}, u32[]{:S(2)}) async-start(bf16[16,128,128]{2,1,0:T(8,128)(2,1)} %get-tuple-element.48), calls=%async_computation.1 | async-start | bytes 1048576 | tf_op jit(solution)/shard_map/all_to_all | solution.py:291
  50.8 1.9 %collective-permute-start.4 = (bf16[3,128,128]{2,1,0:T(8,128)(2,1)}, bf16[3,128,128]{2,1,0:T(8,128)(2,1)S(1)}, u32[]{:S(2)}, u32[]{:S(2)}) collective-permute-start(bf16[3,128,128]{2,1,0:T(8,128)(2,1)} %get-tuple-element.49), channel_id=1, source_target_pairs={{0,32},{16,48},{32,64},{48,80},{64,96},{80,112},{96,128},{112,144}... | collective-permute-start | bytes 294920 | tf_op jit(solution)/shard_map/ppermute | solution.py:287
  52.7 1.9 %collective-permute-start.5 = (bf16[3,128,128]{2,1,0:T(8,128)(2,1)}, bf16[3,128,128]{2,1,0:T(8,128)(2,1)S(1)}, u32[]{:S(2)}, u32[]{:S(2)}) collective-permute-start(bf16[3,128,128]{2,1,0:T(8,128)(2,1)} %get-tuple-element.50), channel_id=1, source_target_pairs={{0,16},{16,32},{32,48},{48,64},{64,80},{80,96},{96,112},{112,128},... | collective-permute-start | bytes 294920 | tf_op jit(solution)/shard_map/ppermute | solution.py:287
  54.6 9.6 %collective-permute-start.6 = (bf16[3,128,128]{2,1,0:T(8,128)(2,1)}, bf16[3,128,128]{2,1,0:T(8,128)(2,1)S(1)}, u32[]{:S(2)}, u32[]{:S(2)}) collective-permute-start(bf16[3,128,128]{2,1,0:T(8,128)(2,1)} %get-tuple-element.51), channel_id=1, source_target_pairs={{0,496},{16,0},{32,16},{48,32},{64,48},{80,64},{96,80},{112,96},{1... | collective-permute-start | bytes 294920 | tf_op jit(solution)/shard_map/ppermute | solution.py:287
  64.3 4.3 %collective-permute-start.7 = (bf16[3,128,128]{2,1,0:T(8,128)(2,1)}, bf16[3,128,128]{2,1,0:T(8,128)(2,1)S(1)}, u32[]{:S(2)}, u32[]{:S(2)}) collective-permute-start(bf16[3,128,128]{2,1,0:T(8,128)(2,1)} %get-tuple-element.52), channel_id=1, source_target_pairs={{0,480},{16,496},{32,0},{48,16},{64,32},{80,48},{96,64},{112,80},{... | collective-permute-start | bytes 294920 | tf_op jit(solution)/shard_map/ppermute | solution.py:287
  68.5 0.0 all-to-all-done.1.early_ref.field_ref
  68.6 2.4 %shard_map.67 = (bf16[3,128,128]{2,1,0:T(8,128)(2,1)}, bf16[3,128,128]{2,1,0:T(8,128)(2,1)}, bf16[3,128,128]{2,1,0:T(8,128)(2,1)}, bf16[3,128,128]{2,1,0:T(8,128)(2,1)}) custom-call(bf16[16,128,128]{2,1,0:T(8,128)(2,1)} %all-to-all-done.1.early_ref.field_ref, f32[24,128]{1,0:T(8,128)S(1)} %get-tuple-element.47.inv_ref, s32[1,4,3]{2,1,0:T(4,128)S(1)} %copy.8.send_ref), custom_call_target="tpu_custom_call" | custom-call | bytes 929840 | tf_op jit(solution)/shard_map/pallas_call | solution.py:26
  71.0 0.0 copy-start.7
  71.0 0.0 copy-start.6
  71.0 0.0 copy-start.5
  71.0 0.0 copy-start.4
  71.0 0.0 collective-permute-done.4.r0
  71.0 0.0 collective-permute-done.5.r1
  71.0 0.0 collective-permute-done.6.r2
  71.1 1.4 collective-permute-done.7.r3
  72.4 3.9 %shard_map.68 = bf16[16,128,128]{2,1,0:T(8,128)(2,1)} custom-call(bf16[256,2048]{1,0:T(8,128)(2,1)} %bitcast.5, bf16[3,128,128]{2,1,0:T(8,128)(2,1)S(1)} %collective-permute-done.4.r0, bf16[3,128,128]{2,1,0:T(8,128)(2,1)S(1)} %collective-permute-done.5.r1, bf16[3,128,128]{2,1,0:T(8,128)(2,1)S(1)} %collective-permute-done.6.r2, ...), custom_call_target="tpu_custom_call" | custom-call | flops 335544320 | bytes 5124416 | tf_op jit(solution)/shard_map/pallas_call | solution.py:26
  76.3 7.0 %all-to-all-start.2 = ((bf16[16,128,128]{2,1,0:T(8,128)(2,1)}), bf16[16,128,128]{2,1,0:T(8,128)(2,1)}, u32[]{:S(2)}, u32[]{:S(2)}) async-start(bf16[16,128,128]{2,1,0:T(8,128)(2,1)} %shard_map.68), calls=%async_computation.2 | async-start | bytes 1048576 | tf_op jit(solution)/shard_map/all_to_all | solution.py:291
  83.3 0.0 copy-done.7
  83.3 1.9 %collective-permute-start.8 = (bf16[3,128,128]{2,1,0:T(8,128)(2,1)S(1)}, bf16[3,128,128]{2,1,0:T(8,128)(2,1)S(1)}, u32[]{:S(2)}, u32[]{:S(2)}) collective-permute-start(bf16[3,128,128]{2,1,0:T(8,128)(2,1)S(1)} %copy-done.7), channel_id=1, source_target_pairs={{0,32},{16,48},{32,64},{48,80},{64,96},{80,112},{96,128},{112,144}... | collective-permute-start | bytes 294920 | tf_op jit(solution)/shard_map/ppermute | solution.py:287
  85.2 0.0 copy-done.6
  85.2 1.9 %collective-permute-start.9 = (bf16[3,128,128]{2,1,0:T(8,128)(2,1)S(1)}, bf16[3,128,128]{2,1,0:T(8,128)(2,1)S(1)}, u32[]{:S(2)}, u32[]{:S(2)}) collective-permute-start(bf16[3,128,128]{2,1,0:T(8,128)(2,1)S(1)} %copy-done.6), channel_id=1, source_target_pairs={{0,16},{16,32},{32,48},{48,64},{64,80},{80,96},{96,112},{112,128},... | collective-permute-start | bytes 294920 | tf_op jit(solution)/shard_map/ppermute | solution.py:287
  87.1 0.0 copy-done.5
  87.1 6.7 %collective-permute-start.10 = (bf16[3,128,128]{2,1,0:T(8,128)(2,1)S(1)}, bf16[3,128,128]{2,1,0:T(8,128)(2,1)S(1)}, u32[]{:S(2)}, u32[]{:S(2)}) collective-permute-start(bf16[3,128,128]{2,1,0:T(8,128)(2,1)S(1)} %copy-done.5), channel_id=1, source_target_pairs={{0,496},{16,0},{32,16},{48,32},{64,48},{80,64},{96,80},{112,96},{1... | collective-permute-start | bytes 294920 | tf_op jit(solution)/shard_map/ppermute | solution.py:287
  93.8 0.0 copy-done.4
  93.8 3.7 %collective-permute-start.11 = (bf16[3,128,128]{2,1,0:T(8,128)(2,1)S(1)}, bf16[3,128,128]{2,1,0:T(8,128)(2,1)S(1)}, u32[]{:S(2)}, u32[]{:S(2)}) collective-permute-start(bf16[3,128,128]{2,1,0:T(8,128)(2,1)S(1)} %copy-done.4), channel_id=1, source_target_pairs={{0,480},{16,496},{32,0},{48,16},{64,32},{80,48},{96,64},{112,80},{... | collective-permute-start | bytes 294920 | tf_op jit(solution)/shard_map/ppermute | solution.py:287
  97.5 3.2 %all-to-all-done.2.arrived_ref = bf16[16,128,128]{2,1,0:T(8,128)(2,1)} async-done(((bf16[16,128,128]{2,1,0:T(8,128)(2,1)}), bf16[16,128,128]{2,1,0:T(8,128)(2,1)}, u32[]{:S(2)}, u32[]{:S(2)}) %all-to-all-start.2) | async-done | bytes 524320 | tf_op jit(solution)/shard_map/all_to_all | solution.py:291
  100.7 2.5 %shard_map.69 = bf16[16,128,128]{2,1,0:T(8,128)(2,1)} custom-call(bf16[16,128,128]{2,1,0:T(8,128)(2,1)} %all-to-all-done.2.arrived_ref, bf16[512,512]{1,0:T(8,128)(2,1)} %get-tuple-element.64.mix_ref), custom_call_target="tpu_custom_call" | custom-call | flops 268435456 | bytes 1572864 | tf_op jit(solution)/shard_map/pallas_call | solution.py:26
  103.2 0.0 collective-permute-done.8.r0
  103.2 0.0 collective-permute-done.9.r1
  103.2 0.0 collective-permute-done.10.r2
  103.2 0.0 collective-permute-done.11.r3
  103.2 3.9 %shard_map.70 = (bf16[16,128,128]{2,1,0:T(8,128)(2,1)}, bf16[3,128,128]{2,1,0:T(8,128)(2,1)}, bf16[3,128,128]{2,1,0:T(8,128)(2,1)}, bf16[3,128,128]{2,1,0:T(8,128)(2,1)}, bf16[3,128,128]{2,1,0:T(8,128)(2,1)}) custom-call(bf16[16,128,128]{2,1,0:T(8,128)(2,1)} %all-to-all-done.1.early_ref.field_ref, bf16[3,128,128]{2,1,0:T(8,128)(2,1)S(1)} %collective-permute-done.8.r0, ...), custom_call_target="tpu_custom_call" | custom-call | flops 335544320 | bytes 4469104 | tf_op jit(solution)/shard_map/pallas_call | solution.py:26
  107.1 6.4 %all-to-all-start.3 = ((bf16[16,128,128]{2,1,0:T(8,128)(2,1)}), bf16[16,128,128]{2,1,0:T(8,128)(2,1)}, u32[]{:S(2)}, u32[]{:S(2)}) async-start(bf16[16,128,128]{2,1,0:T(8,128)(2,1)} %shard_map.69), calls=%async_computation.3 | async-start | bytes 1048576 | tf_op jit(solution)/shard_map/all_to_all | solution.py:291
  113.5 1.9 %collective-permute-start.12 = (bf16[3,128,128]{2,1,0:T(8,128)(2,1)}, bf16[3,128,128]{2,1,0:T(8,128)(2,1)S(1)}, u32[]{:S(2)}, u32[]{:S(2)}) collective-permute-start(bf16[3,128,128]{2,1,0:T(8,128)(2,1)} %get-tuple-element.75), channel_id=1, source_target_pairs={{0,32},{16,48},{32,64},{48,80},{64,96},{80,112},{96,128},{112,144}... | collective-permute-start | bytes 294920 | tf_op jit(solution)/shard_map/ppermute | solution.py:287
  115.4 1.9 %collective-permute-start.13 = (bf16[3,128,128]{2,1,0:T(8,128)(2,1)}, bf16[3,128,128]{2,1,0:T(8,128)(2,1)S(1)}, u32[]{:S(2)}, u32[]{:S(2)}) collective-permute-start(bf16[3,128,128]{2,1,0:T(8,128)(2,1)} %get-tuple-element.76), channel_id=1, source_target_pairs={{0,16},{16,32},{32,48},{48,64},{64,80},{80,96},{96,112},{112,128},... | collective-permute-start | bytes 294920 | tf_op jit(solution)/shard_map/ppermute | solution.py:287
  117.4 6.7 %collective-permute-start.14 = (bf16[3,128,128]{2,1,0:T(8,128)(2,1)}, bf16[3,128,128]{2,1,0:T(8,128)(2,1)S(1)}, u32[]{:S(2)}, u32[]{:S(2)}) collective-permute-start(bf16[3,128,128]{2,1,0:T(8,128)(2,1)} %get-tuple-element.77), channel_id=1, source_target_pairs={{0,496},{16,0},{32,16},{48,32},{64,48},{80,64},{96,80},{112,96},{1... | collective-permute-start | bytes 294920 | tf_op jit(solution)/shard_map/ppermute | solution.py:287
  124.1 3.7 %collective-permute-start.15 = (bf16[3,128,128]{2,1,0:T(8,128)(2,1)}, bf16[3,128,128]{2,1,0:T(8,128)(2,1)S(1)}, u32[]{:S(2)}, u32[]{:S(2)}) collective-permute-start(bf16[3,128,128]{2,1,0:T(8,128)(2,1)} %get-tuple-element.78), channel_id=1, source_target_pairs={{0,480},{16,496},{32,0},{48,16},{64,32},{80,48},{96,64},{112,80},{... | collective-permute-start | bytes 294920 | tf_op jit(solution)/shard_map/ppermute | solution.py:287
  127.7 3.2 %all-to-all-done.3.late_ref = bf16[16,128,128]{2,1,0:T(8,128)(2,1)} async-done(((bf16[16,128,128]{2,1,0:T(8,128)(2,1)}), bf16[16,128,128]{2,1,0:T(8,128)(2,1)}, u32[]{:S(2)}, u32[]{:S(2)}) %all-to-all-start.3) | async-done | bytes 524320 | tf_op jit(solution)/shard_map/all_to_all | solution.py:291
  130.9 2.0 %shard_map.71._ = bf16[256,2048]{1,0:T(8,128)(2,1)} custom-call(bf16[16,128,128]{2,1,0:T(8,128)(2,1)} %all-to-all-done.3.late_ref), custom_call_target="tpu_custom_call" | custom-call | bytes 1572864 | tf_op jit(solution)/shard_map/pallas_call | solution.py:26
  132.9 0.0 collective-permute-done.12.r0
  132.9 0.0 collective-permute-done.13.r1
  132.9 0.0 collective-permute-done.14.r2
  132.9 0.0 collective-permute-done.15.r3
  133.0 3.8 %shard_map.72 = bf16[256,2048]{1,0:T(8,128)(2,1)} custom-call(bf16[16,128,128]{2,1,0:T(8,128)(2,1)} %all-to-all-done.1.early_ref.field_ref, bf16[3,128,128]{2,1,0:T(8,128)(2,1)S(1)} %collective-permute-done.12.r0, bf16[3,128,128]{2,1,0:T(8,128)(2,1)S(1)} %collective-permute-done.13.r1, ...), custom_call_target="tpu_custom_call", output_to_operand_aliasing={{}: (9, {})} | custom-call | flops 335544320 | bytes 6172992 | tf_op jit(solution)/shard_map/pallas_call | solution.py:26
  (3 shorter events, 0.0 us)
Async XLA Ops:
  0.0 13.2 %copy-start.3 = (s32[1,4,3]{1,0,2:T(1,128)S(1)}, s32[1,4,3]{1,0,2:T(1,128)}, u32[]{:S(2)}) copy-start(s32[1,4,3]{1,0,2:T(1,128)} %param.8) | copy-start | bytes 148
  0.0 13.3 %copy-start = (bf16[16,5,128,128]{3,2,1,0:T(8,128)(2,1)S(1)}, bf16[16,5,128,128]{3,2,1,0:T(8,128)(2,1)}, u32[]{:S(2)}) copy-start(bf16[16,5,128,128]{3,2,1,0:T(8,128)(2,1)} %weights_ref.9) | copy-start | bytes 7864324
  0.0 13.3 %copy-start.1 = (f32[3]{0:T(128)S(1)}, f32[3]{0:T(128)}, u32[]{:S(2)}) copy-start(f32[3]{0:T(128)} %coef_ref.1) | copy-start | bytes 40
  2.3 32.6 %copy-start.2 = (s32[16,5]{0,1:T(8,128)S(1)}, s32[16,5]{0,1:T(8,128)}, u32[]{:S(2)}) copy-start(s32[16,5]{0,1:T(8,128)} %param.9) | copy-start | bytes 964
  2.3 39.0 %all-to-all-start = ((bf16[16,256,128]{2,1,0:T(8,128)(2,1)}), bf16[16,256,128]{2,1,0:T(8,128)(2,1)}, u32[]{:S(2)}, u32[]{:S(2)}) async-start(bf16[16,256,128]{2,1,0:T(8,128)(2,1)} %shard_map.65), calls=%async_computation | async-start | bytes 2097152 | tf_op jit(solution)/shard_map/all_to_all | solution.py:291
  16.2 18.8 %collective-permute-start = (bf16[3,128,128]{2,1,0:T(8,128)(2,1)}, bf16[3,128,128]{2,1,0:T(8,128)(2,1)S(1)}, u32[]{:S(2)}, u32[]{:S(2)}) collective-permute-start(bf16[3,128,128]{2,1,0:T(8,128)(2,1)} %get-tuple-element.43), channel_id=1, source_target_pairs={{0,32},{16,48},{32,64},{48,80},{64,96},{80,112},{96,128},{112,144}... | collective-permute-start | bytes 294920 | tf_op jit(solution)/shard_map/ppermute | solution.py:287
  18.5 16.4 %collective-permute-start.1 = (bf16[3,128,128]{2,1,0:T(8,128)(2,1)}, bf16[3,128,128]{2,1,0:T(8,128)(2,1)S(1)}, u32[]{:S(2)}, u32[]{:S(2)}) collective-permute-start(bf16[3,128,128]{2,1,0:T(8,128)(2,1)} %get-tuple-element.44), channel_id=1, source_target_pairs={{0,16},{16,32},{32,48},{48,64},{64,80},{80,96},{96,112},{112,128},... | collective-permute-start | bytes 294920 | tf_op jit(solution)/shard_map/ppermute | solution.py:287
  20.8 14.2 %collective-permute-start.2 = (bf16[3,128,128]{2,1,0:T(8,128)(2,1)}, bf16[3,128,128]{2,1,0:T(8,128)(2,1)S(1)}, u32[]{:S(2)}, u32[]{:S(2)}) collective-permute-start(bf16[3,128,128]{2,1,0:T(8,128)(2,1)} %get-tuple-element.45), channel_id=1, source_target_pairs={{0,496},{16,0},{32,16},{48,32},{64,48},{80,64},{96,80},{112,96},{1... | collective-permute-start | bytes 294920 | tf_op jit(solution)/shard_map/ppermute | solution.py:287
  30.6 7.6 %collective-permute-start.3 = (bf16[3,128,128]{2,1,0:T(8,128)(2,1)}, bf16[3,128,128]{2,1,0:T(8,128)(2,1)S(1)}, u32[]{:S(2)}, u32[]{:S(2)}) collective-permute-start(bf16[3,128,128]{2,1,0:T(8,128)(2,1)} %get-tuple-element.46), channel_id=1, source_target_pairs={{0,480},{16,496},{32,0},{48,16},{64,32},{80,48},{96,64},{112,80},{... | collective-permute-start | bytes 294920 | tf_op jit(solution)/shard_map/ppermute | solution.py:287
  45.7 22.8 %all-to-all-start.1 = ((bf16[16,128,128]{2,1,0:T(8,128)(2,1)}), bf16[16,128,128]{2,1,0:T(8,128)(2,1)}, u32[]{:S(2)}, u32[]{:S(2)}) async-start(bf16[16,128,128]{2,1,0:T(8,128)(2,1)} %get-tuple-element.48), calls=%async_computation.1 | async-start | bytes 1048576 | tf_op jit(solution)/shard_map/all_to_all | solution.py:291
  50.8 20.2 %collective-permute-start.4 = (bf16[3,128,128]{2,1,0:T(8,128)(2,1)}, bf16[3,128,128]{2,1,0:T(8,128)(2,1)S(1)}, u32[]{:S(2)}, u32[]{:S(2)}) collective-permute-start(bf16[3,128,128]{2,1,0:T(8,128)(2,1)} %get-tuple-element.49), channel_id=1, source_target_pairs={{0,32},{16,48},{32,64},{48,80},{64,96},{80,112},{96,128},{112,144}... | collective-permute-start | bytes 294920 | tf_op jit(solution)/shard_map/ppermute | solution.py:287
  52.7 18.3 %collective-permute-start.5 = (bf16[3,128,128]{2,1,0:T(8,128)(2,1)}, bf16[3,128,128]{2,1,0:T(8,128)(2,1)S(1)}, u32[]{:S(2)}, u32[]{:S(2)}) collective-permute-start(bf16[3,128,128]{2,1,0:T(8,128)(2,1)} %get-tuple-element.50), channel_id=1, source_target_pairs={{0,16},{16,32},{32,48},{48,64},{64,80},{80,96},{96,112},{112,128},... | collective-permute-start | bytes 294920 | tf_op jit(solution)/shard_map/ppermute | solution.py:287
  54.6 16.4 %collective-permute-start.6 = (bf16[3,128,128]{2,1,0:T(8,128)(2,1)}, bf16[3,128,128]{2,1,0:T(8,128)(2,1)S(1)}, u32[]{:S(2)}, u32[]{:S(2)}) collective-permute-start(bf16[3,128,128]{2,1,0:T(8,128)(2,1)} %get-tuple-element.51), channel_id=1, source_target_pairs={{0,496},{16,0},{32,16},{48,32},{64,48},{80,64},{96,80},{112,96},{1... | collective-permute-start | bytes 294920 | tf_op jit(solution)/shard_map/ppermute | solution.py:287
  64.3 8.1 %collective-permute-start.7 = (bf16[3,128,128]{2,1,0:T(8,128)(2,1)}, bf16[3,128,128]{2,1,0:T(8,128)(2,1)S(1)}, u32[]{:S(2)}, u32[]{:S(2)}) collective-permute-start(bf16[3,128,128]{2,1,0:T(8,128)(2,1)} %get-tuple-element.52), channel_id=1, source_target_pairs={{0,480},{16,496},{32,0},{48,16},{64,32},{80,48},{96,64},{112,80},{... | collective-permute-start | bytes 294920 | tf_op jit(solution)/shard_map/ppermute | solution.py:287
  71.0 12.3 %copy-start.7 = (bf16[3,128,128]{2,1,0:T(8,128)(2,1)S(1)}, bf16[3,128,128]{2,1,0:T(8,128)(2,1)}, u32[]{:S(2)}) copy-start(bf16[3,128,128]{2,1,0:T(8,128)(2,1)} %get-tuple-element.67) | copy-start | bytes 294916
  71.0 14.2 %copy-start.6 = (bf16[3,128,128]{2,1,0:T(8,128)(2,1)S(1)}, bf16[3,128,128]{2,1,0:T(8,128)(2,1)}, u32[]{:S(2)}) copy-start(bf16[3,128,128]{2,1,0:T(8,128)(2,1)} %get-tuple-element.68) | copy-start | bytes 294916
  71.0 16.1 %copy-start.5 = (bf16[3,128,128]{2,1,0:T(8,128)(2,1)S(1)}, bf16[3,128,128]{2,1,0:T(8,128)(2,1)}, u32[]{:S(2)}) copy-start(bf16[3,128,128]{2,1,0:T(8,128)(2,1)} %get-tuple-element.69) | copy-start | bytes 294916
  71.0 22.8 %copy-start.4 = (bf16[3,128,128]{2,1,0:T(8,128)(2,1)S(1)}, bf16[3,128,128]{2,1,0:T(8,128)(2,1)}, u32[]{:S(2)}) copy-start(bf16[3,128,128]{2,1,0:T(8,128)(2,1)} %get-tuple-element.70) | copy-start | bytes 294916
  76.3 24.4 %all-to-all-start.2 = ((bf16[16,128,128]{2,1,0:T(8,128)(2,1)}), bf16[16,128,128]{2,1,0:T(8,128)(2,1)}, u32[]{:S(2)}, u32[]{:S(2)}) async-start(bf16[16,128,128]{2,1,0:T(8,128)(2,1)} %shard_map.68), calls=%async_computation.2 | async-start | bytes 1048576 | tf_op jit(solution)/shard_map/all_to_all | solution.py:291
  83.3 19.9 %collective-permute-start.8 = (bf16[3,128,128]{2,1,0:T(8,128)(2,1)S(1)}, bf16[3,128,128]{2,1,0:T(8,128)(2,1)S(1)}, u32[]{:S(2)}, u32[]{:S(2)}) collective-permute-start(bf16[3,128,128]{2,1,0:T(8,128)(2,1)S(1)} %copy-done.7), channel_id=1, source_target_pairs={{0,32},{16,48},{32,64},{48,80},{64,96},{80,112},{96,128},{112,144}... | collective-permute-start | bytes 294920 | tf_op jit(solution)/shard_map/ppermute | solution.py:287
  85.2 18.0 %collective-permute-start.9 = (bf16[3,128,128]{2,1,0:T(8,128)(2,1)S(1)}, bf16[3,128,128]{2,1,0:T(8,128)(2,1)S(1)}, u32[]{:S(2)}, u32[]{:S(2)}) collective-permute-start(bf16[3,128,128]{2,1,0:T(8,128)(2,1)S(1)} %copy-done.6), channel_id=1, source_target_pairs={{0,16},{16,32},{32,48},{48,64},{64,80},{80,96},{96,112},{112,128},... | collective-permute-start | bytes 294920 | tf_op jit(solution)/shard_map/ppermute | solution.py:287
  87.1 16.1 %collective-permute-start.10 = (bf16[3,128,128]{2,1,0:T(8,128)(2,1)S(1)}, bf16[3,128,128]{2,1,0:T(8,128)(2,1)S(1)}, u32[]{:S(2)}, u32[]{:S(2)}) collective-permute-start(bf16[3,128,128]{2,1,0:T(8,128)(2,1)S(1)} %copy-done.5), channel_id=1, source_target_pairs={{0,496},{16,0},{32,16},{48,32},{64,48},{80,64},{96,80},{112,96},{1... | collective-permute-start | bytes 294920 | tf_op jit(solution)/shard_map/ppermute | solution.py:287
  93.8 9.4 %collective-permute-start.11 = (bf16[3,128,128]{2,1,0:T(8,128)(2,1)S(1)}, bf16[3,128,128]{2,1,0:T(8,128)(2,1)S(1)}, u32[]{:S(2)}, u32[]{:S(2)}) collective-permute-start(bf16[3,128,128]{2,1,0:T(8,128)(2,1)S(1)} %copy-done.4), channel_id=1, source_target_pairs={{0,480},{16,496},{32,0},{48,16},{64,32},{80,48},{96,64},{112,80},{... | collective-permute-start | bytes 294920 | tf_op jit(solution)/shard_map/ppermute | solution.py:287
  107.1 23.8 %all-to-all-start.3 = ((bf16[16,128,128]{2,1,0:T(8,128)(2,1)}), bf16[16,128,128]{2,1,0:T(8,128)(2,1)}, u32[]{:S(2)}, u32[]{:S(2)}) async-start(bf16[16,128,128]{2,1,0:T(8,128)(2,1)} %shard_map.69), calls=%async_computation.3 | async-start | bytes 1048576 | tf_op jit(solution)/shard_map/all_to_all | solution.py:291
  113.5 19.4 %collective-permute-start.12 = (bf16[3,128,128]{2,1,0:T(8,128)(2,1)}, bf16[3,128,128]{2,1,0:T(8,128)(2,1)S(1)}, u32[]{:S(2)}, u32[]{:S(2)}) collective-permute-start(bf16[3,128,128]{2,1,0:T(8,128)(2,1)} %get-tuple-element.75), channel_id=1, source_target_pairs={{0,32},{16,48},{32,64},{48,80},{64,96},{80,112},{96,128},{112,144}... | collective-permute-start | bytes 294920 | tf_op jit(solution)/shard_map/ppermute | solution.py:287
  115.4 17.5 %collective-permute-start.13 = (bf16[3,128,128]{2,1,0:T(8,128)(2,1)}, bf16[3,128,128]{2,1,0:T(8,128)(2,1)S(1)}, u32[]{:S(2)}, u32[]{:S(2)}) collective-permute-start(bf16[3,128,128]{2,1,0:T(8,128)(2,1)} %get-tuple-element.76), channel_id=1, source_target_pairs={{0,16},{16,32},{32,48},{48,64},{64,80},{80,96},{96,112},{112,128},... | collective-permute-start | bytes 294920 | tf_op jit(solution)/shard_map/ppermute | solution.py:287
  117.4 15.6 %collective-permute-start.14 = (bf16[3,128,128]{2,1,0:T(8,128)(2,1)}, bf16[3,128,128]{2,1,0:T(8,128)(2,1)S(1)}, u32[]{:S(2)}, u32[]{:S(2)}) collective-permute-start(bf16[3,128,128]{2,1,0:T(8,128)(2,1)} %get-tuple-element.77), channel_id=1, source_target_pairs={{0,496},{16,0},{32,16},{48,32},{64,48},{80,64},{96,80},{112,96},{1... | collective-permute-start | bytes 294920 | tf_op jit(solution)/shard_map/ppermute | solution.py:287
  124.1 8.9 %collective-permute-start.15 = (bf16[3,128,128]{2,1,0:T(8,128)(2,1)}, bf16[3,128,128]{2,1,0:T(8,128)(2,1)S(1)}, u32[]{:S(2)}, u32[]{:S(2)}) collective-permute-start(bf16[3,128,128]{2,1,0:T(8,128)(2,1)} %get-tuple-element.78), channel_id=1, source_target_pairs={{0,480},{16,496},{32,0},{48,16},{64,32},{80,48},{96,64},{112,80},{... | collective-permute-start | bytes 294920 | tf_op jit(solution)/shard_map/ppermute | solution.py:287
